TPU v7x, 32 devices: a whole 2x2x4 slice. The times are simulated.
32 devices in a mesh: section: 2 (over y), tensor: 4 (over x, core), dp: 4 (over z).
Axes of the slice: x: 2, y: 2, z: 4, core: 2. Of those that a mesh axis runs over, the one named last changes fastest.
Arguments:
- tokens: bfloat16 [12288, 768], P('dp'), may hold values from -6 to 6
- doc_lengths: int32 [8, 4], P('dp'), may hold values from 1 to 1152, 1536 in all within a row
- routes: int32 [2, 12288, 2], P('section', 'dp'), may hold values from 0 to 7, all different within a row; in each aligned block of 1536 rows (0 to 1535, 1536 to 3071, ..., all dimensions but the last counted through in order) at most 480 rows name the same one
- gain_attn: bfloat16 [2, 768], P('section'), may hold values from 0.5 to 1.5
- w_query: bfloat16 [2, 768, 768], P('section', None, 'tensor'), may hold values from -0.21875 to 0.21875
- w_key: bfloat16 [2, 768, 768], P('section', None, 'tensor'), may hold values from -0.21875 to 0.21875
- w_value: bfloat16 [2, 768, 768], P('section', None, 'tensor'), may hold values from -0.21875 to 0.21875
- w_output: bfloat16 [2, 768, 768], P('section', 'tensor'), may hold values from -0.875 to 0.875
- gain_ffn: bfloat16 [2, 768], P('section'), may hold values from 0.5 to 1.5
- w_router: bfloat16 [2, 768, 8], P('section'), may hold values from -0.15625 to 0.15625
- w_gate_exp: bfloat16 [2, 8, 768, 2048], P('section', None, None, 'tensor'), may hold values from -0.21875 to 0.21875
- w_up_exp: bfloat16 [2, 8, 768, 2048], P('section', None, None, 'tensor'), may hold values from -0.21875 to 0.21875
- w_down_exp: bfloat16 [2, 8, 2048, 768], P('section', None, 'tensor'), may hold values from -0.5 to 0.5
- w_gate_sh: bfloat16 [2, 768, 2048], P('section', None, 'tensor'), may hold values from -0.21875 to 0.21875
- w_up_sh: bfloat16 [2, 768, 2048], P('section', None, 'tensor'), may hold values from -0.21875 to 0.21875
- w_down_sh: bfloat16 [2, 2048, 768], P('section', 'tensor'), may hold values from -0.25 to 0.25
- cotangent: bfloat16 [12288, 768], P('dp'), may hold values from -6 to 6
Outputs:
- layer_out: bfloat16 [2, 12288, 768], P('section', 'dp')
- input_grad: float32 [2, 12288, 768], P('section', 'dp')
- grad_gain_attn: float32 [2, 768], P('section', 'dp')
- grad_query: float32 [2, 768, 768], P('section', 'dp', 'tensor')
- grad_key: float32 [2, 768, 768], P('section', 'dp', 'tensor')
- grad_value: float32 [2, 768, 768], P('section', 'dp', 'tensor')
- grad_output: float32 [2, 768, 768], P('section', 'tensor', 'dp')
- grad_gain_ffn: float32 [2, 768], P('section', 'dp')
- grad_router: float32 [2, 768, 8], P('section', 'dp')
- grad_gate_exp: float32 [2, 8, 768, 2048], P('section', None, 'dp', 'tensor')
- grad_up_exp: float32 [2, 8, 768, 2048], P('section', None, 'dp', 'tensor')
- grad_down_exp: float32 [2, 8, 2048, 768], P('section', None, 'tensor', 'dp')
- grad_gate_sh: float32 [2, 768, 2048], P('section', 'dp', 'tensor')
- grad_up_sh: float32 [2, 768, 2048], P('section', 'dp', 'tensor')
- grad_down_sh: float32 [2, 2048, 768], P('section', 'tensor', 'dp')
Inputs may be any that keep to these rules, and one draw needn't show every extreme that they name: `doc_lengths`: each row holds the lengths of 4 documents that fill one sequence of 1536 tokens. `routes`: each token names two different experts in each layer; within each sequence's 1536 tokens no expert is named by more than 480 tokens, and in some sequence one is named by exactly that many.
All inputs are finite; a program needn't handle non-finite values.
Results may differ from a plain program's by a relative error of at most 0.035.
Values may be sent and summed in bfloat16 or wider, within the bound.
A program may use at most 512 MiB of HBM per device.

v0:
```python
import jax
import jax.numpy as jnp
from jax import lax
from jax.sharding import PartitionSpec as P

HEAD_DIM = 64
EXPERTS = 8
SEQ_LEN = 1536
WINDOW = 1024
Q_BLOCK = 512
CAPACITY = 480


def from_behind(block, axis, distance):
    devices = range(lax.axis_size(axis))
    route = [(i - distance, i) for i in devices if i - distance in devices]
    return lax.ppermute(block, axis, route)


def rms_norm(values, gain):
    return gain * values * lax.rsqrt(jnp.mean(values * values, axis=-1, keepdims=True) + 1e-06)


def rotary_tables():
    half = HEAD_DIM // 2
    rates = jnp.exp(-jnp.log(10000.0) * jnp.arange(half, dtype=jnp.float32) * 2.0 / HEAD_DIM)
    angles = jnp.arange(SEQ_LEN, dtype=jnp.float32)[:, None] * rates[None, :]
    return (jnp.cos(angles)[:, None, :], jnp.sin(angles)[:, None, :])


def rotate(values, cosine, sine):
    half = HEAD_DIM // 2
    first = values[..., :half]
    second = values[..., half:]
    return jnp.concatenate(
        [first * cosine - second * sine, second * cosine + first * sine], axis=-1
    )


def document_ids(lengths):
    ends = jnp.cumsum(lengths)
    positions = jnp.arange(SEQ_LEN, dtype=jnp.int32)
    return jnp.sum((positions[:, None] >= ends[None, :]).astype(jnp.int32), axis=1)


def allowed_keys(index, padded):
    starting = index * Q_BLOCK
    query_pos = starting + jnp.arange(Q_BLOCK, dtype=jnp.int32)
    key_pos = starting - WINDOW + jnp.arange(WINDOW + Q_BLOCK, dtype=jnp.int32)
    query_doc = lax.dynamic_slice_in_dim(padded, starting + WINDOW, Q_BLOCK, 0)
    key_doc = lax.dynamic_slice_in_dim(padded, starting, WINDOW + Q_BLOCK, 0)
    causal = key_pos[None, :] <= query_pos[:, None]
    inside = query_pos[:, None] - key_pos[None, :] < WINDOW
    return causal & inside & (query_doc[:, None] == key_doc[None, :])


def routing(routes):
    flat = routes.reshape(-1)
    onehot = (flat[:, None] == jnp.arange(EXPERTS, dtype=jnp.int32)[None, :]).astype(jnp.int32)
    before = jnp.cumsum(onehot, axis=0) - onehot
    rank = jnp.sum(before * onehot, axis=1)
    slot = flat * CAPACITY + rank
    order = jnp.arange(2 * SEQ_LEN, dtype=jnp.int32)
    source_route = jnp.full((EXPERTS * CAPACITY,), 2 * SEQ_LEN, jnp.int32).at[slot].set(order)
    return (slot.reshape(SEQ_LEN, 2), source_route)


def guarded(active, work, operands):

    def busy(items):
        return work(*items)

    def resting(items):
        return jax.tree.map(lambda value: jnp.zeros(value.shape, value.dtype), work(*items))

    return lax.cond(active, busy, resting, operands)


def padded_inputs(keys, values, doc_ids):
    blank = jnp.zeros((WINDOW,) + keys.shape[1:], jnp.bfloat16)
    key_pad = jnp.concatenate([blank, keys], axis=0)
    value_pad = jnp.concatenate([blank, values], axis=0)
    id_pad = jnp.concatenate([jnp.full((WINDOW,), -1, jnp.int32), doc_ids])
    return (key_pad, value_pad, id_pad)


def attention_forward(query, keys, values, doc_ids):
    scale = HEAD_DIM ** (-0.5)
    key_pad, value_pad, id_pad = padded_inputs(keys, values, doc_ids)

    def block(index):
        starting = index * Q_BLOCK
        query_block = lax.dynamic_slice_in_dim(query, starting, Q_BLOCK, 0)
        key_block = lax.dynamic_slice_in_dim(key_pad, starting, WINDOW + Q_BLOCK, 0)
        value_block = lax.dynamic_slice_in_dim(value_pad, starting, WINDOW + Q_BLOCK, 0)
        scores = (
            jnp.einsum("qhd,khd->hqk", query_block, key_block, preferred_element_type=jnp.float32)
            * scale
        )
        masked = jnp.where(allowed_keys(index, id_pad)[None], scores, -1e30)
        top = jnp.max(masked, axis=-1, keepdims=True)
        weights = jnp.exp(masked - top)
        total = jnp.sum(weights, axis=-1, keepdims=True)
        probs = (weights / total).astype(jnp.bfloat16)
        mixed = jnp.einsum("hqk,khd->qhd", probs, value_block, preferred_element_type=jnp.float32)
        return (mixed, (top + jnp.log(total))[..., 0])

    mixed, logsum = lax.map(block, jnp.arange(SEQ_LEN // Q_BLOCK, dtype=jnp.int32))
    return (mixed.reshape(SEQ_LEN, query.shape[1], HEAD_DIM), logsum)


def attention_backward(query, keys, values, doc_ids, logsum, grad_mixed):
    scale = HEAD_DIM ** (-0.5)
    key_pad, value_pad, id_pad = padded_inputs(keys, values, doc_ids)
    empty = jnp.zeros(key_pad.shape, jnp.float32)

    def block(carry, index):
        key_grads, value_grads = carry
        starting = index * Q_BLOCK
        query_block = lax.dynamic_slice_in_dim(query, starting, Q_BLOCK, 0)
        key_block = lax.dynamic_slice_in_dim(key_pad, starting, WINDOW + Q_BLOCK, 0)
        value_block = lax.dynamic_slice_in_dim(value_pad, starting, WINDOW + Q_BLOCK, 0)
        grad_block = lax.dynamic_slice_in_dim(grad_mixed, starting, Q_BLOCK, 0)
        scores = (
            jnp.einsum("qhd,khd->hqk", query_block, key_block, preferred_element_type=jnp.float32)
            * scale
        )
        masked = jnp.where(allowed_keys(index, id_pad)[None], scores, -1e30)
        probs = jnp.exp(masked - logsum[index][:, :, None])
        value_part = jnp.einsum(
            "hqk,qhd->khd",
            probs.astype(jnp.bfloat16),
            grad_block,
            preferred_element_type=jnp.float32,
        )
        grad_probs = jnp.einsum(
            "qhd,khd->hqk", grad_block, value_block, preferred_element_type=jnp.float32
        )
        inner = jnp.sum(probs * grad_probs, axis=-1, keepdims=True)
        grad_scores = (probs * (grad_probs - inner)).astype(jnp.bfloat16)
        query_part = (
            jnp.einsum("hqk,khd->qhd", grad_scores, key_block, preferred_element_type=jnp.float32)
            * scale
        )
        key_part = (
            jnp.einsum("hqk,qhd->khd", grad_scores, query_block, preferred_element_type=jnp.float32)
            * scale
        )
        key_grads = lax.dynamic_update_slice_in_dim(
            key_grads,
            lax.dynamic_slice_in_dim(key_grads, starting, WINDOW + Q_BLOCK, 0) + key_part,
            starting,
            0,
        )
        value_grads = lax.dynamic_update_slice_in_dim(
            value_grads,
            lax.dynamic_slice_in_dim(value_grads, starting, WINDOW + Q_BLOCK, 0) + value_part,
            starting,
            0,
        )
        return ((key_grads, value_grads), query_part)

    (key_grads, value_grads), query_parts = lax.scan(
        block, (empty, empty), jnp.arange(SEQ_LEN // Q_BLOCK, dtype=jnp.int32)
    )
    return (
        query_parts.reshape(query.shape[0], query.shape[1], HEAD_DIM),
        key_grads[WINDOW:],
        value_grads[WINDOW:],
    )


def attention_inputs(layer_in, params, cosine, sine):
    gain_attn, w_query, w_key, w_value = (params[0], params[1], params[2], params[3])
    heads = w_query.shape[1] // HEAD_DIM
    normed = rms_norm(layer_in, gain_attn).astype(jnp.bfloat16)
    query_pre = jnp.dot(normed, w_query, preferred_element_type=jnp.float32).reshape(
        SEQ_LEN, heads, HEAD_DIM
    )
    key_pre = jnp.dot(normed, w_key, preferred_element_type=jnp.float32).reshape(
        SEQ_LEN, heads, HEAD_DIM
    )
    values = (
        jnp.dot(normed, w_value, preferred_element_type=jnp.float32)
        .reshape(SEQ_LEN, heads, HEAD_DIM)
        .astype(jnp.bfloat16)
    )
    query = rotate(query_pre, cosine, sine).astype(jnp.bfloat16)
    keys = rotate(key_pre, cosine, sine).astype(jnp.bfloat16)
    return (normed, query_pre, key_pre, query, keys, values)


def attention_part(layer_in, doc_ids, params, cosine, sine):
    normed, query_pre, key_pre, query, keys, values = attention_inputs(
        layer_in, params, cosine, sine
    )
    mixed, logsum = attention_forward(query, keys, values, doc_ids)
    mixed = mixed.reshape(SEQ_LEN, -1).astype(jnp.bfloat16)
    return (jnp.dot(mixed, params[4], preferred_element_type=jnp.float32), mixed, logsum)


def feed_inputs(state, routes, params):
    normed = rms_norm(state, params[5]).astype(jnp.bfloat16)
    logits = jnp.dot(normed, params[6], preferred_element_type=jnp.float32)
    slot, source_route = routing(routes)
    padded = jnp.concatenate([normed, jnp.zeros((1, normed.shape[1]), jnp.bfloat16)], axis=0)
    expert_in = padded[source_route // 2].reshape(EXPERTS, CAPACITY, normed.shape[1])
    return (normed, logits, slot, source_route, expert_in)


def gate_choice(logits, routes):
    return jnp.take_along_axis(jax.nn.softmax(logits, axis=-1), routes, axis=1)


def expert_forward(expert_in, params):
    gate_value = jnp.einsum(
        "ecd,edf->ecf", expert_in, params[7], preferred_element_type=jnp.float32
    )
    lift_value = jnp.einsum(
        "ecd,edf->ecf", expert_in, params[8], preferred_element_type=jnp.float32
    )
    hidden = (jax.nn.silu(gate_value) * lift_value).astype(jnp.bfloat16)
    expert_out = jnp.einsum("ecf,efd->ecd", hidden, params[9], preferred_element_type=jnp.float32)
    return (gate_value, lift_value, hidden, expert_out.reshape(EXPERTS * CAPACITY, -1))


def shared_forward(normed, params):
    shared_gate = jnp.dot(normed, params[10], preferred_element_type=jnp.float32)
    shared_lift = jnp.dot(normed, params[11], preferred_element_type=jnp.float32)
    shared_hidden = (jax.nn.silu(shared_gate) * shared_lift).astype(jnp.bfloat16)
    return (shared_gate, shared_lift, shared_hidden)


def ffn_part(state, routes, params):
    normed, logits, slot, source_route, expert_in = feed_inputs(state, routes, params)
    gates = gate_choice(logits, routes)
    gate_value, lift_value, hidden, expert_out = expert_forward(expert_in, params)
    routed = gates[:, 0:1] * expert_out[slot[:, 0]] + gates[:, 1:2] * expert_out[slot[:, 1]]
    shared_gate, shared_lift, shared_hidden = shared_forward(normed, params)
    shared_out = jnp.dot(shared_hidden, params[12], preferred_element_type=jnp.float32)
    return routed + shared_out


def swish_grads(grad_hidden, gate_value, lift_value):
    sigma = jax.nn.sigmoid(gate_value)
    grad_gate = grad_hidden * lift_value * sigma * (1.0 + gate_value * (1.0 - sigma))
    grad_lift = grad_hidden * gate_value * sigma
    return (grad_gate.astype(jnp.bfloat16), grad_lift.astype(jnp.bfloat16))


def ffn_backward(state, grad_out, routes, params):
    normed, logits, slot, source_route, expert_in = feed_inputs(state, routes, params)
    gates = gate_choice(logits, routes)
    gate_value, lift_value, hidden, expert_out = expert_forward(expert_in, params)
    width = grad_out.shape[1]
    grad_rows = jnp.concatenate([grad_out, jnp.zeros((1, width), jnp.float32)], axis=0)
    gate_rows = jnp.concatenate([gates.reshape(-1), jnp.zeros((1,), jnp.float32)], axis=0)
    grad_expert = (gate_rows[source_route][:, None] * grad_rows[source_route // 2]).astype(
        jnp.bfloat16
    )
    grad_expert = grad_expert.reshape(EXPERTS, CAPACITY, width)
    grad_down_exp = jnp.einsum(
        "ecf,ecd->efd", hidden, grad_expert, preferred_element_type=jnp.float32
    )
    grad_hidden = jnp.einsum(
        "ecd,efd->ecf", grad_expert, params[9], preferred_element_type=jnp.float32
    )
    grad_gate, grad_lift = swish_grads(grad_hidden, gate_value, lift_value)
    grad_gate_exp = jnp.einsum(
        "ecd,ecf->edf", expert_in, grad_gate, preferred_element_type=jnp.float32
    )
    grad_up_exp = jnp.einsum(
        "ecd,ecf->edf", expert_in, grad_lift, preferred_element_type=jnp.float32
    )
    grad_slots = jnp.einsum(
        "ecf,edf->ecd", grad_gate, params[7], preferred_element_type=jnp.float32
    )
    grad_slots = grad_slots + jnp.einsum(
        "ecf,edf->ecd", grad_lift, params[8], preferred_element_type=jnp.float32
    )
    grad_slots = grad_slots.reshape(EXPERTS * CAPACITY, width)
    routed_grad = grad_slots[slot[:, 0]] + grad_slots[slot[:, 1]]
    grad_choice = jnp.stack(
        [
            jnp.sum(grad_out * expert_out[slot[:, 0]], axis=1),
            jnp.sum(grad_out * expert_out[slot[:, 1]], axis=1),
        ],
        axis=1,
    )
    shared_gate, shared_lift, shared_hidden = shared_forward(normed, params)
    grad_shared = grad_out.astype(jnp.bfloat16)
    grad_down_sh = jnp.einsum(
        "tf,td->fd", shared_hidden, grad_shared, preferred_element_type=jnp.float32
    )
    shared_grad_hidden = jnp.einsum(
        "td,fd->tf", grad_shared, params[12], preferred_element_type=jnp.float32
    )
    shared_grad_gate, shared_grad_lift = swish_grads(shared_grad_hidden, shared_gate, shared_lift)
    grad_gate_sh = jnp.einsum(
        "td,tf->df", normed, shared_grad_gate, preferred_element_type=jnp.float32
    )
    grad_up_sh = jnp.einsum(
        "td,tf->df", normed, shared_grad_lift, preferred_element_type=jnp.float32
    )
    shared_in = jnp.einsum(
        "tf,df->td", shared_grad_gate, params[10], preferred_element_type=jnp.float32
    )
    shared_in = shared_in + jnp.einsum(
        "tf,df->td", shared_grad_lift, params[11], preferred_element_type=jnp.float32
    )
    weight_grads = (
        grad_gate_exp,
        grad_up_exp,
        grad_down_exp,
        grad_gate_sh,
        grad_up_sh,
        grad_down_sh,
    )
    return (weight_grads, routed_grad + shared_in, grad_choice)


def attention_grads(
    layer_in,
    state,
    mixed,
    logsum,
    grad_out,
    grad_normed_sum,
    grad_choice,
    routes,
    doc_ids,
    params,
    cosine,
    sine,
):
    gain_ffn, w_router, w_output = (params[5], params[6], params[4])
    normed_ffn = rms_norm(state, gain_ffn).astype(jnp.bfloat16)
    logits = jnp.dot(normed_ffn, w_router, preferred_element_type=jnp.float32)
    unused, pull_gates = jax.vjp(lambda values: gate_choice(values, routes), logits)
    grad_logits = pull_gates(grad_choice)[0].astype(jnp.bfloat16)
    grad_router = jnp.einsum(
        "td,te->de", normed_ffn, grad_logits, preferred_element_type=jnp.float32
    )
    grad_normed = grad_normed_sum + jnp.einsum(
        "te,de->td", grad_logits, w_router, preferred_element_type=jnp.float32
    )
    unused, pull_norm = jax.vjp(rms_norm, state, gain_ffn.astype(jnp.float32))
    grad_from_norm, grad_gain_ffn = pull_norm(grad_normed)
    grad_state = grad_out + grad_from_norm
    grad_attn = grad_state.astype(jnp.bfloat16)
    grad_output = jnp.einsum("tk,td->kd", mixed, grad_attn, preferred_element_type=jnp.float32)
    normed, query_pre, key_pre, query, keys, values = attention_inputs(
        layer_in, params, cosine, sine
    )
    grad_mixed = jnp.einsum(
        "td,kd->tk", grad_attn, w_output, preferred_element_type=jnp.float32
    ).astype(jnp.bfloat16)
    grad_mixed = grad_mixed.reshape(query.shape)
    grad_query, grad_keys, grad_values = attention_backward(
        query, keys, values, doc_ids, logsum, grad_mixed
    )
    unused, pull_rotate = jax.vjp(lambda values: rotate(values, cosine, sine), query_pre)
    grad_query = pull_rotate(grad_query)[0].reshape(SEQ_LEN, -1).astype(jnp.bfloat16)
    grad_keys = pull_rotate(grad_keys)[0].reshape(SEQ_LEN, -1).astype(jnp.bfloat16)
    grad_values = grad_values.reshape(SEQ_LEN, -1).astype(jnp.bfloat16)
    grad_w_query = jnp.einsum("td,tk->dk", normed, grad_query, preferred_element_type=jnp.float32)
    grad_w_key = jnp.einsum("td,tk->dk", normed, grad_keys, preferred_element_type=jnp.float32)
    grad_w_value = jnp.einsum("td,tk->dk", normed, grad_values, preferred_element_type=jnp.float32)
    grad_normed_attn = jnp.einsum(
        "tk,dk->td", grad_query, params[1], preferred_element_type=jnp.float32
    )
    grad_normed_attn = grad_normed_attn + jnp.einsum(
        "tk,dk->td", grad_keys, params[2], preferred_element_type=jnp.float32
    )
    grad_normed_attn = grad_normed_attn + jnp.einsum(
        "tk,dk->td", grad_values, params[3], preferred_element_type=jnp.float32
    )
    weight_grads = (grad_output, grad_gain_ffn, grad_router, grad_w_query, grad_w_key, grad_w_value)
    return (weight_grads, grad_state, grad_normed_attn)


def input_part(layer_in, gain_attn, grad_normed_attn, grad_state):
    unused, pull_norm = jax.vjp(rms_norm, layer_in, gain_attn.astype(jnp.float32))
    grad_layer, grad_gain_attn = pull_norm(grad_normed_attn)
    return (grad_gain_attn, grad_state + grad_layer)


def on_device(
    tokens,
    doc_lengths,
    routes,
    gain_attn,
    w_query,
    w_key,
    w_value,
    w_output,
    gain_ffn,
    w_router,
    w_gate_exp,
    w_up_exp,
    w_down_exp,
    w_gate_sh,
    w_up_sh,
    w_down_sh,
    cotangent,
):
    params = tuple(
        (
            weight[0]
            for weight in (
                gain_attn,
                w_query,
                w_key,
                w_value,
                w_output,
                gain_ffn,
                w_router,
                w_gate_exp,
                w_up_exp,
                w_down_exp,
                w_gate_sh,
                w_up_sh,
                w_down_sh,
            )
        )
    )
    section = lax.axis_index("section")
    micro_count = doc_lengths.shape[0]
    width = tokens.shape[1]
    heads = w_query.shape[2] // HEAD_DIM
    blocks = SEQ_LEN // Q_BLOCK
    cosine, sine = rotary_tables()
    route_rows = routes[0]
    doc_ids_all = jax.vmap(document_ids)(doc_lengths)

    def micro_rows(source, index):
        return lax.dynamic_slice_in_dim(source, index * SEQ_LEN, SEQ_LEN, 0)

    def store(buffer, index, value, active):
        current = lax.dynamic_slice_in_dim(buffer, index, 1, 0)
        return lax.dynamic_update_slice_in_dim(
            buffer, jnp.where(active, value[None], current), index, 0
        )

    def forward_tick(tick, carry):
        received, inputs_kept, states_kept, mixed_kept, logsum_kept, outputs = carry
        index_raw = tick - section
        active = (index_raw >= 0) & (index_raw < micro_count)
        index = jnp.clip(index_raw, 0, micro_count - 1)
        layer_in = jnp.where(
            section == 0,
            micro_rows(tokens, index).astype(jnp.float32),
            received.astype(jnp.float32),
        )
        doc_ids = doc_ids_all[index]
        rows = micro_rows(route_rows, index)
        partial_value, mixed, logsum = guarded(
            active,
            lambda values, marks: attention_part(values, marks, params, cosine, sine),
            (layer_in, doc_ids),
        )
        state = layer_in + lax.psum(partial_value.astype(jnp.bfloat16), "tensor").astype(
            jnp.float32
        )
        branch = guarded(
            active, lambda values, choices: ffn_part(values, choices, params), (state, rows)
        )
        result = (
            state + lax.psum(branch.astype(jnp.bfloat16), "tensor").astype(jnp.float32)
        ).astype(jnp.bfloat16)
        inputs_kept = store(inputs_kept, index, layer_in, active)
        states_kept = store(states_kept, index, state, active)
        mixed_kept = store(mixed_kept, index, mixed, active)
        logsum_kept = store(logsum_kept, index, logsum, active)
        outputs = store(outputs, index, result, active)
        received = from_behind(result, "section", 1)
        return (received, inputs_kept, states_kept, mixed_kept, logsum_kept, outputs)

    start_forward = (
        jnp.zeros((SEQ_LEN, width), jnp.bfloat16),
        jnp.zeros((micro_count, SEQ_LEN, width), jnp.float32),
        jnp.zeros((micro_count, SEQ_LEN, width), jnp.float32),
        jnp.zeros((micro_count, SEQ_LEN, heads * HEAD_DIM), jnp.bfloat16),
        jnp.zeros((micro_count, blocks, heads, Q_BLOCK), jnp.float32),
        jnp.zeros((micro_count, SEQ_LEN, width), jnp.bfloat16),
    )
    unused, inputs_kept, states_kept, mixed_kept, logsum_kept, outputs = lax.fori_loop(
        0, micro_count + 1, forward_tick, start_forward
    )
    totals = tuple((jnp.zeros(weight.shape, jnp.float32) for weight in params))

    def backward_tick(tick, carry):
        received, totals, input_grads = carry
        index_raw = tick - 1 + section
        active = (index_raw >= 0) & (index_raw < micro_count)
        index = jnp.clip(index_raw, 0, micro_count - 1)
        grad_out = jnp.where(
            section == 1,
            micro_rows(cotangent, index).astype(jnp.float32),
            received.astype(jnp.float32),
        )
        layer_in = inputs_kept[index]
        state = states_kept[index]
        rows = micro_rows(route_rows, index)
        doc_ids = doc_ids_all[index]
        ffn_grads, grad_part, choice_part = guarded(
            active,
            lambda values, grads, choices: ffn_backward(values, grads, choices, params),
            (state, grad_out, rows),
        )
        grad_normed_sum, grad_choice = (
            lax.psum(grad_part.astype(jnp.bfloat16), "tensor").astype(jnp.float32),
            lax.psum(choice_part.astype(jnp.bfloat16), "tensor").astype(jnp.float32),
        )
        attn_grads, grad_state, grad_attn_part = guarded(
            active,
            lambda *items: attention_grads(*items, params, cosine, sine),
            (
                layer_in,
                state,
                mixed_kept[index],
                logsum_kept[index],
                grad_out,
                grad_normed_sum,
                grad_choice,
                rows,
                doc_ids,
            ),
        )
        grad_normed_attn = lax.psum(grad_attn_part.astype(jnp.bfloat16), "tensor").astype(
            jnp.float32
        )
        grad_gain_attn, grad_input = guarded(
            active,
            lambda values, grads, states: input_part(values, params[0], grads, states),
            (layer_in, grad_normed_attn, grad_state),
        )
        input_grads = store(input_grads, index, grad_input, active)
        received = from_behind(grad_input.astype(jnp.bfloat16), "section", -1)
        grad_output, grad_gain_ffn, grad_router, grad_w_query, grad_w_key, grad_w_value = attn_grads
        grad_gate_exp, grad_up_exp, grad_down_exp, grad_gate_sh, grad_up_sh, grad_down_sh = (
            ffn_grads
        )
        tick_grads = (
            grad_gain_attn,
            grad_w_query,
            grad_w_key,
            grad_w_value,
            grad_output,
            grad_gain_ffn,
            grad_router,
            grad_gate_exp,
            grad_up_exp,
            grad_down_exp,
            grad_gate_sh,
            grad_up_sh,
            grad_down_sh,
        )
        totals = tuple(jax.tree.map(jnp.add, totals, tick_grads))
        return (received, totals, input_grads)

    start_backward = (
        jnp.zeros((SEQ_LEN, width), jnp.bfloat16),
        totals,
        jnp.zeros((micro_count, SEQ_LEN, width), jnp.float32),
    )
    unused, totals, input_grads = lax.fori_loop(0, micro_count + 1, backward_tick, start_backward)
    totals = (
        lax.psum_scatter(
            totals[0].astype(jnp.bfloat16), "dp", scatter_dimension=0, tiled=True
        ).astype(jnp.float32),
        lax.psum_scatter(
            totals[1].astype(jnp.bfloat16), "dp", scatter_dimension=0, tiled=True
        ).astype(jnp.float32),
        lax.psum_scatter(
            totals[2].astype(jnp.bfloat16), "dp", scatter_dimension=0, tiled=True
        ).astype(jnp.float32),
        lax.psum_scatter(
            totals[3].astype(jnp.bfloat16), "dp", scatter_dimension=0, tiled=True
        ).astype(jnp.float32),
        lax.psum_scatter(
            totals[4].astype(jnp.bfloat16), "dp", scatter_dimension=1, tiled=True
        ).astype(jnp.float32),
        lax.psum_scatter(
            totals[5].astype(jnp.bfloat16), "dp", scatter_dimension=0, tiled=True
        ).astype(jnp.float32),
        lax.psum_scatter(
            totals[6].astype(jnp.bfloat16), "dp", scatter_dimension=0, tiled=True
        ).astype(jnp.float32),
        lax.psum_scatter(
            totals[7].astype(jnp.bfloat16), "dp", scatter_dimension=1, tiled=True
        ).astype(jnp.float32),
        lax.psum_scatter(
            totals[8].astype(jnp.bfloat16), "dp", scatter_dimension=1, tiled=True
        ).astype(jnp.float32),
        lax.psum_scatter(
            totals[9].astype(jnp.bfloat16), "dp", scatter_dimension=2, tiled=True
        ).astype(jnp.float32),
        lax.psum_scatter(
            totals[10].astype(jnp.bfloat16), "dp", scatter_dimension=0, tiled=True
        ).astype(jnp.float32),
        lax.psum_scatter(
            totals[11].astype(jnp.bfloat16), "dp", scatter_dimension=0, tiled=True
        ).astype(jnp.float32),
        lax.psum_scatter(
            totals[12].astype(jnp.bfloat16), "dp", scatter_dimension=1, tiled=True
        ).astype(jnp.float32),
    )
    layer_out = outputs.reshape(1, micro_count * SEQ_LEN, width)
    input_grad = input_grads.reshape(1, micro_count * SEQ_LEN, width)
    return (
        layer_out,
        input_grad,
        totals[0][None],
        totals[1][None],
        totals[2][None],
        totals[3][None],
        totals[4][None],
        totals[5][None],
        totals[6][None],
        totals[7][None],
        totals[8][None],
        totals[9][None],
        totals[10][None],
        totals[11][None],
        totals[12][None],
    )


def solution(mesh):
    return jax.shard_map(
        on_device,
        mesh=mesh,
        in_specs=(
            P("dp", None),
            P("dp", None),
            P("section", "dp", None),
            P("section", None),
            P("section", None, "tensor"),
            P("section", None, "tensor"),
            P("section", None, "tensor"),
            P("section", "tensor", None),
            P("section", None),
            P("section", None, None),
            P("section", None, None, "tensor"),
            P("section", None, None, "tensor"),
            P("section", None, "tensor", None),
            P("section", None, "tensor"),
            P("section", None, "tensor"),
            P("section", "tensor", None),
            P("dp", None),
        ),
        out_specs=(
            P("section", "dp", None),
            P("section", "dp", None),
            P("section", "dp"),
            P("section", "dp", "tensor"),
            P("section", "dp", "tensor"),
            P("section", "dp", "tensor"),
            P("section", "tensor", "dp"),
            P("section", "dp"),
            P("section", "dp", None),
            P("section", None, "dp", "tensor"),
            P("section", None, "dp", "tensor"),
            P("section", None, "tensor", "dp"),
            P("section", "dp", "tensor"),
            P("section", "dp", "tensor"),
            P("section", "tensor", "dp"),
        ),
        check_vma=False,
    )
```

profile of v0, /device:TPU:0, one launch (start us, length us, event | category | flops | bytes accessed | tf_op | source)
XLA Modules:
  0.0 3787.2 jit_solution(9086900416086377808)
XLA Ops:
  29.8 1108.0 %while.117 = (s32[]{:T(128)}, bf16[1536,768]{1,0:T(8,128)(2,1)S(1)}, f32[2,1536,768]{2,1,0:T(8,128)}, f32[2,1536,768]{2,1,0:T(8,128)}, bf16[2,1536,192]{1,2,0:T(...) while((s32[]{:T(128)}, bf16[1536,768]{1,0:T(8,128)(2,1)S(1)}, ...), condition=%wide.region_21.23_spmd.clone.clone.clone, body=%wide.region_2.22_spmd.clone.clone.clone.sunk | while | flops 15212099584 | bytes 345143584 | solution.py:487
  61.1 49.2 %conditional.28 = (bf16[1536,768]{1,0:T(8,128)(2,1)}, bf16[1,1536,192]{1,2,0:T(8,128)(2,1)}, f32[1,3,3,512]{3,2,1,0:T(4,128)}) conditional(s32[]{:T(128)} %convert_element_type.590, () %tuple.333, (bf16[768]{0:T(1024)(128)(2,1)S(1)}, f32[1536,768]{1,0:T(8,128)}, bf16[768,192]{1,0:T(8,128)(2,1)S(1)}, f32[1536,1,32]{0,2,1:T(8,128)S(1)}, ...), branch_computations={%region_3.3_spmd, %region_4.9_spmd.clone} | conditional | flops 2462124800 | bytes 77081168 | solution.py:76
  72.3 33.5 while.115
  110.3 57.5 %all-reduce.21.cloned.1.call-done = bf16[1536,768]{1,0:T(8,128)(2,1)} async-done(((bf16[1536,768]{1,0:T(8,128)(2,1)}), bf16[1536,768]{1,0:T(8,128)(2,1)}) %all-reduce.21.cloned.1.call-update) | async-done | bytes 2359312 | tf_op jit(solution)/shard_map/while/body/eval_jaxpr/psum | solution.py:462
  176.7 121.2 %conditional.29 = (bf16[1536,768]{1,0:T(8,128)(2,1)}) conditional(s32[]{:T(128)} %convert_element_type.590, () %tuple.335, (bf16[768]{0:T(1024)(128)(2,1)S(1)}, f32[1536,768]{1,0:T(8,128)}, bf16[768,8]{0,1:T(8,128)(2,1)S(1)}, s32[3072,2]{1,0:T(8,128)S(1)}, s32[]{:T(128)}, /*index=5*/bf16[8,768,512]{2,1,0:T(8,128)(2,1)}, ...), branch_computations={%region_11.11_spmd, %region_12.20_spmd} | conditional | flops 12734290944 | bytes 165980160 | solution.py:76
  225.1 14.5 fusion.60
  263.8 18.2 gather_fusion.11
  298.0 55.0 %all-reduce.23.cloned.1.call-done = bf16[1536,768]{1,0:T(8,128)(2,1)} async-done(((bf16[1536,768]{1,0:T(8,128)(2,1)}), bf16[1536,768]{1,0:T(8,128)(2,1)}) %all-reduce.23.cloned.1.call-update) | async-done | bytes 2359312 | tf_op jit(solution)/shard_map/while/body/eval_jaxpr/psum | solution.py:469
  366.9 47.0 %collective-permute-done.1 = bf16[1536,768]{1,0:T(8,128)(2,1)S(1)} collective-permute-done((bf16[1536,768]{1,0:T(8,128)(2,1)}, bf16[1536,768]{1,0:T(8,128)(2,1)S(1)}, u32[]{:S(2)}, u32[]{:S(2)}) %collective-permute-start.1) | collective-permute-done | bytes 2359328 | tf_op jit(solution)/shard_map/while/body/eval_jaxpr/ppermute | solution.py:17
  422.7 49.2 %conditional.28 = (bf16[1536,768]{1,0:T(8,128)(2,1)}, bf16[1,1536,192]{1,2,0:T(8,128)(2,1)}, f32[1,3,3,512]{3,2,1,0:T(4,128)}) conditional(s32[]{:T(128)} %convert_element_type.590, () %tuple.333, (bf16[768]{0:T(1024)(128)(2,1)S(1)}, f32[1536,768]{1,0:T(8,128)}, bf16[768,192]{1,0:T(8,128)(2,1)S(1)}, f32[1536,1,32]{0,2,1:T(8,128)S(1)}, ...), branch_computations={%region_3.3_spmd, %region_4.9_spmd.clone} | conditional | flops 2462124800 | bytes 77081168 | solution.py:76
  433.9 33.5 while.115
  472.0 56.8 %all-reduce.21.cloned.1.call-done = bf16[1536,768]{1,0:T(8,128)(2,1)} async-done(((bf16[1536,768]{1,0:T(8,128)(2,1)}), bf16[1536,768]{1,0:T(8,128)(2,1)}) %all-reduce.21.cloned.1.call-update) | async-done | bytes 2359312 | tf_op jit(solution)/shard_map/while/body/eval_jaxpr/psum | solution.py:462
  537.7 121.3 %conditional.29 = (bf16[1536,768]{1,0:T(8,128)(2,1)}) conditional(s32[]{:T(128)} %convert_element_type.590, () %tuple.335, (bf16[768]{0:T(1024)(128)(2,1)S(1)}, f32[1536,768]{1,0:T(8,128)}, bf16[768,8]{0,1:T(8,128)(2,1)S(1)}, s32[3072,2]{1,0:T(8,128)S(1)}, s32[]{:T(128)}, /*index=5*/bf16[8,768,512]{2,1,0:T(8,128)(2,1)}, ...), branch_computations={%region_11.11_spmd, %region_12.20_spmd} | conditional | flops 12734290944 | bytes 165980160 | solution.py:76
  586.1 14.5 fusion.60
  624.9 18.2 gather_fusion.11
  659.0 55.8 %all-reduce.23.cloned.1.call-done = bf16[1536,768]{1,0:T(8,128)(2,1)} async-done(((bf16[1536,768]{1,0:T(8,128)(2,1)}), bf16[1536,768]{1,0:T(8,128)(2,1)}) %all-reduce.23.cloned.1.call-update) | async-done | bytes 2359312 | tf_op jit(solution)/shard_map/while/body/eval_jaxpr/psum | solution.py:469
  728.8 47.0 %collective-permute-done.1 = bf16[1536,768]{1,0:T(8,128)(2,1)S(1)} collective-permute-done((bf16[1536,768]{1,0:T(8,128)(2,1)}, bf16[1536,768]{1,0:T(8,128)(2,1)S(1)}, u32[]{:S(2)}, u32[]{:S(2)}) %collective-permute-start.1) | collective-permute-done | bytes 2359328 | tf_op jit(solution)/shard_map/while/body/eval_jaxpr/ppermute | solution.py:17
  787.7 103.0 %all-reduce.21.cloned.1.call-done = bf16[1536,768]{1,0:T(8,128)(2,1)} async-done(((bf16[1536,768]{1,0:T(8,128)(2,1)}), bf16[1536,768]{1,0:T(8,128)(2,1)}) %all-reduce.21.cloned.1.call-update) | async-done | bytes 2359312 | tf_op jit(solution)/shard_map/while/body/eval_jaxpr/psum | solution.py:462
  901.3 175.6 %all-reduce.23.cloned.1.call-done = bf16[1536,768]{1,0:T(8,128)(2,1)} async-done(((bf16[1536,768]{1,0:T(8,128)(2,1)}), bf16[1536,768]{1,0:T(8,128)(2,1)}) %all-reduce.23.cloned.1.call-update) | async-done | bytes 2359312 | tf_op jit(solution)/shard_map/while/body/eval_jaxpr/psum | solution.py:469
  1090.6 47.2 %collective-permute-done.1 = bf16[1536,768]{1,0:T(8,128)(2,1)S(1)} collective-permute-done((bf16[1536,768]{1,0:T(8,128)(2,1)}, bf16[1536,768]{1,0:T(8,128)(2,1)S(1)}, u32[]{:S(2)}, u32[]{:S(2)}) %collective-permute-start.1) | collective-permute-done | bytes 2359328 | tf_op jit(solution)/shard_map/while/body/eval_jaxpr/ppermute | solution.py:17
  1145.4 2108.0 %while.118 = (s32[]{:T(128)}, bf16[1536,768]{1,0:T(8,128)(2,1)S(1)}, f32[768]{0:T(1024)}, f32[768,192]{0,1:T(8,128)}, f32[768,192]{0,1:T(8,128)}, /*index=5*/f32...) while((s32[]{:T(128)}, bf16[1536,768]{1,0:T(8,128)(2,1)S(1)}, ...), condition=%wide.region_55.57_spmd.clone.clone.clone.clone, body=%wide.region_22.56_spmd.clone.clone.clone.clone.sunk | while | flops 43615236096 | bytes 1350687488 | solution.py:567
  1161.7 30.8 conditional.30
  1193.5 14.2 psum.92
  1207.7 20.8 select_add_fusion.29
  1238.3 257.9 %all-reduce.25.cloned.1.call-done = bf16[1536,768]{1,0:T(8,128)(2,1)} async-done(((bf16[1536,768]{1,0:T(8,128)(2,1)}), bf16[1536,768]{1,0:T(8,128)(2,1)}) %all-reduce.25.cloned.1.call-update) | async-done | bytes 2359312 | tf_op jit(solution)/shard_map/while/body/eval_jaxpr/psum | solution.py:512
  1496.2 14.0 conditional.31
  1524.8 258.4 %all-reduce.27.cloned.1.call-done = bf16[1536,768]{1,0:T(8,128)(2,1)} async-done(((bf16[1536,768]{1,0:T(8,128)(2,1)}), bf16[1536,768]{1,0:T(8,128)(2,1)}) %all-reduce.27.cloned.1.call-update) | async-done | bytes 2359312 | tf_op jit(solution)/shard_map/while/body/eval_jaxpr/psum | solution.py:530
  1805.0 46.6 %collective-permute-done = bf16[1536,768]{1,0:T(8,128)(2,1)S(1)} collective-permute-done((bf16[1536,768]{1,0:T(8,128)(2,1)}, bf16[1536,768]{1,0:T(8,128)(2,1)S(1)}, u32[]{:S(2)}, u32[]{:S(2)}) %collective-permute-start) | collective-permute-done | bytes 2359328 | tf_op jit(solution)/shard_map/while/body/eval_jaxpr/ppermute | solution.py:17
  1861.1 273.7 %conditional.30 = (f32[8,768,512]{2,1,0:T(8,128)}, f32[8,768,512]{2,1,0:T(8,128)}, f32[8,512,768]{2,1,0:T(8,128)}, f32[768,512]{1,0:T(8,128)}, f32[768,512]{1,0:...) conditional(s32[]{:T(128)} %convert_element_type.593, () %tuple.343, ...), branch_computations={%region_23.24_spmd, %region_24.34_spmd} | conditional | flops 36944035840 | bytes 675690240 | solution.py:76
  1887.4 18.7 gather_fusion.7
  1907.4 20.2 gather_fusion.1
  1932.5 17.3 gather_fusion.2
  1987.2 14.0 multiply_convert_fusion.5
  2096.5 13.7 fusion.80
  2135.9 20.1 psum.92
  2156.0 27.7 select_add_fusion.29
  2194.6 227.0 %conditional.31 = (f32[192,768]{1,0:T(8,128)}, f32[768]{0:T(1024)}, f32[768,8]{0,1:T(8,128)}, f32[768,192]{0,1:T(8,128)}, f32[768,192]{0,1:T(8,128)}, /*index=5*...) conditional(s32[]{:T(128)} %convert_element_type.593, () %tuple.342, ...), branch_computations={%region_36.37_spmd, %region_37.49_spmd.clone} | conditional | flops 6620402688 | bytes 340428288 | solution.py:76
  2206.6 16.7 scatter_custom_fusion.3
  2245.7 156.3 %while.116 = (s32[]{:T(128)}, f32[2560,3,64]{0,2,1:T(8,128)}, f32[2560,3,64]{0,2,1:T(8,128)}, f32[3,512,3,64]{1,0,3,2:T(4,128)}, s32[3]{0:T(128)S(1)}, /*index=5...) while((s32[]{:T(128)}, f32[2560,3,64]{0,2,1:T(8,128)}, ...), condition=%wide.region_48.48_spmd, body=%wide.region_46.47_spmd.sunk | while | flops 1536885248 | bytes 81748432 | solution.py:163
  2425.6 14.1 select_add_fusion.30
  2439.8 41.5 %all-reduce.27.cloned.1.call-done = bf16[1536,768]{1,0:T(8,128)(2,1)} async-done(((bf16[1536,768]{1,0:T(8,128)(2,1)}), bf16[1536,768]{1,0:T(8,128)(2,1)}) %all-reduce.27.cloned.1.call-update) | async-done | bytes 2359312 | tf_op jit(solution)/shard_map/while/body/eval_jaxpr/psum | solution.py:530
  2514.0 36.6 collective-permute-done
  2560.4 273.2 %conditional.30 = (f32[8,768,512]{2,1,0:T(8,128)}, f32[8,768,512]{2,1,0:T(8,128)}, f32[8,512,768]{2,1,0:T(8,128)}, f32[768,512]{1,0:T(8,128)}, f32[768,512]{1,0:...) conditional(s32[]{:T(128)} %convert_element_type.593, () %tuple.343, ...), branch_computations={%region_23.24_spmd, %region_24.34_spmd} | conditional | flops 36944035840 | bytes 675690240 | solution.py:76
  2586.7 18.4 gather_fusion.7
  2606.4 20.2 gather_fusion.1
  2631.4 17.3 gather_fusion.2
  2686.2 14.0 multiply_convert_fusion.5
  2795.5 13.7 fusion.80
  2834.7 20.2 psum.92
  2854.8 27.7 select_add_fusion.29
  2893.5 227.1 %conditional.31 = (f32[192,768]{1,0:T(8,128)}, f32[768]{0:T(1024)}, f32[768,8]{0,1:T(8,128)}, f32[768,192]{0,1:T(8,128)}, f32[768,192]{0,1:T(8,128)}, /*index=5*...) conditional(s32[]{:T(128)} %convert_element_type.593, () %tuple.342, ...), branch_computations={%region_36.37_spmd, %region_37.49_spmd.clone} | conditional | flops 6620402688 | bytes 340428288 | solution.py:76
  2905.5 17.0 scatter_custom_fusion.3
  2944.8 156.3 %while.116 = (s32[]{:T(128)}, f32[2560,3,64]{0,2,1:T(8,128)}, f32[2560,3,64]{0,2,1:T(8,128)}, f32[3,512,3,64]{1,0,3,2:T(4,128)}, s32[3]{0:T(128)S(1)}, /*index=5...) while((s32[]{:T(128)}, f32[2560,3,64]{0,2,1:T(8,128)}, ...), condition=%wide.region_48.48_spmd, body=%wide.region_46.47_spmd.sunk | while | flops 1536885248 | bytes 81748432 | solution.py:163
  3124.6 14.4 select_add_fusion.30
  3139.1 40.3 %all-reduce.27.cloned.1.call-done = bf16[1536,768]{1,0:T(8,128)(2,1)} async-done(((bf16[1536,768]{1,0:T(8,128)(2,1)}), bf16[1536,768]{1,0:T(8,128)(2,1)}) %all-reduce.27.cloned.1.call-update) | async-done | bytes 2359312 | tf_op jit(solution)/shard_map/while/body/eval_jaxpr/psum | solution.py:530
  3212.0 36.6 collective-permute-done
  3320.3 19.9 reduce-scatter.38.cloned.1.call-done
  3342.0 19.2 reduce-scatter.40.cloned.1.call-done
  3362.9 22.4 reduce-scatter.32.cloned.1.call-done
  3387.0 23.6 reduce-scatter.30.cloned.1.call-done
  3412.4 23.6 reduce-scatter.28.cloned.1.call-done
  3437.8 110.7 %reduce-scatter.26.cloned.1.call-done = bf16[8,512,192]{1,2,0:T(8,128)(2,1)} async-done(((bf16[8,512,768]{1,2,0:T(8,128)(2,1)}), bf16[8,512,192]{1,2,0:T(8,128)(2,1)}) %reduce-scatter.26.cloned.1.call-update) | async-done | bytes 1572880 | tf_op jit(solution)/shard_map/reduce_scatter | solution.py:596
  3552.0 110.1 %reduce-scatter.24.cloned.1.call-done = bf16[8,192,512]{2,1,0:T(8,128)(2,1)} async-done(((bf16[8,768,512]{2,1,0:T(8,128)(2,1)}), bf16[8,192,512]{2,1,0:T(8,128)(2,1)}) %reduce-scatter.24.cloned.1.call-update) | async-done | bytes 1572880 | tf_op jit(solution)/shard_map/reduce_scatter | solution.py:593
  3665.6 110.0 %reduce-scatter.22.cloned.1.call-done = bf16[8,192,512]{2,1,0:T(8,128)(2,1)} async-done(((bf16[8,768,512]{2,1,0:T(8,128)(2,1)}), bf16[8,192,512]{2,1,0:T(8,128)(2,1)}) %reduce-scatter.22.cloned.1.call-update) | async-done | bytes 1572880 | tf_op jit(solution)/shard_map/reduce_scatter | solution.py:590
  (1279 shorter events, 1496.1 us)
Async XLA Ops:
  52.4 115.4 %all-reduce.21.cloned.1.call-start = ((), (), s32[]{:S(2)}) async-start(), calls=%async_computation.22 | async-start | bytes 4718592 | tf_op jit(solution)/shard_map/while/body/eval_jaxpr/psum | solution.py:462
  72.3 34.2 copy-start.49
  110.3 242.7 %all-reduce.23.cloned.1.call-start = ((), (), s32[]{:S(2)}) async-start(), calls=%async_computation.23 | async-start | bytes 4718592 | tf_op jit(solution)/shard_map/while/body/eval_jaxpr/psum | solution.py:469
  353.0 60.9 %copy-start.26 = (bf16[768,192]{1,0:T(8,128)(2,1)S(1)}, bf16[768,192]{1,0:T(8,128)(2,1)}, u32[]{:S(2)}) copy-start(bf16[768,192]{1,0:T(8,128)(2,1)} %copy-done.25) | copy-start | bytes 884740 | tf_op jit(solution)/shard_map/while
  353.0 60.9 %copy-start.32 = (bf16[768,192]{1,0:T(8,128)(2,1)S(1)}, bf16[768,192]{1,0:T(8,128)(2,1)}, u32[]{:S(2)}) copy-start(bf16[768,192]{1,0:T(8,128)(2,1)} %copy-done.31) | copy-start | bytes 884740 | tf_op jit(solution)/shard_map/while
  353.0 60.9 %copy-start.37 = (bf16[768,192]{1,0:T(8,128)(2,1)S(1)}, bf16[768,192]{1,0:T(8,128)(2,1)}, u32[]{:S(2)}) copy-start(bf16[768,192]{1,0:T(8,128)(2,1)} %copy-done.36) | copy-start | bytes 884740 | tf_op jit(solution)/shard_map/while
  353.0 60.9 %copy-start.79 = (bf16[768]{0:T(1024)(128)(2,1)S(1)}, bf16[768]{0:T(1024)(128)(2,1)}, u32[]{:S(2)}) copy-start(bf16[768]{0:T(1024)(128)(2,1)} %copy-done.78) | copy-start | bytes 4612 | tf_op jit(solution)/shard_map/while
  353.0 60.9 %copy-start.96 = (f32[32]{0:T(128)S(1)}, f32[32]{0:T(128)}, u32[]{:S(2)}) copy-start(f32[32]{0:T(128)} %copy-done.95) | copy-start | bytes 388 | tf_op jit(solution)/shard_map/while
  359.8 54.1 %collective-permute-start.1 = (bf16[1536,768]{1,0:T(8,128)(2,1)}, bf16[1536,768]{1,0:T(8,128)(2,1)S(1)}, u32[]{:S(2)}, u32[]{:S(2)}) collective-permute-start(bf16[1536,768]{1,0:T(8,128)(2,1)} %get-tuple-element.4105), channel_id=1, source_target_pairs={{0,16},{1,17},{2,18},{3,19},{4,20},{5,21},{6,22},{7,23},{8,24},{9,... | collective-permute-start | bytes 7077896 | tf_op jit(solution)/shard_map/while/body/eval_jaxpr/ppermute | solution.py:17
  414.0 114.8 %all-reduce.21.cloned.1.call-start = ((), (), s32[]{:S(2)}) async-start(), calls=%async_computation.22 | async-start | bytes 4718592 | tf_op jit(solution)/shard_map/while/body/eval_jaxpr/psum | solution.py:462
  433.9 34.2 copy-start.49
  471.9 242.9 %all-reduce.23.cloned.1.call-start = ((), (), s32[]{:S(2)}) async-start(), calls=%async_computation.23 | async-start | bytes 4718592 | tf_op jit(solution)/shard_map/while/body/eval_jaxpr/psum | solution.py:469
  714.8 60.9 %copy-start.26 = (bf16[768,192]{1,0:T(8,128)(2,1)S(1)}, bf16[768,192]{1,0:T(8,128)(2,1)}, u32[]{:S(2)}) copy-start(bf16[768,192]{1,0:T(8,128)(2,1)} %copy-done.25) | copy-start | bytes 884740 | tf_op jit(solution)/shard_map/while
  714.8 60.9 %copy-start.32 = (bf16[768,192]{1,0:T(8,128)(2,1)S(1)}, bf16[768,192]{1,0:T(8,128)(2,1)}, u32[]{:S(2)}) copy-start(bf16[768,192]{1,0:T(8,128)(2,1)} %copy-done.31) | copy-start | bytes 884740 | tf_op jit(solution)/shard_map/while
  714.8 60.9 %copy-start.37 = (bf16[768,192]{1,0:T(8,128)(2,1)S(1)}, bf16[768,192]{1,0:T(8,128)(2,1)}, u32[]{:S(2)}) copy-start(bf16[768,192]{1,0:T(8,128)(2,1)} %copy-done.36) | copy-start | bytes 884740 | tf_op jit(solution)/shard_map/while
  714.8 60.9 %copy-start.79 = (bf16[768]{0:T(1024)(128)(2,1)S(1)}, bf16[768]{0:T(1024)(128)(2,1)}, u32[]{:S(2)}) copy-start(bf16[768]{0:T(1024)(128)(2,1)} %copy-done.78) | copy-start | bytes 4612 | tf_op jit(solution)/shard_map/while
  714.8 60.9 %copy-start.96 = (f32[32]{0:T(128)S(1)}, f32[32]{0:T(128)}, u32[]{:S(2)}) copy-start(f32[32]{0:T(128)} %copy-done.95) | copy-start | bytes 388 | tf_op jit(solution)/shard_map/while
  721.6 54.1 %collective-permute-start.1 = (bf16[1536,768]{1,0:T(8,128)(2,1)}, bf16[1536,768]{1,0:T(8,128)(2,1)S(1)}, u32[]{:S(2)}, u32[]{:S(2)}) collective-permute-start(bf16[1536,768]{1,0:T(8,128)(2,1)} %get-tuple-element.4105), channel_id=1, source_target_pairs={{0,16},{1,17},{2,18},{3,19},{4,20},{5,21},{6,22},{7,23},{8,24},{9,... | collective-permute-start | bytes 7077896 | tf_op jit(solution)/shard_map/while/body/eval_jaxpr/ppermute | solution.py:17
  775.8 114.9 %all-reduce.21.cloned.1.call-start = ((), (), s32[]{:S(2)}) async-start(), calls=%async_computation.22 | async-start | bytes 4718592 | tf_op jit(solution)/shard_map/while/body/eval_jaxpr/psum | solution.py:462
  787.7 289.2 %all-reduce.23.cloned.1.call-start = ((), (), s32[]{:S(2)}) async-start(), calls=%async_computation.23 | async-start | bytes 4718592 | tf_op jit(solution)/shard_map/while/body/eval_jaxpr/psum | solution.py:469
  1076.9 60.9 %copy-start.26 = (bf16[768,192]{1,0:T(8,128)(2,1)S(1)}, bf16[768,192]{1,0:T(8,128)(2,1)}, u32[]{:S(2)}) copy-start(bf16[768,192]{1,0:T(8,128)(2,1)} %copy-done.25) | copy-start | bytes 884740 | tf_op jit(solution)/shard_map/while
  1076.9 60.9 %copy-start.32 = (bf16[768,192]{1,0:T(8,128)(2,1)S(1)}, bf16[768,192]{1,0:T(8,128)(2,1)}, u32[]{:S(2)}) copy-start(bf16[768,192]{1,0:T(8,128)(2,1)} %copy-done.31) | copy-start | bytes 884740 | tf_op jit(solution)/shard_map/while
  1076.9 60.9 %copy-start.37 = (bf16[768,192]{1,0:T(8,128)(2,1)S(1)}, bf16[768,192]{1,0:T(8,128)(2,1)}, u32[]{:S(2)}) copy-start(bf16[768,192]{1,0:T(8,128)(2,1)} %copy-done.36) | copy-start | bytes 884740 | tf_op jit(solution)/shard_map/while
  1076.9 60.9 %copy-start.79 = (bf16[768]{0:T(1024)(128)(2,1)S(1)}, bf16[768]{0:T(1024)(128)(2,1)}, u32[]{:S(2)}) copy-start(bf16[768]{0:T(1024)(128)(2,1)} %copy-done.78) | copy-start | bytes 4612 | tf_op jit(solution)/shard_map/while
  1076.9 60.9 %copy-start.96 = (f32[32]{0:T(128)S(1)}, f32[32]{0:T(128)}, u32[]{:S(2)}) copy-start(f32[32]{0:T(128)} %copy-done.95) | copy-start | bytes 388 | tf_op jit(solution)/shard_map/while
  1083.7 54.1 %collective-permute-start.1 = (bf16[1536,768]{1,0:T(8,128)(2,1)}, bf16[1536,768]{1,0:T(8,128)(2,1)S(1)}, u32[]{:S(2)}, u32[]{:S(2)}) collective-permute-start(bf16[1536,768]{1,0:T(8,128)(2,1)} %get-tuple-element.4105), channel_id=1, source_target_pairs={{0,16},{1,17},{2,18},{3,19},{4,20},{5,21},{6,22},{7,23},{8,24},{9,... | collective-permute-start | bytes 7077896 | tf_op jit(solution)/shard_map/while/body/eval_jaxpr/ppermute | solution.py:17
  1152.4 343.8 %all-reduce.25.cloned.1.call-start = ((), (), s32[]{:S(2)}) async-start(), calls=%async_computation.24 | async-start | bytes 4718592 | tf_op jit(solution)/shard_map/while/body/eval_jaxpr/psum | solution.py:512
  1192.5 590.7 %all-reduce.27.cloned.1.call-start = ((), (), s32[]{:S(2)}) async-start(), calls=%async_computation.25 | async-start | bytes 4718592 | tf_op jit(solution)/shard_map/while/body/eval_jaxpr/psum | solution.py:530
  1234.0 262.2 %copy-start.28 = (bf16[768,192]{1,0:T(8,128)(2,1)S(1)}, bf16[768,192]{1,0:T(8,128)(2,1)}, u32[]{:S(2)}) copy-start(bf16[768,192]{1,0:T(8,128)(2,1)} %get-tuple-element.4562) | copy-start | bytes 884740 | tf_op jit(solution)/shard_map/while
  1234.0 262.2 %copy-start.75 = (s32[1536,2]{0,1:T(2,128)S(1)}, s32[1536,2]{0,1:T(2,128)}, u32[]{:S(2)}) copy-start(s32[1536,2]{0,1:T(2,128)} %copy-done.74) | copy-start | bytes 36868 | tf_op jit(solution)/shard_map/while
  1234.0 262.2 %copy-start.81 = (bf16[768]{0:T(1024)(128)(2,1)S(1)}, bf16[768]{0:T(1024)(128)(2,1)}, u32[]{:S(2)}) copy-start(bf16[768]{0:T(1024)(128)(2,1)} %get-tuple-element.4561) | copy-start | bytes 4612 | tf_op jit(solution)/shard_map/while
  1514.2 269.0 %copy-start.82 = (bf16[768]{0:T(1024)(128)(2,1)S(1)}, bf16[768]{0:T(1024)(128)(2,1)}, u32[]{:S(2)}) copy-start(bf16[768]{0:T(1024)(128)(2,1)} %get-tuple-element.4561) | copy-start | bytes 4612 | tf_op jit(solution)/shard_map/while
  1787.3 64.2 %collective-permute-start = (bf16[1536,768]{1,0:T(8,128)(2,1)}, bf16[1536,768]{1,0:T(8,128)(2,1)S(1)}, u32[]{:S(2)}, u32[]{:S(2)}) collective-permute-start(bf16[1536,768]{1,0:T(8,128)(2,1)} %convert_element_type.595), channel_id=1, source_target_pairs={{16,0},{17,1},{18,2},{19,3},{20,4},{21,5},{22,6},{23,7},{24,8},{25... | collective-permute-start | bytes 7077896 | tf_op jit(solution)/shard_map/while/body/eval_jaxpr/ppermute | solution.py:17
  1799.9 51.7 %copy-start.70 = (bf16[768,8]{0,1:T(8,128)(2,1)S(1)}, bf16[768,8]{0,1:T(8,128)(2,1)}, u32[]{:S(2)}) copy-start(bf16[768,8]{0,1:T(8,128)(2,1)} %get-tuple-element.4660) | copy-start | bytes 36868 | tf_op jit(solution)/shard_map/while
  1799.9 51.7 %copy-start.85 = (bf16[768]{0:T(1024)(128)(2,1)S(1)}, bf16[768]{0:T(1024)(128)(2,1)}, u32[]{:S(2)}) copy-start(bf16[768]{0:T(1024)(128)(2,1)} %get-tuple-element.4728) | copy-start | bytes 4612 | tf_op jit(solution)/shard_map/while
  1851.8 342.8 %all-reduce.25.cloned.1.call-start = ((), (), s32[]{:S(2)}) async-start(), calls=%async_computation.24 | async-start | bytes 4718592 | tf_op jit(solution)/shard_map/while/body/eval_jaxpr/psum | solution.py:512
  1861.4 24.7 copy-start.10
  2134.9 346.4 %all-reduce.27.cloned.1.call-start = ((), (), s32[]{:S(2)}) async-start(), calls=%async_computation.25 | async-start | bytes 4718592 | tf_op jit(solution)/shard_map/while/body/eval_jaxpr/psum | solution.py:530
  2194.6 42.5 %copy-start.29 = (bf16[768,192]{1,0:T(8,128)(2,1)}, bf16[768,192]{1,0:T(8,128)(2,1)S(1)}, u32[]{:S(2)}) copy-start(bf16[768,192]{1,0:T(8,128)(2,1)S(1)} %get-tuple-element.3335) | copy-start | bytes 884740 | tf_op jit(solution)/shard_map/while/body/eval_jaxpr/cond
  2201.1 37.0 copy-start.5
  2425.6 55.7 %copy-start.82 = (bf16[768]{0:T(1024)(128)(2,1)S(1)}, bf16[768]{0:T(1024)(128)(2,1)}, u32[]{:S(2)}) copy-start(bf16[768]{0:T(1024)(128)(2,1)} %get-tuple-element.4561) | copy-start | bytes 4612 | tf_op jit(solution)/shard_map/while
  2495.4 55.1 %collective-permute-start = (bf16[1536,768]{1,0:T(8,128)(2,1)}, bf16[1536,768]{1,0:T(8,128)(2,1)S(1)}, u32[]{:S(2)}, u32[]{:S(2)}) collective-permute-start(bf16[1536,768]{1,0:T(8,128)(2,1)} %convert_element_type.595), channel_id=1, source_target_pairs={{16,0},{17,1},{18,2},{19,3},{20,4},{21,5},{22,6},{23,7},{24,8},{25... | collective-permute-start | bytes 7077896 | tf_op jit(solution)/shard_map/while/body/eval_jaxpr/ppermute | solution.py:17
  2508.8 41.8 %copy-start.70 = (bf16[768,8]{0,1:T(8,128)(2,1)S(1)}, bf16[768,8]{0,1:T(8,128)(2,1)}, u32[]{:S(2)}) copy-start(bf16[768,8]{0,1:T(8,128)(2,1)} %get-tuple-element.4660) | copy-start | bytes 36868 | tf_op jit(solution)/shard_map/while
  2508.8 41.8 %copy-start.85 = (bf16[768]{0:T(1024)(128)(2,1)S(1)}, bf16[768]{0:T(1024)(128)(2,1)}, u32[]{:S(2)}) copy-start(bf16[768]{0:T(1024)(128)(2,1)} %get-tuple-element.4728) | copy-start | bytes 4612 | tf_op jit(solution)/shard_map/while
  2551.1 342.4 %all-reduce.25.cloned.1.call-start = ((), (), s32[]{:S(2)}) async-start(), calls=%async_computation.24 | async-start | bytes 4718592 | tf_op jit(solution)/shard_map/while/body/eval_jaxpr/psum | solution.py:512
  2560.7 24.7 copy-start.10
  2833.7 345.7 %all-reduce.27.cloned.1.call-start = ((), (), s32[]{:S(2)}) async-start(), calls=%async_computation.25 | async-start | bytes 4718592 | tf_op jit(solution)/shard_map/while/body/eval_jaxpr/psum | solution.py:530
  2893.5 42.7 %copy-start.29 = (bf16[768,192]{1,0:T(8,128)(2,1)}, bf16[768,192]{1,0:T(8,128)(2,1)S(1)}, u32[]{:S(2)}) copy-start(bf16[768,192]{1,0:T(8,128)(2,1)S(1)} %get-tuple-element.3335) | copy-start | bytes 884740 | tf_op jit(solution)/shard_map/while/body/eval_jaxpr/cond
  2899.9 37.3 copy-start.5
  3124.6 54.7 %copy-start.82 = (bf16[768]{0:T(1024)(128)(2,1)S(1)}, bf16[768]{0:T(1024)(128)(2,1)}, u32[]{:S(2)}) copy-start(bf16[768]{0:T(1024)(128)(2,1)} %get-tuple-element.4561) | copy-start | bytes 4612 | tf_op jit(solution)/shard_map/while
  3193.5 55.1 %collective-permute-start = (bf16[1536,768]{1,0:T(8,128)(2,1)}, bf16[1536,768]{1,0:T(8,128)(2,1)S(1)}, u32[]{:S(2)}, u32[]{:S(2)}) collective-permute-start(bf16[1536,768]{1,0:T(8,128)(2,1)} %convert_element_type.595), channel_id=1, source_target_pairs={{16,0},{17,1},{18,2},{19,3},{20,4},{21,5},{22,6},{23,7},{24,8},{25... | collective-permute-start | bytes 7077896 | tf_op jit(solution)/shard_map/while/body/eval_jaxpr/ppermute | solution.py:17
  3206.8 41.8 %copy-start.70 = (bf16[768,8]{0,1:T(8,128)(2,1)S(1)}, bf16[768,8]{0,1:T(8,128)(2,1)}, u32[]{:S(2)}) copy-start(bf16[768,8]{0,1:T(8,128)(2,1)} %get-tuple-element.4660) | copy-start | bytes 36868 | tf_op jit(solution)/shard_map/while
  3206.8 41.8 %copy-start.85 = (bf16[768]{0:T(1024)(128)(2,1)S(1)}, bf16[768]{0:T(1024)(128)(2,1)}, u32[]{:S(2)}) copy-start(bf16[768]{0:T(1024)(128)(2,1)} %get-tuple-element.4728) | copy-start | bytes 4612 | tf_op jit(solution)/shard_map/while
  3253.4 56.4 %reduce-scatter.42.cloned.1.call-start = ((), (), s32[]{:S(2)}) async-start(), calls=%async_computation.21 | async-start | bytes 245760
  3255.1 56.2 %reduce-scatter.34.cloned.1.call-start = ((), (), s32[]{:S(2)}) async-start(), calls=%async_computation.17 | async-start | bytes 491520
  3257.2 61.3 %reduce-scatter.36.cloned.1.call-start = ((), (), s32[]{:S(2)}) async-start(), calls=%async_computation.18 | async-start | bytes 491520
  3259.3 80.9 %reduce-scatter.38.cloned.1.call-start = ((), (), s32[]{:S(2)}) async-start(), calls=%async_computation.19 | async-start | bytes 491520
  3260.3 100.9 %reduce-scatter.40.cloned.1.call-start = ((), (), s32[]{:S(2)}) async-start(), calls=%async_computation.20 | async-start | bytes 491520
  3261.4 123.9 %reduce-scatter.32.cloned.1.call-start = ((), (), s32[]{:S(2)}) async-start(), calls=%async_computation.16 | async-start | bytes 983040 | tf_op jit(solution)/shard_map/reduce_scatter | solution.py:605
  3264.0 146.6 %reduce-scatter.30.cloned.1.call-start = ((), (), s32[]{:S(2)}) async-start(), calls=%async_computation.15 | async-start | bytes 983040 | tf_op jit(solution)/shard_map/reduce_scatter | solution.py:602
  3266.5 169.5 %reduce-scatter.28.cloned.1.call-start = ((), (), s32[]{:S(2)}) async-start(), calls=%async_computation.14 | async-start | bytes 983040 | tf_op jit(solution)/shard_map/reduce_scatter | solution.py:599
  3269.0 279.5 %reduce-scatter.26.cloned.1.call-start = ((), (), s32[]{:S(2)}) async-start(), calls=%async_computation.13 | async-start | bytes 7864320 | tf_op jit(solution)/shard_map/reduce_scatter | solution.py:596
  3279.1 383.0 %reduce-scatter.24.cloned.1.call-start = ((), (), s32[]{:S(2)}) async-start(), calls=%async_computation.12 | async-start | bytes 7864320 | tf_op jit(solution)/shard_map/reduce_scatter | solution.py:593
  3287.3 488.3 %reduce-scatter.22.cloned.1.call-start = ((), (), s32[]{:S(2)}) async-start(), calls=%async_computation.11 | async-start | bytes 7864320 | tf_op jit(solution)/shard_map/reduce_scatter | solution.py:590
  (234 other events, 1462.3 us)
Sparse Core Ops, SparseCore 0:
  110.4 57.3 all-reduce.20
  298.1 54.8 all-reduce.22
  472.1 56.6 all-reduce.20
  659.1 55.6 all-reduce.22
  787.8 102.9 all-reduce.20
  901.4 175.4 all-reduce.22
  1192.6 303.5 all-reduce.24
  1514.3 268.8 all-reduce.26
  2135.0 59.2 all-reduce.24
  2425.8 55.5 all-reduce.26
  2833.8 59.2 all-reduce.24
  3124.7 54.5 all-reduce.26
Sparse Core Ops, SparseCore 1:
  3256.7 18.7 reduce-scatter.41
  3278.3 18.7 reduce-scatter.33
  3299.8 18.7 reduce-scatter.35
  3321.5 18.7 reduce-scatter.37
  3342.5 18.7 reduce-scatter.39
  3364.2 21.0 reduce-scatter.31
  3388.2 22.5 reduce-scatter.29
  3413.5 22.5 reduce-scatter.27
  3438.3 110.1 reduce-scatter.25
  3550.9 111.1 reduce-scatter.23
  3664.4 111.1 reduce-scatter.21
where the time goes:
time: 3800 us; the launch traced here: 3790 us
  waiting for transfers between devices  1810 us (48%)
  local copies, waits for them, and re-layouts  660 us (17%)
  other arithmetic  575 us (15%)
  matrix products  574 us (15%)
  loops' own time  71.6 us (2%)
  blocking collectives  66.1 us (2%)
    psum x3, waiting for transfers between devices, backward_tick(): lax.psum(grad_attn_part.astype(jnp.bfloat16), 'tensor').astype(jnp.float32)  340 us
    psum x3, waiting for transfers between devices, forward_tick(): lax.psum(branch.astype(jnp.bfloat16), 'tensor').astype(jnp.float32)  286 us
    ppermute x6, waiting for transfers between devices, from_behind(): return lax.ppermute(block, axis, route)  261 us
    psum x3, waiting for transfers between devices, backward_tick(): lax.psum(grad_part.astype(jnp.bfloat16), 'tensor').astype(jnp.float32)  258 us
    psum x3, waiting for transfers between devices, forward_tick(): lax.psum(partial_value.astype(jnp.bfloat16), 'tensor').astype(jnp.float32)  217 us
    add x30, other arithmetic, backward_tick(): totals = tuple(jax.tree.map(jnp.add, totals, tick_grads))  163 us
    reduce_scatter x1, waiting for transfers between devices, on_device(): lax.psum_scatter(totals[9].astype(jnp.bfloat16), 'dp', scatter_dimension=...  111 us
    reduce_scatter x1, waiting for transfers between devices, on_device(): lax.psum_scatter(totals[8].astype(jnp.bfloat16), 'dp', scatter_dimension=...  110 us
  transfers between devices with their start and end apart: 29, of which 25 were waited for; matrix products, arithmetic and copies ran while one was open for 7% of the time, Pallas kernels for 0%

commit v1 on v0

v1 whole, which is shorter than its diff:
```python
import functools

import jax
import jax.numpy as jnp
import numpy as np
from jax import lax
from jax.experimental import pallas as pl
from jax.experimental.pallas import tpu as pltpu
from jax.sharding import PartitionSpec as P

HEAD_DIM = 64
EXPERTS = 8
SEQ_LEN = 1536
WINDOW = 1024
CAPACITY = 480
BLOCK = 256
BLOCKS = SEQ_LEN // BLOCK
LANES = 128
SLOTS = 3
VMEM_BYTES = 60 * 2**20
MESH = pl.DeviceIdType.MESH
F32 = jnp.float32
BF16 = jnp.bfloat16
NT = (((1,), (1,)), ((), ()))
TN = (((0,), (0,)), ((), ()))


def shape_of(shape, dtype):
    return jax.ShapeDtypeStruct(shape, dtype)


def dot(left, right):
    return jnp.dot(left, right, preferred_element_type=F32)


def dot_nt(left, right):
    return lax.dot_general(left, right, NT, preferred_element_type=F32)


def dot_tn(left, right):
    return lax.dot_general(left, right, TN, preferred_element_type=F32)


def once(shape, index):
    return pl.BlockSpec(shape, index, pipeline_mode=pl.Buffered(1))


def loop(count, body):
    lax.fori_loop(0, count, lambda step, none: (body(step), none)[1], 0)


def rows_of(step, size):
    return pl.ds(pl.multiple_of(step * size, size), size)


def greet(partners):
    barrier = pltpu.get_barrier_semaphore()
    for partner in partners:
        pl.semaphore_signal(barrier, inc=1, device_id=partner, device_id_type=MESH)
    pl.semaphore_wait(barrier, len(partners))


def remote(source, target, send, recv, device):
    return pltpu.make_async_remote_copy(
        src_ref=source,
        dst_ref=target,
        send_sem=send,
        recv_sem=recv,
        device_id=device,
        device_id_type=MESH,
    )


def partners_of():
    place = lax.axis_index("tensor")
    core = lax.rem(place, 2)
    near = {"tensor": place + 1 - 2 * core}
    far = {"tensor": lax.rem(place + 2, 4)}
    return core, near, far


def halves(rows, pieces):
    size = rows // 2
    part = size // pieces
    return [(size, step * part, part) for step in range(pieces)]


def sum_kernel(counts, *refs):
    arrays = len(counts)
    ins, outs = refs[:arrays], refs[arrays : 2 * arrays]
    first, kept, second = (refs[(2 + k) * arrays : (3 + k) * arrays] for k in range(3))
    send1, recv1, send2, recv2, send3, recv3 = refs[5 * arrays :]
    core, near, far = partners_of()
    greet([near, far])
    steps = []
    for which, count in enumerate(counts):
        for size, offset, part in halves(ins[which].shape[0], count):
            steps.append((which, size, offset, part))
    copies = []
    for number, (which, size, offset, part) in enumerate(steps):
        other = pl.ds(pl.multiple_of((1 - core) * size + offset, 16), part)
        copies.append(
            remote(
                ins[which].at[other],
                first[which].at[pl.ds(offset, part)],
                send1.at[number],
                recv1.at[number],
                near,
            )
        )
        copies[-1].start()
    crossing = []
    for number, (which, size, offset, part) in enumerate(steps):
        mine = pl.ds(pl.multiple_of(core * size + offset, 16), part)
        local = pl.ds(offset, part)
        copies[number].wait_recv()
        kept[which][local, :] = (
            ins[which][mine, :].astype(F32) + first[which][local, :].astype(F32)
        ).astype(BF16)
        crossing.append(
            remote(
                kept[which].at[local],
                second[which].at[local],
                send2.at[number],
                recv2.at[number],
                far,
            )
        )
        crossing[-1].start()
    back = []
    for number, (which, size, offset, part) in enumerate(steps):
        mine = pl.ds(pl.multiple_of(core * size + offset, 16), part)
        local = pl.ds(offset, part)
        crossing[number].wait_recv()
        outs[which][mine, :] = (
            kept[which][local, :].astype(F32) + second[which][local, :].astype(F32)
        ).astype(BF16)
        back.append(
            remote(
                outs[which].at[mine],
                outs[which].at[mine],
                send3.at[number],
                recv3.at[number],
                near,
            )
        )
        back[-1].start()
    for copy in back:
        copy.wait_recv()
    for copy in copies + crossing + back:
        copy.wait_send()


def tensor_sum(arrays, counts, identity):
    scratch = []
    for copy in range(3):
        scratch += [pltpu.VMEM((a.shape[0] // 2, a.shape[1]), BF16) for a in arrays]
    total = sum(counts)
    scratch += [pltpu.SemaphoreType.DMA((total,))] * 6
    return pl.pallas_call(
        functools.partial(sum_kernel, counts),
        out_shape=[shape_of(a.shape, BF16) for a in arrays],
        in_specs=[pl.BlockSpec(memory_space=pltpu.VMEM)] * len(arrays),
        out_specs=[pl.BlockSpec(memory_space=pltpu.VMEM)] * len(arrays),
        scratch_shapes=scratch,
        compiler_params=pltpu.CompilerParams(
            collective_id=identity, has_side_effects=True, vmem_limit_bytes=VMEM_BYTES
        ),
        name="tensor_sum",
    )(*arrays)


def relay_kernel(
    pieces,
    finish,
    part_ref,
    extra_refs,
    full_ref,
    next_ref,
    first,
    kept,
    second,
    sends,
    recvs,
):
    core, near, far = partners_of()
    across = {"section": 1 - lax.axis_index("section")}
    greet([near, far, across])
    steps = halves(part_ref.shape[0], pieces)

    def place(size, offset, part, side):
        return pl.ds(pl.multiple_of(side * size + offset, 16), part)

    copies = []
    for number, (size, offset, part) in enumerate(steps):
        copies.append(
            remote(
                part_ref.at[place(size, offset, part, 1 - core)],
                first.at[pl.ds(offset, part)],
                sends.at[0, number],
                recvs.at[0, number],
                near,
            )
        )
        copies[-1].start()
    crossing = []
    for number, (size, offset, part) in enumerate(steps):
        local = pl.ds(offset, part)
        copies[number].wait_recv()
        kept[local, :] = (
            part_ref[place(size, offset, part, core), :].astype(F32)
            + first[local, :].astype(F32)
        ).astype(BF16)
        crossing.append(
            remote(
                kept.at[local],
                second.at[local],
                sends.at[1, number],
                recvs.at[1, number],
                far,
            )
        )
        crossing[-1].start()
    back, passed = [], []
    for number, (size, offset, part) in enumerate(steps):
        local = pl.ds(offset, part)
        mine = place(size, offset, part, core)
        crossing[number].wait_recv()
        total = (kept[local, :].astype(F32) + second[local, :].astype(F32)).astype(BF16)
        source, given = finish(total, mine, local, True)
        back.append(
            remote(
                source,
                source,
                sends.at[2, number],
                recvs.at[2, number],
                near,
            )
        )
        back[-1].start()
        passed.append(
            remote(
                given,
                next_ref.at[mine],
                sends.at[3, number],
                recvs.at[3, number],
                across,
            )
        )
        passed[-1].start()
    spread = []
    for number, (size, offset, part) in enumerate(steps):
        mine = place(size, offset, part, core)
        passed[number].wait_recv()
        spread.append(
            remote(
                next_ref.at[mine],
                next_ref.at[mine],
                sends.at[4, number],
                recvs.at[4, number],
                near,
            )
        )
        spread[-1].start()
    for number, (size, offset, part) in enumerate(steps):
        back[number].wait_recv()
        finish(None, place(size, offset, part, 1 - core), pl.ds(offset, part), False)
    for copy in spread:
        copy.wait_recv()
    for copy in copies + crossing + back + passed + spread:
        copy.wait_send()


def output_kernel(pieces, part_ref, state_ref, out_ref, next_ref, first, kept, second, sends, recvs):
    def finish(total, rows, local, own):
        if own:
            out_ref[rows, :] = (state_ref[rows, :] + total.astype(F32)).astype(BF16)
            return out_ref.at[rows], out_ref.at[rows]

    relay_kernel(
        pieces, finish, part_ref, None, out_ref, next_ref, first, kept, second, sends, recvs
    )


def input_kernel(
    pieces,
    part_ref,
    layer_in_ref,
    grad_state_ref,
    gain_ref,
    grad_ref,
    next_ref,
    grad_gain_ref,
    first,
    kept,
    second,
    full,
    given,
    gains,
    sends,
    recvs,
):
    gains[...] = jnp.zeros_like(gains)

    def rows_back(rows, side):
        grad_normed = full[rows, :].astype(F32)
        values = layer_in_ref[rows, :].astype(F32)
        scale = lax.rsqrt(jnp.mean(values * values, axis=-1, keepdims=True) + 1e-06)
        normed = values * scale
        scaled = gain_ref[...] * grad_normed
        inner = jnp.mean(normed * scaled, axis=-1, keepdims=True)
        grad = grad_state_ref[rows, :] + scale * (scaled - normed * inner)
        grad_ref[rows, :] = grad
        gains[side : side + 1, :] += jnp.sum(grad_normed * normed, axis=0, keepdims=True)
        return grad

    def finish(total, rows, local, own):
        if own:
            full[rows, :] = total
            given[local, :] = rows_back(rows, 0).astype(BF16)
            return full.at[rows], given.at[local]
        rows_back(rows, 1)

    relay_kernel(
        pieces, finish, part_ref, None, full, next_ref, first, kept, second, sends, recvs
    )
    grad_gain_ref[...] = gains[0:1, :] + gains[1:2, :]


def relay_scratch(rows, width, pieces):
    half = [pltpu.VMEM((rows // 2, width), BF16)] * 3
    return half, [pltpu.SemaphoreType.DMA((5, pieces))] * 2


def output_relay(part, state, identity, pieces=6):
    rows, width = part.shape
    half, semaphores = relay_scratch(rows, width, pieces)
    whole = pl.BlockSpec(memory_space=pltpu.VMEM)
    return pl.pallas_call(
        functools.partial(output_kernel, pieces),
        out_shape=[shape_of((rows, width), BF16)] * 2,
        in_specs=[whole] * 2,
        out_specs=[whole] * 2,
        scratch_shapes=half + semaphores,
        compiler_params=pltpu.CompilerParams(
            collective_id=identity, has_side_effects=True, vmem_limit_bytes=VMEM_BYTES
        ),
        name="output_relay",
    )(part, state)


def input_relay(part, layer_in, grad_state, gain, identity, pieces=6):
    rows, width = part.shape
    half, semaphores = relay_scratch(rows, width, pieces)
    whole = pl.BlockSpec(memory_space=pltpu.VMEM)
    return pl.pallas_call(
        functools.partial(input_kernel, pieces),
        out_shape=[
            shape_of((rows, width), F32),
            shape_of((rows, width), BF16),
            shape_of((1, width), F32),
        ],
        in_specs=[whole] * 4,
        out_specs=[whole] * 3,
        scratch_shapes=half
        + [
            pltpu.VMEM((rows, width), BF16),
            pltpu.VMEM((rows // 2, width), BF16),
            pltpu.VMEM((8, width), F32),
        ]
        + semaphores,
        compiler_params=pltpu.CompilerParams(
            collective_id=identity, has_side_effects=True, vmem_limit_bytes=VMEM_BYTES
        ),
        name="input_relay",
    )(part, layer_in, grad_state, gain)


def attention_forward_kernel(
    stored,
    meta,
    first_block,
    tok_ref,
    rec_ref,
    gain_ref,
    wall_ref,
    wo_ref,
    cos_ref,
    sin_ref,
    low_ref,
    *rest,
):
    rest = rest[stored:]
    part_ref, x_ref, a_ref, qkv_ref, o_ref, lse_ref = rest[:6]
    keys, values, scores, tops, sums, mixed = rest[6:]
    index = pl.program_id(0)
    heads = wo_ref.shape[0] // LANES
    wide = heads * LANES
    x = jnp.where(meta[0] == 0, tok_ref[...], rec_ref[...])
    x_ref[0] = x
    x = x.astype(F32)
    normed = gain_ref[...] * x * lax.rsqrt(jnp.mean(x * x, axis=-1, keepdims=True) + 1e-06)
    normed = normed.astype(BF16)
    a_ref[0] = normed
    cosine, sine = cos_ref[...], sin_ref[...]
    here = rows_of(index, BLOCK)
    for group in range(2 * heads):
        columns = slice(group * LANES, (group + 1) * LANES)
        pre = dot(normed, wall_ref[:, columns])
        turned = pre * cosine + pltpu.roll(pre, HEAD_DIM, 1) * sine
        if group < heads:
            turned = turned * 0.0625
        qkv_ref[0, :, columns] = turned.astype(BF16)
    qkv_ref[0, :, 2 * wide :] = dot(normed, wall_ref[:, 2 * wide :]).astype(BF16)
    keys[here, :] = qkv_ref[0, :, wide : 2 * wide]
    values[here, :] = qkv_ref[0, :, 2 * wide :]
    low = low_ref[0]
    query_at = index * BLOCK + lax.broadcasted_iota(jnp.int32, (BLOCK, BLOCK), 0)
    key_at = lax.broadcasted_iota(jnp.int32, (BLOCK, BLOCK), 1)
    tops[...] = jnp.full_like(tops, -1e30)
    sums[...] = jnp.zeros_like(sums)
    mixed[...] = jnp.zeros_like(mixed)
    begin = first_block[meta[2] * BLOCKS + index]

    def score(block, none):
        at = key_at + block * BLOCK
        valid = (at >= low) & (at <= query_at)
        there = rows_of(block, BLOCK)
        for head in range(heads):
            columns = slice(head * LANES, (head + 1) * LANES)
            raw = dot_nt(qkv_ref[0, :, columns], keys[there, columns])
            raw = jnp.where(valid, raw, -1e30)
            scores[head, block] = raw
            tops[head] = jnp.maximum(
                tops[head], jnp.maximum(raw[:, :LANES], raw[:, LANES:])
            )
        return none

    lax.fori_loop(begin, index + 1, score, 0)
    top = [jnp.max(tops[head], axis=1, keepdims=True) for head in range(heads)]

    def mix(block, none):
        there = rows_of(block, BLOCK)
        for head in range(heads):
            columns = slice(head * LANES, (head + 1) * LANES)
            weights = jnp.exp(scores[head, block] - top[head])
            sums[head] += weights[:, :LANES] + weights[:, LANES:]
            mixed[:, columns] += dot(weights.astype(BF16), values[there, columns])
        return none

    lax.fori_loop(begin, index + 1, mix, 0)
    for head in range(heads):
        columns = slice(head * LANES, (head + 1) * LANES)
        total = jnp.sum(sums[head], axis=1, keepdims=True)
        o_ref[0, :, columns] = (mixed[:, columns] / total).astype(BF16)
        logsum = jnp.broadcast_to(top[head] + jnp.log(total), (BLOCK, LANES))
        lse_ref[0, head : head + 1, :] = logsum.T[0:1, :]
    part_ref[...] = dot(o_ref[0], wo_ref[...]).astype(BF16)


def attention_forward(meta, first_block, tokens, received, gain, wall, wo, cosine, sine, low, kept):
    width = tokens.shape[1]
    wide = wo.shape[0]
    heads = wide // LANES
    stored = 0 if kept is None else 5
    saved = [
        shape_of((SLOTS, SEQ_LEN, width), BF16),
        shape_of((SLOTS, SEQ_LEN, width), BF16),
        shape_of((SLOTS, SEQ_LEN, 3 * wide), BF16),
        shape_of((SLOTS, SEQ_LEN, wide), BF16),
        shape_of((SLOTS, 8, SEQ_LEN), F32),
    ]

    def slot_rows(columns):
        return pl.BlockSpec((1, BLOCK, columns), lambda i, m, f: (m[1], i, 0))

    grid_spec = pltpu.PrefetchScalarGridSpec(
        num_scalar_prefetch=2,
        grid=(BLOCKS,),
        in_specs=[
            pl.BlockSpec((BLOCK, width), lambda i, m, f: (m[2] * BLOCKS + i, 0)),
            pl.BlockSpec((BLOCK, width), lambda i, m, f: (i, 0)),
            once((1, width), lambda i, m, f: (0, 0)),
            once(wall.shape, lambda i, m, f: (0, 0)),
            once(wo.shape, lambda i, m, f: (0, 0)),
            pl.BlockSpec((BLOCK, LANES), lambda i, m, f: (i, 0)),
            pl.BlockSpec((BLOCK, LANES), lambda i, m, f: (i, 0)),
            pl.BlockSpec((1, BLOCK, 1), lambda i, m, f: (m[2], i, 0)),
        ]
        + [pl.BlockSpec(memory_space=pl.ANY)] * stored,
        out_specs=[
            pl.BlockSpec((BLOCK, width), lambda i, m, f: (i, 0)),
            slot_rows(width),
            slot_rows(width),
            slot_rows(3 * wide),
            slot_rows(wide),
            pl.BlockSpec((1, 8, BLOCK), lambda i, m, f: (m[1], 0, i)),
        ],
        scratch_shapes=[
            pltpu.VMEM((SEQ_LEN, wide), BF16),
            pltpu.VMEM((SEQ_LEN, wide), BF16),
            pltpu.VMEM((heads, BLOCKS, BLOCK, BLOCK), F32),
            pltpu.VMEM((heads, BLOCK, LANES), F32),
            pltpu.VMEM((heads, BLOCK, LANES), F32),
            pltpu.VMEM((BLOCK, wide), F32),
        ],
    )
    outs = pl.pallas_call(
        functools.partial(attention_forward_kernel, stored),
        grid_spec=grid_spec,
        out_shape=[shape_of((SEQ_LEN, width), BF16)] + saved,
        input_output_aliases={10 + k: 1 + k for k in range(stored)},
        compiler_params=pltpu.CompilerParams(vmem_limit_bytes=VMEM_BYTES),
        name="attention_forward",
    )(
        meta,
        first_block,
        tokens,
        received,
        gain,
        wall,
        wo,
        cosine,
        sine,
        low,
        *(kept or ()),
    )
    return outs[0], outs[1:]


CHUNK = 96
ROW_CHUNK = 128


def pick_matrices(expert, post_ref, pos_ref, pick, put):
    def by_slot(step):
        slot_at = step * CHUNK + lax.broadcasted_iota(jnp.int32, (CHUNK, SEQ_LEN), 0)
        pick[rows_of(step, CHUNK), :] = jnp.where(
            slot_at == post_ref[0, pl.ds(expert, 1), :], 1.0, 0.0
        ).astype(BF16)

    loop(CAPACITY // CHUNK, by_slot)

    def by_token(step):
        rows = rows_of(step, ROW_CHUNK)
        places = pos_ref[0, rows, :]
        lane = lax.broadcasted_iota(jnp.int32, places.shape, 1)
        place = jnp.sum(jnp.where(lane == expert, places, 0), axis=1, keepdims=True)
        slot_at = lax.broadcasted_iota(jnp.int32, (ROW_CHUNK, CAPACITY), 1)
        put[rows, :] = jnp.where(slot_at == place, 1.0, 0.0).astype(BF16)

    loop(SEQ_LEN // ROW_CHUNK, by_token)


def slot_gates(expert, post_ref, probs_ref, gates):
    def body(step):
        slot_at = step * CHUNK + lax.broadcasted_iota(jnp.int32, (CHUNK, SEQ_LEN), 0)
        chosen = jnp.where(
            slot_at == post_ref[0, pl.ds(expert, 1), :], probs_ref[0, pl.ds(expert, 1), :], 0.0
        )
        gates[rows_of(step, CHUNK), :] = jnp.broadcast_to(
            jnp.sum(chosen, axis=1, keepdims=True), (CHUNK, LANES)
        )

    loop(CAPACITY // CHUNK, body)


def put_back(put, rows_in, total):
    def body(step):
        rows = rows_of(step, 2 * BLOCK)
        total[rows, :] += dot(put[rows, :], rows_in[...])

    loop(SEQ_LEN // (2 * BLOCK), body)


def feed_forward_kernel(
    stored,
    meta,
    x_ref,
    ar_ref,
    gain_ref,
    router_ref,
    post_ref,
    pos_ref,
    wg_ref,
    wu_ref,
    wd_ref,
    wgs_ref,
    wus_ref,
    wds_ref,
    *rest,
):
    rest = rest[stored:]
    part_ref, state_ref, h_ref, b_ref, xe_ref, g_ref, u_ref, gs_ref, us_ref, probs_ref = rest[:10]
    total, pick, put, gates, gate_value, lift_value, hidden, scaled = rest[10:]
    expert = pl.program_id(0)

    @pl.when(expert == 0)
    def _():
        def body(step):
            rows = rows_of(step, ROW_CHUNK)
            state = x_ref[0, rows, :].astype(F32) + ar_ref[rows, :].astype(F32)
            state_ref[rows, :] = state
            h_ref[0, rows, :] = state
            scale = lax.rsqrt(jnp.mean(state * state, axis=-1, keepdims=True) + 1e-06)
            b_ref[0, rows, :] = (gain_ref[...] * state * scale).astype(BF16)
            total[rows, :] = jnp.zeros((ROW_CHUNK, total.shape[1]), F32)

        loop(SEQ_LEN // ROW_CHUNK, body)
        logits = dot_nt(router_ref[...], b_ref[0])
        weights = jnp.exp(logits - jnp.max(logits, axis=0, keepdims=True))
        probs_ref[0] = weights / jnp.sum(weights, axis=0, keepdims=True)

    def activate(gate_in, lift_in, gate_out, lift_out, out, count):
        def body(step):
            rows = rows_of(step, CHUNK)
            gate, lift = gate_in[rows, :], lift_in[rows, :]
            gate_out[rows, :] = gate.astype(BF16)
            lift_out[rows, :] = lift.astype(BF16)
            out[rows, :] = (gate / (1.0 + jnp.exp(-gate)) * lift).astype(BF16)

        loop(count // CHUNK, body)

    @pl.when(expert < EXPERTS)
    def _():
        pick_matrices(expert, post_ref, pos_ref, pick, put)
        slot_gates(expert, post_ref, probs_ref, gates)
        xe_ref[0, 0] = dot(pick[...], b_ref[0]).astype(BF16)
        gate_value[:CAPACITY, :] = dot(xe_ref[0, 0], wg_ref[0])
        lift_value[:CAPACITY, :] = dot(xe_ref[0, 0], wu_ref[0])
        activate(
            gate_value, lift_value, g_ref.at[0, 0], u_ref.at[0, 0], hidden, CAPACITY
        )
        scaled[...] = (dot(hidden[:CAPACITY, :], wd_ref[0]) * gates[:, 0:1]).astype(BF16)
        put_back(put, scaled, total)

    @pl.when(expert == EXPERTS)
    def _():
        gate_value[...] = dot(b_ref[0], wgs_ref[...])
        lift_value[...] = dot(b_ref[0], wus_ref[...])
        activate(gate_value, lift_value, gs_ref.at[0], us_ref.at[0], hidden, SEQ_LEN)

        def body(step):
            rows = rows_of(step, 2 * BLOCK)
            part_ref[rows, :] = (total[rows, :] + dot(hidden[rows, :], wds_ref[...])).astype(BF16)

        loop(SEQ_LEN // (2 * BLOCK), body)


def feed_forward(meta, layer_in, ar, gain, router, post, pos, weights, kept):
    width = ar.shape[1]
    wg, wu, wd, wgs, wus, wds = weights
    hidden = wg.shape[2]
    stored = 0 if kept is None else 8
    saved = [
        shape_of((SLOTS, SEQ_LEN, width), F32),
        shape_of((SLOTS, SEQ_LEN, width), BF16),
        shape_of((SLOTS, EXPERTS, CAPACITY, width), BF16),
        shape_of((SLOTS, EXPERTS, CAPACITY, hidden), BF16),
        shape_of((SLOTS, EXPERTS, CAPACITY, hidden), BF16),
        shape_of((SLOTS, SEQ_LEN, hidden), BF16),
        shape_of((SLOTS, SEQ_LEN, hidden), BF16),
        shape_of((SLOTS, EXPERTS, SEQ_LEN), F32),
    ]

    def slot_whole(columns):
        return once((1, SEQ_LEN, columns), lambda e, m: (m[1], 0, 0))

    def slot_expert(columns):
        return pl.BlockSpec(
            (1, 1, CAPACITY, columns), lambda e, m: (m[1], jnp.minimum(e, EXPERTS - 1), 0, 0)
        )

    def fixed(shape):
        return once(shape, lambda e, m: (0,) * len(shape))

    def of_expert(array):
        return pl.BlockSpec(
            (1,) + array.shape[1:], lambda e, m: (jnp.minimum(e, EXPERTS - 1), 0, 0)
        )

    grid_spec = pltpu.PrefetchScalarGridSpec(
        num_scalar_prefetch=1,
        grid=(EXPERTS + 1,),
        in_specs=[
            slot_whole(width),
            fixed(ar.shape),
            fixed(gain.shape),
            fixed(router.shape),
            once((1, EXPERTS, SEQ_LEN), lambda e, m: (m[2], 0, 0)),
            once((1, SEQ_LEN, EXPERTS), lambda e, m: (m[2], 0, 0)),
            of_expert(wg),
            of_expert(wu),
            of_expert(wd),
            fixed(wgs.shape),
            fixed(wus.shape),
            fixed(wds.shape),
        ]
        + [pl.BlockSpec(memory_space=pl.ANY)] * stored,
        out_specs=[
            fixed((SEQ_LEN, width)),
            fixed((SEQ_LEN, width)),
            slot_whole(width),
            slot_whole(width),
            slot_expert(width),
            slot_expert(hidden),
            slot_expert(hidden),
            slot_whole(hidden),
            slot_whole(hidden),
            once((1, EXPERTS, SEQ_LEN), lambda e, m: (m[1], 0, 0)),
        ],
        scratch_shapes=[
            pltpu.VMEM((SEQ_LEN, width), F32),
            pltpu.VMEM((CAPACITY, SEQ_LEN), BF16),
            pltpu.VMEM((SEQ_LEN, CAPACITY), BF16),
            pltpu.VMEM((CAPACITY, LANES), F32),
            pltpu.VMEM((SEQ_LEN, hidden), F32),
            pltpu.VMEM((SEQ_LEN, hidden), F32),
            pltpu.VMEM((SEQ_LEN, hidden), BF16),
            pltpu.VMEM((CAPACITY, width), BF16),
        ],
    )
    outs = pl.pallas_call(
        functools.partial(feed_forward_kernel, stored),
        grid_spec=grid_spec,
        out_shape=[shape_of((SEQ_LEN, width), BF16), shape_of((SEQ_LEN, width), F32)] + saved,
        input_output_aliases={13 + k: 2 + k for k in range(stored)},
        compiler_params=pltpu.CompilerParams(vmem_limit_bytes=VMEM_BYTES),
        name="feed_forward",
    )(meta, layer_in, ar, gain, router, post, pos, wg, wu, wd, wgs, wus, wds, *(kept or ()))
    return outs[0], outs[1], outs[2:]


def feed_backward_kernel(
    stored,
    meta,
    cot_ref,
    rec_ref,
    post_ref,
    pos_ref,
    g_ref,
    u_ref,
    gs_ref,
    us_ref,
    probs_ref,
    wg_ref,
    wu_ref,
    wd_ref,
    wgs_ref,
    wus_ref,
    wds_ref,
    *rest,
):
    rest = rest[stored:]
    part_ref, choice_ref = rest[:2]
    dy_ref, hid_ref, dg_ref, du_ref, de_ref, hids_ref, dgs_ref, dus_ref = rest[2:10]
    total, pick, put, gates, back, rows_in, choice = rest[10:]
    expert = pl.program_id(0)

    @pl.when(expert == 0)
    def _():
        def body(step):
            rows = rows_of(step, ROW_CHUNK)
            given = jnp.where(meta[0] == 1, cot_ref[rows, :], rec_ref[rows, :])
            dy_ref[0, rows, :] = jnp.where(meta[0] == 0, jnp.zeros_like(given), given)
            total[rows, :] = jnp.zeros((ROW_CHUNK, total.shape[1]), F32)

        loop(SEQ_LEN // ROW_CHUNK, body)
        choice[...] = jnp.zeros_like(choice)

    def pull(gate_in, lift_in, weight, rows, hid, grad_gate, grad_lift):
        gate, lift = gate_in[rows, :].astype(F32), lift_in[rows, :].astype(F32)
        sigma = 1.0 / (1.0 + jnp.exp(-gate))
        swish = gate * sigma
        hidden = (swish * lift).astype(BF16)
        hid[rows, :] = hidden
        grad = back[rows, :]
        inner = jnp.sum(hidden.astype(F32) * grad, axis=1, keepdims=True)
        if weight is not None:
            grad = grad * weight
        grad_gate[rows, :] = (grad * lift * sigma * (1.0 + gate * (1.0 - sigma))).astype(BF16)
        grad_lift[rows, :] = (grad * swish).astype(BF16)
        return inner

    @pl.when(expert < EXPERTS)
    def _():
        pick_matrices(expert, post_ref, pos_ref, pick, put)
        slot_gates(expert, post_ref, probs_ref, gates)
        rows_in[...] = dot(pick[...], dy_ref[0]).astype(BF16)
        back[:CAPACITY, :] = dot_nt(rows_in[...], wd_ref[0])

        def body(step):
            rows = rows_of(step, CHUNK)
            weight = gates[rows, 0:1]
            inner = pull(
                g_ref.at[0, 0],
                u_ref.at[0, 0],
                weight,
                rows,
                hid_ref.at[0, 0],
                dg_ref.at[0, 0],
                du_ref.at[0, 0],
            )
            de_ref[0, 0, rows, :] = (weight * rows_in[rows, :].astype(F32)).astype(BF16)
            slot_at = step * CHUNK + lax.broadcasted_iota(jnp.int32, (CHUNK, SEQ_LEN), 0)
            mine = slot_at == post_ref[0, pl.ds(expert, 1), :]
            choice[pl.ds(expert, 1), :] += jnp.sum(
                jnp.where(mine, inner, 0.0), axis=0, keepdims=True
            )

        loop(CAPACITY // CHUNK, body)
        rows_in[...] = (
            dot_nt(dg_ref[0, 0], wg_ref[0]) + dot_nt(du_ref[0, 0], wu_ref[0])
        ).astype(BF16)
        put_back(put, rows_in, total)

    @pl.when(expert == EXPERTS)
    def _():
        back[...] = dot_nt(dy_ref[0], wds_ref[...])

        def body(step):
            pull(
                gs_ref.at[0],
                us_ref.at[0],
                None,
                rows_of(step, CHUNK),
                hids_ref.at[0],
                dgs_ref.at[0],
                dus_ref.at[0],
            )

        loop(SEQ_LEN // CHUNK, body)

        def finish(step):
            rows = rows_of(step, 2 * BLOCK)
            part_ref[rows, :] = (
                total[rows, :]
                + dot_nt(dgs_ref[0, rows, :], wgs_ref[...])
                + dot_nt(dus_ref[0, rows, :], wus_ref[...])
            ).astype(BF16)

        loop(SEQ_LEN // (2 * BLOCK), finish)
        half = SEQ_LEN // 2
        blank = jnp.zeros((8, half), F32)
        choice_ref[...] = jnp.concatenate(
            [choice[:, :half], blank, choice[:, half:], blank], axis=0
        ).astype(BF16)


def feed_backward(meta, cotangent, received, post, pos, forward_kept, weights, kept):
    width = cotangent.shape[1]
    wg, wu, wd, wgs, wus, wds = weights
    hidden = wg.shape[2]
    stored = 0 if kept is None else 8
    unused_h, unused_b, unused_x, gate, lift, gate_sh, lift_sh, probs = forward_kept
    saved = [
        shape_of((SLOTS, SEQ_LEN, width), BF16),
        shape_of((SLOTS, EXPERTS, CAPACITY, hidden), BF16),
        shape_of((SLOTS, EXPERTS, CAPACITY, hidden), BF16),
        shape_of((SLOTS, EXPERTS, CAPACITY, hidden), BF16),
        shape_of((SLOTS, EXPERTS, CAPACITY, width), BF16),
        shape_of((SLOTS, SEQ_LEN, hidden), BF16),
        shape_of((SLOTS, SEQ_LEN, hidden), BF16),
        shape_of((SLOTS, SEQ_LEN, hidden), BF16),
    ]

    def slot_whole(columns, which):
        return once((1, SEQ_LEN, columns), lambda e, m: (m[which], 0, 0))

    def slot_expert(columns, which):
        return pl.BlockSpec(
            (1, 1, CAPACITY, columns), lambda e, m: (m[which], jnp.minimum(e, EXPERTS - 1), 0, 0)
        )

    def fixed(shape):
        return once(shape, lambda e, m: (0,) * len(shape))

    def of_expert(array):
        return pl.BlockSpec(
            (1,) + array.shape[1:], lambda e, m: (jnp.minimum(e, EXPERTS - 1), 0, 0)
        )

    grid_spec = pltpu.PrefetchScalarGridSpec(
        num_scalar_prefetch=1,
        grid=(EXPERTS + 1,),
        in_specs=[
            once((SEQ_LEN, width), lambda e, m: (m[2], 0)),
            fixed((SEQ_LEN, width)),
            once((1, EXPERTS, SEQ_LEN), lambda e, m: (m[2], 0, 0)),
            once((1, SEQ_LEN, EXPERTS), lambda e, m: (m[2], 0, 0)),
            slot_expert(hidden, 3),
            slot_expert(hidden, 3),
            slot_whole(hidden, 3),
            slot_whole(hidden, 3),
            once((1, EXPERTS, SEQ_LEN), lambda e, m: (m[3], 0, 0)),
            of_expert(wg),
            of_expert(wu),
            of_expert(wd),
            fixed(wgs.shape),
            fixed(wus.shape),
            fixed(wds.shape),
        ]
        + [pl.BlockSpec(memory_space=pl.ANY)] * stored,
        out_specs=[
            fixed((SEQ_LEN, width)),
            fixed((32, SEQ_LEN // 2)),
            slot_whole(width, 1),
            slot_expert(hidden, 1),
            slot_expert(hidden, 1),
            slot_expert(hidden, 1),
            slot_expert(width, 1),
            slot_whole(hidden, 1),
            slot_whole(hidden, 1),
            slot_whole(hidden, 1),
        ],
        scratch_shapes=[
            pltpu.VMEM((SEQ_LEN, width), F32),
            pltpu.VMEM((CAPACITY, SEQ_LEN), BF16),
            pltpu.VMEM((SEQ_LEN, CAPACITY), BF16),
            pltpu.VMEM((CAPACITY, LANES), F32),
            pltpu.VMEM((SEQ_LEN, hidden), F32),
            pltpu.VMEM((CAPACITY, width), BF16),
            pltpu.VMEM((EXPERTS, SEQ_LEN), F32),
        ],
    )
    outs = pl.pallas_call(
        functools.partial(feed_backward_kernel, stored),
        grid_spec=grid_spec,
        out_shape=[shape_of((SEQ_LEN, width), BF16), shape_of((32, SEQ_LEN // 2), BF16)] + saved,
        input_output_aliases={16 + k: 2 + k for k in range(stored)},
        compiler_params=pltpu.CompilerParams(vmem_limit_bytes=VMEM_BYTES),
        name="feed_backward",
    )(
        meta,
        cotangent,
        received,
        post,
        pos,
        gate,
        lift,
        gate_sh,
        lift_sh,
        probs,
        wg,
        wu,
        wd,
        wgs,
        wus,
        wds,
        *(kept or ()),
    )
    return outs[0], outs[1], outs[2:]


def attention_backward_kernel(
    stored,
    meta,
    first_block,
    sum_ref,
    choice_ref,
    probs_ref,
    dy_ref,
    h_ref,
    b_ref,
    gain_ref,
    router_ref,
    wall_ref,
    wo_ref,
    cos_ref,
    sin_ref,
    qkv_ref,
    o_ref,
    lse_ref,
    low_ref,
    *rest,
):
    rest = rest[stored:]
    part_ref, dh_ref, gain_grad_ref, router_grad_ref, dqkv_ref, dattn_ref = rest[:6]
    dk_all, dv_all, dq_all, do_all, inner_all = rest[6:]
    step = pl.program_id(0)
    index = BLOCKS - 1 - step
    heads = wo_ref.shape[0] // LANES
    wide = heads * LANES

    @pl.when(step == 0)
    def _():
        gain_grad_ref[...] = jnp.zeros_like(gain_grad_ref)
        router_grad_ref[...] = jnp.zeros_like(router_grad_ref)
        dk_all[...] = jnp.zeros_like(dk_all)
        dv_all[...] = jnp.zeros_like(dv_all)

    probs = probs_ref[0]
    chosen = choice_ref[0:8, :].astype(F32)
    logit_grads = probs * (chosen - jnp.sum(probs * chosen, axis=0, keepdims=True))
    logit_grads = logit_grads.astype(BF16)
    router_grad_ref[...] += dot(logit_grads, b_ref[0])
    grad_normed = sum_ref[...].astype(F32) + dot_tn(logit_grads, router_ref[...])
    state = h_ref[0]
    scale = lax.rsqrt(jnp.mean(state * state, axis=-1, keepdims=True) + 1e-06)
    normed = state * scale
    gain_grad_ref[...] += jnp.sum(grad_normed * normed, axis=0, keepdims=True)
    scaled = gain_ref[...] * grad_normed
    inner = jnp.mean(normed * scaled, axis=-1, keepdims=True)
    grad_state = dy_ref[0].astype(F32) + scale * (scaled - normed * inner)
    dh_ref[...] = grad_state
    dattn = grad_state.astype(BF16)
    dattn_ref[0] = dattn
    do = dot_nt(dattn, wo_ref[...]).astype(BF16)
    do_all[...] = do
    products = do.astype(F32) * o_ref[0].astype(F32)
    for head in range(heads):
        columns = slice(head * LANES, (head + 1) * LANES)
        row = jnp.sum(products[:, columns], axis=1, keepdims=True)
        inner_all[head : head + 1, :] = jnp.broadcast_to(row, (BLOCK, LANES)).T[0:1, :]
    dq_all[...] = jnp.zeros_like(dq_all)
    here = rows_of(index, BLOCK)
    low = low_ref[0]
    query_at = index * BLOCK + lax.broadcasted_iota(jnp.int32, (BLOCK, BLOCK), 1)
    key_at = lax.broadcasted_iota(jnp.int32, (BLOCK, BLOCK), 0)

    def body(block, none):
        at = key_at + block * BLOCK
        valid = (at >= low) & (at <= query_at)
        there = rows_of(block, BLOCK)
        for head in range(heads):
            columns = slice(head * LANES, (head + 1) * LANES)
            key_columns = slice(wide + head * LANES, wide + (head + 1) * LANES)
            value_columns = slice(2 * wide + head * LANES, 2 * wide + (head + 1) * LANES)
            query = qkv_ref[0, here, columns]
            keys = qkv_ref[0, there, key_columns]
            scores = jnp.where(valid, dot_nt(keys, query), -1e30)
            probs = jnp.exp(scores - lse_ref[0, head : head + 1, :])
            grad_probs = dot_nt(qkv_ref[0, there, value_columns], do_all[:, columns])
            grad_scores = (probs * (grad_probs - inner_all[head : head + 1, :])).astype(BF16)
            dv_all[there, columns] += dot(probs.astype(BF16), do_all[:, columns])
            dk_all[there, columns] += dot(grad_scores, query)
            dq_all[:, columns] += dot_tn(grad_scores, keys)
        return none

    lax.fori_loop(first_block[meta[2] * BLOCKS + index], index + 1, body, 0)
    cosine, sine = cos_ref[...], sin_ref[...]
    for head in range(heads):
        columns = slice(head * LANES, (head + 1) * LANES)
        key_columns = slice(wide + head * LANES, wide + (head + 1) * LANES)
        value_columns = slice(2 * wide + head * LANES, 2 * wide + (head + 1) * LANES)
        dq = dq_all[:, columns] * 0.0625
        dk = dk_all[here, columns]
        dqkv_ref[0, :, columns] = (dq * cosine - pltpu.roll(dq, HEAD_DIM, 1) * sine).astype(BF16)
        dqkv_ref[0, :, key_columns] = (
            dk * cosine - pltpu.roll(dk, HEAD_DIM, 1) * sine
        ).astype(BF16)
        dqkv_ref[0, :, value_columns] = dv_all[here, columns].astype(BF16)
    part_ref[...] = dot_nt(dqkv_ref[0], wall_ref[...]).astype(BF16)


def attention_backward(
    meta, first_block, summed, choice, forward_kept, attention_kept, dy, gain, router, wall, wo, cosine, sine, low, kept
):
    width = summed.shape[1]
    wide = wo.shape[0]
    stored = 0 if kept is None else 2
    h, b, probs = forward_kept[0], forward_kept[1], forward_kept[7]
    unused_x, unused_a, qkv, o, lse = attention_kept
    saved = [
        shape_of((SLOTS, SEQ_LEN, 3 * wide), BF16),
        shape_of((SLOTS, SEQ_LEN, width), BF16),
    ]

    def at(step):
        return BLOCKS - 1 - step

    def slot_rows(columns, which):
        return pl.BlockSpec((1, BLOCK, columns), lambda s, m, f: (m[which], at(s), 0))

    def fixed(shape):
        return once(shape, lambda s, m, f: (0,) * len(shape))

    halves_of = BLOCKS // 2
    grid_spec = pltpu.PrefetchScalarGridSpec(
        num_scalar_prefetch=2,
        grid=(BLOCKS,),
        in_specs=[
            pl.BlockSpec((BLOCK, width), lambda s, m, f: (at(s), 0)),
            pl.BlockSpec((16, BLOCK), lambda s, m, f: (at(s) // halves_of, at(s) % halves_of)),
            pl.BlockSpec((1, EXPERTS, BLOCK), lambda s, m, f: (m[3], 0, at(s))),
            slot_rows(width, 1),
            slot_rows(width, 3),
            slot_rows(width, 3),
            fixed(gain.shape),
            fixed(router.shape),
            fixed(wall.shape),
            fixed(wo.shape),
            pl.BlockSpec((BLOCK, LANES), lambda s, m, f: (at(s), 0)),
            pl.BlockSpec((BLOCK, LANES), lambda s, m, f: (at(s), 0)),
            once((1, SEQ_LEN, 3 * wide), lambda s, m, f: (m[3], 0, 0)),
            slot_rows(wide, 3),
            pl.BlockSpec((1, 8, BLOCK), lambda s, m, f: (m[3], 0, at(s))),
            pl.BlockSpec((1, 1, BLOCK), lambda s, m, f: (m[2], 0, at(s))),
        ]
        + [pl.BlockSpec(memory_space=pl.ANY)] * stored,
        out_specs=[
            pl.BlockSpec((BLOCK, width), lambda s, m, f: (at(s), 0)),
            pl.BlockSpec((BLOCK, width), lambda s, m, f: (at(s), 0)),
            fixed((1, width)),
            fixed((8, width)),
            slot_rows(3 * wide, 1),
            slot_rows(width, 1),
        ],
        scratch_shapes=[
            pltpu.VMEM((SEQ_LEN, wide), F32),
            pltpu.VMEM((SEQ_LEN, wide), F32),
            pltpu.VMEM((BLOCK, wide), F32),
            pltpu.VMEM((BLOCK, wide), BF16),
            pltpu.VMEM((8, BLOCK), F32),
        ],
    )
    outs = pl.pallas_call(
        functools.partial(attention_backward_kernel, stored),
        grid_spec=grid_spec,
        out_shape=[
            shape_of((SEQ_LEN, width), BF16),
            shape_of((SEQ_LEN, width), F32),
            shape_of((1, width), F32),
            shape_of((8, width), F32),
        ]
        + saved,
        input_output_aliases={18 + k: 4 + k for k in range(stored)},
        compiler_params=pltpu.CompilerParams(vmem_limit_bytes=VMEM_BYTES),
        name="attention_backward",
    )(
        meta,
        first_block,
        summed,
        choice,
        probs,
        dy,
        h,
        b,
        gain,
        router,
        wall,
        wo,
        cosine,
        sine,
        qkv,
        o,
        lse,
        low,
        *(kept or ()),
    )
    return outs[:4], outs[4:]


def expert_grads_kernel(*refs):
    ins, out_ref = refs[:-1], refs[-1]
    (xa, xb), (ga, gb), (ua, ub), (ea, eb), (ha, hb) = (ins[2 * k : 2 * k + 2] for k in range(5))
    devices, unused, rows, unused = out_ref.shape
    pairs = [((xa, xb), (ga, gb)), ((xa, xb), (ua, ub)), ((ea, eb), (ha, hb))]
    for number, (left, right) in enumerate(pairs):
        for device in range(devices):
            columns = slice(device * rows, (device + 1) * rows)
            out_ref[device, number] = (
                dot_tn(left[0][0, 0, :, columns], right[0][0, 0])
                + dot_tn(left[1][0, 0, :, columns], right[1][0, 0])
            ).astype(BF16)


def expert_grads(first, count, devices, picked, hid, grad_gate, grad_lift, grad_expert):
    width, hidden = picked.shape[3], hid.shape[3]
    rows = width // devices

    def pair(columns):
        return [
            pl.BlockSpec(
                (1, 1, CAPACITY, columns), functools.partial(lambda slot, e: (slot, first + e, 0, 0), slot)
            )
            for slot in (1, 2)
        ]

    return pl.pallas_call(
        expert_grads_kernel,
        grid=(count,),
        in_specs=pair(width) + pair(hidden) + pair(hidden) + pair(width) + pair(hidden),
        out_specs=pl.BlockSpec((devices, 3, rows, hidden), lambda e: (0, e, 0, 0)),
        out_shape=shape_of((devices, 3 * count, rows, hidden), BF16),
        compiler_params=pltpu.CompilerParams(vmem_limit_bytes=VMEM_BYTES),
        name="expert_grads",
    )(
        *(picked, picked, grad_gate, grad_gate, grad_lift, grad_lift),
        *(grad_expert, grad_expert, hid, hid),
    )


def token_grads_kernel(count, *refs):
    lefts, rights = refs[:count], refs[count : 2 * count]
    outs, totals = refs[2 * count : 3 * count], refs[3 * count :]
    step = pl.program_id(0)

    @pl.when(step == 0)
    def _():
        for total in totals:
            total[...] = jnp.zeros_like(total)

    for left, right, total in zip(lefts, rights, totals):
        total[...] += dot_tn(left[0], right[0])

    @pl.when(step == pl.num_programs(0) - 1)
    def _():
        for out, total in zip(outs, totals):
            out[...] = total[...].astype(BF16)


def token_grads(lefts, rights):
    count = len(lefts)
    rows = 2 * BLOCK
    steps = SEQ_LEN // rows

    def spec(array):
        return pl.BlockSpec((1, rows, array.shape[2]), lambda s: (1 + s // steps, s % steps, 0))

    shapes = [(left.shape[2], right.shape[2]) for left, right in zip(lefts, rights)]
    return pl.pallas_call(
        functools.partial(token_grads_kernel, count),
        grid=(2 * steps,),
        in_specs=[spec(a) for a in lefts] + [spec(a) for a in rights],
        out_specs=[once(shape, lambda s: (0, 0)) for shape in shapes],
        out_shape=[shape_of(shape, BF16) for shape in shapes],
        scratch_shapes=[pltpu.VMEM(shape, F32) for shape in shapes],
        compiler_params=pltpu.CompilerParams(vmem_limit_bytes=VMEM_BYTES),
        name="token_grads",
    )(*lefts, *rights)


def rotary_tables():
    half = HEAD_DIM // 2
    rates = np.exp(-np.log(10000.0) * np.arange(half) * 2.0 / HEAD_DIM)
    angles = np.arange(SEQ_LEN)[:, None] * rates[None, :]
    cosine, sine = np.cos(angles), np.sin(angles)
    cosine = np.concatenate([cosine] * 4, axis=1)
    sine = np.concatenate([sine, sine, -sine, -sine], axis=1)
    return jnp.asarray(cosine, F32), jnp.asarray(sine, F32)


def paired(weight):
    rows = weight.shape[0]
    heads = weight.shape[1] // HEAD_DIM
    half = HEAD_DIM // 2
    split = weight.reshape(rows, heads, HEAD_DIM)
    swapped = jnp.concatenate([-split[:, :, half:], split[:, :, :half]], axis=2)
    return jnp.concatenate([split, swapped], axis=2).reshape(rows, heads * LANES)


def padded(weight):
    rows = weight.shape[0]
    heads = weight.shape[1] // HEAD_DIM
    split = weight.reshape(rows, heads, HEAD_DIM)
    return jnp.concatenate([split, jnp.zeros_like(split)], axis=2).reshape(rows, heads * LANES)


def unpadded(grads):
    rows = grads.shape[0]
    return grads.reshape(rows, -1, LANES)[:, :, :HEAD_DIM].reshape(rows, -1)


def places(routes):
    experts = jnp.arange(EXPERTS, dtype=jnp.int32)
    named = jnp.any(routes[:, :, :, None] == experts, axis=2)
    before = (
        jnp.arange(SEQ_LEN, dtype=jnp.int32)[:, None] > jnp.arange(SEQ_LEN, dtype=jnp.int32)
    ).astype(BF16)
    rank = jnp.einsum("ts,nse->nte", before, named.astype(BF16), preferred_element_type=F32)
    by_token = jnp.where(named, rank.astype(jnp.int32), -1)
    return by_token, jnp.swapaxes(by_token, 1, 2)


def first_allowed(lengths):
    ends = jnp.cumsum(lengths, axis=1)
    at = jnp.arange(SEQ_LEN, dtype=jnp.int32)
    starts = jnp.max(jnp.where(ends[:, None, :] <= at[None, :, None], ends[:, None, :], 0), axis=2)
    return jnp.maximum(starts, at[None, :] - (WINDOW - 1)).astype(jnp.int32)


def on_device(
    tokens,
    doc_lengths,
    routes,
    gain_attn,
    w_query,
    w_key,
    w_value,
    w_output,
    gain_ffn,
    w_router,
    w_gate_exp,
    w_up_exp,
    w_down_exp,
    w_gate_sh,
    w_up_sh,
    w_down_sh,
    cotangent,
):
    section = lax.axis_index("section")
    devices = lax.axis_size("dp")
    count = doc_lengths.shape[0]
    width = tokens.shape[1]
    cosine, sine = rotary_tables()
    wall = jnp.concatenate([paired(w_query[0]), paired(w_key[0]), padded(w_value[0])], axis=1)
    wo = padded(w_output[0].T).T
    router = w_router[0].T
    gain_a, gain_f = gain_attn.astype(F32), gain_ffn.astype(F32)
    feed_weights = (
        w_gate_exp[0],
        w_up_exp[0],
        w_down_exp[0],
        w_gate_sh[0],
        w_up_sh[0],
        w_down_sh[0],
    )
    pos, post = places(routes[0].reshape(count, SEQ_LEN, 2))
    low = first_allowed(doc_lengths)
    first_block = (low[:, ::BLOCK] // BLOCK).reshape(-1)
    low_column, low_row = low[:, :, None], low[:, None, :]

    received = jnp.zeros((SEQ_LEN, width), BF16)
    attention_kept, feed_kept, results = None, None, []
    for tick in range(count + 1):
        raw = tick - section
        active = (raw >= 0) & (raw < count)
        sequence = jnp.clip(raw, 0, count - 1)
        meta = jnp.stack([section, jnp.where(active, sequence + 1, 0), sequence]).astype(jnp.int32)
        part, attention_kept = attention_forward(
            meta,
            first_block,
            tokens,
            received,
            gain_a,
            wall,
            wo,
            cosine,
            sine,
            low_column,
            attention_kept,
        )
        (summed,) = tensor_sum([part], (6,), 0)
        part, state, feed_kept = feed_forward(
            meta, attention_kept[0], summed, gain_f, router, post, pos, feed_weights, feed_kept
        )
        result, received = output_relay(part, state, 1)
        results.append(result)

    received = jnp.zeros((SEQ_LEN, width), BF16)
    grads_kept, attention_grads_kept, inputs = None, None, []
    small = jnp.zeros((10, width), F32)
    for tick in range(count + 1):
        raw = tick - 1 + section
        active = (raw >= 0) & (raw < count)
        sequence = jnp.clip(raw, 0, count - 1)
        source = jnp.where(active, 2 - section, 0)
        meta = jnp.stack(
            [source, jnp.where(active, sequence + 1, 0), sequence, sequence + 1]
        ).astype(jnp.int32)
        part, choice, grads_kept = feed_backward(
            meta, cotangent, received, post, pos, feed_kept, feed_weights, grads_kept
        )
        summed, choice = tensor_sum([part, choice], (6, 1), 2)
        (part, grad_state, gain_grad, router_grad), attention_grads_kept = attention_backward(
            meta,
            first_block,
            summed,
            choice,
            feed_kept,
            attention_kept,
            grads_kept[0],
            gain_f,
            router,
            wall,
            wo,
            cosine,
            sine,
            low_row,
            attention_grads_kept,
        )
        layer_in = lax.dynamic_index_in_dim(attention_kept[0], sequence + 1, 0, False)
        grad_input, received, gain_attn_grad = input_relay(part, layer_in, grad_state, gain_a, 3)
        inputs.append(grad_input)
        small = small + jnp.concatenate([gain_attn_grad, gain_grad, router_grad], axis=0)

    def spread(array):
        return lax.psum_scatter(array, "dp", scatter_dimension=0, tiled=False)

    dy, hid, grad_gate, grad_lift, grad_expert, hid_sh, grad_gate_sh, grad_lift_sh = grads_kept
    groups = 4
    size = EXPERTS // groups
    expert_parts = [
        spread(
            expert_grads(
                group * size, size, devices, feed_kept[2], hid, grad_gate, grad_lift, grad_expert
            )
        )
        for group in range(groups)
    ]
    rows = width // devices
    shared = token_grads([feed_kept[1], feed_kept[1], dy], [grad_gate_sh, grad_lift_sh, hid_sh])
    shared = spread(jnp.stack(shared).reshape(3, devices, rows, -1).swapaxes(0, 1))
    projections, outward = token_grads(
        [attention_kept[1], attention_grads_kept[1]], [attention_grads_kept[0], attention_kept[3]]
    )
    wide = wo.shape[0]
    columns = w_query.shape[2]
    packed = jnp.concatenate(
        [
            2.0 * unpadded(projections[:, : 2 * wide]),
            unpadded(projections[:, 2 * wide :]),
            unpadded(outward),
            jnp.pad(small, ((0, 6), (0, 0))).T.astype(BF16),
        ],
        axis=1,
    )
    packed = spread(packed.reshape(devices, rows, -1)).astype(F32)
    shared = shared.astype(F32)
    experts = jnp.concatenate(expert_parts, axis=0).astype(F32)
    experts = experts.reshape(EXPERTS, 3, rows, -1)

    def choose(items):
        return jnp.concatenate(
            [jnp.where(section == 0, items[k], items[k + 1]) for k in range(count)], axis=0
        )

    layer_out = choose(results)
    input_grad = jnp.concatenate(
        [jnp.where(section == 0, inputs[k + 1], inputs[k]) for k in range(count)], axis=0
    )
    extra = 4 * columns
    return (
        layer_out[None],
        input_grad[None],
        packed[None, :, extra],
        packed[None, :, :columns],
        packed[None, :, columns : 2 * columns],
        packed[None, :, 2 * columns : 3 * columns],
        packed[:, 3 * columns : extra].T[None],
        packed[None, :, extra + 1],
        packed[None, :, extra + 2 : extra + 10],
        experts[None, :, 0],
        experts[None, :, 1],
        jnp.swapaxes(experts[:, 2], 1, 2)[None],
        shared[None, 0],
        shared[None, 1],
        shared[2].T[None],
    )


def solution(mesh):
    return jax.shard_map(
        on_device,
        mesh=mesh,
        in_specs=(
            P("dp", None),
            P("dp", None),
            P("section", "dp", None),
            P("section", None),
            P("section", None, "tensor"),
            P("section", None, "tensor"),
            P("section", None, "tensor"),
            P("section", "tensor", None),
            P("section", None),
            P("section", None, None),
            P("section", None, None, "tensor"),
            P("section", None, None, "tensor"),
            P("section", None, "tensor", None),
            P("section", None, "tensor"),
            P("section", None, "tensor"),
            P("section", "tensor", None),
            P("dp", None),
        ),
        out_specs=(
            P("section", "dp", None),
            P("section", "dp", None),
            P("section", "dp"),
            P("section", "dp", "tensor"),
            P("section", "dp", "tensor"),
            P("section", "dp", "tensor"),
            P("section", "tensor", "dp"),
            P("section", "dp"),
            P("section", "dp", None),
            P("section", None, "dp", "tensor"),
            P("section", None, "dp", "tensor"),
            P("section", None, "tensor", "dp"),
            P("section", "dp", "tensor"),
            P("section", "dp", "tensor"),
            P("section", "tensor", "dp"),
        ),
        check_vma=False,
    )
```

time: 3800 us -> 1660 us (0.44)
  waiting for transfers between devices: 1810 us -> 297 us
  Pallas kernels: 0 us -> 1270 us
  local copies, waits for them, and re-layouts: 660 us -> 31.8 us
  matrix products: 574 us -> 3.58 us
  other arithmetic: 575 us -> 41.5 us
  loops' own time: 71.6 us -> 0 us
  blocking collectives: 66.1 us -> 0 us
    pallas_call x0 -> x30, Pallas kernels: none -> 1270 us  [the longest x3 269 us: feed_backward(): pl.pallas_call(functools.partial(feed_backward_kernel, stored), grid_spec...]
    psum x12 -> x0, waiting for transfers between devices: 1100 us -> none  [the longest x3 340 us: backward_tick(): lax.psum(grad_attn_part.astype(jnp.bfloat16), 'tensor').astype(jnp.float32)]
    dot_general x124 -> x1, matrix products: 574 us -> 3.58 us  [places(): jnp.einsum('ts,nse->nte', before, named.astype(BF16), preferred_element_t...]
    gather x32 -> x0, local copies, waits for them, and re-layouts: 337 us -> none  [the longest x12 79.6 us: gate_choice(): return jnp.take_along_axis(jax.nn.softmax(logits, axis=-1), routes, axis=1)]
    ppermute x6 -> x0, waiting for transfers between devices: 261 us -> none  [from_behind(): return lax.ppermute(block, axis, route)]
    add x62 -> x0, other arithmetic: 181 us -> none  [the longest x30 163 us: backward_tick(): totals = tuple(jax.tree.map(jnp.add, totals, tick_grads))]
    convert_element_type x53 -> x5, other arithmetic: 117 us -> 6.13 us  [the longest x2 2.54 us: on_device(): gain_a, gain_f = (gain_attn.astype(F32), gain_ffn.astype(F32))]
    reduce_scatter x6, waiting for transfers between devices: 401 us -> 297 us  [spread(): return lax.psum_scatter(array, 'dp', scatter_dimension=0, tiled=False)]
  transfers between devices with their start and end apart: 29 -> 6, of which waited for: 25 -> 4; matrix products, arithmetic and copies ran while one was open for 7% -> 1% of each run, Pallas kernels for 0% -> 7%
where the time goes in v1:
time: 1660 us
  Pallas kernels  1270 us (77%)
  waiting for transfers between devices  297 us (18%)
  other arithmetic  41.5 us (2%)
  local copies, waits for them, and re-layouts  31.8 us (2%)
    reduce_scatter x6, waiting for transfers between devices, spread(): return lax.psum_scatter(array, 'dp', scatter_dimension=0, tiled=False)  297 us
    pallas_call x3, Pallas kernels, feed_backward(): pl.pallas_call(functools.partial(feed_backward_kernel, stored), grid_spec...  269 us
    pallas_call x3, Pallas kernels, feed_forward(): pl.pallas_call(functools.partial(feed_forward_kernel, stored), grid_spec=...  246 us
    pallas_call x6, Pallas kernels, tensor_sum(): pl.pallas_call(functools.partial(sum_kernel, counts), out_shape=[shape_of...  207 us
    pallas_call x3, Pallas kernels, input_relay(): pl.pallas_call(functools.partial(input_kernel, pieces), out_shape=[shape_...  135 us
    pallas_call x3, Pallas kernels, output_relay(): pl.pallas_call(functools.partial(output_kernel, pieces), out_shape=[shape...  131 us
    pallas_call x3, Pallas kernels, attention_backward(): pl.pallas_call(functools.partial(attention_backward_kernel, stored), grid...  120 us
    pallas_call x3, Pallas kernels, attention_forward(): pl.pallas_call(functools.partial(attention_forward_kernel, stored), grid_...  78.4 us
  transfers between devices with their start and end apart: 6, of which 4 were waited for; matrix products, arithmetic and copies ran while one was open for 1% of the time, Pallas kernels for 7%

profile of v1, /device:TPU:0, one launch (start us, length us, event | category | flops | bytes accessed | tf_op | source)
XLA Modules:
  0.0 1655.4 jit_solution(4092383629139087454)
XLA Ops:
  9.0 1.3 convert_element_type.38.gain_ref
  10.2 1.3 convert_element_type.39.gain_ref
  13.0 1.0 slice_negate_fusion.1
  14.0 1.0 pad_maximum_fusion.3
  15.3 1.0 slice_negate_fusion
  16.7 1.2 copy.244
  18.3 1.8 concatenate.48
  20.6 1.4 broadcast_maximum_fusion.low_ref
  22.1 3.6 bitcast_select_fusion.1
  25.7 2.5 copy.247.post_ref
  28.1 2.3 bitcast_select_fusion.pos_ref
  30.4 1.4 pad_maximum_fusion.1.wall_ref
  32.5 1.6 broadcast_6_rec_ref.2.rec_ref
  34.0 27.2 %attention_forward.3 = (bf16[1536,768]{1,0:T(8,128)(2,1)}, bf16[3,1536,768]{2,1,0:T(8,128)(2,1)}, bf16[3,1536,768]{2,1,0:T(8,128)(2,1)}, bf16[3,1536,1152]{2,1,0...) custom-call(s32[3]{0:T(128)} %get-tuple-element.355.meta, s32[12]{0:T(128)} %reshape.148.first_block, ...), custom_call_target="tpu_custom_call" | custom-call | tf_op jit(solution)/shard_map/attention_forward/pallas_call | solution.py:508
  61.2 35.1 %tensor_sum.6.ar_ref = bf16[1536,768]{1,0:T(8,128)(2,1)} custom-call(bf16[1536,768]{1,0:T(8,128)(2,1)} %get-tuple-element.136.refs_0_), custom_call_target="tpu_custom_call" | custom-call | tf_op jit(solution)/shard_map/tensor_sum/pallas_call | solution.py:160
  96.3 82.1 %feed_forward.3 = (bf16[1536,768]{1,0:T(8,128)(2,1)}, f32[1536,768]{1,0:T(8,128)}, f32[3,1536,768]{2,1,0:T(8,128)}, bf16[3,1536,768]{2,1,0:T(8,128)(2,1)}, bf16[...) custom-call(s32[3]{0:T(128)} %get-tuple-element.355.meta, ...), custom_call_target="tpu_custom_call" | custom-call | tf_op jit(solution)/shard_map/feed_forward/pallas_call | solution.py:723
  178.4 43.4 %output_relay.3 = (bf16[1536,768]{1,0:T(8,128)(2,1)}, bf16[1536,768]{1,0:T(8,128)(2,1)}) custom-call(bf16[1536,768]{1,0:T(8,128)(2,1)} %get-tuple-element.137.part_ref, f32[1536,768]{1,0:T(8,128)} %get-tuple-element.138.state_ref), custom_call_target="tpu_custom_call" | custom-call | tf_op jit(solution)/shard_map/output_relay/pallas_call | solution.py:339
  221.9 25.8 %attention_forward.4 = (bf16[1536,768]{1,0:T(8,128)(2,1)}, bf16[3,1536,768]{2,1,0:T(8,128)(2,1)}, bf16[3,1536,768]{2,1,0:T(8,128)(2,1)}, bf16[3,1536,1152]{2,1,0...) custom-call(s32[3]{0:T(128)} %get-tuple-element.356.meta, ...), custom_call_target="tpu_custom_call", output_to_operand_aliasing={{1}: (10, {}), {2}: (11, {}), {3}: (12, {}), {4}: (13, {}),... | custom-call | tf_op jit(solution)/shard_map/attention_forward/pallas_call | solution.py:508
  247.6 34.2 %tensor_sum.7.ar_ref = bf16[1536,768]{1,0:T(8,128)(2,1)} custom-call(bf16[1536,768]{1,0:T(8,128)(2,1)} %get-tuple-element.146.refs_0_), custom_call_target="tpu_custom_call" | custom-call | tf_op jit(solution)/shard_map/tensor_sum/pallas_call | solution.py:160
  282.4 82.0 %feed_forward.4 = (bf16[1536,768]{1,0:T(8,128)(2,1)}, f32[1536,768]{1,0:T(8,128)}, f32[3,1536,768]{2,1,0:T(8,128)}, bf16[3,1536,768]{2,1,0:T(8,128)(2,1)}, bf16[...) custom-call(s32[3]{0:T(128)} %get-tuple-element.356.meta, ...), custom_call_target="tpu_custom_call", output_to_operand_aliasing={{2}: (13, {}), {3}: (14, {}), {4}: (15, {}), {5}: (16, {}),... | custom-call | tf_op jit(solution)/shard_map/feed_forward/pallas_call | solution.py:723
  364.4 44.2 %output_relay.4 = (bf16[1536,768]{1,0:T(8,128)(2,1)}, bf16[1536,768]{1,0:T(8,128)(2,1)}) custom-call(bf16[1536,768]{1,0:T(8,128)(2,1)} %get-tuple-element.155.part_ref, f32[1536,768]{1,0:T(8,128)} %get-tuple-element.156.state_ref), custom_call_target="tpu_custom_call" | custom-call | tf_op jit(solution)/shard_map/output_relay/pallas_call | solution.py:339
  408.6 25.4 %attention_forward.5 = (bf16[1536,768]{1,0:T(8,128)(2,1)}, bf16[3,1536,768]{2,1,0:T(8,128)(2,1)}, bf16[3,1536,768]{2,1,0:T(8,128)(2,1)}, bf16[3,1536,1152]{2,1,0...) custom-call(s32[3]{0:T(128)} %pad_add_fusion.2.meta, ...), custom_call_target="tpu_custom_call", output_to_operand_aliasing={{1}: (10, {}), {2}: (11, {}), {3}: (12, {}), {4}: (13, {}),... | custom-call | tf_op jit(solution)/shard_map/attention_forward/pallas_call | solution.py:508
  434.1 34.2 %tensor_sum.8.ar_ref = bf16[1536,768]{1,0:T(8,128)(2,1)} custom-call(bf16[1536,768]{1,0:T(8,128)(2,1)} %get-tuple-element.164.refs_0_), custom_call_target="tpu_custom_call" | custom-call | tf_op jit(solution)/shard_map/tensor_sum/pallas_call | solution.py:160
  468.8 82.1 %feed_forward.5 = (bf16[1536,768]{1,0:T(8,128)(2,1)}, f32[1536,768]{1,0:T(8,128)}, f32[3,1536,768]{2,1,0:T(8,128)}, bf16[3,1536,768]{2,1,0:T(8,128)(2,1)}, bf16[...) custom-call(s32[3]{0:T(128)} %pad_add_fusion.2.meta, ...), custom_call_target="tpu_custom_call", output_to_operand_aliasing={{2}: (13, {}), {3}: (14, {}), {4}: (15, {}), {5}: (16, {}),... | custom-call | tf_op jit(solution)/shard_map/feed_forward/pallas_call | solution.py:723
  550.9 89.7 %feed_backward.3 = (bf16[1536,768]{1,0:T(8,128)(2,1)}, bf16[32,768]{1,0:T(8,128)(2,1)}, bf16[3,1536,768]{2,1,0:T(8,128)(2,1)}, bf16[3,8,480,512]{3,2,1,0:T(8,128...) custom-call(s32[4]{0:T(128)} %get-tuple-element.358.meta, ...), custom_call_target="tpu_custom_call" | custom-call | tf_op jit(solution)/shard_map/feed_backward/pallas_call | solution.py:926
  640.6 34.5 %tensor_sum.9 = (bf16[1536,768]{1,0:T(8,128)(2,1)}, bf16[32,768]{1,0:T(8,128)(2,1)}) custom-call(bf16[1536,768]{1,0:T(8,128)(2,1)} %get-tuple-element.181.refs_0_, bf16[32,768]{1,0:T(8,128)(2,1)} %get-tuple-element.182.refs_1_), custom_call_target="tpu_custom_call" | custom-call | tf_op jit(solution)/shard_map/tensor_sum/pallas_call | solution.py:160
  675.2 6.3 dynamic-slice_bitcast_fusion
  681.4 40.9 %attention_backward.3 = (bf16[1536,768]{1,0:T(8,128)(2,1)}, f32[1536,768]{1,0:T(8,128)}, f32[1,768]{1,0:T(1,128)}, f32[8,768]{1,0:T(8,128)}, bf16[3,1536,1152]{2...) custom-call(s32[4]{0:T(128)} %get-tuple-element.358.meta, s32[12]{0:T(128)} %reshape.148.first_block, ...), custom_call_target="tpu_custom_call" | custom-call | tf_op jit(solution)/shard_map/attention_backward/pallas_call | solution.py:1117
  722.4 44.6 %input_relay.3 = (f32[1536,768]{1,0:T(8,128)}, bf16[1536,768]{1,0:T(8,128)(2,1)}, f32[1,768]{1,0:T(1,128)}) custom-call(bf16[1536,768]{1,0:T(8,128)(2,1)} %get-tuple-element.191.part_ref, bf16[1536,768]{1,0:T(8,128)(2,1)} %get-tuple-element.337.layer_in_ref, f32[1536,768]{1,0:T(8,128)} %get-tuple-element.192.grad_state_ref, ...), custom_call_target="tpu_custom_call" | custom-call | tf_op jit(solution)/shard_map/input_relay/pallas_call | solution.py:356
  767.0 89.5 %feed_backward.4 = (bf16[1536,768]{1,0:T(8,128)(2,1)}, bf16[32,768]{1,0:T(8,128)(2,1)}, bf16[3,1536,768]{2,1,0:T(8,128)(2,1)}, bf16[3,8,480,512]{3,2,1,0:T(8,128...) custom-call(s32[4]{0:T(128)} %get-tuple-element.357.meta, ...), custom_call_target="tpu_custom_call", output_to_operand_aliasing={{2}: (16, {}), {3}: (17, {}), {4}: (18, {}), {5}: (19, {}),... | custom-call | tf_op jit(solution)/shard_map/feed_backward/pallas_call | solution.py:926
  856.6 34.3 %tensor_sum.10 = (bf16[1536,768]{1,0:T(8,128)(2,1)}, bf16[32,768]{1,0:T(8,128)(2,1)}) custom-call(bf16[1536,768]{1,0:T(8,128)(2,1)} %get-tuple-element.201.refs_0_, bf16[32,768]{1,0:T(8,128)(2,1)} %get-tuple-element.202.refs_1_), custom_call_target="tpu_custom_call" | custom-call | tf_op jit(solution)/shard_map/tensor_sum/pallas_call | solution.py:160
  890.9 41.2 %attention_backward.4 = (bf16[1536,768]{1,0:T(8,128)(2,1)}, f32[1536,768]{1,0:T(8,128)}, f32[1,768]{1,0:T(1,128)}, f32[8,768]{1,0:T(8,128)}, bf16[3,1536,1152]{2...) custom-call(s32[4]{0:T(128)} %get-tuple-element.357.meta, ...), custom_call_target="tpu_custom_call", output_to_operand_aliasing={{4}: (18, {}), {5}: (19, {})} | custom-call | tf_op jit(solution)/shard_map/attention_backward/pallas_call | solution.py:1117
  932.1 45.0 %input_relay.4 = (f32[1536,768]{1,0:T(8,128)}, bf16[1536,768]{1,0:T(8,128)(2,1)}, f32[1,768]{1,0:T(1,128)}) custom-call(bf16[1536,768]{1,0:T(8,128)(2,1)} %get-tuple-element.208.part_ref, bf16[1536,768]{1,0:T(8,128)(2,1)} %get-tuple-element.336.layer_in_ref, f32[1536,768]{1,0:T(8,128)} %get-tuple-element.209.grad_state_ref, ...), custom_call_target="tpu_custom_call" | custom-call | tf_op jit(solution)/shard_map/input_relay/pallas_call | solution.py:356
  977.7 89.7 %feed_backward.5 = (bf16[1536,768]{1,0:T(8,128)(2,1)}, bf16[32,768]{1,0:T(8,128)(2,1)}, bf16[3,1536,768]{2,1,0:T(8,128)(2,1)}, bf16[3,8,480,512]{3,2,1,0:T(8,128...) custom-call(s32[4]{0:T(128)} %pad_add_fusion.5.meta, ...), custom_call_target="tpu_custom_call", output_to_operand_aliasing={{2}: (16, {}), {3}: (17, {}), {4}: (18, {}), {5}: (19, {}),... | custom-call | tf_op jit(solution)/shard_map/feed_backward/pallas_call | solution.py:926
  1067.4 34.3 %tensor_sum.11 = (bf16[1536,768]{1,0:T(8,128)(2,1)}, bf16[32,768]{1,0:T(8,128)(2,1)}) custom-call(bf16[1536,768]{1,0:T(8,128)(2,1)} %get-tuple-element.220.refs_0_, bf16[32,768]{1,0:T(8,128)(2,1)} %get-tuple-element.221.refs_1_), custom_call_target="tpu_custom_call" | custom-call | tf_op jit(solution)/shard_map/tensor_sum/pallas_call | solution.py:160
  1101.7 37.4 %attention_backward.5 = (bf16[1536,768]{1,0:T(8,128)(2,1)}, f32[1536,768]{1,0:T(8,128)}, f32[1,768]{1,0:T(1,128)}, f32[8,768]{1,0:T(8,128)}, bf16[3,1536,1152]{2...) custom-call(s32[4]{0:T(128)} %pad_add_fusion.5.meta, ...), custom_call_target="tpu_custom_call", output_to_operand_aliasing={{4}: (18, {}), {5}: (19, {})} | custom-call | tf_op jit(solution)/shard_map/attention_backward/pallas_call | solution.py:1117
  1139.0 14.3 token_grads.2
  1153.4 1.2 slice.83
  1154.6 1.3 slice.81
  1156.3 45.0 %input_relay.5 = (f32[1536,768]{1,0:T(8,128)}, bf16[1536,768]{1,0:T(8,128)(2,1)}, f32[1,768]{1,0:T(1,128)}) custom-call(bf16[1536,768]{1,0:T(8,128)(2,1)} %get-tuple-element.227.part_ref, bf16[1536,768]{1,0:T(8,128)(2,1)} %get-tuple-element.335.layer_in_ref, f32[1536,768]{1,0:T(8,128)} %get-tuple-element.228.grad_state_ref, ...), custom_call_target="tpu_custom_call" | custom-call | tf_op jit(solution)/shard_map/input_relay/pallas_call | solution.py:356
  1204.7 1.5 pad_maximum_fusion.2
  1206.2 2.7 copy.256
  1208.9 14.9 token_grads.3
  1223.7 3.3 maximum_bitcast_fusion.2
  1227.1 13.4 expert_grads.7
  1240.6 12.9 expert_grads.6
  1253.6 12.9 expert_grads.4
  1266.6 13.1 expert_grads.5
  1279.7 43.0 %output_relay.5 = (bf16[1536,768]{1,0:T(8,128)(2,1)}, bf16[1536,768]{1,0:T(8,128)(2,1)}) custom-call(bf16[1536,768]{1,0:T(8,128)(2,1)} %get-tuple-element.173.part_ref, f32[1536,768]{1,0:T(8,128)} %get-tuple-element.174.state_ref), custom_call_target="tpu_custom_call" | custom-call | tf_op jit(solution)/shard_map/output_relay/pallas_call | solution.py:339
  1322.8 2.1 broadcast_select_fusion.3
  1324.8 2.5 maximum_bitcast_fusion.1
  1327.3 4.8 broadcast_select_fusion.1
  1332.1 4.3 maximum_bitcast_fusion
  1336.5 1.0 bitcast_convert_fusion
  1338.3 0.9 slice_bitcast_fusion.6
  1340.8 1.2 convert_element_type.47
  1342.0 1.0 slice_bitcast_fusion.3
  1343.0 32.5 %reduce-scatter.15.cloned.1.call-done = bf16[1,6,192,512]{3,2,1,0:T(8,128)(2,1)} async-done(((bf16[4,6,192,512]{3,2,1,0:T(8,128)(2,1)}), bf16[1,6,192,512]{3,2,1,0:T(8,128)(2,1)}) %reduce-scatter.15.cloned.1.call-update) | async-done | bytes 1179664 | tf_op jit(solution)/shard_map/reduce_scatter | solution.py:1389
  1375.6 88.1 %reduce-scatter.13.cloned.1.call-done = bf16[1,6,192,512]{3,2,1,0:T(8,128)(2,1)} async-done(((bf16[4,6,192,512]{3,2,1,0:T(8,128)(2,1)}), bf16[1,6,192,512]{3,2,1,0:T(8,128)(2,1)}) %reduce-scatter.13.cloned.1.call-update) | async-done | bytes 1179664 | tf_op jit(solution)/shard_map/reduce_scatter | solution.py:1389
  1463.6 88.1 %reduce-scatter.9.cloned.1.call-done = bf16[1,6,192,512]{3,2,1,0:T(8,128)(2,1)} async-done(((bf16[4,6,192,512]{3,2,1,0:T(8,128)(2,1)}), bf16[1,6,192,512]{3,2,1,0:T(8,128)(2,1)}) %reduce-scatter.9.cloned.1.call-update) | async-done | bytes 1179664 | tf_op jit(solution)/shard_map/reduce_scatter | solution.py:1389
  1551.7 88.1 %reduce-scatter.11.cloned.1.call-done = bf16[1,6,192,512]{3,2,1,0:T(8,128)(2,1)} async-done(((bf16[4,6,192,512]{3,2,1,0:T(8,128)(2,1)}), bf16[1,6,192,512]{3,2,1,0:T(8,128)(2,1)}) %reduce-scatter.11.cloned.1.call-update) | async-done | bytes 1179664 | tf_op jit(solution)/shard_map/reduce_scatter | solution.py:1389
  1639.8 3.2 pad_maximum_fusion
  1643.0 1.3 convert.8
  1644.3 4.0 slice_bitcast_fusion
  (73 shorter events, 13.2 us)
Async XLA Ops:
  7.2 9.2 copy-start.1
  7.2 10.8 copy-start.3
  7.2 1329.3 %reduce-scatter.7.cloned.1.call-start = ((), (), s32[]{:S(2)}) async-start(), calls=%async_computation.6 | async-start | bytes 1720320 | tf_op jit(solution)/shard_map/reduce_scatter | solution.py:1389
  1153.4 2.6 copy-start.2
  1156.2 45.1 %copy-start.4 = (f32[8,768]{1,0:T(8,128)S(1)}, f32[8,768]{1,0:T(8,128)}, u32[]{:S(2)}) copy-start(f32[8,768]{1,0:T(8,128)} %get-tuple-element.237) | copy-start | bytes 73732
  1156.2 45.1 %copy-start.5 = (f32[8,768]{1,0:T(8,128)S(1)}, f32[8,768]{1,0:T(8,128)}, u32[]{:S(2)}) copy-start(f32[8,768]{1,0:T(8,128)} %get-tuple-element.240) | copy-start | bytes 73732
  1156.2 45.1 %copy-start.6 = (f32[8,768]{1,0:T(8,128)S(1)}, f32[8,768]{1,0:T(8,128)}, u32[]{:S(2)}) copy-start(f32[8,768]{1,0:T(8,128)} %get-tuple-element.243) | copy-start | bytes 73732
  1156.3 45.1 %copy-start.7 = (f32[1,768]{1,0:T(1,128)S(1)}, f32[1,768]{1,0:T(1,128)}, u32[]{:S(2)}) copy-start(f32[1,768]{1,0:T(1,128)} %get-tuple-element.236) | copy-start | bytes 9220
  1156.3 45.1 %copy-start.8 = (f32[1,768]{1,0:T(1,128)S(1)}, f32[1,768]{1,0:T(1,128)}, u32[]{:S(2)}) copy-start(f32[1,768]{1,0:T(1,128)} %get-tuple-element.235) | copy-start | bytes 9220
  1156.3 45.1 %copy-start.9 = (f32[1,768]{1,0:T(1,128)S(1)}, f32[1,768]{1,0:T(1,128)}, u32[]{:S(2)}) copy-start(f32[1,768]{1,0:T(1,128)} %get-tuple-element.239) | copy-start | bytes 9220
  1156.3 45.1 %copy-start.10 = (f32[1,768]{1,0:T(1,128)S(1)}, f32[1,768]{1,0:T(1,128)}, u32[]{:S(2)}) copy-start(f32[1,768]{1,0:T(1,128)} %get-tuple-element.238) | copy-start | bytes 9220
  1156.3 45.1 %copy-start.11 = (f32[1,768]{1,0:T(1,128)S(1)}, f32[1,768]{1,0:T(1,128)}, u32[]{:S(2)}) copy-start(f32[1,768]{1,0:T(1,128)} %get-tuple-element.242) | copy-start | bytes 9220
  1208.8 131.9 %reduce-scatter.17.cloned.1.call-start = ((), (), s32[]{:S(2)}) async-start(), calls=%async_computation.11 | async-start | bytes 2949120 | tf_op jit(solution)/shard_map/reduce_scatter | solution.py:1389
  1227.0 148.5 %reduce-scatter.15.cloned.1.call-start = ((), (), s32[]{:S(2)}) async-start(), calls=%async_computation.10 | async-start | bytes 5898240 | tf_op jit(solution)/shard_map/reduce_scatter | solution.py:1389
  1240.5 223.1 %reduce-scatter.13.cloned.1.call-start = ((), (), s32[]{:S(2)}) async-start(), calls=%async_computation.9 | async-start | bytes 5898240 | tf_op jit(solution)/shard_map/reduce_scatter | solution.py:1389
  1253.5 298.2 %reduce-scatter.9.cloned.1.call-start = ((), (), s32[]{:S(2)}) async-start(), calls=%async_computation.7 | async-start | bytes 5898240 | tf_op jit(solution)/shard_map/reduce_scatter | solution.py:1389
  1266.5 373.2 %reduce-scatter.11.cloned.1.call-start = ((), (), s32[]{:S(2)}) async-start(), calls=%async_computation.8 | async-start | bytes 5898240 | tf_op jit(solution)/shard_map/reduce_scatter | solution.py:1389
  1279.7 43.0 %copy-start = (bf16[1536,768]{1,0:T(8,128)(2,1)S(1)}, bf16[1536,768]{1,0:T(8,128)(2,1)}, u32[]{:S(2)}) copy-start(bf16[1536,768]{1,0:T(8,128)(2,1)} %get-tuple-element.139) | copy-start | bytes 7077892
Sparse Core Ops, SparseCore 0:
  1209.0 29.4 reduce-scatter.6
  1241.4 46.8 reduce-scatter.16
  1290.8 84.7 reduce-scatter.14
  1377.8 85.7 reduce-scatter.12
  1465.9 85.7 reduce-scatter.8
  1554.0 85.7 reduce-scatter.10

commit v2 on v1

--- a/solution.py
+++ b/solution.py
@@ -170,12 +170,76 @@
     )(*arrays)
 
 
+def gather_kernel(pieces, own_ref, out_ref, sends, recvs):
+    place = lax.axis_index("tensor")
+    core, near, far = partners_of()
+    greet([near, far])
+    far_place = lax.rem(place + 2, 4)
+    size = own_ref.shape[0] // pieces
+    first, crossing, passed = [], [], []
+    for piece in range(pieces):
+        rows = pl.ds(piece * size, size)
+        crossing.append(
+            remote(
+                own_ref.at[rows],
+                out_ref.at[place, rows],
+                sends.at[0, piece],
+                recvs.at[0, piece],
+                far,
+            )
+        )
+        crossing[-1].start()
+    for piece in range(pieces):
+        rows = pl.ds(piece * size, size)
+        first.append(
+            remote(
+                own_ref.at[rows],
+                out_ref.at[place, rows],
+                sends.at[1, piece],
+                recvs.at[1, piece],
+                near,
+            )
+        )
+        first[-1].start()
+    out_ref[place] = own_ref[...]
+    for piece in range(pieces):
+        rows = pl.ds(piece * size, size)
+        crossing[piece].wait_recv()
+        passed.append(
+            remote(
+                out_ref.at[far_place, rows],
+                out_ref.at[far_place, rows],
+                sends.at[2, piece],
+                recvs.at[2, piece],
+                near,
+            )
+        )
+        passed[-1].start()
+    for copy in first + passed:
+        copy.wait_recv()
+    for copy in first + crossing + passed:
+        copy.wait_send()
+
+
+def tensor_gather(own, identity, pieces=6):
+    whole = pl.BlockSpec(memory_space=pltpu.VMEM)
+    return pl.pallas_call(
+        functools.partial(gather_kernel, pieces),
+        out_shape=shape_of((4,) + own.shape, BF16),
+        in_specs=[whole],
+        out_specs=whole,
+        scratch_shapes=[pltpu.SemaphoreType.DMA((3, pieces))] * 2,
+        compiler_params=pltpu.CompilerParams(
+            collective_id=identity, has_side_effects=True, vmem_limit_bytes=VMEM_BYTES
+        ),
+        name="tensor_gather",
+    )(own)
+
+
 def relay_kernel(
     pieces,
     finish,
     part_ref,
-    extra_refs,
-    full_ref,
     next_ref,
     first,
     kept,
@@ -271,15 +335,39 @@
         copy.wait_send()
 
 
-def output_kernel(pieces, part_ref, state_ref, out_ref, next_ref, first, kept, second, sends, recvs):
+def output_kernel(
+    pieces,
+    tick,
+    part_ref,
+    states_ref,
+    out_ref,
+    next_ref,
+    first,
+    kept,
+    second,
+    state,
+    loaded,
+    sends,
+    recvs,
+):
+    core = lax.rem(lax.axis_index("tensor"), 2)
+    half = part_ref.shape[0] // 2
+    slot = lax.rem(tick + 1 - lax.axis_index("section"), states_ref.shape[0])
+    load = pltpu.make_async_copy(
+        states_ref.at[slot, pl.ds(pl.multiple_of(core * half, 16), half)], state, loaded
+    )
+    load.start()
+    arrived = []
+
     def finish(total, rows, local, own):
         if own:
-            out_ref[rows, :] = (state_ref[rows, :] + total.astype(F32)).astype(BF16)
+            if not arrived:
+                load.wait()
+                arrived.append(True)
+            out_ref[rows, :] = (state[local, :] + total.astype(F32)).astype(BF16)
             return out_ref.at[rows], out_ref.at[rows]
 
-    relay_kernel(
-        pieces, finish, part_ref, None, out_ref, next_ref, first, kept, second, sends, recvs
-    )
+    relay_kernel(pieces, finish, part_ref, next_ref, first, kept, second, sends, recvs)
 
 
 def input_kernel(
@@ -321,9 +409,7 @@
             return full.at[rows], given.at[local]
         rows_back(rows, 1)
 
-    relay_kernel(
-        pieces, finish, part_ref, None, full, next_ref, first, kept, second, sends, recvs
-    )
+    relay_kernel(pieces, finish, part_ref, next_ref, first, kept, second, sends, recvs)
     grad_gain_ref[...] = gains[0:1, :] + gains[1:2, :]
 
 
@@ -332,24 +418,26 @@
     return half, [pltpu.SemaphoreType.DMA((5, pieces))] * 2
 
 
-def output_relay(part, state, identity, pieces=6):
+def output_relay(part, states, tick, identity, pieces=12):
     rows, width = part.shape
     half, semaphores = relay_scratch(rows, width, pieces)
     whole = pl.BlockSpec(memory_space=pltpu.VMEM)
     return pl.pallas_call(
-        functools.partial(output_kernel, pieces),
+        functools.partial(output_kernel, pieces, tick),
         out_shape=[shape_of((rows, width), BF16)] * 2,
-        in_specs=[whole] * 2,
+        in_specs=[whole, pl.BlockSpec(memory_space=pl.ANY)],
         out_specs=[whole] * 2,
-        scratch_shapes=half + semaphores,
+        scratch_shapes=half
+        + [pltpu.VMEM((rows // 2, width), F32), pltpu.SemaphoreType.DMA]
+        + semaphores,
         compiler_params=pltpu.CompilerParams(
             collective_id=identity, has_side_effects=True, vmem_limit_bytes=VMEM_BYTES
         ),
         name="output_relay",
-    )(part, state)
-
-
-def input_relay(part, layer_in, grad_state, gain, identity, pieces=6):
+    )(part, states)
+
+
+def input_relay(part, layer_in, grad_state, gain, identity, pieces=12):
     rows, width = part.shape
     half, semaphores = relay_scratch(rows, width, pieces)
     whole = pl.BlockSpec(memory_space=pltpu.VMEM)
@@ -384,17 +472,16 @@
     rec_ref,
     gain_ref,
     wall_ref,
-    wo_ref,
     cos_ref,
     sin_ref,
     low_ref,
     *rest,
 ):
     rest = rest[stored:]
-    part_ref, x_ref, a_ref, qkv_ref, o_ref, lse_ref = rest[:6]
+    packed_ref, x_ref, a_ref, qkv_ref, o_ref, lse_ref = rest[:6]
     keys, values, scores, tops, sums, mixed = rest[6:]
     index = pl.program_id(0)
-    heads = wo_ref.shape[0] // LANES
+    heads = wall_ref.shape[1] // (3 * LANES)
     wide = heads * LANES
     x = jnp.where(meta[0] == 0, tok_ref[...], rec_ref[...])
     x_ref[0] = x
@@ -455,12 +542,20 @@
         o_ref[0, :, columns] = (mixed[:, columns] / total).astype(BF16)
         logsum = jnp.broadcast_to(top[head] + jnp.log(total), (BLOCK, LANES))
         lse_ref[0, head : head + 1, :] = logsum.T[0:1, :]
-    part_ref[...] = dot(o_ref[0], wo_ref[...]).astype(BF16)
-
-
-def attention_forward(meta, first_block, tokens, received, gain, wall, wo, cosine, sine, low, kept):
+    half = BLOCK // 2
+    packed_ref[...] = jnp.concatenate(
+        [
+            o_ref[0, side * half : (side + 1) * half, head * LANES : head * LANES + HEAD_DIM]
+            for side in range(2)
+            for head in range(heads)
+        ],
+        axis=1,
+    )
+
+
+def attention_forward(meta, first_block, tokens, received, gain, wall, cosine, sine, low, kept):
     width = tokens.shape[1]
-    wide = wo.shape[0]
+    wide = wall.shape[1] // 3
     heads = wide // LANES
     stored = 0 if kept is None else 5
     saved = [
@@ -482,14 +577,13 @@
             pl.BlockSpec((BLOCK, width), lambda i, m, f: (i, 0)),
             once((1, width), lambda i, m, f: (0, 0)),
             once(wall.shape, lambda i, m, f: (0, 0)),
-            once(wo.shape, lambda i, m, f: (0, 0)),
             pl.BlockSpec((BLOCK, LANES), lambda i, m, f: (i, 0)),
             pl.BlockSpec((BLOCK, LANES), lambda i, m, f: (i, 0)),
             pl.BlockSpec((1, BLOCK, 1), lambda i, m, f: (m[2], i, 0)),
         ]
         + [pl.BlockSpec(memory_space=pl.ANY)] * stored,
         out_specs=[
-            pl.BlockSpec((BLOCK, width), lambda i, m, f: (i, 0)),
+            pl.BlockSpec((BLOCK // 2, wide), lambda i, m, f: (i, 0)),
             slot_rows(width),
             slot_rows(width),
             slot_rows(3 * wide),
@@ -508,8 +602,8 @@
     outs = pl.pallas_call(
         functools.partial(attention_forward_kernel, stored),
         grid_spec=grid_spec,
-        out_shape=[shape_of((SEQ_LEN, width), BF16)] + saved,
-        input_output_aliases={10 + k: 1 + k for k in range(stored)},
+        out_shape=[shape_of((SEQ_LEN // 2, wide), BF16)] + saved,
+        input_output_aliases={9 + k: 1 + k for k in range(stored)},
         compiler_params=pltpu.CompilerParams(vmem_limit_bytes=VMEM_BYTES),
         name="attention_forward",
     )(
@@ -519,7 +613,6 @@
         received,
         gain,
         wall,
-        wo,
         cosine,
         sine,
         low,
@@ -528,56 +621,61 @@
     return outs[0], outs[1:]
 
 
+PAIR = 2
+ROWS = 512
+ROW_STEPS = SEQ_LEN // ROWS
+PAIR_STEPS = EXPERTS // PAIR
+SPAN = 512
 CHUNK = 96
-ROW_CHUNK = 128
-
-
-def pick_matrices(expert, post_ref, pos_ref, pick, put):
-    def by_slot(step):
+
+
+def build_pick(first, chunks, post_ref, probs, pick, gates):
+    for which, step in chunks:
+        row = pl.ds(first + which, 1)
         slot_at = step * CHUNK + lax.broadcasted_iota(jnp.int32, (CHUNK, SEQ_LEN), 0)
-        pick[rows_of(step, CHUNK), :] = jnp.where(
-            slot_at == post_ref[0, pl.ds(expert, 1), :], 1.0, 0.0
+        here = slot_at == post_ref[0, row, :]
+        rows = slice(which * CAPACITY + step * CHUNK, which * CAPACITY + (step + 1) * CHUNK)
+        pick[rows, :] = jnp.where(here, 1.0, 0.0).astype(BF16)
+        if probs is not None:
+            chosen = jnp.sum(jnp.where(here, probs[row, :], 0.0), axis=1, keepdims=True)
+            gates[rows, :] = jnp.broadcast_to(chosen, (CHUNK, LANES))
+
+
+def build_gates(first, post_ref, probs, gates):
+    for which in range(PAIR):
+        row = pl.ds(first + which, 1)
+        for step in range(CAPACITY // CHUNK):
+            slot_at = step * CHUNK + lax.broadcasted_iota(jnp.int32, (CHUNK, SEQ_LEN), 0)
+            here = slot_at == post_ref[0, row, :]
+            rows = slice(which * CAPACITY + step * CHUNK, which * CAPACITY + (step + 1) * CHUNK)
+            chosen = jnp.sum(jnp.where(here, probs[row, :], 0.0), axis=1, keepdims=True)
+            gates[rows, :] = jnp.broadcast_to(chosen, (CHUNK, LANES))
+
+
+def build_put(first, rows, pos_ref, put):
+    places = pos_ref[0, rows, :]
+    lane = lax.broadcasted_iota(jnp.int32, places.shape, 1)
+    slot_at = lax.broadcasted_iota(jnp.int32, (places.shape[0], SPAN), 1)
+    for which in range(PAIR):
+        place = jnp.sum(jnp.where(lane == first + which, places, 0), axis=1, keepdims=True)
+        put[rows, which * SPAN : (which + 1) * SPAN] = jnp.where(
+            slot_at == place, 1.0, 0.0
         ).astype(BF16)
 
-    loop(CAPACITY // CHUNK, by_slot)
-
-    def by_token(step):
-        rows = rows_of(step, ROW_CHUNK)
-        places = pos_ref[0, rows, :]
-        lane = lax.broadcasted_iota(jnp.int32, places.shape, 1)
-        place = jnp.sum(jnp.where(lane == expert, places, 0), axis=1, keepdims=True)
-        slot_at = lax.broadcasted_iota(jnp.int32, (ROW_CHUNK, CAPACITY), 1)
-        put[rows, :] = jnp.where(slot_at == place, 1.0, 0.0).astype(BF16)
-
-    loop(SEQ_LEN // ROW_CHUNK, by_token)
-
-
-def slot_gates(expert, post_ref, probs_ref, gates):
-    def body(step):
-        slot_at = step * CHUNK + lax.broadcasted_iota(jnp.int32, (CHUNK, SEQ_LEN), 0)
-        chosen = jnp.where(
-            slot_at == post_ref[0, pl.ds(expert, 1), :], probs_ref[0, pl.ds(expert, 1), :], 0.0
-        )
-        gates[rows_of(step, CHUNK), :] = jnp.broadcast_to(
-            jnp.sum(chosen, axis=1, keepdims=True), (CHUNK, LANES)
-        )
-
-    loop(CAPACITY // CHUNK, body)
-
-
-def put_back(put, rows_in, total):
-    def body(step):
-        rows = rows_of(step, 2 * BLOCK)
-        total[rows, :] += dot(put[rows, :], rows_in[...])
-
-    loop(SEQ_LEN // (2 * BLOCK), body)
+
+ALL_CHUNKS = [(which, step) for which in range(PAIR) for step in range(CAPACITY // CHUNK)]
+
+
+def of_pair(which):
+    return slice(which * CAPACITY, (which + 1) * CAPACITY)
 
 
 def feed_forward_kernel(
     stored,
     meta,
     x_ref,
-    ar_ref,
+    ag_ref,
+    wo_ref,
     gain_ref,
     router_ref,
     post_ref,
@@ -591,64 +689,104 @@
     *rest,
 ):
     rest = rest[stored:]
-    part_ref, state_ref, h_ref, b_ref, xe_ref, g_ref, u_ref, gs_ref, us_ref, probs_ref = rest[:10]
-    total, pick, put, gates, gate_value, lift_value, hidden, scaled = rest[10:]
-    expert = pl.program_id(0)
-
-    @pl.when(expert == 0)
+    part_ref, h_ref, b_ref, xe_ref, g_ref, u_ref, gs_ref, us_ref, probs_ref = rest[:9]
+    total, normed, probs, pick, put, gates, scaled = rest[9:]
+    step = pl.program_id(0)
+    pair = jnp.maximum(step - ROW_STEPS, 0)
+
+    def activate(gate, lift, gate_out, lift_out):
+        gate_out[...] = gate.astype(BF16)
+        lift_out[...] = lift.astype(BF16)
+        return (gate / (1.0 + jnp.exp(-gate)) * lift).astype(BF16)
+
+    @pl.when(step < ROW_STEPS)
     def _():
-        def body(step):
-            rows = rows_of(step, ROW_CHUNK)
-            state = x_ref[0, rows, :].astype(F32) + ar_ref[rows, :].astype(F32)
-            state_ref[rows, :] = state
-            h_ref[0, rows, :] = state
-            scale = lax.rsqrt(jnp.mean(state * state, axis=-1, keepdims=True) + 1e-06)
-            b_ref[0, rows, :] = (gain_ref[...] * state * scale).astype(BF16)
-            total[rows, :] = jnp.zeros((ROW_CHUNK, total.shape[1]), F32)
-
-        loop(SEQ_LEN // ROW_CHUNK, body)
-        logits = dot_nt(router_ref[...], b_ref[0])
+        half = BLOCK // 2
+        columns = ag_ref.shape[2] // 2
+        mixed = jnp.concatenate(
+            [
+                jnp.concatenate(
+                    [
+                        ag_ref[device, block : block + half, side * columns : (side + 1) * columns]
+                        for device in range(4)
+                    ],
+                    axis=1,
+                )
+                for block in range(0, ROWS // 2, half)
+                for side in range(2)
+            ],
+            axis=0,
+        )
+        state = x_ref[0].astype(F32) + dot(mixed, wo_ref[...])
+        h_ref[0] = state
+        scale = lax.rsqrt(jnp.mean(state * state, axis=-1, keepdims=True) + 1e-06)
+        b = (gain_ref[...] * state * scale).astype(BF16)
+        b_ref[0] = b
+        here = rows_of(step, ROWS)
+        normed[here, :] = b
+        logits = dot_nt(router_ref[...], b)
         weights = jnp.exp(logits - jnp.max(logits, axis=0, keepdims=True))
-        probs_ref[0] = weights / jnp.sum(weights, axis=0, keepdims=True)
-
-    def activate(gate_in, lift_in, gate_out, lift_out, out, count):
-        def body(step):
-            rows = rows_of(step, CHUNK)
-            gate, lift = gate_in[rows, :], lift_in[rows, :]
-            gate_out[rows, :] = gate.astype(BF16)
-            lift_out[rows, :] = lift.astype(BF16)
-            out[rows, :] = (gate / (1.0 + jnp.exp(-gate)) * lift).astype(BF16)
-
-        loop(count // CHUNK, body)
-
-    @pl.when(expert < EXPERTS)
+        weights = weights / jnp.sum(weights, axis=0, keepdims=True)
+        probs_ref[0] = weights
+        probs[:, here] = weights
+        hidden = activate(dot(b, wgs_ref[...]), dot(b, wus_ref[...]), gs_ref.at[0], us_ref.at[0])
+        total[here, :] = dot(hidden, wds_ref[...])
+
+    @pl.when(step == 0)
     def _():
-        pick_matrices(expert, post_ref, pos_ref, pick, put)
-        slot_gates(expert, post_ref, probs_ref, gates)
-        xe_ref[0, 0] = dot(pick[...], b_ref[0]).astype(BF16)
-        gate_value[:CAPACITY, :] = dot(xe_ref[0, 0], wg_ref[0])
-        lift_value[:CAPACITY, :] = dot(xe_ref[0, 0], wu_ref[0])
-        activate(
-            gate_value, lift_value, g_ref.at[0, 0], u_ref.at[0, 0], hidden, CAPACITY
-        )
-        scaled[...] = (dot(hidden[:CAPACITY, :], wd_ref[0]) * gates[:, 0:1]).astype(BF16)
-        put_back(put, scaled, total)
-
-    @pl.when(expert == EXPERTS)
+        build_pick(0, ALL_CHUNKS, post_ref, None, pick, gates)
+        scaled[...] = jnp.zeros_like(scaled)
+
+    def experts(combine):
+        for start in range(0, SEQ_LEN, ROWS):
+            rows = pl.ds(start, ROWS)
+            if combine:
+                total[rows, :] += dot(put[rows, :], scaled[...])
+            build_put(pair * PAIR, rows, pos_ref, put)
+        picked = dot(pick[...], normed[...]).astype(BF16)
+        build_gates(pair * PAIR, post_ref, probs, gates)
+        build_pick(
+            jnp.minimum(pair + 1, PAIR_STEPS - 1) * PAIR, ALL_CHUNKS, post_ref, None, pick, gates
+        )
+        for which in range(PAIR):
+            rows = picked[of_pair(which), :]
+            xe_ref[0, which] = rows
+            hidden = activate(
+                dot(rows, wg_ref[which]), dot(rows, wu_ref[which]), g_ref.at[0, which], u_ref.at[0, which]
+            )
+            scaled[which * SPAN : which * SPAN + CAPACITY, :] = (
+                dot(hidden, wd_ref[which]) * gates[of_pair(which), 0:1]
+            ).astype(BF16)
+
+    @pl.when(step == ROW_STEPS)
     def _():
-        gate_value[...] = dot(b_ref[0], wgs_ref[...])
-        lift_value[...] = dot(b_ref[0], wus_ref[...])
-        activate(gate_value, lift_value, gs_ref.at[0], us_ref.at[0], hidden, SEQ_LEN)
-
-        def body(step):
-            rows = rows_of(step, 2 * BLOCK)
-            part_ref[rows, :] = (total[rows, :] + dot(hidden[rows, :], wds_ref[...])).astype(BF16)
-
-        loop(SEQ_LEN // (2 * BLOCK), body)
-
-
-def feed_forward(meta, layer_in, ar, gain, router, post, pos, weights, kept):
-    width = ar.shape[1]
+        experts(False)
+
+    @pl.when((step > ROW_STEPS) & (step < ROW_STEPS + PAIR_STEPS))
+    def _():
+        experts(True)
+
+    @pl.when(step == ROW_STEPS + PAIR_STEPS)
+    def _():
+        for start in range(0, SEQ_LEN, ROWS):
+            rows = pl.ds(start, ROWS)
+            part_ref[rows, :] = (total[rows, :] + dot(put[rows, :], scaled[...])).astype(BF16)
+
+
+def step_specs():
+    def row_at(step):
+        return jnp.minimum(step, ROW_STEPS - 1)
+
+    def pair_at(step):
+        return jnp.clip(step - ROW_STEPS, 0, PAIR_STEPS - 1)
+
+    return row_at, pair_at
+
+
+def feed_forward(
+    meta, layer_in, gathered, out_weight, gain, router, post, pos, weights, kept
+):
+    width = layer_in.shape[2]
     wg, wu, wd, wgs, wus, wds = weights
     hidden = wg.shape[2]
     stored = 0 if kept is None else 8
@@ -662,36 +800,34 @@
         shape_of((SLOTS, SEQ_LEN, hidden), BF16),
         shape_of((SLOTS, EXPERTS, SEQ_LEN), F32),
     ]
-
-    def slot_whole(columns):
-        return once((1, SEQ_LEN, columns), lambda e, m: (m[1], 0, 0))
-
-    def slot_expert(columns):
-        return pl.BlockSpec(
-            (1, 1, CAPACITY, columns), lambda e, m: (m[1], jnp.minimum(e, EXPERTS - 1), 0, 0)
-        )
+    row_at, pair_at = step_specs()
+
+    def slot_rows(columns):
+        return pl.BlockSpec((1, ROWS, columns), lambda s, m: (m[1], row_at(s), 0))
+
+    def slot_pair(columns):
+        return pl.BlockSpec((1, PAIR, CAPACITY, columns), lambda s, m: (m[1], pair_at(s), 0, 0))
 
     def fixed(shape):
-        return once(shape, lambda e, m: (0,) * len(shape))
-
-    def of_expert(array):
-        return pl.BlockSpec(
-            (1,) + array.shape[1:], lambda e, m: (jnp.minimum(e, EXPERTS - 1), 0, 0)
-        )
+        return once(shape, lambda s, m: (0,) * len(shape))
+
+    def of_pairs(array):
+        return pl.BlockSpec((PAIR,) + array.shape[1:], lambda s, m: (pair_at(s), 0, 0))
 
     grid_spec = pltpu.PrefetchScalarGridSpec(
         num_scalar_prefetch=1,
-        grid=(EXPERTS + 1,),
+        grid=(ROW_STEPS + PAIR_STEPS + 1,),
         in_specs=[
-            slot_whole(width),
-            fixed(ar.shape),
+            slot_rows(width),
+            pl.BlockSpec((4, ROWS // 2, gathered.shape[2]), lambda s, m: (0, row_at(s), 0)),
+            fixed(out_weight.shape),
             fixed(gain.shape),
             fixed(router.shape),
-            once((1, EXPERTS, SEQ_LEN), lambda e, m: (m[2], 0, 0)),
-            once((1, SEQ_LEN, EXPERTS), lambda e, m: (m[2], 0, 0)),
-            of_expert(wg),
-            of_expert(wu),
-            of_expert(wd),
+            once((1, EXPERTS, SEQ_LEN), lambda s, m: (m[2], 0, 0)),
+            once((1, SEQ_LEN, EXPERTS), lambda s, m: (m[2], 0, 0)),
+            of_pairs(wg),
+            of_pairs(wu),
+            of_pairs(wd),
             fixed(wgs.shape),
             fixed(wus.shape),
             fixed(wds.shape),
@@ -699,36 +835,50 @@
         + [pl.BlockSpec(memory_space=pl.ANY)] * stored,
         out_specs=[
             fixed((SEQ_LEN, width)),
-            fixed((SEQ_LEN, width)),
-            slot_whole(width),
-            slot_whole(width),
-            slot_expert(width),
-            slot_expert(hidden),
-            slot_expert(hidden),
-            slot_whole(hidden),
-            slot_whole(hidden),
-            once((1, EXPERTS, SEQ_LEN), lambda e, m: (m[1], 0, 0)),
+            slot_rows(width),
+            slot_rows(width),
+            slot_pair(width),
+            slot_pair(hidden),
+            slot_pair(hidden),
+            slot_rows(hidden),
+            slot_rows(hidden),
+            pl.BlockSpec((1, EXPERTS, ROWS), lambda s, m: (m[1], 0, row_at(s))),
         ],
         scratch_shapes=[
             pltpu.VMEM((SEQ_LEN, width), F32),
-            pltpu.VMEM((CAPACITY, SEQ_LEN), BF16),
-            pltpu.VMEM((SEQ_LEN, CAPACITY), BF16),
-            pltpu.VMEM((CAPACITY, LANES), F32),
-            pltpu.VMEM((SEQ_LEN, hidden), F32),
-            pltpu.VMEM((SEQ_LEN, hidden), F32),
-            pltpu.VMEM((SEQ_LEN, hidden), BF16),
-            pltpu.VMEM((CAPACITY, width), BF16),
+            pltpu.VMEM((SEQ_LEN, width), BF16),
+            pltpu.VMEM((EXPERTS, SEQ_LEN), F32),
+            pltpu.VMEM((PAIR * CAPACITY, SEQ_LEN), BF16),
+            pltpu.VMEM((SEQ_LEN, PAIR * SPAN), BF16),
+            pltpu.VMEM((PAIR * CAPACITY, LANES), F32),
+            pltpu.VMEM((PAIR * SPAN, width), BF16),
         ],
     )
     outs = pl.pallas_call(
         functools.partial(feed_forward_kernel, stored),
         grid_spec=grid_spec,
-        out_shape=[shape_of((SEQ_LEN, width), BF16), shape_of((SEQ_LEN, width), F32)] + saved,
-        input_output_aliases={13 + k: 2 + k for k in range(stored)},
+        out_shape=[shape_of((SEQ_LEN, width), BF16)] + saved,
+        input_output_aliases={14 + k: 1 + k for k in range(stored)},
         compiler_params=pltpu.CompilerParams(vmem_limit_bytes=VMEM_BYTES),
         name="feed_forward",
-    )(meta, layer_in, ar, gain, router, post, pos, wg, wu, wd, wgs, wus, wds, *(kept or ()))
-    return outs[0], outs[1], outs[2:]
+    )(
+        meta,
+        layer_in,
+        gathered,
+        out_weight,
+        gain,
+        router,
+        post,
+        pos,
+        wg,
+        wu,
+        wd,
+        wgs,
+        wus,
+        wds,
+        *(kept or ()),
+    )
+    return outs[0], outs[1:]
 
 
 def feed_backward_kernel(
@@ -754,92 +904,91 @@
     rest = rest[stored:]
     part_ref, choice_ref = rest[:2]
     dy_ref, hid_ref, dg_ref, du_ref, de_ref, hids_ref, dgs_ref, dus_ref = rest[2:10]
-    total, pick, put, gates, back, rows_in, choice = rest[10:]
-    expert = pl.program_id(0)
-
-    @pl.when(expert == 0)
-    def _():
-        def body(step):
-            rows = rows_of(step, ROW_CHUNK)
-            given = jnp.where(meta[0] == 1, cot_ref[rows, :], rec_ref[rows, :])
-            dy_ref[0, rows, :] = jnp.where(meta[0] == 0, jnp.zeros_like(given), given)
-            total[rows, :] = jnp.zeros((ROW_CHUNK, total.shape[1]), F32)
-
-        loop(SEQ_LEN // ROW_CHUNK, body)
-        choice[...] = jnp.zeros_like(choice)
-
-    def pull(gate_in, lift_in, weight, rows, hid, grad_gate, grad_lift):
-        gate, lift = gate_in[rows, :].astype(F32), lift_in[rows, :].astype(F32)
+    total, given, pick, put, gates, slots, choice = rest[10:]
+    step = pl.program_id(0)
+    pair = jnp.maximum(step - ROW_STEPS, 0)
+
+    def pull(grad, weight, gate, lift):
+        gate, lift = gate.astype(F32), lift.astype(F32)
         sigma = 1.0 / (1.0 + jnp.exp(-gate))
         swish = gate * sigma
         hidden = (swish * lift).astype(BF16)
-        hid[rows, :] = hidden
-        grad = back[rows, :]
-        inner = jnp.sum(hidden.astype(F32) * grad, axis=1, keepdims=True)
+        inner = None
         if weight is not None:
+            inner = jnp.sum(hidden.astype(F32) * grad, axis=1, keepdims=True)
             grad = grad * weight
-        grad_gate[rows, :] = (grad * lift * sigma * (1.0 + gate * (1.0 - sigma))).astype(BF16)
-        grad_lift[rows, :] = (grad * swish).astype(BF16)
-        return inner
-
-    @pl.when(expert < EXPERTS)
+        grad_gate = (grad * lift * (sigma + swish * (1.0 - sigma))).astype(BF16)
+        return hidden, grad_gate, (grad * swish).astype(BF16), inner
+
+    @pl.when(step < ROW_STEPS)
     def _():
-        pick_matrices(expert, post_ref, pos_ref, pick, put)
-        slot_gates(expert, post_ref, probs_ref, gates)
-        rows_in[...] = dot(pick[...], dy_ref[0]).astype(BF16)
-        back[:CAPACITY, :] = dot_nt(rows_in[...], wd_ref[0])
-
-        def body(step):
-            rows = rows_of(step, CHUNK)
-            weight = gates[rows, 0:1]
-            inner = pull(
-                g_ref.at[0, 0],
-                u_ref.at[0, 0],
-                weight,
-                rows,
-                hid_ref.at[0, 0],
-                dg_ref.at[0, 0],
-                du_ref.at[0, 0],
-            )
-            de_ref[0, 0, rows, :] = (weight * rows_in[rows, :].astype(F32)).astype(BF16)
-            slot_at = step * CHUNK + lax.broadcasted_iota(jnp.int32, (CHUNK, SEQ_LEN), 0)
-            mine = slot_at == post_ref[0, pl.ds(expert, 1), :]
-            choice[pl.ds(expert, 1), :] += jnp.sum(
-                jnp.where(mine, inner, 0.0), axis=0, keepdims=True
-            )
-
-        loop(CAPACITY // CHUNK, body)
-        rows_in[...] = (
-            dot_nt(dg_ref[0, 0], wg_ref[0]) + dot_nt(du_ref[0, 0], wu_ref[0])
-        ).astype(BF16)
-        put_back(put, rows_in, total)
-
-    @pl.when(expert == EXPERTS)
+        dy = jnp.where(meta[0] == 1, cot_ref[...], rec_ref[...])
+        dy = jnp.where(meta[0] == 0, jnp.zeros_like(dy), dy)
+        dy_ref[0] = dy
+        here = rows_of(step, ROWS)
+        given[here, :] = dy
+        hidden, grad_gate, grad_lift, unused = pull(
+            dot_nt(dy, wds_ref[...]), None, gs_ref[0], us_ref[0]
+        )
+        hids_ref[0] = hidden
+        dgs_ref[0] = grad_gate
+        dus_ref[0] = grad_lift
+        total[here, :] = dot_nt(grad_gate, wgs_ref[...]) + dot_nt(grad_lift, wus_ref[...])
+
+    @pl.when(step == 0)
     def _():
-        back[...] = dot_nt(dy_ref[0], wds_ref[...])
-
-        def body(step):
-            pull(
-                gs_ref.at[0],
-                us_ref.at[0],
-                None,
-                rows_of(step, CHUNK),
-                hids_ref.at[0],
-                dgs_ref.at[0],
-                dus_ref.at[0],
-            )
-
-        loop(SEQ_LEN // CHUNK, body)
-
-        def finish(step):
-            rows = rows_of(step, 2 * BLOCK)
-            part_ref[rows, :] = (
-                total[rows, :]
-                + dot_nt(dgs_ref[0, rows, :], wgs_ref[...])
-                + dot_nt(dus_ref[0, rows, :], wus_ref[...])
+        build_pick(0, ALL_CHUNKS, post_ref, None, pick, gates)
+        slots[...] = jnp.zeros_like(slots)
+
+    def experts(combine):
+        for start in range(0, SEQ_LEN, ROWS):
+            rows = pl.ds(start, ROWS)
+            if combine:
+                total[rows, :] += dot(put[rows, :], slots[...])
+            build_put(pair * PAIR, rows, pos_ref, put)
+        picked = dot(pick[...], given[...]).astype(BF16)
+        build_gates(pair * PAIR, post_ref, probs_ref.at[0], gates)
+        build_pick(
+            jnp.minimum(pair + 1, PAIR_STEPS - 1) * PAIR, ALL_CHUNKS, post_ref, None, pick, gates
+        )
+        for which in range(PAIR):
+            rows = picked[of_pair(which), :]
+            weight = gates[of_pair(which), 0:1]
+            hidden, grad_gate, grad_lift, inner = pull(
+                dot_nt(rows, wd_ref[which]), weight, g_ref[0, which], u_ref[0, which]
+            )
+            hid_ref[0, which] = hidden
+            dg_ref[0, which] = grad_gate
+            du_ref[0, which] = grad_lift
+            de_ref[0, which] = (weight * rows.astype(F32)).astype(BF16)
+            row = pl.ds(pair * PAIR + which, 1)
+            chosen = jnp.zeros((1, SEQ_LEN), F32)
+            for chunk in range(CAPACITY // CHUNK):
+                slot_at = chunk * CHUNK + lax.broadcasted_iota(jnp.int32, (CHUNK, SEQ_LEN), 0)
+                here = slot_at == post_ref[0, row, :]
+                chosen += jnp.sum(
+                    jnp.where(here, inner[chunk * CHUNK : (chunk + 1) * CHUNK], 0.0),
+                    axis=0,
+                    keepdims=True,
+                )
+            choice[row, :] = chosen
+            slots[which * SPAN : which * SPAN + CAPACITY, :] = (
+                dot_nt(grad_gate, wg_ref[which]) + dot_nt(grad_lift, wu_ref[which])
             ).astype(BF16)
 
-        loop(SEQ_LEN // (2 * BLOCK), finish)
+    @pl.when(step == ROW_STEPS)
+    def _():
+        experts(False)
+
+    @pl.when((step > ROW_STEPS) & (step < ROW_STEPS + PAIR_STEPS))
+    def _():
+        experts(True)
+
+    @pl.when(step == ROW_STEPS + PAIR_STEPS)
+    def _():
+        for start in range(0, SEQ_LEN, ROWS):
+            rows = pl.ds(start, ROWS)
+            part_ref[rows, :] = (total[rows, :] + dot(put[rows, :], slots[...])).astype(BF16)
         half = SEQ_LEN // 2
         blank = jnp.zeros((8, half), F32)
         choice_ref[...] = jnp.concatenate(
@@ -863,39 +1012,38 @@
         shape_of((SLOTS, SEQ_LEN, hidden), BF16),
         shape_of((SLOTS, SEQ_LEN, hidden), BF16),
     ]
-
-    def slot_whole(columns, which):
-        return once((1, SEQ_LEN, columns), lambda e, m: (m[which], 0, 0))
-
-    def slot_expert(columns, which):
+    row_at, pair_at = step_specs()
+
+    def slot_rows(columns, which):
+        return pl.BlockSpec((1, ROWS, columns), lambda s, m: (m[which], row_at(s), 0))
+
+    def slot_pair(columns, which):
         return pl.BlockSpec(
-            (1, 1, CAPACITY, columns), lambda e, m: (m[which], jnp.minimum(e, EXPERTS - 1), 0, 0)
+            (1, PAIR, CAPACITY, columns), lambda s, m: (m[which], pair_at(s), 0, 0)
         )
 
     def fixed(shape):
-        return once(shape, lambda e, m: (0,) * len(shape))
-
-    def of_expert(array):
-        return pl.BlockSpec(
-            (1,) + array.shape[1:], lambda e, m: (jnp.minimum(e, EXPERTS - 1), 0, 0)
-        )
+        return once(shape, lambda s, m: (0,) * len(shape))
+
+    def of_pairs(array):
+        return pl.BlockSpec((PAIR,) + array.shape[1:], lambda s, m: (pair_at(s), 0, 0))
 
     grid_spec = pltpu.PrefetchScalarGridSpec(
         num_scalar_prefetch=1,
-        grid=(EXPERTS + 1,),
+        grid=(ROW_STEPS + PAIR_STEPS + 1,),
         in_specs=[
-            once((SEQ_LEN, width), lambda e, m: (m[2], 0)),
-            fixed((SEQ_LEN, width)),
-            once((1, EXPERTS, SEQ_LEN), lambda e, m: (m[2], 0, 0)),
-            once((1, SEQ_LEN, EXPERTS), lambda e, m: (m[2], 0, 0)),
-            slot_expert(hidden, 3),
-            slot_expert(hidden, 3),
-            slot_whole(hidden, 3),
-            slot_whole(hidden, 3),
-            once((1, EXPERTS, SEQ_LEN), lambda e, m: (m[3], 0, 0)),
-            of_expert(wg),
-            of_expert(wu),
-            of_expert(wd),
+            pl.BlockSpec((ROWS, width), lambda s, m: (m[2] * ROW_STEPS + row_at(s), 0)),
+            pl.BlockSpec((ROWS, width), lambda s, m: (row_at(s), 0)),
+            once((1, EXPERTS, SEQ_LEN), lambda s, m: (m[2], 0, 0)),
+            once((1, SEQ_LEN, EXPERTS), lambda s, m: (m[2], 0, 0)),
+            slot_pair(hidden, 3),
+            slot_pair(hidden, 3),
+            slot_rows(hidden, 3),
+            slot_rows(hidden, 3),
+            once((1, EXPERTS, SEQ_LEN), lambda s, m: (m[3], 0, 0)),
+            of_pairs(wg),
+            of_pairs(wu),
+            of_pairs(wd),
             fixed(wgs.shape),
             fixed(wus.shape),
             fixed(wds.shape),
@@ -904,22 +1052,22 @@
         out_specs=[
             fixed((SEQ_LEN, width)),
             fixed((32, SEQ_LEN // 2)),
-            slot_whole(width, 1),
-            slot_expert(hidden, 1),
-            slot_expert(hidden, 1),
-            slot_expert(hidden, 1),
-            slot_expert(width, 1),
-            slot_whole(hidden, 1),
-            slot_whole(hidden, 1),
-            slot_whole(hidden, 1),
+            slot_rows(width, 1),
+            slot_pair(hidden, 1),
+            slot_pair(hidden, 1),
+            slot_pair(hidden, 1),
+            slot_pair(width, 1),
+            slot_rows(hidden, 1),
+            slot_rows(hidden, 1),
+            slot_rows(hidden, 1),
         ],
         scratch_shapes=[
             pltpu.VMEM((SEQ_LEN, width), F32),
-            pltpu.VMEM((CAPACITY, SEQ_LEN), BF16),
-            pltpu.VMEM((SEQ_LEN, CAPACITY), BF16),
-            pltpu.VMEM((CAPACITY, LANES), F32),
-            pltpu.VMEM((SEQ_LEN, hidden), F32),
-            pltpu.VMEM((CAPACITY, width), BF16),
+            pltpu.VMEM((SEQ_LEN, width), BF16),
+            pltpu.VMEM((PAIR * CAPACITY, SEQ_LEN), BF16),
+            pltpu.VMEM((SEQ_LEN, PAIR * SPAN), BF16),
+            pltpu.VMEM((PAIR * CAPACITY, LANES), F32),
+            pltpu.VMEM((PAIR * SPAN, width), BF16),
             pltpu.VMEM((EXPERTS, SEQ_LEN), F32),
         ],
     )
@@ -1165,14 +1313,15 @@
             ).astype(BF16)
 
 
-def expert_grads(first, count, devices, picked, hid, grad_gate, grad_lift, grad_expert):
+def expert_grads(first, count, extra, devices, picked, hid, grad_gate, grad_lift, grad_expert):
     width, hidden = picked.shape[3], hid.shape[3]
     rows = width // devices
 
     def pair(columns):
         return [
             pl.BlockSpec(
-                (1, 1, CAPACITY, columns), functools.partial(lambda slot, e: (slot, first + e, 0, 0), slot)
+                (1, 1, CAPACITY, columns),
+                functools.partial(lambda slot, e: (slot, first + e, 0, 0), slot),
             )
             for slot in (1, 2)
         ]
@@ -1182,13 +1331,57 @@
         grid=(count,),
         in_specs=pair(width) + pair(hidden) + pair(hidden) + pair(width) + pair(hidden),
         out_specs=pl.BlockSpec((devices, 3, rows, hidden), lambda e: (0, e, 0, 0)),
-        out_shape=shape_of((devices, 3 * count, rows, hidden), BF16),
+        out_shape=shape_of((devices, 3 * count + extra, rows, hidden), BF16),
         compiler_params=pltpu.CompilerParams(vmem_limit_bytes=VMEM_BYTES),
         name="expert_grads",
     )(
         *(picked, picked, grad_gate, grad_gate, grad_lift, grad_lift),
         *(grad_expert, grad_expert, hid, hid),
     )
+
+
+def shared_grads_kernel(b_ref, dy_ref, gate_ref, lift_ref, hid_ref, before_ref, out_ref, *totals):
+    step = pl.program_id(0)
+    pairs = [(b_ref, gate_ref), (b_ref, lift_ref), (dy_ref, hid_ref)]
+
+    @pl.when(step == 0)
+    def _():
+        for total in totals:
+            total[...] = jnp.zeros_like(total)
+
+    for (left, right), total in zip(pairs, totals):
+        total[...] += dot_tn(left[0], right[0])
+
+    @pl.when(step == pl.num_programs(0) - 1)
+    def _():
+        devices, unused, rows, unused = out_ref.shape
+        for number, total in enumerate(totals):
+            for device in range(devices):
+                out_ref[device, number] = total[device * rows : (device + 1) * rows, :].astype(
+                    BF16
+                )
+
+
+def shared_grads(before, b, dy, grad_gate, grad_lift, hid):
+    devices, matrices, width, hidden = before.shape
+    rows = 2 * BLOCK
+    steps = SEQ_LEN // rows
+
+    def spec(array):
+        return pl.BlockSpec((1, rows, array.shape[2]), lambda s: (1 + s // steps, s % steps, 0))
+
+    return pl.pallas_call(
+        shared_grads_kernel,
+        grid=(2 * steps,),
+        in_specs=[spec(array) for array in (b, dy, grad_gate, grad_lift, hid)]
+        + [pl.BlockSpec(memory_space=pl.ANY)],
+        out_specs=once((devices, 3, width, hidden), lambda s: (0, matrices // 3 - 1, 0, 0)),
+        out_shape=shape_of(before.shape, BF16),
+        scratch_shapes=[pltpu.VMEM((devices * width, hidden), F32)] * 3,
+        input_output_aliases={5: 0},
+        compiler_params=pltpu.CompilerParams(vmem_limit_bytes=VMEM_BYTES),
+        name="shared_grads",
+    )(b, dy, grad_gate, grad_lift, hid, before)
 
 
 def token_grads_kernel(count, *refs):
@@ -1306,6 +1499,7 @@
     cosine, sine = rotary_tables()
     wall = jnp.concatenate([paired(w_query[0]), paired(w_key[0]), padded(w_value[0])], axis=1)
     wo = padded(w_output[0].T).T
+    out_weight = lax.all_gather(w_output[0], "tensor", axis=0, tiled=True)
     router = w_router[0].T
     gain_a, gain_f = gain_attn.astype(F32), gain_ffn.astype(F32)
     feed_weights = (
@@ -1328,25 +1522,36 @@
         active = (raw >= 0) & (raw < count)
         sequence = jnp.clip(raw, 0, count - 1)
         meta = jnp.stack([section, jnp.where(active, sequence + 1, 0), sequence]).astype(jnp.int32)
-        part, attention_kept = attention_forward(
+        own, attention_kept = attention_forward(
             meta,
             first_block,
             tokens,
             received,
             gain_a,
             wall,
-            wo,
             cosine,
             sine,
             low_column,
             attention_kept,
         )
-        (summed,) = tensor_sum([part], (6,), 0)
-        part, state, feed_kept = feed_forward(
-            meta, attention_kept[0], summed, gain_f, router, post, pos, feed_weights, feed_kept
-        )
-        result, received = output_relay(part, state, 1)
+        gathered = tensor_gather(own, 0)
+        part, feed_kept = feed_forward(
+            meta,
+            attention_kept[0],
+            gathered,
+            out_weight,
+            gain_f,
+            router,
+            post,
+            pos,
+            feed_weights,
+            feed_kept,
+        )
+        result, received = output_relay(part, feed_kept[0], tick, 4 + tick)
         results.append(result)
+
+    def spread(array):
+        return lax.psum_scatter(array, "dp", scatter_dimension=0, tiled=False)
 
     received = jnp.zeros((SEQ_LEN, width), BF16)
     grads_kept, attention_grads_kept, inputs = None, None, []
@@ -1362,7 +1567,34 @@
         part, choice, grads_kept = feed_backward(
             meta, cotangent, received, post, pos, feed_kept, feed_weights, grads_kept
         )
-        summed, choice = tensor_sum([part, choice], (6, 1), 2)
+        if tick == count:
+            dy, hid, grad_gate, grad_lift, grad_expert, hid_sh, grad_gate_sh, grad_lift_sh = (
+                grads_kept
+            )
+            lead = 2
+            picked = feed_kept[2]
+            first_grads = expert_grads(
+                0, lead, 0, devices, picked, hid, grad_gate, grad_lift, grad_expert
+            )
+            other_grads = expert_grads(
+                lead,
+                EXPERTS - lead,
+                3,
+                devices,
+                picked,
+                hid,
+                grad_gate,
+                grad_lift,
+                grad_expert,
+            )
+            other_grads = shared_grads(
+                other_grads, feed_kept[1], dy, grad_gate_sh, grad_lift_sh, hid_sh
+            )
+            part, choice, first_grads, other_grads = lax.optimization_barrier(
+                (part, choice, first_grads, other_grads)
+            )
+            first_grads, other_grads = spread(first_grads), spread(other_grads)
+        summed, choice = tensor_sum([part, choice], (12, 1), 2)
         (part, grad_state, gain_grad, router_grad), attention_grads_kept = attention_backward(
             meta,
             first_block,
@@ -1385,27 +1617,11 @@
         inputs.append(grad_input)
         small = small + jnp.concatenate([gain_attn_grad, gain_grad, router_grad], axis=0)
 
-    def spread(array):
-        return lax.psum_scatter(array, "dp", scatter_dimension=0, tiled=False)
-
-    dy, hid, grad_gate, grad_lift, grad_expert, hid_sh, grad_gate_sh, grad_lift_sh = grads_kept
-    groups = 4
-    size = EXPERTS // groups
-    expert_parts = [
-        spread(
-            expert_grads(
-                group * size, size, devices, feed_kept[2], hid, grad_gate, grad_lift, grad_expert
-            )
-        )
-        for group in range(groups)
-    ]
-    rows = width // devices
-    shared = token_grads([feed_kept[1], feed_kept[1], dy], [grad_gate_sh, grad_lift_sh, hid_sh])
-    shared = spread(jnp.stack(shared).reshape(3, devices, rows, -1).swapaxes(0, 1))
     projections, outward = token_grads(
         [attention_kept[1], attention_grads_kept[1]], [attention_grads_kept[0], attention_kept[3]]
     )
     wide = wo.shape[0]
+    rows = width // devices
     columns = w_query.shape[2]
     packed = jnp.concatenate(
         [
@@ -1417,8 +1633,8 @@
         axis=1,
     )
     packed = spread(packed.reshape(devices, rows, -1)).astype(F32)
-    shared = shared.astype(F32)
-    experts = jnp.concatenate(expert_parts, axis=0).astype(F32)
+    shared = other_grads[-3:].astype(F32)
+    experts = jnp.concatenate([first_grads, other_grads[:-3]], axis=0).astype(F32)
     experts = experts.reshape(EXPERTS, 3, rows, -1)
 
     def choose(items):

time: 1660 us -> 1470 us (0.89)
  Pallas kernels: 1270 us -> 1030 us
  waiting for transfers between devices: 297 us -> 347 us
    pallas_call x6 -> x3, Pallas kernels: 207 us -> 103 us  [tensor_sum(): pl.pallas_call(functools.partial(sum_kernel, counts), out_shape=[shape_of...]
    pallas_call x3, Pallas kernels: 269 us -> 190 us  [feed_backward(): pl.pallas_call(functools.partial(feed_backward_kernel, stored), grid_spec...]
    pallas_call x3, Pallas kernels: 246 us -> 168 us  [feed_forward(): pl.pallas_call(functools.partial(feed_forward_kernel, stored), grid_spec=...]
    pallas_call x3 -> x7, Pallas kernels: 131 us -> 192 us  [the longest x3 119 us: output_relay(): pl.pallas_call(functools.partial(output_kernel, pieces, tick), out_shape=...]
    reduce_scatter x6 -> x3, waiting for transfers between devices: 297 us -> 345 us  [spread(): return lax.psum_scatter(array, 'dp', scatter_dimension=0, tiled=False)]
    pallas_call x4 -> x2, Pallas kernels: 52.4 us -> 43.7 us  [expert_grads(): pl.pallas_call(expert_grads_kernel, grid=(count,), in_specs=pair(width) +...]
  transfers between devices with their start and end apart: 6 -> 4, of which waited for: 4 -> 2; matrix products, arithmetic and copies ran while one was open for 1% -> 3% of each run, Pallas kernels for 7% -> 6%
where the time goes in v2:
time: 1470 us; the launch traced here: 1460 us
  Pallas kernels  1030 us (70%)
  waiting for transfers between devices  347 us (24%)
  other arithmetic  34.7 us (2%)
  local copies, waits for them, and re-layouts  33.2 us (2%)
    reduce_scatter x3, waiting for transfers between devices, spread(): return lax.psum_scatter(array, 'dp', scatter_dimension=0, tiled=False)  345 us
    pallas_call x3, Pallas kernels, feed_backward(): pl.pallas_call(functools.partial(feed_backward_kernel, stored), grid_spec...  190 us
    pallas_call x3, Pallas kernels, feed_forward(): pl.pallas_call(functools.partial(feed_forward_kernel, stored), grid_spec=...  168 us
    pallas_call x3, Pallas kernels, input_relay(): pl.pallas_call(functools.partial(input_kernel, pieces), out_shape=[shape_...  132 us
    pallas_call x3, Pallas kernels, output_relay(): pl.pallas_call(functools.partial(output_kernel, pieces, tick), out_shape=...  119 us
    pallas_call x3, Pallas kernels, attention_backward(): pl.pallas_call(functools.partial(attention_backward_kernel, stored), grid...  112 us
    pallas_call x3, Pallas kernels, tensor_sum(): pl.pallas_call(functools.partial(sum_kernel, counts), out_shape=[shape_of...  103 us
    pallas_call x3, Pallas kernels, attention_forward(): pl.pallas_call(functools.partial(attention_forward_kernel, stored), grid_...  72.9 us
  transfers between devices with their start and end apart: 4, of which 2 were waited for; matrix products, arithmetic and copies ran while one was open for 3% of the time, Pallas kernels for 6%

profile of v2, /device:TPU:0, one launch (start us, length us, event | category | flops | bytes accessed | tf_op | source)
XLA Modules:
  0.0 1461.0 jit_solution(13738069300854758371)
XLA Ops:
  8.0 0.9 reduce_window_sum.11
  8.9 1.3 convert_element_type.38.gain_ref
  10.2 1.3 convert_element_type.39.gain_ref
  12.3 0.8 fusion.6
  13.1 1.0 slice_negate_fusion.1
  14.1 1.0 pad_maximum_fusion.3
  15.9 1.2 copy.227
  17.4 0.9 concatenate.48
  18.8 1.4 broadcast_maximum_fusion.low_ref
  20.2 3.6 bitcast_select_fusion.1
  23.8 2.5 copy.230.post_ref
  27.0 1.4 pad_maximum_fusion.1.wall_ref
  28.4 1.6 broadcast_6_rec_ref.2.rec_ref
  29.9 24.4 %attention_forward.3 = (bf16[768,384]{1,0:T(8,128)(2,1)}, bf16[3,1536,768]{2,1,0:T(8,128)(2,1)}, bf16[3,1536,768]{2,1,0:T(8,128)(2,1)}, bf16[3,1536,1152]{2,1,0:...) custom-call(s32[3]{0:T(128)} %get-tuple-element.351.meta, s32[12]{0:T(128)} %reshape.143.first_block, ...), custom_call_target="tpu_custom_call" | custom-call | tf_op jit(solution)/shard_map/attention_forward/pallas_call | solution.py:602
  54.3 20.7 %tensor_gather.3.ag_ref = bf16[4,768,384]{2,1,0:T(8,128)(2,1)} custom-call(bf16[768,384]{1,0:T(8,128)(2,1)} %get-tuple-element.134.own_ref), custom_call_target="tpu_custom_call" | custom-call | tf_op jit(solution)/shard_map/tensor_gather/pallas_call | solution.py:226
  77.4 1.3 bitcast_select_fusion.pos_ref
  78.7 56.0 %feed_forward.3 = (bf16[1536,768]{1,0:T(8,128)(2,1)}, f32[3,1536,768]{2,1,0:T(8,128)}, bf16[3,1536,768]{2,1,0:T(8,128)(2,1)}, bf16[3,8,480,768]{3,2,1,0:T(8,128)...) custom-call(s32[3]{0:T(128)} %get-tuple-element.351.meta, ...), custom_call_target="tpu_custom_call" | custom-call | tf_op jit(solution)/shard_map/feed_forward/pallas_call | solution.py:857
  134.7 39.8 %output_relay.3 = (bf16[1536,768]{1,0:T(8,128)(2,1)}, bf16[1536,768]{1,0:T(8,128)(2,1)}) custom-call(bf16[1536,768]{1,0:T(8,128)(2,1)} %get-tuple-element.135.part_ref, f32[3,1536,768]{2,1,0:T(8,128)} %get-tuple-element.136.states_ref.rest_0_), custom_call_target="tpu_custom_call" | custom-call | tf_op jit(solution)/shard_map/output_relay/pallas_call | solution.py:425
  174.5 24.3 %attention_forward.4 = (bf16[768,384]{1,0:T(8,128)(2,1)}, bf16[3,1536,768]{2,1,0:T(8,128)(2,1)}, bf16[3,1536,768]{2,1,0:T(8,128)(2,1)}, bf16[3,1536,1152]{2,1,0:...) custom-call(s32[3]{0:T(128)} %get-tuple-element.352.meta, ...), custom_call_target="tpu_custom_call", output_to_operand_aliasing={{1}: (9, {}), {2}: (10, {}), {3}: (11, {}), {4}: (12, {}), ... | custom-call | tf_op jit(solution)/shard_map/attention_forward/pallas_call | solution.py:602
  198.8 19.5 %tensor_gather.4.ag_ref = bf16[4,768,384]{2,1,0:T(8,128)(2,1)} custom-call(bf16[768,384]{1,0:T(8,128)(2,1)} %get-tuple-element.144.own_ref), custom_call_target="tpu_custom_call" | custom-call | tf_op jit(solution)/shard_map/tensor_gather/pallas_call | solution.py:226
  218.2 56.0 %feed_forward.4 = (bf16[1536,768]{1,0:T(8,128)(2,1)}, f32[3,1536,768]{2,1,0:T(8,128)}, bf16[3,1536,768]{2,1,0:T(8,128)(2,1)}, bf16[3,8,480,768]{3,2,1,0:T(8,128)...) custom-call(s32[3]{0:T(128)} %get-tuple-element.352.meta, ...), custom_call_target="tpu_custom_call", output_to_operand_aliasing={{1}: (14, {}), {2}: (15, {}), {3}: (16, {}), {4}: (17, {}),... | custom-call | tf_op jit(solution)/shard_map/feed_forward/pallas_call | solution.py:857
  274.2 39.3 %output_relay.4 = (bf16[1536,768]{1,0:T(8,128)(2,1)}, bf16[1536,768]{1,0:T(8,128)(2,1)}) custom-call(bf16[1536,768]{1,0:T(8,128)(2,1)} %get-tuple-element.152.part_ref, f32[3,1536,768]{2,1,0:T(8,128)} %get-tuple-element.153.states_ref.rest_0_), custom_call_target="tpu_custom_call" | custom-call | tf_op jit(solution)/shard_map/output_relay/pallas_call | solution.py:425
  313.6 24.3 %attention_forward.5 = (bf16[768,384]{1,0:T(8,128)(2,1)}, bf16[3,1536,768]{2,1,0:T(8,128)(2,1)}, bf16[3,1536,768]{2,1,0:T(8,128)(2,1)}, bf16[3,1536,1152]{2,1,0:...) custom-call(s32[3]{0:T(128)} %pad_add_fusion.2.meta, ...), custom_call_target="tpu_custom_call", output_to_operand_aliasing={{1}: (9, {}), {2}: (10, {}), {3}: (11, {}), {4}: (12, {}), ... | custom-call | tf_op jit(solution)/shard_map/attention_forward/pallas_call | solution.py:602
  337.8 19.4 %tensor_gather.5.ag_ref = bf16[4,768,384]{2,1,0:T(8,128)(2,1)} custom-call(bf16[768,384]{1,0:T(8,128)(2,1)} %get-tuple-element.161.own_ref), custom_call_target="tpu_custom_call" | custom-call | tf_op jit(solution)/shard_map/tensor_gather/pallas_call | solution.py:226
  357.3 55.7 %feed_forward.5 = (bf16[1536,768]{1,0:T(8,128)(2,1)}, f32[3,1536,768]{2,1,0:T(8,128)}, bf16[3,1536,768]{2,1,0:T(8,128)(2,1)}, bf16[3,8,480,768]{3,2,1,0:T(8,128)...) custom-call(s32[3]{0:T(128)} %pad_add_fusion.2.meta, ...), custom_call_target="tpu_custom_call", output_to_operand_aliasing={{1}: (14, {}), {2}: (15, {}), {3}: (16, {}), {4}: (17, {}),... | custom-call | tf_op jit(solution)/shard_map/feed_forward/pallas_call | solution.py:857
  413.0 72.5 %feed_backward.3 = (bf16[1536,768]{1,0:T(8,128)(2,1)}, bf16[32,768]{1,0:T(8,128)(2,1)}, bf16[3,1536,768]{2,1,0:T(8,128)(2,1)}, bf16[3,8,480,512]{3,2,1,0:T(8,128...) custom-call(s32[4]{0:T(128)} %get-tuple-element.354.meta, ...), custom_call_target="tpu_custom_call" | custom-call | tf_op jit(solution)/shard_map/feed_backward/pallas_call | solution.py:1074
  485.5 34.7 %tensor_sum.3 = (bf16[1536,768]{1,0:T(8,128)(2,1)}, bf16[32,768]{1,0:T(8,128)(2,1)}) custom-call(bf16[1536,768]{1,0:T(8,128)(2,1)} %get-tuple-element.177.refs_0_, bf16[32,768]{1,0:T(8,128)(2,1)} %get-tuple-element.178.refs_1_), custom_call_target="tpu_custom_call" | custom-call | tf_op jit(solution)/shard_map/tensor_sum/pallas_call | solution.py:160
  520.3 6.2 dynamic-slice_bitcast_fusion
  526.4 37.3 %attention_backward.3 = (bf16[1536,768]{1,0:T(8,128)(2,1)}, f32[1536,768]{1,0:T(8,128)}, f32[1,768]{1,0:T(1,128)}, f32[8,768]{1,0:T(8,128)}, bf16[3,1536,1152]{2...) custom-call(s32[4]{0:T(128)} %get-tuple-element.354.meta, s32[12]{0:T(128)} %reshape.143.first_block, ...), custom_call_target="tpu_custom_call" | custom-call | tf_op jit(solution)/shard_map/attention_backward/pallas_call | solution.py:1265
  563.8 44.1 %input_relay.3 = (f32[1536,768]{1,0:T(8,128)}, bf16[1536,768]{1,0:T(8,128)(2,1)}, f32[1,768]{1,0:T(1,128)}) custom-call(bf16[1536,768]{1,0:T(8,128)(2,1)} %get-tuple-element.186.part_ref, bf16[1536,768]{1,0:T(8,128)(2,1)} %get-tuple-element.333.layer_in_ref, f32[1536,768]{1,0:T(8,128)} %get-tuple-element.187.grad_state_ref, ...), custom_call_target="tpu_custom_call" | custom-call | tf_op jit(solution)/shard_map/input_relay/pallas_call | solution.py:444
  607.9 58.7 %feed_backward.4 = (bf16[1536,768]{1,0:T(8,128)(2,1)}, bf16[32,768]{1,0:T(8,128)(2,1)}, bf16[3,1536,768]{2,1,0:T(8,128)(2,1)}, bf16[3,8,480,512]{3,2,1,0:T(8,128...) custom-call(s32[4]{0:T(128)} %get-tuple-element.353.meta, ...), custom_call_target="tpu_custom_call", output_to_operand_aliasing={{2}: (16, {}), {3}: (17, {}), {4}: (18, {}), {5}: (19, {}),... | custom-call | tf_op jit(solution)/shard_map/feed_backward/pallas_call | solution.py:1074
  666.6 34.3 %tensor_sum.4 = (bf16[1536,768]{1,0:T(8,128)(2,1)}, bf16[32,768]{1,0:T(8,128)(2,1)}) custom-call(bf16[1536,768]{1,0:T(8,128)(2,1)} %get-tuple-element.196.refs_0_, bf16[32,768]{1,0:T(8,128)(2,1)} %get-tuple-element.197.refs_1_), custom_call_target="tpu_custom_call" | custom-call | tf_op jit(solution)/shard_map/tensor_sum/pallas_call | solution.py:160
  700.9 37.4 %attention_backward.4 = (bf16[1536,768]{1,0:T(8,128)(2,1)}, f32[1536,768]{1,0:T(8,128)}, f32[1,768]{1,0:T(1,128)}, f32[8,768]{1,0:T(8,128)}, bf16[3,1536,1152]{2...) custom-call(s32[4]{0:T(128)} %get-tuple-element.353.meta, ...), custom_call_target="tpu_custom_call", output_to_operand_aliasing={{4}: (18, {}), {5}: (19, {})} | custom-call | tf_op jit(solution)/shard_map/attention_backward/pallas_call | solution.py:1265
  738.2 44.1 %input_relay.4 = (f32[1536,768]{1,0:T(8,128)}, bf16[1536,768]{1,0:T(8,128)(2,1)}, f32[1,768]{1,0:T(1,128)}) custom-call(bf16[1536,768]{1,0:T(8,128)(2,1)} %get-tuple-element.203.part_ref, bf16[1536,768]{1,0:T(8,128)(2,1)} %get-tuple-element.332.layer_in_ref, f32[1536,768]{1,0:T(8,128)} %get-tuple-element.204.grad_state_ref, ...), custom_call_target="tpu_custom_call" | custom-call | tf_op jit(solution)/shard_map/input_relay/pallas_call | solution.py:444
  782.3 58.7 %feed_backward.5 = (bf16[1536,768]{1,0:T(8,128)(2,1)}, bf16[32,768]{1,0:T(8,128)(2,1)}, bf16[3,1536,768]{2,1,0:T(8,128)(2,1)}, bf16[3,8,480,512]{3,2,1,0:T(8,128...) custom-call(s32[4]{0:T(128)} %pad_add_fusion.5.meta, ...), custom_call_target="tpu_custom_call", output_to_operand_aliasing={{2}: (16, {}), {3}: (17, {}), {4}: (18, {}), {5}: (19, {}),... | custom-call | tf_op jit(solution)/shard_map/feed_backward/pallas_call | solution.py:1074
  841.1 12.9 expert_grads.2
  854.0 30.7 %expert_grads.3.before_ref = bf16[4,21,192,512]{3,2,1,0:T(8,128)(2,1)} custom-call(bf16[3,8,480,768]{3,2,1,0:T(8,128)(2,1)} %get-tuple-element.217.refs_0_.refs_1_, bf16[3,8,480,768]{3,2,1,0:T(8,128)(2,1)} %get-tuple-element.217.refs_0_.refs_1_, bf16[3,8,480,512]{3,2,1,0:T(8,128)(2,1)} %get-tuple-element.218.refs_2_.refs_3_, ...), custom_call_target="tpu_custom_call" | custom-call | tf_op jit(solution)/shard_map/expert_grads/pallas_call | solution.py:1329
  884.7 13.4 shared_grads.1
  898.1 34.3 %tensor_sum.5 = (bf16[1536,768]{1,0:T(8,128)(2,1)}, bf16[32,768]{1,0:T(8,128)(2,1)}) custom-call(bf16[1536,768]{1,0:T(8,128)(2,1)} %get-tuple-element.226.refs_0_, bf16[32,768]{1,0:T(8,128)(2,1)} %get-tuple-element.227.refs_1_), custom_call_target="tpu_custom_call" | custom-call | tf_op jit(solution)/shard_map/tensor_sum/pallas_call | solution.py:160
  932.5 37.5 %attention_backward.5 = (bf16[1536,768]{1,0:T(8,128)(2,1)}, f32[1536,768]{1,0:T(8,128)}, f32[1,768]{1,0:T(1,128)}, f32[8,768]{1,0:T(8,128)}, bf16[3,1536,1152]{2...) custom-call(s32[4]{0:T(128)} %pad_add_fusion.5.meta, ...), custom_call_target="tpu_custom_call", output_to_operand_aliasing={{4}: (18, {}), {5}: (19, {})} | custom-call | tf_op jit(solution)/shard_map/attention_backward/pallas_call | solution.py:1265
  970.0 14.2 token_grads.1
  984.2 1.2 slice.93
  985.4 1.3 slice.91
  987.1 44.0 %input_relay.5 = (f32[1536,768]{1,0:T(8,128)}, bf16[1536,768]{1,0:T(8,128)(2,1)}, f32[1,768]{1,0:T(1,128)}) custom-call(bf16[1536,768]{1,0:T(8,128)(2,1)} %get-tuple-element.232.part_ref, bf16[1536,768]{1,0:T(8,128)(2,1)} %get-tuple-element.331.layer_in_ref, f32[1536,768]{1,0:T(8,128)} %get-tuple-element.233.grad_state_ref, ...), custom_call_target="tpu_custom_call" | custom-call | tf_op jit(solution)/shard_map/input_relay/pallas_call | solution.py:444
  1031.2 0.7 fusion.8
  1034.5 1.7 pad_maximum_fusion.2
  1036.2 2.7 copy.239
  1040.2 39.7 %output_relay.5 = (bf16[1536,768]{1,0:T(8,128)(2,1)}, bf16[1536,768]{1,0:T(8,128)(2,1)}) custom-call(bf16[1536,768]{1,0:T(8,128)(2,1)} %get-tuple-element.169.part_ref, f32[3,1536,768]{2,1,0:T(8,128)} %get-tuple-element.170.states_ref.h_ref), custom_call_target="tpu_custom_call" | custom-call | tf_op jit(solution)/shard_map/output_relay/pallas_call | solution.py:425
  1079.9 2.1 broadcast_select_fusion.3
  1081.9 2.5 maximum_bitcast_fusion.1
  1084.4 4.7 broadcast_select_fusion.1
  1089.1 4.3 maximum_bitcast_fusion
  1093.4 1.0 bitcast_convert_fusion
  1095.2 0.9 slice_bitcast_fusion.7
  1096.1 0.8 copy.243
  1096.9 0.8 slice_reduce_fusion
  1097.7 261.4 %reduce-scatter.8.cloned.1.call-done = bf16[1,21,192,512]{3,2,1,0:T(8,128)(2,1)} async-done(((bf16[4,21,192,512]{3,2,1,0:T(8,128)(2,1)}), bf16[1,21,192,512]{3,2,1,0:T(8,128)(2,1)}) %reduce-scatter.8.cloned.1.call-update) | async-done | bytes 4128784 | tf_op jit(solution)/shard_map/reduce_scatter | solution.py:1554
  1359.1 1.2 slice_convert_fusion
  1360.3 1.0 slice_bitcast_fusion.4
  1361.4 2.3 slice_bitcast_fusion
  1363.7 83.5 %reduce-scatter.6.cloned.1.call-done = bf16[1,6,192,512]{3,2,1,0:T(8,128)(2,1)} async-done(((bf16[4,6,192,512]{3,2,1,0:T(8,128)(2,1)}), bf16[1,6,192,512]{3,2,1,0:T(8,128)(2,1)}) %reduce-scatter.6.cloned.1.call-update) | async-done | bytes 1179664 | tf_op jit(solution)/shard_map/reduce_scatter | solution.py:1554
  1447.2 1.7 pad_maximum_fusion
  1448.9 1.3 convert.8
  1450.2 4.0 slice_bitcast_fusion.1
  (69 shorter events, 11.0 us)
Async XLA Ops:
  7.2 8.3 copy-start.3
  7.2 9.9 copy-start.5
  7.2 71.5 %all-gather.3.cloned.1.call-start = ((), (), s32[]{:S(2)}) async-start(), calls=%async_computation.6 | async-start | bytes 1474560 | tf_op jit(solution)/shard_map/all_gather | solution.py:1502
  7.9 1085.5 %reduce-scatter.4.cloned.1.call-start = ((), (), s32[]{:S(2)}) async-start(), calls=%async_computation.3 | async-start | bytes 1720320 | tf_op jit(solution)/shard_map/reduce_scatter | solution.py:1554
  15.1 2.3 copy-start.2
  29.9 47.5 %copy-start.1 = (pred[2,1536,8]{2,1,0:T(8,128)(4,1)S(1)}, pred[2,1536,8]{2,1,0:T(8,128)(4,1)}, u32[]{:S(2)}) copy-start(pred[2,1536,8]{2,1,0:T(8,128)(4,1)} %copy.227) | copy-start | bytes 73732
  984.2 2.5 copy-start.4
  987.0 44.1 %copy-start.6 = (f32[8,768]{1,0:T(8,128)S(1)}, f32[8,768]{1,0:T(8,128)}, u32[]{:S(2)}) copy-start(f32[8,768]{1,0:T(8,128)} %get-tuple-element.242) | copy-start | bytes 73732
  987.0 44.1 %copy-start.7 = (f32[8,768]{1,0:T(8,128)S(1)}, f32[8,768]{1,0:T(8,128)}, u32[]{:S(2)}) copy-start(f32[8,768]{1,0:T(8,128)} %get-tuple-element.245) | copy-start | bytes 73732
  987.1 44.1 %copy-start.8 = (f32[8,768]{1,0:T(8,128)S(1)}, f32[8,768]{1,0:T(8,128)}, u32[]{:S(2)}) copy-start(f32[8,768]{1,0:T(8,128)} %get-tuple-element.248) | copy-start | bytes 73732
  987.1 44.1 %copy-start.9 = (f32[1,768]{1,0:T(1,128)S(1)}, f32[1,768]{1,0:T(1,128)}, u32[]{:S(2)}) copy-start(f32[1,768]{1,0:T(1,128)} %get-tuple-element.241) | copy-start | bytes 9220
  987.1 44.1 %copy-start.10 = (f32[1,768]{1,0:T(1,128)S(1)}, f32[1,768]{1,0:T(1,128)}, u32[]{:S(2)}) copy-start(f32[1,768]{1,0:T(1,128)} %get-tuple-element.240) | copy-start | bytes 9220
  987.1 44.1 %copy-start.11 = (f32[1,768]{1,0:T(1,128)S(1)}, f32[1,768]{1,0:T(1,128)}, u32[]{:S(2)}) copy-start(f32[1,768]{1,0:T(1,128)} %get-tuple-element.244) | copy-start | bytes 9220
  987.1 44.1 %copy-start.12 = (f32[1,768]{1,0:T(1,128)S(1)}, f32[1,768]{1,0:T(1,128)}, u32[]{:S(2)}) copy-start(f32[1,768]{1,0:T(1,128)} %get-tuple-element.243) | copy-start | bytes 9220
  987.1 44.1 %copy-start.13 = (f32[1,768]{1,0:T(1,128)S(1)}, f32[1,768]{1,0:T(1,128)}, u32[]{:S(2)}) copy-start(f32[1,768]{1,0:T(1,128)} %get-tuple-element.247) | copy-start | bytes 9220
  1038.8 320.3 %reduce-scatter.8.cloned.1.call-start = ((), (), s32[]{:S(2)}) async-start(), calls=%async_computation.5 | async-start | bytes 20643840 | tf_op jit(solution)/shard_map/reduce_scatter | solution.py:1554
  1039.6 407.7 %reduce-scatter.6.cloned.1.call-start = ((), (), s32[]{:S(2)}) async-start(), calls=%async_computation.4 | async-start | bytes 5898240 | tf_op jit(solution)/shard_map/reduce_scatter | solution.py:1554
  1040.2 39.7 %copy-start = (bf16[1536,768]{1,0:T(8,128)(2,1)S(1)}, bf16[1536,768]{1,0:T(8,128)(2,1)}, u32[]{:S(2)}) copy-start(bf16[1536,768]{1,0:T(8,128)(2,1)} %get-tuple-element.137) | copy-start | bytes 7077892
Sparse Core Ops, SparseCore 0:
  9.6 20.1 all-gather.2
  1039.0 42.5 reduce-scatter.3
  1084.1 274.9 reduce-scatter.7
  1361.3 85.9 reduce-scatter.5

commit v3 on v2

--- a/solution.py
+++ b/solution.py
@@ -29,6 +29,12 @@
     return jax.ShapeDtypeStruct(shape, dtype)
 
 
+def cost(micros):
+    return pl.CostEstimate(
+        flops=int(micros * 1.15e9), bytes_accessed=int(micros * 3.6e6), transcendentals=0
+    )
+
+
 def dot(left, right):
     return jnp.dot(left, right, preferred_element_type=F32)
 
@@ -74,134 +80,131 @@
 def partners_of():
     place = lax.axis_index("tensor")
     core = lax.rem(place, 2)
-    near = {"tensor": place + 1 - 2 * core}
-    far = {"tensor": lax.rem(place + 2, 4)}
-    return core, near, far
-
-
-def halves(rows, pieces):
-    size = rows // 2
-    part = size // pieces
-    return [(size, step * part, part) for step in range(pieces)]
-
-
-def sum_kernel(counts, *refs):
-    arrays = len(counts)
-    ins, outs = refs[:arrays], refs[arrays : 2 * arrays]
-    first, kept, second = (refs[(2 + k) * arrays : (3 + k) * arrays] for k in range(3))
-    send1, recv1, send2, recv2, send3, recv3 = refs[5 * arrays :]
-    core, near, far = partners_of()
-    greet([near, far])
-    steps = []
-    for which, count in enumerate(counts):
-        for size, offset, part in halves(ins[which].shape[0], count):
-            steps.append((which, size, offset, part))
+    return {"tensor": place + 1 - 2 * core}, {"tensor": lax.rem(place + 2, 4)}
+
+
+def sides(rows):
+    core = lax.rem(lax.axis_index("tensor"), 2)
+    half = rows // 2
+    return core * half, (1 - core) * half
+
+
+def piece_rows(side, step, size):
+    return pl.ds(pl.multiple_of(side + step * size, 16), size)
+
+
+def cross_kernel(pieces, part_ref, mine, first, kept, second, sends, recvs, loaded, use):
+    near, far = partners_of()
+    own, other = sides(part_ref.shape[0])
+    size = mine.shape[0] // pieces
     copies = []
-    for number, (which, size, offset, part) in enumerate(steps):
-        other = pl.ds(pl.multiple_of((1 - core) * size + offset, 16), part)
+    for step in range(pieces):
+        local = pl.ds(step * size, size)
         copies.append(
             remote(
-                ins[which].at[other],
-                first[which].at[pl.ds(offset, part)],
-                send1.at[number],
-                recv1.at[number],
+                part_ref.at[piece_rows(other, step, size)],
+                first.at[local],
+                sends.at[0, step],
+                recvs.at[0, step],
                 near,
             )
         )
         copies[-1].start()
-    crossing = []
-    for number, (which, size, offset, part) in enumerate(steps):
-        mine = pl.ds(pl.multiple_of(core * size + offset, 16), part)
-        local = pl.ds(offset, part)
-        copies[number].wait_recv()
-        kept[which][local, :] = (
-            ins[which][mine, :].astype(F32) + first[which][local, :].astype(F32)
-        ).astype(BF16)
-        crossing.append(
+    load = pltpu.make_async_copy(
+        part_ref.at[pl.ds(pl.multiple_of(own, 16), mine.shape[0])], mine, loaded
+    )
+    load.start()
+    load.wait()
+    for step in range(pieces):
+        local = pl.ds(step * size, size)
+        copies[step].wait_recv()
+        kept[local, :] = (mine[local, :].astype(F32) + first[local, :].astype(F32)).astype(BF16)
+        copies.append(
             remote(
-                kept[which].at[local],
-                second[which].at[local],
-                send2.at[number],
-                recv2.at[number],
-                far,
+                kept.at[local], second.at[local], sends.at[1, step], recvs.at[1, step], far
             )
         )
-        crossing[-1].start()
-    back = []
-    for number, (which, size, offset, part) in enumerate(steps):
-        mine = pl.ds(pl.multiple_of(core * size + offset, 16), part)
-        local = pl.ds(offset, part)
-        crossing[number].wait_recv()
-        outs[which][mine, :] = (
-            kept[which][local, :].astype(F32) + second[which][local, :].astype(F32)
-        ).astype(BF16)
+        copies[-1].start()
+    for step in range(pieces):
+        local = pl.ds(step * size, size)
+        copies[pieces + step].wait_recv()
+        use(step, local, kept[local, :].astype(F32) + second[local, :].astype(F32))
+    return copies
+
+
+def sum_kernel(
+    pieces, part_ref, out_ref, mine, first, kept, second, done, sends, recvs, loaded, stored
+):
+    near, far = partners_of()
+    greet([near, far])
+    own, other = sides(part_ref.shape[0])
+    size = mine.shape[0] // pieces
+    back, local_copies = [], []
+
+    def use(step, local, total):
+        done[local, :] = total.astype(BF16)
+        rows = piece_rows(own, step, size)
         back.append(
-            remote(
-                outs[which].at[mine],
-                outs[which].at[mine],
-                send3.at[number],
-                recv3.at[number],
-                near,
-            )
+            remote(done.at[local], out_ref.at[rows], sends.at[2, step], recvs.at[2, step], near)
         )
         back[-1].start()
+        local_copies.append(
+            pltpu.make_async_copy(done.at[local], out_ref.at[rows], stored.at[step])
+        )
+        local_copies[-1].start()
+
+    copies = cross_kernel(
+        pieces, part_ref, mine, first, kept, second, sends, recvs, loaded, use
+    )
     for copy in back:
         copy.wait_recv()
-    for copy in copies + crossing + back:
+    for copy in copies + back:
         copy.wait_send()
-
-
-def tensor_sum(arrays, counts, identity):
-    scratch = []
-    for copy in range(3):
-        scratch += [pltpu.VMEM((a.shape[0] // 2, a.shape[1]), BF16) for a in arrays]
-    total = sum(counts)
-    scratch += [pltpu.SemaphoreType.DMA((total,))] * 6
+    for copy in local_copies:
+        copy.wait()
+
+
+def tensor_sum(part, identity, pieces):
+    rows, width = part.shape
+    hbm = pl.BlockSpec(memory_space=pl.ANY)
     return pl.pallas_call(
-        functools.partial(sum_kernel, counts),
-        out_shape=[shape_of(a.shape, BF16) for a in arrays],
-        in_specs=[pl.BlockSpec(memory_space=pltpu.VMEM)] * len(arrays),
-        out_specs=[pl.BlockSpec(memory_space=pltpu.VMEM)] * len(arrays),
-        scratch_shapes=scratch,
+        functools.partial(sum_kernel, pieces),
+        out_shape=shape_of((rows, width), BF16),
+        in_specs=[hbm],
+        out_specs=hbm,
+        scratch_shapes=[pltpu.VMEM((rows // 2, width), BF16)] * 5
+        + [pltpu.SemaphoreType.DMA((3, pieces))] * 2
+        + [pltpu.SemaphoreType.DMA, pltpu.SemaphoreType.DMA((pieces,))],
         compiler_params=pltpu.CompilerParams(
             collective_id=identity, has_side_effects=True, vmem_limit_bytes=VMEM_BYTES
         ),
+        cost_estimate=cost(32),
         name="tensor_sum",
-    )(*arrays)
-
-
-def gather_kernel(pieces, own_ref, out_ref, sends, recvs):
+    )(part)
+
+
+def gather_kernel(pieces, own_ref, out_ref, sends, recvs, stored):
     place = lax.axis_index("tensor")
-    core, near, far = partners_of()
+    near, far = partners_of()
     greet([near, far])
     far_place = lax.rem(place + 2, 4)
     size = own_ref.shape[0] // pieces
     first, crossing, passed = [], [], []
-    for piece in range(pieces):
-        rows = pl.ds(piece * size, size)
-        crossing.append(
-            remote(
-                own_ref.at[rows],
-                out_ref.at[place, rows],
-                sends.at[0, piece],
-                recvs.at[0, piece],
-                far,
+    for group, copies, partner in ((0, crossing, far), (1, first, near)):
+        for piece in range(pieces):
+            rows = pl.ds(piece * size, size)
+            copies.append(
+                remote(
+                    own_ref.at[rows],
+                    out_ref.at[place, rows],
+                    sends.at[group, piece],
+                    recvs.at[group, piece],
+                    partner,
+                )
             )
-        )
-        crossing[-1].start()
-    for piece in range(pieces):
-        rows = pl.ds(piece * size, size)
-        first.append(
-            remote(
-                own_ref.at[rows],
-                out_ref.at[place, rows],
-                sends.at[1, piece],
-                recvs.at[1, piece],
-                near,
-            )
-        )
-        first[-1].start()
-    out_ref[place] = own_ref[...]
+            copies[-1].start()
+    local = pltpu.make_async_copy(own_ref, out_ref.at[place], stored)
+    local.start()
     for piece in range(pieces):
         rows = pl.ds(piece * size, size)
         crossing[piece].wait_recv()
@@ -219,120 +222,41 @@
         copy.wait_recv()
     for copy in first + crossing + passed:
         copy.wait_send()
+    local.wait()
 
 
 def tensor_gather(own, identity, pieces=6):
-    whole = pl.BlockSpec(memory_space=pltpu.VMEM)
+    hbm = pl.BlockSpec(memory_space=pl.ANY)
     return pl.pallas_call(
         functools.partial(gather_kernel, pieces),
         out_shape=shape_of((4,) + own.shape, BF16),
-        in_specs=[whole],
-        out_specs=whole,
-        scratch_shapes=[pltpu.SemaphoreType.DMA((3, pieces))] * 2,
+        in_specs=[hbm],
+        out_specs=hbm,
+        scratch_shapes=[pltpu.SemaphoreType.DMA((3, pieces))] * 2 + [pltpu.SemaphoreType.DMA],
         compiler_params=pltpu.CompilerParams(
             collective_id=identity, has_side_effects=True, vmem_limit_bytes=VMEM_BYTES
         ),
+        cost_estimate=cost(18),
         name="tensor_gather",
     )(own)
 
 
-def relay_kernel(
-    pieces,
-    finish,
-    part_ref,
-    next_ref,
-    first,
-    kept,
-    second,
-    sends,
-    recvs,
-):
-    core, near, far = partners_of()
-    across = {"section": 1 - lax.axis_index("section")}
-    greet([near, far, across])
-    steps = halves(part_ref.shape[0], pieces)
-
-    def place(size, offset, part, side):
-        return pl.ds(pl.multiple_of(side * size + offset, 16), part)
-
-    copies = []
-    for number, (size, offset, part) in enumerate(steps):
-        copies.append(
-            remote(
-                part_ref.at[place(size, offset, part, 1 - core)],
-                first.at[pl.ds(offset, part)],
-                sends.at[0, number],
-                recvs.at[0, number],
-                near,
-            )
-        )
-        copies[-1].start()
-    crossing = []
-    for number, (size, offset, part) in enumerate(steps):
-        local = pl.ds(offset, part)
-        copies[number].wait_recv()
-        kept[local, :] = (
-            part_ref[place(size, offset, part, core), :].astype(F32)
-            + first[local, :].astype(F32)
-        ).astype(BF16)
-        crossing.append(
-            remote(
-                kept.at[local],
-                second.at[local],
-                sends.at[1, number],
-                recvs.at[1, number],
-                far,
-            )
-        )
-        crossing[-1].start()
-    back, passed = [], []
-    for number, (size, offset, part) in enumerate(steps):
-        local = pl.ds(offset, part)
-        mine = place(size, offset, part, core)
-        crossing[number].wait_recv()
-        total = (kept[local, :].astype(F32) + second[local, :].astype(F32)).astype(BF16)
-        source, given = finish(total, mine, local, True)
-        back.append(
-            remote(
-                source,
-                source,
-                sends.at[2, number],
-                recvs.at[2, number],
-                near,
-            )
-        )
-        back[-1].start()
-        passed.append(
-            remote(
-                given,
-                next_ref.at[mine],
-                sends.at[3, number],
-                recvs.at[3, number],
-                across,
-            )
-        )
-        passed[-1].start()
+def pass_on(step, source, rows, next_ref, sends, recvs, across):
+    copy = remote(source, next_ref.at[rows], sends.at[3, step], recvs.at[3, step], across)
+    copy.start()
+    return copy
+
+
+def spread_on(pieces, size, own, passed, next_ref, sends, recvs, near):
     spread = []
-    for number, (size, offset, part) in enumerate(steps):
-        mine = place(size, offset, part, core)
-        passed[number].wait_recv()
+    for step in range(pieces):
+        rows = piece_rows(own, step, size)
+        passed[step].wait_recv()
         spread.append(
-            remote(
-                next_ref.at[mine],
-                next_ref.at[mine],
-                sends.at[4, number],
-                recvs.at[4, number],
-                near,
-            )
+            remote(next_ref.at[rows], next_ref.at[rows], sends.at[4, step], recvs.at[4, step], near)
         )
         spread[-1].start()
-    for number, (size, offset, part) in enumerate(steps):
-        back[number].wait_recv()
-        finish(None, place(size, offset, part, 1 - core), pl.ds(offset, part), False)
-    for copy in spread:
-        copy.wait_recv()
-    for copy in copies + crossing + back + passed + spread:
-        copy.wait_send()
+    return spread
 
 
 def output_kernel(
@@ -342,126 +266,205 @@
     states_ref,
     out_ref,
     next_ref,
+    mine,
     first,
     kept,
     second,
+    done,
     state,
-    loaded,
     sends,
     recvs,
+    loaded,
+    state_loaded,
+    stored,
 ):
-    core = lax.rem(lax.axis_index("tensor"), 2)
-    half = part_ref.shape[0] // 2
-    slot = lax.rem(tick + 1 - lax.axis_index("section"), states_ref.shape[0])
+    near, far = partners_of()
+    section = lax.axis_index("section")
+    across = {"section": 1 - section}
+    slot = lax.rem(tick + 1 - section, states_ref.shape[0])
+    own, other = sides(part_ref.shape[0])
+    size = mine.shape[0] // pieces
     load = pltpu.make_async_copy(
-        states_ref.at[slot, pl.ds(pl.multiple_of(core * half, 16), half)], state, loaded
+        states_ref.at[slot, pl.ds(pl.multiple_of(own, 16), mine.shape[0])], state, state_loaded
     )
     load.start()
-    arrived = []
-
-    def finish(total, rows, local, own):
-        if own:
-            if not arrived:
-                load.wait()
-                arrived.append(True)
-            out_ref[rows, :] = (state[local, :] + total.astype(F32)).astype(BF16)
-            return out_ref.at[rows], out_ref.at[rows]
-
-    relay_kernel(pieces, finish, part_ref, next_ref, first, kept, second, sends, recvs)
+    greet([near, far, across])
+    back, passed, local_copies = [], [], []
+
+    def use(step, local, total):
+        if step == 0:
+            load.wait()
+        done[local, :] = (state[local, :] + total.astype(BF16).astype(F32)).astype(BF16)
+        rows = piece_rows(own, step, size)
+        passed.append(pass_on(step, done.at[local], rows, next_ref, sends, recvs, across))
+        back.append(
+            remote(done.at[local], out_ref.at[rows], sends.at[2, step], recvs.at[2, step], near)
+        )
+        back[-1].start()
+        local_copies.append(
+            pltpu.make_async_copy(done.at[local], out_ref.at[rows], stored.at[step])
+        )
+        local_copies[-1].start()
+
+    copies = cross_kernel(
+        pieces, part_ref, mine, first, kept, second, sends, recvs, loaded, use
+    )
+    spread = spread_on(pieces, size, own, passed, next_ref, sends, recvs, near)
+    for copy in back + spread:
+        copy.wait_recv()
+    for copy in copies + back + passed + spread:
+        copy.wait_send()
+    for copy in local_copies:
+        copy.wait()
+
+
+def output_relay(part, states, tick, identity, pieces=12):
+    rows, width = part.shape
+    hbm = pl.BlockSpec(memory_space=pl.ANY)
+    return pl.pallas_call(
+        functools.partial(output_kernel, pieces, tick),
+        out_shape=[shape_of((rows, width), BF16)] * 2,
+        in_specs=[hbm] * 2,
+        out_specs=[hbm] * 2,
+        scratch_shapes=[pltpu.VMEM((rows // 2, width), BF16)] * 5
+        + [pltpu.VMEM((rows // 2, width), F32)]
+        + [pltpu.SemaphoreType.DMA((5, pieces))] * 2
+        + [pltpu.SemaphoreType.DMA] * 2
+        + [pltpu.SemaphoreType.DMA((pieces,))],
+        compiler_params=pltpu.CompilerParams(
+            collective_id=identity, has_side_effects=True, vmem_limit_bytes=VMEM_BYTES
+        ),
+        cost_estimate=cost(38),
+        name="output_relay",
+    )(part, states)
 
 
 def input_kernel(
     pieces,
+    tick,
     part_ref,
-    layer_in_ref,
+    layers_ref,
     grad_state_ref,
     gain_ref,
     grad_ref,
     next_ref,
     grad_gain_ref,
+    mine,
     first,
     kept,
     second,
+    given,
     full,
-    given,
+    layer_in,
+    grad_state,
+    grad,
     gains,
     sends,
     recvs,
+    loaded,
+    inputs_loaded,
+    stored,
 ):
+    near, far = partners_of()
+    section = lax.axis_index("section")
+    across = {"section": 1 - section}
+    slot = lax.rem(tick + section, layers_ref.shape[0])
+    rows = part_ref.shape[0]
+    own, other = sides(rows)
+    half = rows // 2
+    size = half // pieces
+    loads = []
+    for side, start in ((0, own), (1, other)):
+        there = pl.ds(pl.multiple_of(start, 16), half)
+        loads.append(
+            [
+                pltpu.make_async_copy(
+                    layers_ref.at[slot, there], layer_in.at[there], inputs_loaded.at[side, 0]
+                ),
+                pltpu.make_async_copy(
+                    grad_state_ref.at[there], grad_state.at[there], inputs_loaded.at[side, 1]
+                ),
+            ]
+        )
+        for load in loads[-1]:
+            load.start()
+    greet([near, far, across])
     gains[...] = jnp.zeros_like(gains)
-
-    def rows_back(rows, side):
-        grad_normed = full[rows, :].astype(F32)
-        values = layer_in_ref[rows, :].astype(F32)
+    back, passed, local_copies = [], [], []
+
+    def rows_back(here, side, step):
+        grad_normed = full[here, :].astype(F32)
+        values = layer_in[here, :].astype(F32)
         scale = lax.rsqrt(jnp.mean(values * values, axis=-1, keepdims=True) + 1e-06)
         normed = values * scale
         scaled = gain_ref[...] * grad_normed
         inner = jnp.mean(normed * scaled, axis=-1, keepdims=True)
-        grad = grad_state_ref[rows, :] + scale * (scaled - normed * inner)
-        grad_ref[rows, :] = grad
+        result = grad_state[here, :] + scale * (scaled - normed * inner)
+        grad[here, :] = result
         gains[side : side + 1, :] += jnp.sum(grad_normed * normed, axis=0, keepdims=True)
-        return grad
-
-    def finish(total, rows, local, own):
-        if own:
-            full[rows, :] = total
-            given[local, :] = rows_back(rows, 0).astype(BF16)
-            return full.at[rows], given.at[local]
-        rows_back(rows, 1)
-
-    relay_kernel(pieces, finish, part_ref, next_ref, first, kept, second, sends, recvs)
+        local_copies.append(
+            pltpu.make_async_copy(grad.at[here], grad_ref.at[here], stored.at[side, step])
+        )
+        local_copies[-1].start()
+        return result
+
+    def use(step, local, total):
+        if step == 0:
+            for load in loads[0]:
+                load.wait()
+        here = piece_rows(own, step, size)
+        full[here, :] = total.astype(BF16)
+        back.append(
+            remote(full.at[here], full.at[here], sends.at[2, step], recvs.at[2, step], near)
+        )
+        back[-1].start()
+        given[local, :] = rows_back(here, 0, step).astype(BF16)
+        passed.append(pass_on(step, given.at[local], here, next_ref, sends, recvs, across))
+
+    copies = cross_kernel(
+        pieces, part_ref, mine, first, kept, second, sends, recvs, loaded, use
+    )
+    spread = spread_on(pieces, size, own, passed, next_ref, sends, recvs, near)
+    for load in loads[1]:
+        load.wait()
+    for step in range(pieces):
+        back[step].wait_recv()
+        rows_back(piece_rows(other, step, size), 1, step)
     grad_gain_ref[...] = gains[0:1, :] + gains[1:2, :]
-
-
-def relay_scratch(rows, width, pieces):
-    half = [pltpu.VMEM((rows // 2, width), BF16)] * 3
-    return half, [pltpu.SemaphoreType.DMA((5, pieces))] * 2
-
-
-def output_relay(part, states, tick, identity, pieces=12):
+    for copy in spread:
+        copy.wait_recv()
+    for copy in copies + back + passed + spread:
+        copy.wait_send()
+    for copy in local_copies:
+        copy.wait()
+
+
+def input_relay(part, layers, grad_state, gain, tick, identity, pieces=12):
     rows, width = part.shape
-    half, semaphores = relay_scratch(rows, width, pieces)
+    hbm = pl.BlockSpec(memory_space=pl.ANY)
     whole = pl.BlockSpec(memory_space=pltpu.VMEM)
     return pl.pallas_call(
-        functools.partial(output_kernel, pieces, tick),
-        out_shape=[shape_of((rows, width), BF16)] * 2,
-        in_specs=[whole, pl.BlockSpec(memory_space=pl.ANY)],
-        out_specs=[whole] * 2,
-        scratch_shapes=half
-        + [pltpu.VMEM((rows // 2, width), F32), pltpu.SemaphoreType.DMA]
-        + semaphores,
-        compiler_params=pltpu.CompilerParams(
-            collective_id=identity, has_side_effects=True, vmem_limit_bytes=VMEM_BYTES
-        ),
-        name="output_relay",
-    )(part, states)
-
-
-def input_relay(part, layer_in, grad_state, gain, identity, pieces=12):
-    rows, width = part.shape
-    half, semaphores = relay_scratch(rows, width, pieces)
-    whole = pl.BlockSpec(memory_space=pltpu.VMEM)
-    return pl.pallas_call(
-        functools.partial(input_kernel, pieces),
+        functools.partial(input_kernel, pieces, tick),
         out_shape=[
             shape_of((rows, width), F32),
             shape_of((rows, width), BF16),
             shape_of((1, width), F32),
         ],
-        in_specs=[whole] * 4,
-        out_specs=[whole] * 3,
-        scratch_shapes=half
-        + [
-            pltpu.VMEM((rows, width), BF16),
-            pltpu.VMEM((rows // 2, width), BF16),
-            pltpu.VMEM((8, width), F32),
-        ]
-        + semaphores,
+        in_specs=[hbm] * 3 + [whole],
+        out_specs=[hbm] * 2 + [whole],
+        scratch_shapes=[pltpu.VMEM((rows // 2, width), BF16)] * 5
+        + [pltpu.VMEM((rows, width), BF16)] * 2
+        + [pltpu.VMEM((rows, width), F32)] * 2
+        + [pltpu.VMEM((8, width), F32)]
+        + [pltpu.SemaphoreType.DMA((5, pieces))] * 2
+        + [pltpu.SemaphoreType.DMA]
+        + [pltpu.SemaphoreType.DMA((2, 2)), pltpu.SemaphoreType.DMA((2, pieces))],
         compiler_params=pltpu.CompilerParams(
             collective_id=identity, has_side_effects=True, vmem_limit_bytes=VMEM_BYTES
         ),
+        cost_estimate=cost(42),
         name="input_relay",
-    )(part, layer_in, grad_state, gain)
+    )(part, layers, grad_state, gain)
 
 
 def attention_forward_kernel(
@@ -605,6 +608,7 @@
         out_shape=[shape_of((SEQ_LEN // 2, wide), BF16)] + saved,
         input_output_aliases={9 + k: 1 + k for k in range(stored)},
         compiler_params=pltpu.CompilerParams(vmem_limit_bytes=VMEM_BYTES),
+        cost_estimate=cost(24),
         name="attention_forward",
     )(
         meta,
@@ -860,6 +864,7 @@
         out_shape=[shape_of((SEQ_LEN, width), BF16)] + saved,
         input_output_aliases={14 + k: 1 + k for k in range(stored)},
         compiler_params=pltpu.CompilerParams(vmem_limit_bytes=VMEM_BYTES),
+        cost_estimate=cost(56),
         name="feed_forward",
     )(
         meta,
@@ -902,9 +907,8 @@
     *rest,
 ):
     rest = rest[stored:]
-    part_ref, choice_ref = rest[:2]
-    dy_ref, hid_ref, dg_ref, du_ref, de_ref, hids_ref, dgs_ref, dus_ref = rest[2:10]
-    total, given, pick, put, gates, slots, choice = rest[10:]
+    part_ref, dy_ref, hid_ref, dg_ref, du_ref, de_ref, hids_ref, dgs_ref, dus_ref = rest[:9]
+    total, given, pick, put, gates, slots, choice = rest[9:]
     step = pl.program_id(0)
     pair = jnp.maximum(step - ROW_STEPS, 0)
 
@@ -991,7 +995,7 @@
             part_ref[rows, :] = (total[rows, :] + dot(put[rows, :], slots[...])).astype(BF16)
         half = SEQ_LEN // 2
         blank = jnp.zeros((8, half), F32)
-        choice_ref[...] = jnp.concatenate(
+        part_ref[SEQ_LEN:, :] = jnp.concatenate(
             [choice[:, :half], blank, choice[:, half:], blank], axis=0
         ).astype(BF16)
 
@@ -1050,8 +1054,7 @@
         ]
         + [pl.BlockSpec(memory_space=pl.ANY)] * stored,
         out_specs=[
-            fixed((SEQ_LEN, width)),
-            fixed((32, SEQ_LEN // 2)),
+            fixed((SEQ_LEN + 32, width)),
             slot_rows(width, 1),
             slot_pair(hidden, 1),
             slot_pair(hidden, 1),
@@ -1074,9 +1077,10 @@
     outs = pl.pallas_call(
         functools.partial(feed_backward_kernel, stored),
         grid_spec=grid_spec,
-        out_shape=[shape_of((SEQ_LEN, width), BF16), shape_of((32, SEQ_LEN // 2), BF16)] + saved,
-        input_output_aliases={16 + k: 2 + k for k in range(stored)},
+        out_shape=[shape_of((SEQ_LEN + 32, width), BF16)] + saved,
+        input_output_aliases={16 + k: 1 + k for k in range(stored)},
         compiler_params=pltpu.CompilerParams(vmem_limit_bytes=VMEM_BYTES),
+        cost_estimate=cost(60),
         name="feed_backward",
     )(
         meta,
@@ -1097,7 +1101,7 @@
         wds,
         *(kept or ()),
     )
-    return outs[0], outs[1], outs[2:]
+    return outs[0], outs[1:]
 
 
 def attention_backward_kernel(
@@ -1202,7 +1206,7 @@
 
 
 def attention_backward(
-    meta, first_block, summed, choice, forward_kept, attention_kept, dy, gain, router, wall, wo, cosine, sine, low, kept
+    meta, first_block, summed, forward_kept, attention_kept, dy, gain, router, wall, wo, cosine, sine, low, kept
 ):
     width = summed.shape[1]
     wide = wo.shape[0]
@@ -1229,7 +1233,9 @@
         grid=(BLOCKS,),
         in_specs=[
             pl.BlockSpec((BLOCK, width), lambda s, m, f: (at(s), 0)),
-            pl.BlockSpec((16, BLOCK), lambda s, m, f: (at(s) // halves_of, at(s) % halves_of)),
+            pl.BlockSpec(
+                (16, BLOCK), lambda s, m, f: (SEQ_LEN // 16 + at(s) // halves_of, at(s) % halves_of)
+            ),
             pl.BlockSpec((1, EXPERTS, BLOCK), lambda s, m, f: (m[3], 0, at(s))),
             slot_rows(width, 1),
             slot_rows(width, 3),
@@ -1274,12 +1280,13 @@
         + saved,
         input_output_aliases={18 + k: 4 + k for k in range(stored)},
         compiler_params=pltpu.CompilerParams(vmem_limit_bytes=VMEM_BYTES),
+        cost_estimate=cost(37),
         name="attention_backward",
     )(
         meta,
         first_block,
         summed,
-        choice,
+        summed,
         probs,
         dy,
         h,
@@ -1333,6 +1340,7 @@
         out_specs=pl.BlockSpec((devices, 3, rows, hidden), lambda e: (0, e, 0, 0)),
         out_shape=shape_of((devices, 3 * count + extra, rows, hidden), BF16),
         compiler_params=pltpu.CompilerParams(vmem_limit_bytes=VMEM_BYTES),
+        cost_estimate=cost(6 * count),
         name="expert_grads",
     )(
         *(picked, picked, grad_gate, grad_gate, grad_lift, grad_lift),
@@ -1380,6 +1388,7 @@
         scratch_shapes=[pltpu.VMEM((devices * width, hidden), F32)] * 3,
         input_output_aliases={5: 0},
         compiler_params=pltpu.CompilerParams(vmem_limit_bytes=VMEM_BYTES),
+        cost_estimate=cost(13),
         name="shared_grads",
     )(b, dy, grad_gate, grad_lift, hid, before)
 
@@ -1420,6 +1429,7 @@
         out_shape=[shape_of(shape, BF16) for shape in shapes],
         scratch_shapes=[pltpu.VMEM(shape, F32) for shape in shapes],
         compiler_params=pltpu.CompilerParams(vmem_limit_bytes=VMEM_BYTES),
+        cost_estimate=cost(14),
         name="token_grads",
     )(*lefts, *rights)
 
@@ -1517,25 +1527,37 @@
 
     received = jnp.zeros((SEQ_LEN, width), BF16)
     attention_kept, feed_kept, results = None, None, []
-    for tick in range(count + 1):
+    grads_kept, attention_grads_kept, inputs = None, None, []
+    small = jnp.zeros((10, width), F32)
+
+    def spread(array):
+        return lax.psum_scatter(array, "dp", scatter_dimension=0, tiled=False)
+
+    def after(meta, array):
+        return lax.optimization_barrier((meta, array))
+
+    def forward_meta(tick):
         raw = tick - section
         active = (raw >= 0) & (raw < count)
         sequence = jnp.clip(raw, 0, count - 1)
-        meta = jnp.stack([section, jnp.where(active, sequence + 1, 0), sequence]).astype(jnp.int32)
-        own, attention_kept = attention_forward(
-            meta,
-            first_block,
-            tokens,
-            received,
-            gain_a,
-            wall,
-            cosine,
-            sine,
-            low_column,
-            attention_kept,
-        )
-        gathered = tensor_gather(own, 0)
-        part, feed_kept = feed_forward(
+        return jnp.stack([section, jnp.where(active, sequence + 1, 0), sequence]).astype(jnp.int32)
+
+    def backward_meta(tick):
+        raw = tick - 1 + section
+        active = (raw >= 0) & (raw < count)
+        sequence = jnp.clip(raw, 0, count - 1)
+        source = jnp.where(active, 2 - section, 0)
+        return jnp.stack(
+            [source, jnp.where(active, sequence + 1, 0), sequence, sequence + 1]
+        ).astype(jnp.int32)
+
+    def attend(meta, received, kept):
+        return attention_forward(
+            meta, first_block, tokens, received, gain_a, wall, cosine, sine, low_column, kept
+        )
+
+    def feed(meta, gathered, kept):
+        return feed_forward(
             meta,
             attention_kept[0],
             gathered,
@@ -1545,28 +1567,55 @@
             post,
             pos,
             feed_weights,
+            kept,
+        )
+
+    def feed_back(meta, received):
+        return feed_backward(
+            meta, cotangent, received, post, pos, feed_kept, feed_weights, grads_kept
+        )
+
+    def attend_back(meta, summed):
+        return attention_backward(
+            meta,
+            first_block,
+            summed,
             feed_kept,
-        )
+            attention_kept,
+            grads_kept[0],
+            gain_f,
+            router,
+            wall,
+            wo,
+            cosine,
+            sine,
+            low_row,
+            attention_grads_kept,
+        )
+
+    for tick in range(count):
+        meta = forward_meta(tick)
+        own, attention_kept = attend(meta, received, attention_kept)
+        gathered = tensor_gather(own, 0)
+        part, feed_kept = feed(meta, gathered, feed_kept)
         result, received = output_relay(part, feed_kept[0], tick, 4 + tick)
         results.append(result)
 
-    def spread(array):
-        return lax.psum_scatter(array, "dp", scatter_dimension=0, tiled=False)
-
-    received = jnp.zeros((SEQ_LEN, width), BF16)
-    grads_kept, attention_grads_kept, inputs = None, None, []
-    small = jnp.zeros((10, width), F32)
+    blank = jnp.zeros((SEQ_LEN, width), BF16)
+    meta, back_meta = forward_meta(count), backward_meta(0)
+    own, attention_kept = attend(meta, received, attention_kept)
+    back_meta, own = after(back_meta, own)
+    gathered = lax.all_gather(own, "tensor")
+    part, grads_kept = feed_back(back_meta, blank)
+    meta, part = after(meta, part)
+    summed = lax.psum(part, "tensor")
+    last_part, feed_kept = feed(meta, gathered, feed_kept)
+    back_meta, last_part = after(back_meta, last_part)
+
     for tick in range(count + 1):
-        raw = tick - 1 + section
-        active = (raw >= 0) & (raw < count)
-        sequence = jnp.clip(raw, 0, count - 1)
-        source = jnp.where(active, 2 - section, 0)
-        meta = jnp.stack(
-            [source, jnp.where(active, sequence + 1, 0), sequence, sequence + 1]
-        ).astype(jnp.int32)
-        part, choice, grads_kept = feed_backward(
-            meta, cotangent, received, post, pos, feed_kept, feed_weights, grads_kept
-        )
+        if tick > 0:
+            back_meta = backward_meta(tick)
+            part, grads_kept = feed_back(back_meta, received)
         if tick == count:
             dy, hid, grad_gate, grad_lift, grad_expert, hid_sh, grad_gate_sh, grad_lift_sh = (
                 grads_kept
@@ -1575,6 +1624,9 @@
             picked = feed_kept[2]
             first_grads = expert_grads(
                 0, lead, 0, devices, picked, hid, grad_gate, grad_lift, grad_expert
+            )
+            first_grads, picked, grad_gate = lax.optimization_barrier(
+                (first_grads, picked, grad_gate)
             )
             other_grads = expert_grads(
                 lead,
@@ -1590,32 +1642,20 @@
             other_grads = shared_grads(
                 other_grads, feed_kept[1], dy, grad_gate_sh, grad_lift_sh, hid_sh
             )
-            part, choice, first_grads, other_grads = lax.optimization_barrier(
-                (part, choice, first_grads, other_grads)
-            )
+            part, other_grads = lax.optimization_barrier((part, other_grads))
             first_grads, other_grads = spread(first_grads), spread(other_grads)
-        summed, choice = tensor_sum([part, choice], (12, 1), 2)
-        (part, grad_state, gain_grad, router_grad), attention_grads_kept = attention_backward(
-            meta,
-            first_block,
-            summed,
-            choice,
-            feed_kept,
-            attention_kept,
-            grads_kept[0],
-            gain_f,
-            router,
-            wall,
-            wo,
-            cosine,
-            sine,
-            low_row,
-            attention_grads_kept,
-        )
-        layer_in = lax.dynamic_index_in_dim(attention_kept[0], sequence + 1, 0, False)
-        grad_input, received, gain_attn_grad = input_relay(part, layer_in, grad_state, gain_a, 3)
+        if tick > 0:
+            summed = tensor_sum(part, 2, 7)
+        (part, grad_state, gain_grad, router_grad), attention_grads_kept = attend_back(
+            back_meta, summed
+        )
+        grad_input, received, gain_attn_grad = input_relay(
+            part, attention_kept[0], grad_state, gain_a, tick, 4 + count + 1 + tick
+        )
         inputs.append(grad_input)
         small = small + jnp.concatenate([gain_attn_grad, gain_grad, router_grad], axis=0)
+    result, unused = output_relay(last_part, feed_kept[0], count, 4 + count)
+    results.append(result)
 
     projections, outward = token_grads(
         [attention_kept[1], attention_grads_kept[1]], [attention_grads_kept[0], attention_kept[3]]
@@ -1631,6 +1671,9 @@
             jnp.pad(small, ((0, 6), (0, 0))).T.astype(BF16),
         ],
         axis=1,
+    )
+    packed, first_grads, other_grads = lax.optimization_barrier(
+        (packed, first_grads, other_grads)
     )
     packed = spread(packed.reshape(devices, rows, -1)).astype(F32)
     shared = other_grads[-3:].astype(F32)

time: 1470 us -> 1220 us (0.83)
  waiting for transfers between devices: 347 us -> 158 us
  Pallas kernels: 1030 us -> 966 us
    reduce_scatter x3, waiting for transfers between devices: 345 us -> 155 us  [spread(): return lax.psum_scatter(array, 'dp', scatter_dimension=0, tiled=False)]
    pallas_call x6 -> x5, Pallas kernels: 236 us -> 188 us  [the longest x3 124 us: input_relay(): pl.pallas_call(functools.partial(input_kernel, pieces, tick), out_shape=[...]
    pallas_call x3 -> x2, Pallas kernels: 59.6 us -> 42.5 us  [tensor_gather(): pl.pallas_call(functools.partial(gather_kernel, pieces), out_shape=shape_...]
  transfers between devices with their start and end apart: 4 -> 6, of which waited for: 2 -> 3; matrix products, arithmetic and copies ran while one was open for 3% -> 5% of each run, Pallas kernels for 6% -> 31%
where the time goes in v3:
time: 1220 us; the launch traced here: 1210 us
  Pallas kernels  966 us (79%)
  waiting for transfers between devices  158 us (13%)
  other arithmetic  40.8 us (3%)
  local copies, waits for them, and re-layouts  24.8 us (2%)
  between operations  15 us (1%)
    pallas_call x3, Pallas kernels, feed_backward(): pl.pallas_call(functools.partial(feed_backward_kernel, stored), grid_spec...  188 us
    pallas_call x3, Pallas kernels, feed_forward(): pl.pallas_call(functools.partial(feed_forward_kernel, stored), grid_spec=...  181 us
    reduce_scatter x3, waiting for transfers between devices, spread(): return lax.psum_scatter(array, 'dp', scatter_dimension=0, tiled=False)  155 us
    pallas_call x3, Pallas kernels, input_relay(): pl.pallas_call(functools.partial(input_kernel, pieces, tick), out_shape=[...  124 us
    pallas_call x3, Pallas kernels, attention_backward(): pl.pallas_call(functools.partial(attention_backward_kernel, stored), grid...  112 us
    pallas_call x3, Pallas kernels, output_relay(): pl.pallas_call(functools.partial(output_kernel, pieces, tick), out_shape=...  110 us
    pallas_call x3, Pallas kernels, attention_forward(): pl.pallas_call(functools.partial(attention_forward_kernel, stored), grid_...  72.8 us
    pallas_call x2, Pallas kernels, tensor_sum(): pl.pallas_call(functools.partial(sum_kernel, pieces), out_shape=shape_of(...  64.1 us
  transfers between devices with their start and end apart: 6, of which 3 were waited for; matrix products, arithmetic and copies ran while one was open for 5% of the time, Pallas kernels for 31%

profile of v3, /device:TPU:0, one launch (start us, length us, event | category | flops | bytes accessed | tf_op | source)
XLA Modules:
  0.0 1207.7 jit_solution(3902232671556985344)
XLA Ops:
  7.2 0.7 all-gather.5.cloned.1.call-update
  8.0 0.9 reduce_window_sum.11
  9.6 1.3 convert_element_type.37.gain_ref
  10.9 1.3 convert_element_type.38.gain_ref
  12.9 0.8 fusion.6
  13.6 1.0 slice_negate_fusion.1
  14.7 1.0 pad_maximum_fusion.3
  16.4 1.2 copy.179
  18.0 0.9 concatenate.41
  19.4 1.4 broadcast_maximum_fusion.low_ref
  20.8 3.6 bitcast_select_fusion.1
  24.4 2.5 copy.182.post_ref
  26.9 2.4 bitcast_select_fusion.pos_ref
  29.8 1.4 pad_maximum_fusion.1.wall_ref
  33.0 0.7 pad_add_fusion
  33.7 1.6 broadcast_6_rec_ref.2.rec_ref
  35.2 24.3 %attention_forward.3 = (bf16[768,384]{1,0:T(8,128)(2,1)}, bf16[3,1536,768]{2,1,0:T(8,128)(2,1)}, bf16[3,1536,768]{2,1,0:T(8,128)(2,1)}, bf16[3,1536,1152]{2,1,0:...) custom-call(s32[3]{0:T(128)} %get-tuple-element.335.meta, s32[12]{0:T(128)} %reshape.135.first_block, ...), custom_call_target="tpu_custom_call" | custom-call | flops 27599998976 | bytes 86400000 | tf_op jit(solution)/shard_map/attention_forward/pallas_call | solution.py:605
  59.5 22.3 %tensor_gather.2.ag_ref = bf16[4,768,384]{2,1,0:T(8,128)(2,1)} custom-call(bf16[768,384]{1,0:T(8,128)(2,1)} %get-tuple-element.135.own_ref), custom_call_target="tpu_custom_call" | custom-call | flops 20700000256 | bytes 64800000 | tf_op jit(solution)/shard_map/tensor_gather/pallas_call | solution.py:230
  81.8 68.7 %feed_forward.3 = (bf16[1536,768]{1,0:T(8,128)(2,1)}, f32[3,1536,768]{2,1,0:T(8,128)}, bf16[3,1536,768]{2,1,0:T(8,128)(2,1)}, bf16[3,8,480,768]{3,2,1,0:T(8,128)...) custom-call(s32[3]{0:T(128)} %get-tuple-element.335.meta, ...), custom_call_target="tpu_custom_call" | custom-call | flops 64399998976 | bytes 201600000 | tf_op jit(solution)/shard_map/feed_forward/pallas_call | solution.py:861
  150.5 36.9 %output_relay.3 = (bf16[1536,768]{1,0:T(8,128)(2,1)}, bf16[1536,768]{1,0:T(8,128)(2,1)}) custom-call(bf16[1536,768]{1,0:T(8,128)(2,1)} %get-tuple-element.136.part_ref, f32[3,1536,768]{2,1,0:T(8,128)} %get-tuple-element.137.states_ref.rest_0_), custom_call_target="tpu_custom_call" | custom-call | flops 43699998720 | bytes 136800000 | tf_op jit(solution)/shard_map/output_relay/pallas_call | solution.py:324
  187.5 24.3 %attention_forward.4 = (bf16[768,384]{1,0:T(8,128)(2,1)}, bf16[3,1536,768]{2,1,0:T(8,128)(2,1)}, bf16[3,1536,768]{2,1,0:T(8,128)(2,1)}, bf16[3,1536,1152]{2,1,0:...) custom-call(s32[3]{0:T(128)} %get-tuple-element.336.meta, ...), custom_call_target="tpu_custom_call", output_to_operand_aliasing={{1}: (9, {}), {2}: (10, {}), {3}: (11, {}), {4}: (12, {}), ... | custom-call | flops 27599998976 | bytes 86400000 | tf_op jit(solution)/shard_map/attention_forward/pallas_call | solution.py:605
  211.8 20.2 %tensor_gather.3.ag_ref = bf16[4,768,384]{2,1,0:T(8,128)(2,1)} custom-call(bf16[768,384]{1,0:T(8,128)(2,1)} %get-tuple-element.145.own_ref), custom_call_target="tpu_custom_call" | custom-call | flops 20700000256 | bytes 64800000 | tf_op jit(solution)/shard_map/tensor_gather/pallas_call | solution.py:230
  231.9 56.0 %feed_forward.4 = (bf16[1536,768]{1,0:T(8,128)(2,1)}, f32[3,1536,768]{2,1,0:T(8,128)}, bf16[3,1536,768]{2,1,0:T(8,128)(2,1)}, bf16[3,8,480,768]{3,2,1,0:T(8,128)...) custom-call(s32[3]{0:T(128)} %get-tuple-element.336.meta, ...), custom_call_target="tpu_custom_call", output_to_operand_aliasing={{1}: (14, {}), {2}: (15, {}), {3}: (16, {}), {4}: (17, {}),... | custom-call | flops 64399998976 | bytes 201600000 | tf_op jit(solution)/shard_map/feed_forward/pallas_call | solution.py:861
  287.9 36.6 %output_relay.4 = (bf16[1536,768]{1,0:T(8,128)(2,1)}, bf16[1536,768]{1,0:T(8,128)(2,1)}) custom-call(bf16[1536,768]{1,0:T(8,128)(2,1)} %get-tuple-element.153.part_ref, f32[3,1536,768]{2,1,0:T(8,128)} %get-tuple-element.154.states_ref.rest_0_), custom_call_target="tpu_custom_call" | custom-call | flops 43699998720 | bytes 136800000 | tf_op jit(solution)/shard_map/output_relay/pallas_call | solution.py:324
  324.6 24.3 %attention_forward.5 = (bf16[768,384]{1,0:T(8,128)(2,1)}, bf16[3,1536,768]{2,1,0:T(8,128)(2,1)}, bf16[3,1536,768]{2,1,0:T(8,128)(2,1)}, bf16[3,1536,1152]{2,1,0:...) custom-call(s32[3]{0:T(128)} %pad_add_fusion.3.meta, ...), custom_call_target="tpu_custom_call", output_to_operand_aliasing={{1}: (9, {}), {2}: (10, {}), {3}: (11, {}), {4}: (12, {}), ... | custom-call | flops 27599998976 | bytes 86400000 | tf_op jit(solution)/shard_map/attention_forward/pallas_call | solution.py:605
  348.9 71.0 %feed_backward.3 = (bf16[1568,768]{1,0:T(8,128)(2,1)}, bf16[3,1536,768]{2,1,0:T(8,128)(2,1)}, bf16[3,8,480,512]{3,2,1,0:T(8,128)(2,1)}, bf16[3,8,480,512]{3,2,1,...) custom-call(s32[4]{0:T(128)} %pad_add_fusion.2.meta, ...), custom_call_target="tpu_custom_call" | custom-call | flops 69000003584 | bytes 216000000 | tf_op jit(solution)/shard_map/feed_backward/pallas_call | solution.py:1077
  420.0 55.8 %feed_forward.5 = (bf16[1536,768]{1,0:T(8,128)(2,1)}, f32[3,1536,768]{2,1,0:T(8,128)}, bf16[3,1536,768]{2,1,0:T(8,128)(2,1)}, bf16[3,8,480,768]{3,2,1,0:T(8,128)...) custom-call(s32[3]{0:T(128)} %pad_add_fusion.3.meta, ...), custom_call_target="tpu_custom_call", output_to_operand_aliasing={{1}: (14, {}), {2}: (15, {}), {3}: (16, {}), {4}: (17, {}),... | custom-call | flops 64399998976 | bytes 201600000 | tf_op jit(solution)/shard_map/feed_forward/pallas_call | solution.py:861
  475.8 1.3 all-reduce.5.cloned.1.call-done.sum_ref.choice_ref
  477.2 37.4 %attention_backward.3 = (bf16[1536,768]{1,0:T(8,128)(2,1)}, f32[1536,768]{1,0:T(8,128)}, f32[1,768]{1,0:T(1,128)}, f32[8,768]{1,0:T(8,128)}, bf16[3,1536,1152]{2...) custom-call(s32[4]{0:T(128)} %pad_add_fusion.2.meta, s32[12]{0:T(128)} %reshape.135.first_block, ...), custom_call_target="tpu_custom_call" | custom-call | flops 42550001664 | bytes 133200000 | tf_op jit(solution)/shard_map/attention_backward/pallas_call | solution.py:1271
  514.6 41.2 %input_relay.3 = (f32[1536,768]{1,0:T(8,128)}, bf16[1536,768]{1,0:T(8,128)(2,1)}, f32[1,768]{1,0:T(1,128)}) custom-call(bf16[1536,768]{1,0:T(8,128)(2,1)} %get-tuple-element.186.part_ref, bf16[3,1536,768]{2,1,0:T(8,128)(2,1)} %get-tuple-element.170.x_ref.layers_ref, f32[1536,768]{1,0:T(8,128)} %get-tuple-element.187.grad_state_ref, ...), custom_call_target="tpu_custom_call" | custom-call | flops 48299999232 | bytes 151200000 | tf_op jit(solution)/shard_map/input_relay/pallas_call | solution.py:446
  555.8 58.7 %feed_backward.4 = (bf16[1568,768]{1,0:T(8,128)(2,1)}, bf16[3,1536,768]{2,1,0:T(8,128)(2,1)}, bf16[3,8,480,512]{3,2,1,0:T(8,128)(2,1)}, bf16[3,8,480,512]{3,2,1,...) custom-call(s32[4]{0:T(128)} %pad_add_fusion.4.meta, ...), custom_call_target="tpu_custom_call", output_to_operand_aliasing={{1}: (16, {}), {2}: (17, {}), {3}: (18, {}), {4}: (19, {}),... | custom-call | flops 69000003584 | bytes 216000000 | tf_op jit(solution)/shard_map/feed_backward/pallas_call | solution.py:1077
  614.4 32.1 %tensor_sum.2.sum_ref.choice_ref = bf16[1568,768]{1,0:T(8,128)(2,1)} custom-call(bf16[1568,768]{1,0:T(8,128)(2,1)} %get-tuple-element.200.part_ref), custom_call_target="tpu_custom_call" | custom-call | flops 36800000000 | bytes 115200000 | tf_op jit(solution)/shard_map/tensor_sum/pallas_call | solution.py:170
  646.5 37.4 %attention_backward.4 = (bf16[1536,768]{1,0:T(8,128)(2,1)}, f32[1536,768]{1,0:T(8,128)}, f32[1,768]{1,0:T(1,128)}, f32[8,768]{1,0:T(8,128)}, bf16[3,1536,1152]{2...) custom-call(s32[4]{0:T(128)} %pad_add_fusion.4.meta, ...), custom_call_target="tpu_custom_call", output_to_operand_aliasing={{4}: (18, {}), {5}: (19, {})} | custom-call | flops 42550001664 | bytes 133200000 | tf_op jit(solution)/shard_map/attention_backward/pallas_call | solution.py:1271
  683.9 41.2 %input_relay.4 = (f32[1536,768]{1,0:T(8,128)}, bf16[1536,768]{1,0:T(8,128)(2,1)}, f32[1,768]{1,0:T(1,128)}) custom-call(bf16[1536,768]{1,0:T(8,128)(2,1)} %get-tuple-element.204.part_ref, bf16[3,1536,768]{2,1,0:T(8,128)(2,1)} %get-tuple-element.170.x_ref.layers_ref, f32[1536,768]{1,0:T(8,128)} %get-tuple-element.205.grad_state_ref, ...), custom_call_target="tpu_custom_call" | custom-call | flops 48299999232 | bytes 151200000 | tf_op jit(solution)/shard_map/input_relay/pallas_call | solution.py:446
  725.2 58.7 %feed_backward.5 = (bf16[1568,768]{1,0:T(8,128)(2,1)}, bf16[3,1536,768]{2,1,0:T(8,128)(2,1)}, bf16[3,8,480,512]{3,2,1,0:T(8,128)(2,1)}, bf16[3,8,480,512]{3,2,1,...) custom-call(s32[4]{0:T(128)} %pad_add_fusion.5.meta, ...), custom_call_target="tpu_custom_call", output_to_operand_aliasing={{1}: (16, {}), {2}: (17, {}), {3}: (18, {}), {4}: (19, {}),... | custom-call | flops 69000003584 | bytes 216000000 | tf_op jit(solution)/shard_map/feed_backward/pallas_call | solution.py:1077
  783.8 12.9 %expert_grads.2 = bf16[4,6,192,512]{3,2,1,0:T(8,128)(2,1)} custom-call(bf16[3,8,480,768]{3,2,1,0:T(8,128)(2,1)} %get-tuple-element.226.refs_0_.refs_1_, bf16[3,8,480,768]{3,2,1,0:T(8,128)(2,1)} %get-tuple-element.226.refs_0_.refs_1_, bf16[3,8,480,512]{3,2,1,0:T(8,128)(2,1)} %get-tuple-element.227.refs_2_.refs_3_, ...), custom_call_target="tpu_custom_call" | custom-call | flops 13799999488 | bytes 43200000 | tf_op jit(solution)/shard_map/expert_grads/pallas_call | solution.py:1336
  796.8 30.7 %expert_grads.3.before_ref = bf16[4,21,192,512]{3,2,1,0:T(8,128)(2,1)} custom-call(bf16[3,8,480,768]{3,2,1,0:T(8,128)(2,1)} %get-tuple-element.226.refs_0_.refs_1_, bf16[3,8,480,768]{3,2,1,0:T(8,128)(2,1)} %get-tuple-element.226.refs_0_.refs_1_, bf16[3,8,480,512]{3,2,1,0:T(8,128)(2,1)} %get-tuple-element.227.refs_2_.refs_3_, ...), custom_call_target="tpu_custom_call" | custom-call | flops 41400000512 | bytes 129600000 | tf_op jit(solution)/shard_map/expert_grads/pallas_call | solution.py:1336
  827.6 13.5 %shared_grads.1 = bf16[4,21,192,512]{3,2,1,0:T(8,128)(2,1)} custom-call(bf16[3,1536,768]{2,1,0:T(8,128)(2,1)} %get-tuple-element.182.b_ref, bf16[3,1536,768]{2,1,0:T(8,128)(2,1)} %get-tuple-element.217.dy_ref, bf16[3,1536,512]{2,1,0:T(8,128)(2,1)} %get-tuple-element.218.gate_ref, ...), custom_call_target="tpu_custom_call", output_to_operand_aliasing={{}: (5, {})} | custom-call | flops 14949999616 | bytes 46800000 | tf_op jit(solution)/shard_map/shared_grads/pallas_call | solution.py:1381
  841.1 32.1 %tensor_sum.3.sum_ref.choice_ref = bf16[1568,768]{1,0:T(8,128)(2,1)} custom-call(bf16[1568,768]{1,0:T(8,128)(2,1)} %get-tuple-element.228.part_ref), custom_call_target="tpu_custom_call" | custom-call | flops 36800000000 | bytes 115200000 | tf_op jit(solution)/shard_map/tensor_sum/pallas_call | solution.py:170
  873.2 37.5 %attention_backward.5 = (bf16[1536,768]{1,0:T(8,128)(2,1)}, f32[1536,768]{1,0:T(8,128)}, f32[1,768]{1,0:T(1,128)}, f32[8,768]{1,0:T(8,128)}, bf16[3,1536,1152]{2...) custom-call(s32[4]{0:T(128)} %pad_add_fusion.5.meta, ...), custom_call_target="tpu_custom_call", output_to_operand_aliasing={{4}: (18, {}), {5}: (19, {})} | custom-call | flops 42550001664 | bytes 133200000 | tf_op jit(solution)/shard_map/attention_backward/pallas_call | solution.py:1271
  910.7 14.2 %token_grads.1 = (bf16[768,1152]{1,0:T(8,128)(2,1)}, bf16[768,384]{1,0:T(8,128)(2,1)}) custom-call(bf16[3,1536,768]{2,1,0:T(8,128)(2,1)} %get-tuple-element.234.refs_0_, bf16[3,1536,768]{2,1,0:T(8,128)(2,1)} %get-tuple-element.235.refs_1_, bf16[3,1536,1152]{2,1,0:T(8,128)(2,1)} %get-tuple-element.236.refs_2_, ...), custom_call_target="tpu_custom_call" | custom-call | flops 16099999744 | bytes 50400000 | tf_op jit(solution)/shard_map/token_grads/pallas_call | solution.py:1424
  924.9 1.2 slice.82
  926.1 1.3 slice.80
  927.8 0.8 copy.188
  929.0 41.4 %input_relay.5 = (f32[1536,768]{1,0:T(8,128)}, bf16[1536,768]{1,0:T(8,128)(2,1)}, f32[1,768]{1,0:T(1,128)}) custom-call(bf16[1536,768]{1,0:T(8,128)(2,1)} %get-tuple-element.231.part_ref, bf16[3,1536,768]{2,1,0:T(8,128)(2,1)} %get-tuple-element.170.x_ref.layers_ref, f32[1536,768]{1,0:T(8,128)} %get-tuple-element.232.grad_state_ref, ...), custom_call_target="tpu_custom_call" | custom-call | flops 48299999232 | bytes 151200000 | tf_op jit(solution)/shard_map/input_relay/pallas_call | solution.py:446
  970.5 0.7 fusion.8
  971.4 8.4 broadcast_select_fusion.1
  979.8 36.5 %output_relay.5 = (bf16[1536,768]{1,0:T(8,128)(2,1)}, bf16[1536,768]{1,0:T(8,128)(2,1)}) custom-call(bf16[1536,768]{1,0:T(8,128)(2,1)} %get-tuple-element.175.part_ref, f32[3,1536,768]{2,1,0:T(8,128)} %get-tuple-element.176.states_ref.h_ref), custom_call_target="tpu_custom_call" | custom-call | flops 43699998720 | bytes 136800000 | tf_op jit(solution)/shard_map/output_relay/pallas_call | solution.py:324
  1016.4 144.9 %reduce-scatter.6.cloned.1.call-done = bf16[1,21,192,512]{3,2,1,0:T(8,128)(2,1)} async-done(((bf16[4,21,192,512]{3,2,1,0:T(8,128)(2,1)}), bf16[1,21,192,512]{3,2,1,0:T(8,128)(2,1)}) %reduce-scatter.6.cloned.1.call-update) | async-done | bytes 4128784 | tf_op jit(solution)/shard_map/reduce_scatter | solution.py:1534
  1161.3 1.8 copy.191
  1163.1 2.9 broadcast_select_fusion.3
  1166.0 2.5 maximum_bitcast_fusion.1
  1168.5 6.9 maximum_bitcast_fusion
  1175.4 2.5 slice.92
  1178.3 1.3 convert.8
  1179.6 1.2 slice_convert_fusion
  1180.8 1.0 slice_bitcast_fusion.3
  1181.8 4.0 slice_bitcast_fusion
  1185.9 10.5 reduce-scatter.8.cloned.1.call-done
  1196.4 1.0 bitcast_convert_fusion
  1197.4 0.8 slice_reduce_fusion
  1198.3 0.9 slice_bitcast_fusion.4
  1199.2 0.7 copy.196
  1199.9 0.8 copy.195
  (72 shorter events, 7.0 us)
Async XLA Ops:
  7.2 8.8 copy-start.2
  7.2 10.4 copy-start.4
  7.2 74.6 %all-gather.5.cloned.1.call-start = ((), (), s32[]{:S(2)}) async-start(), calls=%async_computation.7 | async-start | bytes 1474560 | tf_op jit(solution)/shard_map/all_gather | solution.py:1512
  7.9 412.0 %all-gather.7.cloned.1.call-start = ((), (), s32[]{:S(2)}) async-start(), calls=%async_computation.8 | async-start | bytes 2949120 | tf_op jit(solution)/shard_map/all_gather | solution.py:1608
  15.7 2.3 copy-start.1
  348.8 128.3 %all-reduce.5.cloned.1.call-start = ((), (), s32[]{:S(2)}) async-start(), calls=%async_computation.3 | async-start | bytes 4816896 | tf_op jit(solution)/shard_map/psum | solution.py:1611
  419.9 596.5 %reduce-scatter.4.cloned.1.call-start = ((), (), s32[]{:S(2)}) async-start(), calls=%async_computation.4 | async-start | bytes 5898240 | tf_op jit(solution)/shard_map/reduce_scatter | solution.py:1534
  796.8 364.5 %reduce-scatter.6.cloned.1.call-start = ((), (), s32[]{:S(2)}) async-start(), calls=%async_computation.5 | async-start | bytes 20643840 | tf_op jit(solution)/shard_map/reduce_scatter | solution.py:1534
  841.1 355.3 %reduce-scatter.8.cloned.1.call-start = ((), (), s32[]{:S(2)}) async-start(), calls=%async_computation.6 | async-start | bytes 1720320 | tf_op jit(solution)/shard_map/reduce_scatter | solution.py:1534
  924.9 2.6 copy-start.3
  928.9 41.5 %copy-start.5 = (f32[8,768]{1,0:T(8,128)S(1)}, f32[8,768]{1,0:T(8,128)}, u32[]{:S(2)}) copy-start(f32[8,768]{1,0:T(8,128)} %get-tuple-element.241) | copy-start | bytes 73732
  928.9 41.5 %copy-start.6 = (f32[8,768]{1,0:T(8,128)S(1)}, f32[8,768]{1,0:T(8,128)}, u32[]{:S(2)}) copy-start(f32[8,768]{1,0:T(8,128)} %get-tuple-element.244) | copy-start | bytes 73732
  928.9 41.5 %copy-start.7 = (f32[8,768]{1,0:T(8,128)S(1)}, f32[8,768]{1,0:T(8,128)}, u32[]{:S(2)}) copy-start(f32[8,768]{1,0:T(8,128)} %get-tuple-element.247) | copy-start | bytes 73732
  928.9 41.5 %copy-start.8 = (f32[1,768]{1,0:T(1,128)S(1)}, f32[1,768]{1,0:T(1,128)}, u32[]{:S(2)}) copy-start(f32[1,768]{1,0:T(1,128)} %get-tuple-element.240) | copy-start | bytes 9220
  928.9 41.5 %copy-start.9 = (f32[1,768]{1,0:T(1,128)S(1)}, f32[1,768]{1,0:T(1,128)}, u32[]{:S(2)}) copy-start(f32[1,768]{1,0:T(1,128)} %get-tuple-element.239) | copy-start | bytes 9220
  929.0 41.5 %copy-start.10 = (f32[1,768]{1,0:T(1,128)S(1)}, f32[1,768]{1,0:T(1,128)}, u32[]{:S(2)}) copy-start(f32[1,768]{1,0:T(1,128)} %get-tuple-element.243) | copy-start | bytes 9220
  929.0 41.5 %copy-start.11 = (f32[1,768]{1,0:T(1,128)S(1)}, f32[1,768]{1,0:T(1,128)}, u32[]{:S(2)}) copy-start(f32[1,768]{1,0:T(1,128)} %get-tuple-element.242) | copy-start | bytes 9220
  929.0 41.5 %copy-start.12 = (f32[1,768]{1,0:T(1,128)S(1)}, f32[1,768]{1,0:T(1,128)}, u32[]{:S(2)}) copy-start(f32[1,768]{1,0:T(1,128)} %get-tuple-element.246) | copy-start | bytes 9220
  1161.3 7.2 slice-start
  1163.0 5.4 slice-start.1
  1175.4 2.5 copy-start
Sparse Core Ops, SparseCore 0:
  9.6 20.1 all-gather.4
  349.0 24.4 all-gather.6
  420.0 57.0 all-reduce.4
  796.9 85.2 reduce-scatter.3
  884.6 276.6 reduce-scatter.5
  1163.4 32.9 reduce-scatter.7

commit v4 on v3

--- a/solution.py
+++ b/solution.py
@@ -13,8 +13,13 @@
 SEQ_LEN = 1536
 WINDOW = 1024
 CAPACITY = 480
-BLOCK = 256
+BLOCK = 512
+PACK = 256
 BLOCKS = SEQ_LEN // BLOCK
+KEYS = 256
+BACK_BLOCK = 384
+BACK_BLOCKS = SEQ_LEN // BACK_BLOCK
+BACK_KEYS = 384
 LANES = 128
 SLOTS = 3
 VMEM_BYTES = 60 * 2**20
@@ -247,16 +252,14 @@
     return copy
 
 
-def spread_on(pieces, size, own, passed, next_ref, sends, recvs, near):
-    spread = []
-    for step in range(pieces):
-        rows = piece_rows(own, step, size)
-        passed[step].wait_recv()
-        spread.append(
-            remote(next_ref.at[rows], next_ref.at[rows], sends.at[4, step], recvs.at[4, step], near)
-        )
-        spread[-1].start()
-    return spread
+LAG = 3
+
+
+def spread_on(step, passed, rows, next_ref, sends, recvs, near):
+    passed[step].wait_recv()
+    copy = remote(next_ref.at[rows], next_ref.at[rows], sends.at[4, step], recvs.at[4, step], near)
+    copy.start()
+    return copy
 
 
 def output_kernel(
@@ -289,7 +292,11 @@
     )
     load.start()
     greet([near, far, across])
-    back, passed, local_copies = [], [], []
+    back, passed, spread, local_copies = [], [], [], []
+
+    def forward(step):
+        rows = piece_rows(own, step, size)
+        spread.append(spread_on(step, passed, rows, next_ref, sends, recvs, near))
 
     def use(step, local, total):
         if step == 0:
@@ -305,11 +312,14 @@
             pltpu.make_async_copy(done.at[local], out_ref.at[rows], stored.at[step])
         )
         local_copies[-1].start()
+        if step >= LAG:
+            forward(step - LAG)
 
     copies = cross_kernel(
         pieces, part_ref, mine, first, kept, second, sends, recvs, loaded, use
     )
-    spread = spread_on(pieces, size, own, passed, next_ref, sends, recvs, near)
+    for step in range(pieces - LAG, pieces):
+        forward(step)
     for copy in back + spread:
         copy.wait_recv()
     for copy in copies + back + passed + spread:
@@ -390,7 +400,7 @@
             load.start()
     greet([near, far, across])
     gains[...] = jnp.zeros_like(gains)
-    back, passed, local_copies = [], [], []
+    back, passed, spread, local_copies = [], [], [], []
 
     def rows_back(here, side, step):
         grad_normed = full[here, :].astype(F32)
@@ -408,6 +418,17 @@
         local_copies[-1].start()
         return result
 
+    def partner_rows(step):
+        if step == 0:
+            for load in loads[1]:
+                load.wait()
+        back[step].wait_recv()
+        rows_back(piece_rows(other, step, size), 1, step)
+
+    def forward(step):
+        here = piece_rows(own, step, size)
+        spread.append(spread_on(step, passed, here, next_ref, sends, recvs, near))
+
     def use(step, local, total):
         if step == 0:
             for load in loads[0]:
@@ -420,16 +441,17 @@
         back[-1].start()
         given[local, :] = rows_back(here, 0, step).astype(BF16)
         passed.append(pass_on(step, given.at[local], here, next_ref, sends, recvs, across))
+        if step > 0:
+            partner_rows(step - 1)
+        if step >= LAG:
+            forward(step - LAG)
 
     copies = cross_kernel(
         pieces, part_ref, mine, first, kept, second, sends, recvs, loaded, use
     )
-    spread = spread_on(pieces, size, own, passed, next_ref, sends, recvs, near)
-    for load in loads[1]:
-        load.wait()
-    for step in range(pieces):
-        back[step].wait_recv()
-        rows_back(piece_rows(other, step, size), 1, step)
+    partner_rows(pieces - 1)
+    for step in range(pieces - LAG, pieces):
+        forward(step)
     grad_gain_ref[...] = gains[0:1, :] + gains[1:2, :]
     for copy in spread:
         copy.wait_recv()
@@ -494,66 +516,82 @@
     a_ref[0] = normed
     cosine, sine = cos_ref[...], sin_ref[...]
     here = rows_of(index, BLOCK)
+    projected = dot(normed, wall_ref[...])
     for group in range(2 * heads):
         columns = slice(group * LANES, (group + 1) * LANES)
-        pre = dot(normed, wall_ref[:, columns])
+        pre = projected[:, columns]
         turned = pre * cosine + pltpu.roll(pre, HEAD_DIM, 1) * sine
         if group < heads:
             turned = turned * 0.0625
         qkv_ref[0, :, columns] = turned.astype(BF16)
-    qkv_ref[0, :, 2 * wide :] = dot(normed, wall_ref[:, 2 * wide :]).astype(BF16)
+    qkv_ref[0, :, 2 * wide :] = projected[:, 2 * wide :].astype(BF16)
     keys[here, :] = qkv_ref[0, :, wide : 2 * wide]
+    low = low_ref[0]
+    query_at = index * BLOCK + lax.broadcasted_iota(jnp.int32, (BLOCK, KEYS), 0)
+    key_at = lax.broadcasted_iota(jnp.int32, (BLOCK, KEYS), 1)
+
+    @pl.when(index * BLOCK % KEYS == 0)
+    def _():
+        values[rows_of(index * BLOCK // KEYS, KEYS), :] = jnp.zeros((KEYS, wide), BF16)
+
     values[here, :] = qkv_ref[0, :, 2 * wide :]
-    low = low_ref[0]
-    query_at = index * BLOCK + lax.broadcasted_iota(jnp.int32, (BLOCK, BLOCK), 0)
-    key_at = lax.broadcasted_iota(jnp.int32, (BLOCK, BLOCK), 1)
     tops[...] = jnp.full_like(tops, -1e30)
     sums[...] = jnp.zeros_like(sums)
     mixed[...] = jnp.zeros_like(mixed)
     begin = first_block[meta[2] * BLOCKS + index]
 
     def score(block, none):
-        at = key_at + block * BLOCK
+        at = key_at + block * KEYS
         valid = (at >= low) & (at <= query_at)
-        there = rows_of(block, BLOCK)
+        there = rows_of(block, KEYS)
         for head in range(heads):
             columns = slice(head * LANES, (head + 1) * LANES)
             raw = dot_nt(qkv_ref[0, :, columns], keys[there, columns])
             raw = jnp.where(valid, raw, -1e30)
             scores[head, block] = raw
-            tops[head] = jnp.maximum(
-                tops[head], jnp.maximum(raw[:, :LANES], raw[:, LANES:])
-            )
+            best = tops[head]
+            for start in range(0, KEYS, LANES):
+                best = jnp.maximum(best, raw[:, start : start + LANES])
+            tops[head] = best
         return none
 
-    lax.fori_loop(begin, index + 1, score, 0)
+    end = ((index + 1) * BLOCK - 1) // KEYS + 1
+    lax.fori_loop(begin, end, score, 0)
     top = [jnp.max(tops[head], axis=1, keepdims=True) for head in range(heads)]
 
     def mix(block, none):
-        there = rows_of(block, BLOCK)
+        there = rows_of(block, KEYS)
         for head in range(heads):
             columns = slice(head * LANES, (head + 1) * LANES)
             weights = jnp.exp(scores[head, block] - top[head])
-            sums[head] += weights[:, :LANES] + weights[:, LANES:]
+            part = weights[:, :LANES]
+            for start in range(LANES, KEYS, LANES):
+                part = part + weights[:, start : start + LANES]
+            sums[head] += part
             mixed[:, columns] += dot(weights.astype(BF16), values[there, columns])
         return none
 
-    lax.fori_loop(begin, index + 1, mix, 0)
+    lax.fori_loop(begin, end, mix, 0)
     for head in range(heads):
         columns = slice(head * LANES, (head + 1) * LANES)
         total = jnp.sum(sums[head], axis=1, keepdims=True)
         o_ref[0, :, columns] = (mixed[:, columns] / total).astype(BF16)
         logsum = jnp.broadcast_to(top[head] + jnp.log(total), (BLOCK, LANES))
         lse_ref[0, head : head + 1, :] = logsum.T[0:1, :]
-    half = BLOCK // 2
-    packed_ref[...] = jnp.concatenate(
-        [
-            o_ref[0, side * half : (side + 1) * half, head * LANES : head * LANES + HEAD_DIM]
-            for side in range(2)
-            for head in range(heads)
-        ],
-        axis=1,
-    )
+    half = PACK // 2
+    for start in range(0, BLOCK, PACK):
+        packed_ref[start // 2 : start // 2 + half, :] = jnp.concatenate(
+            [
+                o_ref[
+                    0,
+                    start + side * half : start + (side + 1) * half,
+                    head * LANES : head * LANES + HEAD_DIM,
+                ]
+                for side in range(2)
+                for head in range(heads)
+            ],
+            axis=1,
+        )
 
 
 def attention_forward(meta, first_block, tokens, received, gain, wall, cosine, sine, low, kept):
@@ -596,7 +634,7 @@
         scratch_shapes=[
             pltpu.VMEM((SEQ_LEN, wide), BF16),
             pltpu.VMEM((SEQ_LEN, wide), BF16),
-            pltpu.VMEM((heads, BLOCKS, BLOCK, BLOCK), F32),
+            pltpu.VMEM((heads, SEQ_LEN // KEYS, BLOCK, KEYS), F32),
             pltpu.VMEM((heads, BLOCK, LANES), F32),
             pltpu.VMEM((heads, BLOCK, LANES), F32),
             pltpu.VMEM((BLOCK, wide), F32),
@@ -623,6 +661,17 @@
         *(kept or ()),
     )
     return outs[0], outs[1:]
+
+
+def reserve(shapes):
+    return pl.pallas_call(
+        lambda *refs: None,
+        out_shape=shapes,
+        out_specs=[pl.BlockSpec(memory_space=pl.ANY)] * len(shapes),
+        compiler_params=pltpu.CompilerParams(has_side_effects=True),
+        cost_estimate=cost(1),
+        name="reserve",
+    )()
 
 
 PAIR = 2
@@ -705,7 +754,7 @@
 
     @pl.when(step < ROW_STEPS)
     def _():
-        half = BLOCK // 2
+        half = PACK // 2
         columns = ag_ref.shape[2] // 2
         mixed = jnp.concatenate(
             [
@@ -793,7 +842,7 @@
     width = layer_in.shape[2]
     wg, wu, wd, wgs, wus, wds = weights
     hidden = wg.shape[2]
-    stored = 0 if kept is None else 8
+    stored = 8
     saved = [
         shape_of((SLOTS, SEQ_LEN, width), F32),
         shape_of((SLOTS, SEQ_LEN, width), BF16),
@@ -881,9 +930,22 @@
         wgs,
         wus,
         wds,
-        *(kept or ()),
+        *(reserve(saved) if kept is None else kept),
     )
     return outs[0], outs[1:]
+
+
+def pull(grad, weight, gate, lift):
+    gate, lift = gate.astype(F32), lift.astype(F32)
+    sigma = 1.0 / (1.0 + jnp.exp(-gate))
+    swish = gate * sigma
+    hidden = (swish * lift).astype(BF16)
+    inner = None
+    if weight is not None:
+        inner = jnp.sum(hidden.astype(F32) * grad, axis=1, keepdims=True)
+        grad = grad * weight
+    grad_gate = (grad * lift * (sigma + swish * (1.0 - sigma))).astype(BF16)
+    return hidden, grad_gate, (grad * swish).astype(BF16), inner
 
 
 def feed_backward_kernel(
@@ -912,18 +974,6 @@
     step = pl.program_id(0)
     pair = jnp.maximum(step - ROW_STEPS, 0)
 
-    def pull(grad, weight, gate, lift):
-        gate, lift = gate.astype(F32), lift.astype(F32)
-        sigma = 1.0 / (1.0 + jnp.exp(-gate))
-        swish = gate * sigma
-        hidden = (swish * lift).astype(BF16)
-        inner = None
-        if weight is not None:
-            inner = jnp.sum(hidden.astype(F32) * grad, axis=1, keepdims=True)
-            grad = grad * weight
-        grad_gate = (grad * lift * (sigma + swish * (1.0 - sigma))).astype(BF16)
-        return hidden, grad_gate, (grad * swish).astype(BF16), inner
-
     @pl.when(step < ROW_STEPS)
     def _():
         dy = jnp.where(meta[0] == 1, cot_ref[...], rec_ref[...])
@@ -1004,7 +1054,7 @@
     width = cotangent.shape[1]
     wg, wu, wd, wgs, wus, wds = weights
     hidden = wg.shape[2]
-    stored = 0 if kept is None else 8
+    stored = 8
     unused_h, unused_b, unused_x, gate, lift, gate_sh, lift_sh, probs = forward_kept
     saved = [
         shape_of((SLOTS, SEQ_LEN, width), BF16),
@@ -1099,7 +1149,7 @@
         wgs,
         wus,
         wds,
-        *(kept or ()),
+        *(reserve(saved) if kept is None else kept),
     )
     return outs[0], outs[1:]
 
@@ -1130,7 +1180,7 @@
     part_ref, dh_ref, gain_grad_ref, router_grad_ref, dqkv_ref, dattn_ref = rest[:6]
     dk_all, dv_all, dq_all, do_all, inner_all = rest[6:]
     step = pl.program_id(0)
-    index = BLOCKS - 1 - step
+    index = BACK_BLOCKS - 1 - step
     heads = wo_ref.shape[0] // LANES
     wide = heads * LANES
 
@@ -1163,17 +1213,17 @@
     for head in range(heads):
         columns = slice(head * LANES, (head + 1) * LANES)
         row = jnp.sum(products[:, columns], axis=1, keepdims=True)
-        inner_all[head : head + 1, :] = jnp.broadcast_to(row, (BLOCK, LANES)).T[0:1, :]
+        inner_all[head : head + 1, :] = jnp.broadcast_to(row, (BACK_BLOCK, LANES)).T[0:1, :]
     dq_all[...] = jnp.zeros_like(dq_all)
-    here = rows_of(index, BLOCK)
+    here = rows_of(index, BACK_BLOCK)
     low = low_ref[0]
-    query_at = index * BLOCK + lax.broadcasted_iota(jnp.int32, (BLOCK, BLOCK), 1)
-    key_at = lax.broadcasted_iota(jnp.int32, (BLOCK, BLOCK), 0)
+    query_at = index * BACK_BLOCK + lax.broadcasted_iota(jnp.int32, (BACK_KEYS, BACK_BLOCK), 1)
+    key_at = lax.broadcasted_iota(jnp.int32, (BACK_KEYS, BACK_BLOCK), 0)
 
     def body(block, none):
-        at = key_at + block * BLOCK
+        at = key_at + block * BACK_KEYS
         valid = (at >= low) & (at <= query_at)
-        there = rows_of(block, BLOCK)
+        there = rows_of(block, BACK_KEYS)
         for head in range(heads):
             columns = slice(head * LANES, (head + 1) * LANES)
             key_columns = slice(wide + head * LANES, wide + (head + 1) * LANES)
@@ -1189,7 +1239,9 @@
             dq_all[:, columns] += dot_tn(grad_scores, keys)
         return none
 
-    lax.fori_loop(first_block[meta[2] * BLOCKS + index], index + 1, body, 0)
+    lax.fori_loop(
+        first_block[meta[2] * BACK_BLOCKS + index], ((index + 1) * BACK_BLOCK - 1) // BACK_KEYS + 1, body, 0
+    )
     cosine, sine = cos_ref[...], sin_ref[...]
     for head in range(heads):
         columns = slice(head * LANES, (head + 1) * LANES)
@@ -1219,24 +1271,24 @@
     ]
 
     def at(step):
-        return BLOCKS - 1 - step
+        return BACK_BLOCKS - 1 - step
 
     def slot_rows(columns, which):
-        return pl.BlockSpec((1, BLOCK, columns), lambda s, m, f: (m[which], at(s), 0))
+        return pl.BlockSpec((1, BACK_BLOCK, columns), lambda s, m, f: (m[which], at(s), 0))
 
     def fixed(shape):
         return once(shape, lambda s, m, f: (0,) * len(shape))
 
-    halves_of = BLOCKS // 2
+    halves_of = BACK_BLOCKS // 2
     grid_spec = pltpu.PrefetchScalarGridSpec(
         num_scalar_prefetch=2,
-        grid=(BLOCKS,),
+        grid=(BACK_BLOCKS,),
         in_specs=[
-            pl.BlockSpec((BLOCK, width), lambda s, m, f: (at(s), 0)),
+            pl.BlockSpec((BACK_BLOCK, width), lambda s, m, f: (at(s), 0)),
             pl.BlockSpec(
-                (16, BLOCK), lambda s, m, f: (SEQ_LEN // 16 + at(s) // halves_of, at(s) % halves_of)
+                (16, BACK_BLOCK), lambda s, m, f: (SEQ_LEN // 16 + at(s) // halves_of, at(s) % halves_of)
             ),
-            pl.BlockSpec((1, EXPERTS, BLOCK), lambda s, m, f: (m[3], 0, at(s))),
+            pl.BlockSpec((1, EXPERTS, BACK_BLOCK), lambda s, m, f: (m[3], 0, at(s))),
             slot_rows(width, 1),
             slot_rows(width, 3),
             slot_rows(width, 3),
@@ -1244,17 +1296,17 @@
             fixed(router.shape),
             fixed(wall.shape),
             fixed(wo.shape),
-            pl.BlockSpec((BLOCK, LANES), lambda s, m, f: (at(s), 0)),
-            pl.BlockSpec((BLOCK, LANES), lambda s, m, f: (at(s), 0)),
+            pl.BlockSpec((BACK_BLOCK, LANES), lambda s, m, f: (at(s), 0)),
+            pl.BlockSpec((BACK_BLOCK, LANES), lambda s, m, f: (at(s), 0)),
             once((1, SEQ_LEN, 3 * wide), lambda s, m, f: (m[3], 0, 0)),
             slot_rows(wide, 3),
-            pl.BlockSpec((1, 8, BLOCK), lambda s, m, f: (m[3], 0, at(s))),
-            pl.BlockSpec((1, 1, BLOCK), lambda s, m, f: (m[2], 0, at(s))),
+            pl.BlockSpec((1, 8, BACK_BLOCK), lambda s, m, f: (m[3], 0, at(s))),
+            pl.BlockSpec((1, 1, BACK_BLOCK), lambda s, m, f: (m[2], 0, at(s))),
         ]
         + [pl.BlockSpec(memory_space=pl.ANY)] * stored,
         out_specs=[
-            pl.BlockSpec((BLOCK, width), lambda s, m, f: (at(s), 0)),
-            pl.BlockSpec((BLOCK, width), lambda s, m, f: (at(s), 0)),
+            pl.BlockSpec((BACK_BLOCK, width), lambda s, m, f: (at(s), 0)),
+            pl.BlockSpec((BACK_BLOCK, width), lambda s, m, f: (at(s), 0)),
             fixed((1, width)),
             fixed((8, width)),
             slot_rows(3 * wide, 1),
@@ -1263,9 +1315,9 @@
         scratch_shapes=[
             pltpu.VMEM((SEQ_LEN, wide), F32),
             pltpu.VMEM((SEQ_LEN, wide), F32),
-            pltpu.VMEM((BLOCK, wide), F32),
-            pltpu.VMEM((BLOCK, wide), BF16),
-            pltpu.VMEM((8, BLOCK), F32),
+            pltpu.VMEM((BACK_BLOCK, wide), F32),
+            pltpu.VMEM((BACK_BLOCK, wide), BF16),
+            pltpu.VMEM((8, BACK_BLOCK), F32),
         ],
     )
     outs = pl.pallas_call(
@@ -1348,6 +1400,129 @@
     )
 
 
+def lead_grads_kernel(
+    meta,
+    cot_ref,
+    rec_ref,
+    post_ref,
+    probs_ref,
+    g_ref,
+    u_ref,
+    wd_ref,
+    xa_ref,
+    xb_ref,
+    ga_ref,
+    ua_ref,
+    ea_ref,
+    ha_ref,
+    out_ref,
+    given,
+    pick,
+    gates,
+    rows_in,
+    grad_gate,
+    grad_lift,
+    grad_rows,
+    hidden,
+):
+    step = pl.program_id(0)
+
+    @pl.when(step == 0)
+    def _():
+        given[...] = jnp.where(meta[0] == 1, cot_ref[...], rec_ref[...])
+
+    @pl.when(step > 0)
+    def _():
+        chunks = [(0, chunk) for chunk in range(CAPACITY // CHUNK)]
+        build_pick(step - 1, chunks, post_ref, probs_ref.at[0], pick, gates)
+        rows_in[...] = dot(pick[...], given[...]).astype(BF16)
+        weight = gates[:, 0:1]
+        grad_rows[...] = (weight * rows_in[...].astype(F32)).astype(BF16)
+        hidden[...], grad_gate[...], grad_lift[...], unused = pull(
+            dot_nt(rows_in[...], wd_ref[0]), weight, g_ref[0, 0], u_ref[0, 0]
+        )
+        devices, unused, rows, unused = out_ref.shape
+        pairs = [
+            (xa_ref.at[0, 0], ga_ref.at[0, 0], xb_ref.at[0, 0], grad_gate),
+            (xa_ref.at[0, 0], ua_ref.at[0, 0], xb_ref.at[0, 0], grad_lift),
+            (ea_ref.at[0, 0], ha_ref.at[0, 0], grad_rows, hidden),
+        ]
+        for number, (left, right, left_last, right_last) in enumerate(pairs):
+            for device in range(devices):
+                columns = slice(device * rows, (device + 1) * rows)
+                out_ref[device, number] = (
+                    dot_tn(left[:, columns], right[...])
+                    + dot_tn(left_last[:, columns], right_last[...])
+                ).astype(BF16)
+
+
+def lead_grads(count, devices, meta, cotangent, received, post, forward_kept, kept, down):
+    unused_h, unused_b, picked, gate, lift, unused_gate, unused_lift, probs = forward_kept
+    unused_dy, hid, grad_gate, grad_lift, grad_expert = kept[:5]
+    width, inner = picked.shape[3], gate.shape[3]
+    rows = width // devices
+
+    def at(step):
+        return jnp.maximum(step - 1, 0)
+
+    def of_slot(columns, which):
+        return pl.BlockSpec((1, 1, CAPACITY, columns), lambda s, m: (m[which], at(s), 0, 0))
+
+    grid_spec = pltpu.PrefetchScalarGridSpec(
+        num_scalar_prefetch=1,
+        grid=(count + 1,),
+        in_specs=[
+            once((SEQ_LEN, width), lambda s, m: (m[1], 0)),
+            once((SEQ_LEN, width), lambda s, m: (0, 0)),
+            once((1, EXPERTS, SEQ_LEN), lambda s, m: (m[1], 0, 0)),
+            once((1, EXPERTS, SEQ_LEN), lambda s, m: (m[2], 0, 0)),
+            of_slot(inner, 2),
+            of_slot(inner, 2),
+            pl.BlockSpec((1,) + down.shape[1:], lambda s, m: (at(s), 0, 0)),
+            of_slot(width, 3),
+            of_slot(width, 2),
+            of_slot(inner, 3),
+            of_slot(inner, 3),
+            of_slot(width, 3),
+            of_slot(inner, 3),
+        ],
+        out_specs=pl.BlockSpec((devices, 3, rows, inner), lambda s, m: (0, at(s), 0, 0)),
+        scratch_shapes=[
+            pltpu.VMEM((SEQ_LEN, width), BF16),
+            pltpu.VMEM((CAPACITY, SEQ_LEN), BF16),
+            pltpu.VMEM((CAPACITY, LANES), F32),
+            pltpu.VMEM((CAPACITY, width), BF16),
+            pltpu.VMEM((CAPACITY, inner), BF16),
+            pltpu.VMEM((CAPACITY, inner), BF16),
+            pltpu.VMEM((CAPACITY, width), BF16),
+            pltpu.VMEM((CAPACITY, inner), BF16),
+        ],
+    )
+    return pl.pallas_call(
+        lead_grads_kernel,
+        grid_spec=grid_spec,
+        out_shape=shape_of((devices, 3 * count, rows, inner), BF16),
+        compiler_params=pltpu.CompilerParams(vmem_limit_bytes=VMEM_BYTES),
+        cost_estimate=cost(20),
+        name="lead_grads",
+    )(
+        meta,
+        cotangent,
+        received,
+        post,
+        probs,
+        gate,
+        lift,
+        down,
+        picked,
+        picked,
+        grad_gate,
+        grad_lift,
+        grad_expert,
+        hid,
+    )
+
+
 def shared_grads_kernel(b_ref, dy_ref, gate_ref, lift_ref, hid_ref, before_ref, out_ref, *totals):
     step = pl.program_id(0)
     pairs = [(b_ref, gate_ref), (b_ref, lift_ref), (dy_ref, hid_ref)]
@@ -1372,7 +1547,7 @@
 
 def shared_grads(before, b, dy, grad_gate, grad_lift, hid):
     devices, matrices, width, hidden = before.shape
-    rows = 2 * BLOCK
+    rows = ROWS
     steps = SEQ_LEN // rows
 
     def spec(array):
@@ -1414,7 +1589,7 @@
 
 def token_grads(lefts, rights):
     count = len(lefts)
-    rows = 2 * BLOCK
+    rows = ROWS
     steps = SEQ_LEN // rows
 
     def spec(array):
@@ -1522,7 +1697,8 @@
     )
     pos, post = places(routes[0].reshape(count, SEQ_LEN, 2))
     low = first_allowed(doc_lengths)
-    first_block = (low[:, ::BLOCK] // BLOCK).reshape(-1)
+    first_block = (low[:, ::BLOCK] // KEYS).reshape(-1)
+    back_first = (low[:, ::BACK_BLOCK] // BACK_KEYS).reshape(-1)
     low_column, low_row = low[:, :, None], low[:, None, :]
 
     received = jnp.zeros((SEQ_LEN, width), BF16)
@@ -1578,7 +1754,7 @@
     def attend_back(meta, summed):
         return attention_backward(
             meta,
-            first_block,
+            back_first,
             summed,
             feed_kept,
             attention_kept,
@@ -1596,7 +1772,7 @@
     for tick in range(count):
         meta = forward_meta(tick)
         own, attention_kept = attend(meta, received, attention_kept)
-        gathered = tensor_gather(own, 0)
+        gathered = lax.all_gather(own, "tensor") if tick == 0 else tensor_gather(own, 0)
         part, feed_kept = feed(meta, gathered, feed_kept)
         result, received = output_relay(part, feed_kept[0], tick, 4 + tick)
         results.append(result)
@@ -1615,22 +1791,41 @@
     for tick in range(count + 1):
         if tick > 0:
             back_meta = backward_meta(tick)
+        if tick == count:
+            lead, middle = 2, 3
+            lead_meta = jnp.stack(
+                [2 - section, jnp.full_like(section, count - 1), jnp.full_like(section, count)]
+                + [jnp.full_like(section, count - 1)]
+            ).astype(jnp.int32)
+            lead_part = lead_grads(
+                lead,
+                devices,
+                lead_meta,
+                cotangent,
+                received,
+                post,
+                feed_kept,
+                grads_kept,
+                feed_weights[2],
+            )
+            back_meta, lead_part = after(back_meta, lead_part)
+        if tick > 0:
             part, grads_kept = feed_back(back_meta, received)
         if tick == count:
             dy, hid, grad_gate, grad_lift, grad_expert, hid_sh, grad_gate_sh, grad_lift_sh = (
                 grads_kept
             )
-            lead = 2
             picked = feed_kept[2]
-            first_grads = expert_grads(
-                0, lead, 0, devices, picked, hid, grad_gate, grad_lift, grad_expert
+            middle_part = expert_grads(
+                lead, middle, 0, devices, picked, hid, grad_gate, grad_lift, grad_expert
             )
-            first_grads, picked, grad_gate = lax.optimization_barrier(
-                (first_grads, picked, grad_gate)
+            middle_part, picked, grad_gate = lax.optimization_barrier(
+                (middle_part, picked, grad_gate)
             )
-            other_grads = expert_grads(
-                lead,
-                EXPERTS - lead,
+            first = lead + middle
+            last_grads = expert_grads(
+                first,
+                EXPERTS - first,
                 3,
                 devices,
                 picked,
@@ -1639,11 +1834,11 @@
                 grad_lift,
                 grad_expert,
             )
-            other_grads = shared_grads(
-                other_grads, feed_kept[1], dy, grad_gate_sh, grad_lift_sh, hid_sh
+            last_grads = shared_grads(
+                last_grads, feed_kept[1], dy, grad_gate_sh, grad_lift_sh, hid_sh
             )
-            part, other_grads = lax.optimization_barrier((part, other_grads))
-            first_grads, other_grads = spread(first_grads), spread(other_grads)
+            part, last_grads = lax.optimization_barrier((part, last_grads))
+            parts = [spread(lead_part), spread(middle_part), spread(last_grads)]
         if tick > 0:
             summed = tensor_sum(part, 2, 7)
         (part, grad_state, gain_grad, router_grad), attention_grads_kept = attend_back(
@@ -1672,12 +1867,10 @@
         ],
         axis=1,
     )
-    packed, first_grads, other_grads = lax.optimization_barrier(
-        (packed, first_grads, other_grads)
-    )
+    packed, *parts = lax.optimization_barrier((packed, *parts))
     packed = spread(packed.reshape(devices, rows, -1)).astype(F32)
-    shared = other_grads[-3:].astype(F32)
-    experts = jnp.concatenate([first_grads, other_grads[:-3]], axis=0).astype(F32)
+    shared = parts[2][-3:].astype(F32)
+    experts = jnp.concatenate([parts[0], parts[1], parts[2][:-3]], axis=0).astype(F32)
     experts = experts.reshape(EXPERTS, 3, rows, -1)
 
     def choose(items):

time: 1220 us -> 1130 us (0.926)
  Pallas kernels: 966 us -> 907 us
  waiting for transfers between devices: 158 us -> 132 us
    reduce_scatter x3 -> x4, waiting for transfers between devices: 155 us -> 113 us  [spread(): return lax.psum_scatter(array, 'dp', scatter_dimension=0, tiled=False)]
    pallas_call x2 -> x1, Pallas kernels: 42.5 us -> 20.1 us  [tensor_gather(): pl.pallas_call(functools.partial(gather_kernel, pieces), out_shape=shape_...]
    pallas_call x3, Pallas kernels: 112 us -> 92.9 us  [attention_backward(): pl.pallas_call(functools.partial(attention_backward_kernel, stored), grid...]
    pallas_call x0 -> x3, Pallas kernels: none -> 17.2 us  [the longest x1 17.2 us: lead_grads(): pl.pallas_call(lead_grads_kernel, grid_spec=grid_spec, out_shape=shape_of...]
    all_gather x0 -> x1, waiting for transfers between devices: none -> 15.7 us  [on_device(): lax.all_gather(own, 'tensor')]
    pallas_call x3, Pallas kernels: 181 us -> 168 us  [feed_forward(): pl.pallas_call(functools.partial(feed_forward_kernel, stored), grid_spec=...]
  transfers between devices with their start and end apart: 6 -> 8, of which waited for: 3 -> 4; matrix products, arithmetic and copies ran while one was open for 5% -> 5% of each run, Pallas kernels for 31% -> 36%
where the time goes in v4:
time: 1130 us; the launch traced here: 1120 us
  Pallas kernels  907 us (80%)
  waiting for transfers between devices  132 us (12%)
  other arithmetic  42.6 us (4%)
  local copies, waits for them, and re-layouts  24.3 us (2%)
  between operations  14.9 us (1%)
    pallas_call x3, Pallas kernels, feed_backward(): pl.pallas_call(functools.partial(feed_backward_kernel, stored), grid_spec...  189 us
    pallas_call x3, Pallas kernels, feed_forward(): pl.pallas_call(functools.partial(feed_forward_kernel, stored), grid_spec=...  168 us
    pallas_call x3, Pallas kernels, input_relay(): pl.pallas_call(functools.partial(input_kernel, pieces, tick), out_shape=[...  118 us
    reduce_scatter x4, waiting for transfers between devices, spread(): return lax.psum_scatter(array, 'dp', scatter_dimension=0, tiled=False)  113 us
    pallas_call x3, Pallas kernels, output_relay(): pl.pallas_call(functools.partial(output_kernel, pieces, tick), out_shape=...  112 us
    pallas_call x3, Pallas kernels, attention_backward(): pl.pallas_call(functools.partial(attention_backward_kernel, stored), grid...  92.9 us
    pallas_call x2, Pallas kernels, tensor_sum(): pl.pallas_call(functools.partial(sum_kernel, pieces), out_shape=shape_of(...  64.1 us
    pallas_call x3, Pallas kernels, attention_forward(): pl.pallas_call(functools.partial(attention_forward_kernel, stored), grid_...  63.8 us
  transfers between devices with their start and end apart: 8, of which 4 were waited for; matrix products, arithmetic and copies ran while one was open for 5% of the time, Pallas kernels for 36%

profile of v4, /device:TPU:0, one launch (start us, length us, event | category | flops | bytes accessed | tf_op | source)
XLA Modules:
  0.0 1123.7 jit_solution(13649417515775446873)
XLA Ops:
  7.2 0.7 all-gather.9.cloned.1.call-update
  8.0 0.9 reduce_window_sum.11
  8.9 1.3 convert_element_type.37.gain_ref
  11.0 1.0 slice_negate_fusion.1
  12.0 1.0 pad_maximum_fusion.3
  13.3 1.0 slice_negate_fusion
  14.3 1.0 pad_maximum_fusion.4
  16.5 1.5 broadcast_maximum_fusion.low_ref
  18.0 1.4 pad_maximum_fusion.1.wall_ref
  20.0 1.6 broadcast_10_rec_ref.2.rec_ref
  21.5 22.4 %attention_forward.3 = (bf16[768,384]{1,0:T(8,128)(2,1)}, bf16[3,1536,768]{2,1,0:T(8,128)(2,1)}, bf16[3,1536,768]{2,1,0:T(8,128)(2,1)}, bf16[3,1536,1152]{2,1,0:...) custom-call(s32[3]{0:T(128)} %get-tuple-element.373.meta, s32[6]{0:T(128)} %reshape.138.first_block, ...), custom_call_target="tpu_custom_call" | custom-call | flops 27599998976 | bytes 86400000 | tf_op jit(solution)/shard_map/attention_forward/pallas_call | solution.py:643
  46.1 0.9 concatenate.41
  46.9 2.2 bitcast_select_fusion.1
  49.1 1.1 copy.202.post_ref
  53.9 1.3 bitcast_select_fusion.pos_ref
  55.2 15.7 %all-gather.7.cloned.1.call-done = bf16[3072,384]{1,0:T(8,128)(2,1)} async-done(((bf16[768,384]{1,0:T(8,128)(2,1)}), bf16[3072,384]{1,0:T(8,128)(2,1)}) %all-gather.7.cloned.1.call-update) | async-done | bytes 2359312 | tf_op jit(solution)/shard_map/all_gather | solution.py:1775
  70.9 55.9 %feed_forward.3 = (bf16[1536,768]{1,0:T(8,128)(2,1)}, f32[3,1536,768]{2,1,0:T(8,128)}, bf16[3,1536,768]{2,1,0:T(8,128)(2,1)}, bf16[3,8,480,768]{3,2,1,0:T(8,128)...) custom-call(s32[3]{0:T(128)} %get-tuple-element.373.meta, ...), custom_call_target="tpu_custom_call", output_to_operand_aliasing={{1}: (14, {}), {2}: (15, {}), {3}: (16, {}), {4}: (17, {}),... | custom-call | flops 64399998976 | bytes 201600000 | tf_op jit(solution)/shard_map/feed_forward/pallas_call | solution.py:910
  126.9 36.9 %output_relay.3 = (bf16[1536,768]{1,0:T(8,128)(2,1)}, bf16[1536,768]{1,0:T(8,128)(2,1)}) custom-call(bf16[1536,768]{1,0:T(8,128)(2,1)} %get-tuple-element.163.part_ref, f32[3,1536,768]{2,1,0:T(8,128)} %get-tuple-element.164.states_ref.rest_0_), custom_call_target="tpu_custom_call" | custom-call | flops 43699998720 | bytes 136800000 | tf_op jit(solution)/shard_map/output_relay/pallas_call | solution.py:334
  163.8 20.7 %attention_forward.4 = (bf16[768,384]{1,0:T(8,128)(2,1)}, bf16[3,1536,768]{2,1,0:T(8,128)(2,1)}, bf16[3,1536,768]{2,1,0:T(8,128)(2,1)}, bf16[3,1536,1152]{2,1,0:...) custom-call(s32[3]{0:T(128)} %get-tuple-element.374.meta, ...), custom_call_target="tpu_custom_call", output_to_operand_aliasing={{1}: (9, {}), {2}: (10, {}), {3}: (11, {}), {4}: (12, {}), ... | custom-call | flops 27599998976 | bytes 86400000 | tf_op jit(solution)/shard_map/attention_forward/pallas_call | solution.py:643
  184.5 20.1 %tensor_gather.1.ag_ref = bf16[4,768,384]{2,1,0:T(8,128)(2,1)} custom-call(bf16[768,384]{1,0:T(8,128)(2,1)} %get-tuple-element.172.own_ref), custom_call_target="tpu_custom_call" | custom-call | flops 20700000256 | bytes 64800000 | tf_op jit(solution)/shard_map/tensor_gather/pallas_call | solution.py:235
  204.6 56.0 %feed_forward.4 = (bf16[1536,768]{1,0:T(8,128)(2,1)}, f32[3,1536,768]{2,1,0:T(8,128)}, bf16[3,1536,768]{2,1,0:T(8,128)(2,1)}, bf16[3,8,480,768]{3,2,1,0:T(8,128)...) custom-call(s32[3]{0:T(128)} %get-tuple-element.374.meta, ...), custom_call_target="tpu_custom_call", output_to_operand_aliasing={{1}: (14, {}), {2}: (15, {}), {3}: (16, {}), {4}: (17, {}),... | custom-call | flops 64399998976 | bytes 201600000 | tf_op jit(solution)/shard_map/feed_forward/pallas_call | solution.py:910
  260.6 38.2 %output_relay.4 = (bf16[1536,768]{1,0:T(8,128)(2,1)}, bf16[1536,768]{1,0:T(8,128)(2,1)}) custom-call(bf16[1536,768]{1,0:T(8,128)(2,1)} %get-tuple-element.180.part_ref, f32[3,1536,768]{2,1,0:T(8,128)} %get-tuple-element.181.states_ref.rest_0_), custom_call_target="tpu_custom_call" | custom-call | flops 43699998720 | bytes 136800000 | tf_op jit(solution)/shard_map/output_relay/pallas_call | solution.py:334
  298.9 20.7 %attention_forward.5 = (bf16[768,384]{1,0:T(8,128)(2,1)}, bf16[3,1536,768]{2,1,0:T(8,128)(2,1)}, bf16[3,1536,768]{2,1,0:T(8,128)(2,1)}, bf16[3,1536,1152]{2,1,0:...) custom-call(s32[3]{0:T(128)} %pad_add_fusion.3.meta, ...), custom_call_target="tpu_custom_call", output_to_operand_aliasing={{1}: (9, {}), {2}: (10, {}), {3}: (11, {}), {4}: (12, {}), ... | custom-call | flops 27599998976 | bytes 86400000 | tf_op jit(solution)/shard_map/attention_forward/pallas_call | solution.py:643
  319.6 71.1 %feed_backward.3 = (bf16[1568,768]{1,0:T(8,128)(2,1)}, bf16[3,1536,768]{2,1,0:T(8,128)(2,1)}, bf16[3,8,480,512]{3,2,1,0:T(8,128)(2,1)}, bf16[3,8,480,512]{3,2,1,...) custom-call(s32[4]{0:T(128)} %pad_add_fusion.2.meta, ...), custom_call_target="tpu_custom_call", output_to_operand_aliasing={{1}: (16, {}), {2}: (17, {}), {3}: (18, {}), {4}: (19, {}),... | custom-call | flops 69000003584 | bytes 216000000 | tf_op jit(solution)/shard_map/feed_backward/pallas_call | solution.py:1127
  390.8 55.8 %feed_forward.5 = (bf16[1536,768]{1,0:T(8,128)(2,1)}, f32[3,1536,768]{2,1,0:T(8,128)}, bf16[3,1536,768]{2,1,0:T(8,128)(2,1)}, bf16[3,8,480,768]{3,2,1,0:T(8,128)...) custom-call(s32[3]{0:T(128)} %pad_add_fusion.3.meta, ...), custom_call_target="tpu_custom_call", output_to_operand_aliasing={{1}: (14, {}), {2}: (15, {}), {3}: (16, {}), {4}: (17, {}),... | custom-call | flops 64399998976 | bytes 201600000 | tf_op jit(solution)/shard_map/feed_forward/pallas_call | solution.py:910
  446.7 2.7 all-reduce.5.cloned.1.call-done.sum_ref.choice_ref
  449.3 32.4 %attention_backward.3 = (bf16[1536,768]{1,0:T(8,128)(2,1)}, f32[1536,768]{1,0:T(8,128)}, f32[1,768]{1,0:T(1,128)}, f32[8,768]{1,0:T(8,128)}, bf16[3,1536,1152]{2...) custom-call(s32[4]{0:T(128)} %pad_add_fusion.2.meta, s32[8]{0:T(128)} %reshape.142.first_block, ...), custom_call_target="tpu_custom_call" | custom-call | flops 42550001664 | bytes 133200000 | tf_op jit(solution)/shard_map/attention_backward/pallas_call | solution.py:1323
  481.7 39.3 %input_relay.3 = (f32[1536,768]{1,0:T(8,128)}, bf16[1536,768]{1,0:T(8,128)(2,1)}, f32[1,768]{1,0:T(1,128)}) custom-call(bf16[1536,768]{1,0:T(8,128)(2,1)} %get-tuple-element.221.part_ref, bf16[3,1536,768]{2,1,0:T(8,128)(2,1)} %get-tuple-element.205.x_ref.layers_ref, f32[1536,768]{1,0:T(8,128)} %get-tuple-element.222.grad_state_ref, ...), custom_call_target="tpu_custom_call" | custom-call | flops 48299999232 | bytes 151200000 | tf_op jit(solution)/shard_map/input_relay/pallas_call | solution.py:468
  521.0 58.8 %feed_backward.4 = (bf16[1568,768]{1,0:T(8,128)(2,1)}, bf16[3,1536,768]{2,1,0:T(8,128)(2,1)}, bf16[3,8,480,512]{3,2,1,0:T(8,128)(2,1)}, bf16[3,8,480,512]{3,2,1,...) custom-call(s32[4]{0:T(128)} %pad_add_fusion.4.meta, ...), custom_call_target="tpu_custom_call", output_to_operand_aliasing={{1}: (16, {}), {2}: (17, {}), {3}: (18, {}), {4}: (19, {}),... | custom-call | flops 69000003584 | bytes 216000000 | tf_op jit(solution)/shard_map/feed_backward/pallas_call | solution.py:1127
  579.8 32.1 %tensor_sum.2.sum_ref.choice_ref = bf16[1568,768]{1,0:T(8,128)(2,1)} custom-call(bf16[1568,768]{1,0:T(8,128)(2,1)} %get-tuple-element.235.part_ref), custom_call_target="tpu_custom_call" | custom-call | flops 36800000000 | bytes 115200000 | tf_op jit(solution)/shard_map/tensor_sum/pallas_call | solution.py:175
  611.8 32.4 %attention_backward.4 = (bf16[1536,768]{1,0:T(8,128)(2,1)}, f32[1536,768]{1,0:T(8,128)}, f32[1,768]{1,0:T(1,128)}, f32[8,768]{1,0:T(8,128)}, bf16[3,1536,1152]{2...) custom-call(s32[4]{0:T(128)} %pad_add_fusion.4.meta, ...), custom_call_target="tpu_custom_call", output_to_operand_aliasing={{4}: (18, {}), {5}: (19, {})} | custom-call | flops 42550001664 | bytes 133200000 | tf_op jit(solution)/shard_map/attention_backward/pallas_call | solution.py:1323
  644.2 38.4 %input_relay.4 = (f32[1536,768]{1,0:T(8,128)}, bf16[1536,768]{1,0:T(8,128)(2,1)}, f32[1,768]{1,0:T(1,128)}) custom-call(bf16[1536,768]{1,0:T(8,128)(2,1)} %get-tuple-element.239.part_ref, bf16[3,1536,768]{2,1,0:T(8,128)(2,1)} %get-tuple-element.205.x_ref.layers_ref, f32[1536,768]{1,0:T(8,128)} %get-tuple-element.240.grad_state_ref, ...), custom_call_target="tpu_custom_call" | custom-call | flops 48299999232 | bytes 151200000 | tf_op jit(solution)/shard_map/input_relay/pallas_call | solution.py:468
  682.6 17.2 %lead_grads.1 = bf16[4,6,192,512]{3,2,1,0:T(8,128)(2,1)} custom-call(s32[4]{0:T(128)} %pad_add_fusion.6.meta, bf16[3072,768]{1,0:T(8,128)(2,1)} %cot_ref.7, bf16[1536,768]{1,0:T(8,128)(2,1)} %get-tuple-element.243.rec_ref, s32[2,8,1536]{2,1,0:T(8,128)} %copy.202.post_ref, f32[3,8,1536]{2,1,0:T(8,128)} %get-tuple-element.215.probs_ref, ...), custom_call_target="tpu_custom_call" | custom-call | flops 23000000512 | bytes 72000000 | tf_op jit(solution)/shard_map/lead_grads/pallas_call | solution.py:1501
  699.9 58.7 %feed_backward.5 = (bf16[1568,768]{1,0:T(8,128)(2,1)}, bf16[3,1536,768]{2,1,0:T(8,128)(2,1)}, bf16[3,8,480,512]{3,2,1,0:T(8,128)(2,1)}, bf16[3,8,480,512]{3,2,1,...) custom-call(s32[4]{0:T(128)} %pad_add_fusion.5.meta, ...), custom_call_target="tpu_custom_call", output_to_operand_aliasing={{1}: (16, {}), {2}: (17, {}), {3}: (18, {}), {4}: (19, {}),... | custom-call | flops 69000003584 | bytes 216000000 | tf_op jit(solution)/shard_map/feed_backward/pallas_call | solution.py:1127
  758.6 17.4 %expert_grads.2 = bf16[4,9,192,512]{3,2,1,0:T(8,128)(2,1)} custom-call(bf16[3,8,480,768]{3,2,1,0:T(8,128)(2,1)} %get-tuple-element.262.xa_ref.xb_ref.refs_0_.refs_1_, bf16[3,8,480,768]{3,2,1,0:T(8,128)(2,1)} %get-tuple-element.262.xa_ref.xb_ref.refs_0_.refs_1_, bf16[3,8,480,512]{3,2,1,0:T(8,128)(2,1)} %get-tuple-element.263.refs_2_.refs_3_, ...), custom_call_target="tpu_custom_call" | custom-call | flops 20700000256 | bytes 64800000 | tf_op jit(solution)/shard_map/expert_grads/pallas_call | solution.py:1388
  776.1 17.4 %expert_grads.3.before_ref = bf16[4,12,192,512]{3,2,1,0:T(8,128)(2,1)} custom-call(bf16[3,8,480,768]{3,2,1,0:T(8,128)(2,1)} %get-tuple-element.262.xa_ref.xb_ref.refs_0_.refs_1_, bf16[3,8,480,768]{3,2,1,0:T(8,128)(2,1)} %get-tuple-element.262.xa_ref.xb_ref.refs_0_.refs_1_, bf16[3,8,480,512]{3,2,1,0:T(8,128)(2,1)} %get-tuple-element.263.refs_2_.refs_3_, ...), custom_call_target="tpu_custom_call" | custom-call | flops 20700000256 | bytes 64800000 | tf_op jit(solution)/shard_map/expert_grads/pallas_call | solution.py:1388
  793.5 14.4 %shared_grads.1 = bf16[4,12,192,512]{3,2,1,0:T(8,128)(2,1)} custom-call(bf16[3,1536,768]{2,1,0:T(8,128)(2,1)} %get-tuple-element.217.b_ref, bf16[3,1536,768]{2,1,0:T(8,128)(2,1)} %get-tuple-element.254.dy_ref, bf16[3,1536,512]{2,1,0:T(8,128)(2,1)} %get-tuple-element.255.gate_ref, ...), custom_call_target="tpu_custom_call", output_to_operand_aliasing={{}: (5, {})} | custom-call | flops 14949999616 | bytes 46800000 | tf_op jit(solution)/shard_map/shared_grads/pallas_call | solution.py:1556
  807.9 32.1 %tensor_sum.3.sum_ref.choice_ref = bf16[1568,768]{1,0:T(8,128)(2,1)} custom-call(bf16[1568,768]{1,0:T(8,128)(2,1)} %get-tuple-element.264.part_ref), custom_call_target="tpu_custom_call" | custom-call | flops 36800000000 | bytes 115200000 | tf_op jit(solution)/shard_map/tensor_sum/pallas_call | solution.py:175
  840.0 28.1 %attention_backward.5 = (bf16[1536,768]{1,0:T(8,128)(2,1)}, f32[1536,768]{1,0:T(8,128)}, f32[1,768]{1,0:T(1,128)}, f32[8,768]{1,0:T(8,128)}, bf16[3,1536,1152]{2...) custom-call(s32[4]{0:T(128)} %pad_add_fusion.5.meta, ...), custom_call_target="tpu_custom_call", output_to_operand_aliasing={{4}: (18, {}), {5}: (19, {})} | custom-call | flops 42550001664 | bytes 133200000 | tf_op jit(solution)/shard_map/attention_backward/pallas_call | solution.py:1323
  868.1 14.1 %token_grads.1 = (bf16[768,1152]{1,0:T(8,128)(2,1)}, bf16[768,384]{1,0:T(8,128)(2,1)}) custom-call(bf16[3,1536,768]{2,1,0:T(8,128)(2,1)} %get-tuple-element.270.refs_0_, bf16[3,1536,768]{2,1,0:T(8,128)(2,1)} %get-tuple-element.271.refs_1_, bf16[3,1536,1152]{2,1,0:T(8,128)(2,1)} %get-tuple-element.272.refs_2_, ...), custom_call_target="tpu_custom_call" | custom-call | flops 16099999744 | bytes 50400000 | tf_op jit(solution)/shard_map/token_grads/pallas_call | solution.py:1599
  882.2 1.1 slice.86
  883.4 1.3 slice.84
  884.7 1.3 copy.211
  886.1 0.9 copy.209
  887.3 40.3 %input_relay.5 = (f32[1536,768]{1,0:T(8,128)}, bf16[1536,768]{1,0:T(8,128)(2,1)}, f32[1,768]{1,0:T(1,128)}) custom-call(bf16[1536,768]{1,0:T(8,128)(2,1)} %get-tuple-element.267.part_ref, bf16[3,1536,768]{2,1,0:T(8,128)(2,1)} %get-tuple-element.205.x_ref.layers_ref, f32[1536,768]{1,0:T(8,128)} %get-tuple-element.268.grad_state_ref, ...), custom_call_target="tpu_custom_call" | custom-call | flops 48299999232 | bytes 151200000 | tf_op jit(solution)/shard_map/input_relay/pallas_call | solution.py:468
  927.7 0.7 fusion.8
  928.5 1.1 pad_maximum_fusion.2
  929.6 36.5 %output_relay.5 = (bf16[1536,768]{1,0:T(8,128)(2,1)}, bf16[1536,768]{1,0:T(8,128)(2,1)}) custom-call(bf16[1536,768]{1,0:T(8,128)(2,1)} %get-tuple-element.210.part_ref, f32[3,1536,768]{2,1,0:T(8,128)} %get-tuple-element.211.states_ref.h_ref), custom_call_target="tpu_custom_call" | custom-call | flops 43699998720 | bytes 136800000 | tf_op jit(solution)/shard_map/output_relay/pallas_call | solution.py:334
  966.1 4.4 broadcast_select_fusion.3
  970.4 6.8 broadcast_select_fusion.1
  977.3 99.3 %reduce-scatter.9.cloned.1.call-done = bf16[1,12,192,512]{3,2,1,0:T(8,128)(2,1)} async-done(((bf16[4,12,192,512]{3,2,1,0:T(8,128)(2,1)}), bf16[1,12,192,512]{3,2,1,0:T(8,128)(2,1)}) %reduce-scatter.9.cloned.1.call-update) | async-done | bytes 2359312 | tf_op jit(solution)/shard_map/reduce_scatter | solution.py:1710
  1076.6 2.5 copy.212
  1079.1 4.3 maximum_bitcast_fusion.1
  1083.5 6.9 maximum_bitcast_fusion
  1090.5 1.3 copy-done.2
  1092.3 1.3 convert.8
  1093.8 1.0 slice_bitcast_fusion.3
  1094.9 4.0 slice_bitcast_fusion
  1098.9 13.4 %reduce-scatter.11.cloned.1.call-done = bf16[1,192,784]{2,1,0:T(8,128)(2,1)} async-done(((bf16[4,192,784]{2,1,0:T(8,128)(2,1)}), bf16[1,192,784]{2,1,0:T(8,128)(2,1)}) %reduce-scatter.11.cloned.1.call-update) | async-done | bytes 301072 | tf_op jit(solution)/shard_map/reduce_scatter | solution.py:1710
  1112.3 1.0 bitcast_convert_fusion
  1113.4 0.8 slice_reduce_fusion
  1114.2 0.9 slice_bitcast_fusion.4
  1115.2 0.7 copy.217
  1115.8 0.8 copy.216
  (96 shorter events, 10.4 us)
Async XLA Ops:
  7.2 8.5 copy-start.5
  7.2 48.0 %all-gather.9.cloned.1.call-start = ((), (), s32[]{:S(2)}) async-start(), calls=%async_computation.10 | async-start | bytes 1474560 | tf_op jit(solution)/shard_map/all_gather | solution.py:1687
  7.9 63.0 %all-gather.7.cloned.1.call-start = ((), (), s32[]{:S(2)}) async-start(), calls=%async_computation.9 | async-start | bytes 2949120 | tf_op jit(solution)/shard_map/all_gather | solution.py:1775
  8.0 8.5 copy-start.6
  21.5 22.6 %copy-start.13 = (bf16[1,768]{1,0:T(2,128)(2,1)S(1)}, bf16[1,768]{1,0:T(2,128)(2,1)}, u32[]{:S(2)}) copy-start(bf16[1,768]{1,0:T(2,128)(2,1)} %param.27) | copy-start | bytes 4612
  21.5 23.9 %copy-start.12 = (s32[1,3072,2]{1,2,0:T(2,128)S(1)}, s32[1,3072,2]{1,2,0:T(2,128)}, u32[]{:S(2)}) copy-start(s32[1,3072,2]{1,2,0:T(2,128)} %param.21) | copy-start | bytes 73732
  21.5 24.5 %copy-start.4 = (bf16[1,192,768]{2,1,0:T(8,128)(2,1)S(1)}, bf16[1,192,768]{2,1,0:T(8,128)(2,1)}, u32[]{:S(2)}) copy-start(bf16[1,192,768]{2,1,0:T(8,128)(2,1)} %param.26) | copy-start | bytes 884740
  44.0 346.8 %all-gather.11.cloned.1.call-start = ((), (), s32[]{:S(2)}) async-start(), calls=%async_computation.11 | async-start | bytes 2949120 | tf_op jit(solution)/shard_map/all_gather | solution.py:1784
  45.4 0.7 copy-start.8
  50.2 3.1 copy-start.7
  319.6 129.7 %all-reduce.5.cloned.1.call-start = ((), (), s32[]{:S(2)}) async-start(), calls=%async_computation.4 | async-start | bytes 4816896 | tf_op jit(solution)/shard_map/psum | solution.py:1787
  390.8 586.5 %reduce-scatter.5.cloned.1.call-start = ((), (), s32[]{:S(2)}) async-start(), calls=%async_computation.5 | async-start | bytes 5898240 | tf_op jit(solution)/shard_map/reduce_scatter | solution.py:1710
  699.8 277.4 %reduce-scatter.7.cloned.1.call-start = ((), (), s32[]{:S(2)}) async-start(), calls=%async_computation.6 | async-start | bytes 8847360 | tf_op jit(solution)/shard_map/reduce_scatter | solution.py:1710
  776.0 300.6 %reduce-scatter.9.cloned.1.call-start = ((), (), s32[]{:S(2)}) async-start(), calls=%async_computation.7 | async-start | bytes 11796480 | tf_op jit(solution)/shard_map/reduce_scatter | solution.py:1710
  807.9 304.5 %reduce-scatter.11.cloned.1.call-start = ((), (), s32[]{:S(2)}) async-start(), calls=%async_computation.8 | async-start | bytes 1720320 | tf_op jit(solution)/shard_map/reduce_scatter | solution.py:1710
  887.2 40.4 %copy-start.9 = (f32[8,768]{1,0:T(8,128)S(1)}, f32[8,768]{1,0:T(8,128)}, u32[]{:S(2)}) copy-start(f32[8,768]{1,0:T(8,128)} %get-tuple-element.277) | copy-start | bytes 73732
  887.2 40.4 %copy-start.10 = (f32[8,768]{1,0:T(8,128)S(1)}, f32[8,768]{1,0:T(8,128)}, u32[]{:S(2)}) copy-start(f32[8,768]{1,0:T(8,128)} %get-tuple-element.280) | copy-start | bytes 73732
  887.2 40.4 %copy-start.11 = (f32[8,768]{1,0:T(8,128)S(1)}, f32[8,768]{1,0:T(8,128)}, u32[]{:S(2)}) copy-start(f32[8,768]{1,0:T(8,128)} %get-tuple-element.283) | copy-start | bytes 73732
  887.3 40.4 %copy-start.14 = (f32[1,768]{1,0:T(1,128)S(1)}, f32[1,768]{1,0:T(1,128)}, u32[]{:S(2)}) copy-start(f32[1,768]{1,0:T(1,128)} %get-tuple-element.276) | copy-start | bytes 9220
  887.3 40.4 %copy-start.15 = (f32[1,768]{1,0:T(1,128)S(1)}, f32[1,768]{1,0:T(1,128)}, u32[]{:S(2)}) copy-start(f32[1,768]{1,0:T(1,128)} %get-tuple-element.275) | copy-start | bytes 9220
  887.3 40.4 %copy-start.16 = (f32[1,768]{1,0:T(1,128)S(1)}, f32[1,768]{1,0:T(1,128)}, u32[]{:S(2)}) copy-start(f32[1,768]{1,0:T(1,128)} %get-tuple-element.279) | copy-start | bytes 9220
  887.3 40.4 %copy-start.17 = (f32[1,768]{1,0:T(1,128)S(1)}, f32[1,768]{1,0:T(1,128)}, u32[]{:S(2)}) copy-start(f32[1,768]{1,0:T(1,128)} %get-tuple-element.278) | copy-start | bytes 9220
  887.3 40.4 %copy-start.18 = (f32[1,768]{1,0:T(1,128)S(1)}, f32[1,768]{1,0:T(1,128)}, u32[]{:S(2)}) copy-start(f32[1,768]{1,0:T(1,128)} %get-tuple-element.282) | copy-start | bytes 9220
  966.1 4.4 copy-start
  1079.1 4.3 slice-start
  1079.1 4.3 slice-start.1
  1083.4 6.9 copy-start.1
  1083.4 7.1 copy-start.3
  1090.3 1.5 copy-start.2
Sparse Core Ops, SparseCore 0:
  9.6 20.1 all-gather.8
  44.1 26.7 all-gather.6
  319.7 25.8 all-gather.10
  390.9 58.3 all-reduce.4
  700.0 85.3 reduce-scatter.4
  787.7 124.0 reduce-scatter.6
  914.8 161.7 reduce-scatter.8
  1079.2 33.0 reduce-scatter.10

commit v5 on v4

--- a/solution.py
+++ b/solution.py
@@ -328,7 +328,7 @@
         copy.wait()
 
 
-def output_relay(part, states, tick, identity, pieces=12):
+def output_relay(part, states, tick, identity, pieces=16):
     rows, width = part.shape
     hbm = pl.BlockSpec(memory_space=pl.ANY)
     return pl.pallas_call(
@@ -461,7 +461,7 @@
         copy.wait()
 
 
-def input_relay(part, layers, grad_state, gain, tick, identity, pieces=12):
+def input_relay(part, layers, grad_state, gain, tick, identity, pieces=16):
     rows, width = part.shape
     hbm = pl.BlockSpec(memory_space=pl.ANY)
     whole = pl.BlockSpec(memory_space=pltpu.VMEM)
@@ -705,15 +705,59 @@
             gates[rows, :] = jnp.broadcast_to(chosen, (CHUNK, LANES))
 
 
-def build_put(first, rows, pos_ref, put):
+WINDOW_SLOTS = 256
+
+
+def is_narrow(starts, sequence):
+    return starts[starts.shape[0] - SLOTS + 1 + sequence] > 0
+
+
+def window_at(starts, sequence, expert, chunk):
+    place = starts[(sequence * EXPERTS + expert) * (ROW_STEPS + 1) + chunk]
+    return jnp.minimum(place // 16 * 16, SPAN - WINDOW_SLOTS)
+
+
+def chunk_rows(chunk):
+    return pl.ds(chunk * ROWS, ROWS)
+
+
+def token_places(expert, rows, pos_ref):
     places = pos_ref[0, rows, :]
     lane = lax.broadcasted_iota(jnp.int32, places.shape, 1)
-    slot_at = lax.broadcasted_iota(jnp.int32, (places.shape[0], SPAN), 1)
+    return jnp.sum(jnp.where(lane == expert, places, 0), axis=1, keepdims=True)
+
+
+def build_put(starts, sequence, pair, chunk, pos_ref, put):
+    rows = chunk_rows(chunk)
+    slot_at = lax.broadcasted_iota(jnp.int32, (ROWS, WINDOW_SLOTS), 1)
     for which in range(PAIR):
-        place = jnp.sum(jnp.where(lane == first + which, places, 0), axis=1, keepdims=True)
-        put[rows, which * SPAN : (which + 1) * SPAN] = jnp.where(
-            slot_at == place, 1.0, 0.0
+        expert = pair * PAIR + which
+        begin = jnp.where(
+            is_narrow(starts, sequence), window_at(starts, sequence, expert, chunk), -SEQ_LEN
+        )
+        put[rows, which * WINDOW_SLOTS : (which + 1) * WINDOW_SLOTS] = jnp.where(
+            slot_at == token_places(expert, rows, pos_ref) - begin, 1.0, 0.0
         ).astype(BF16)
+
+
+def put_back(starts, sequence, pair, chunk, put, slots, window):
+    for which in range(PAIR):
+        begin = window_at(starts, sequence, pair * PAIR + which, chunk)
+        there = pl.ds(pl.multiple_of(which * SPAN + begin, 16), WINDOW_SLOTS)
+        window[which * WINDOW_SLOTS : (which + 1) * WINDOW_SLOTS, :] = slots[there, :]
+    return dot(put[chunk_rows(chunk), : PAIR * WINDOW_SLOTS], window[...])
+
+
+def put_back_wide(pair, pos_ref, put, slots, total):
+    def body(step):
+        which, chunk = step // ROW_STEPS, step % ROW_STEPS
+        rows = rows_of(chunk, ROWS)
+        slot_at = lax.broadcasted_iota(jnp.int32, (ROWS, SPAN), 1)
+        place = token_places(pair * PAIR + which, rows, pos_ref)
+        put[rows, SPAN:] = jnp.where(slot_at == place, 1.0, 0.0).astype(BF16)
+        total[rows, :] += dot(put[rows, SPAN:], slots[rows_of(which, SPAN), :])
+
+    loop(PAIR * ROW_STEPS, body)
 
 
 ALL_CHUNKS = [(which, step) for which in range(PAIR) for step in range(CAPACITY // CHUNK)]
@@ -726,6 +770,7 @@
 def feed_forward_kernel(
     stored,
     meta,
+    starts,
     x_ref,
     ag_ref,
     wo_ref,
@@ -743,7 +788,7 @@
 ):
     rest = rest[stored:]
     part_ref, h_ref, b_ref, xe_ref, g_ref, u_ref, gs_ref, us_ref, probs_ref = rest[:9]
-    total, normed, probs, pick, put, gates, scaled = rest[9:]
+    total, normed, probs, pick, put, gates, scaled, window = rest[9:]
     step = pl.program_id(0)
     pair = jnp.maximum(step - ROW_STEPS, 0)
 
@@ -789,13 +834,28 @@
     def _():
         build_pick(0, ALL_CHUNKS, post_ref, None, pick, gates)
         scaled[...] = jnp.zeros_like(scaled)
-
-    def experts(combine):
-        for start in range(0, SEQ_LEN, ROWS):
-            rows = pl.ds(start, ROWS)
-            if combine:
-                total[rows, :] += dot(put[rows, :], scaled[...])
-            build_put(pair * PAIR, rows, pos_ref, put)
+        put[:, : PAIR * WINDOW_SLOTS] = jnp.zeros((SEQ_LEN, PAIR * WINDOW_SLOTS), BF16)
+
+    before = jnp.maximum(pair - 1, 0)
+
+    @pl.when((step > ROW_STEPS) & jnp.logical_not(is_narrow(starts, meta[2])))
+    def _():
+        put_back_wide(before, pos_ref, put, scaled, total)
+
+    @pl.when(step == ROW_STEPS + PAIR_STEPS)
+    def _():
+        for chunk in range(ROW_STEPS):
+            rows = chunk_rows(chunk)
+            values = put_back(starts, meta[2], before, chunk, put, scaled, window)
+            part_ref[rows, :] = (total[rows, :] + values).astype(BF16)
+
+    @pl.when((step >= ROW_STEPS) & (step < ROW_STEPS + PAIR_STEPS))
+    def _():
+        for chunk in range(ROW_STEPS):
+            total[chunk_rows(chunk), :] += put_back(
+                starts, meta[2], before, chunk, put, scaled, window
+            )
+            build_put(starts, meta[2], pair, chunk, pos_ref, put)
         picked = dot(pick[...], normed[...]).astype(BF16)
         build_gates(pair * PAIR, post_ref, probs, gates)
         build_pick(
@@ -811,20 +871,6 @@
                 dot(hidden, wd_ref[which]) * gates[of_pair(which), 0:1]
             ).astype(BF16)
 
-    @pl.when(step == ROW_STEPS)
-    def _():
-        experts(False)
-
-    @pl.when((step > ROW_STEPS) & (step < ROW_STEPS + PAIR_STEPS))
-    def _():
-        experts(True)
-
-    @pl.when(step == ROW_STEPS + PAIR_STEPS)
-    def _():
-        for start in range(0, SEQ_LEN, ROWS):
-            rows = pl.ds(start, ROWS)
-            part_ref[rows, :] = (total[rows, :] + dot(put[rows, :], scaled[...])).astype(BF16)
-
 
 def step_specs():
     def row_at(step):
@@ -837,7 +883,7 @@
 
 
 def feed_forward(
-    meta, layer_in, gathered, out_weight, gain, router, post, pos, weights, kept
+    meta, starts, layer_in, gathered, out_weight, gain, router, post, pos, weights, kept
 ):
     width = layer_in.shape[2]
     wg, wu, wd, wgs, wus, wds = weights
@@ -856,28 +902,28 @@
     row_at, pair_at = step_specs()
 
     def slot_rows(columns):
-        return pl.BlockSpec((1, ROWS, columns), lambda s, m: (m[1], row_at(s), 0))
+        return pl.BlockSpec((1, ROWS, columns), lambda s, m, f: (m[1], row_at(s), 0))
 
     def slot_pair(columns):
-        return pl.BlockSpec((1, PAIR, CAPACITY, columns), lambda s, m: (m[1], pair_at(s), 0, 0))
+        return pl.BlockSpec((1, PAIR, CAPACITY, columns), lambda s, m, f: (m[1], pair_at(s), 0, 0))
 
     def fixed(shape):
-        return once(shape, lambda s, m: (0,) * len(shape))
+        return once(shape, lambda s, m, f: (0,) * len(shape))
 
     def of_pairs(array):
-        return pl.BlockSpec((PAIR,) + array.shape[1:], lambda s, m: (pair_at(s), 0, 0))
+        return pl.BlockSpec((PAIR,) + array.shape[1:], lambda s, m, f: (pair_at(s), 0, 0))
 
     grid_spec = pltpu.PrefetchScalarGridSpec(
-        num_scalar_prefetch=1,
+        num_scalar_prefetch=2,
         grid=(ROW_STEPS + PAIR_STEPS + 1,),
         in_specs=[
             slot_rows(width),
-            pl.BlockSpec((4, ROWS // 2, gathered.shape[2]), lambda s, m: (0, row_at(s), 0)),
+            pl.BlockSpec((4, ROWS // 2, gathered.shape[2]), lambda s, m, f: (0, row_at(s), 0)),
             fixed(out_weight.shape),
             fixed(gain.shape),
             fixed(router.shape),
-            once((1, EXPERTS, SEQ_LEN), lambda s, m: (m[2], 0, 0)),
-            once((1, SEQ_LEN, EXPERTS), lambda s, m: (m[2], 0, 0)),
+            once((1, EXPERTS, SEQ_LEN), lambda s, m, f: (m[2], 0, 0)),
+            once((1, SEQ_LEN, EXPERTS), lambda s, m, f: (m[2], 0, 0)),
             of_pairs(wg),
             of_pairs(wu),
             of_pairs(wd),
@@ -895,7 +941,7 @@
             slot_pair(hidden),
             slot_rows(hidden),
             slot_rows(hidden),
-            pl.BlockSpec((1, EXPERTS, ROWS), lambda s, m: (m[1], 0, row_at(s))),
+            pl.BlockSpec((1, EXPERTS, ROWS), lambda s, m, f: (m[1], 0, row_at(s))),
         ],
         scratch_shapes=[
             pltpu.VMEM((SEQ_LEN, width), F32),
@@ -905,18 +951,20 @@
             pltpu.VMEM((SEQ_LEN, PAIR * SPAN), BF16),
             pltpu.VMEM((PAIR * CAPACITY, LANES), F32),
             pltpu.VMEM((PAIR * SPAN, width), BF16),
+            pltpu.VMEM((PAIR * WINDOW_SLOTS, width), BF16),
         ],
     )
     outs = pl.pallas_call(
         functools.partial(feed_forward_kernel, stored),
         grid_spec=grid_spec,
         out_shape=[shape_of((SEQ_LEN, width), BF16)] + saved,
-        input_output_aliases={14 + k: 1 + k for k in range(stored)},
+        input_output_aliases={15 + k: 1 + k for k in range(stored)},
         compiler_params=pltpu.CompilerParams(vmem_limit_bytes=VMEM_BYTES),
         cost_estimate=cost(56),
         name="feed_forward",
     )(
         meta,
+        starts,
         layer_in,
         gathered,
         out_weight,
@@ -951,6 +999,7 @@
 def feed_backward_kernel(
     stored,
     meta,
+    starts,
     cot_ref,
     rec_ref,
     post_ref,
@@ -970,7 +1019,7 @@
 ):
     rest = rest[stored:]
     part_ref, dy_ref, hid_ref, dg_ref, du_ref, de_ref, hids_ref, dgs_ref, dus_ref = rest[:9]
-    total, given, pick, put, gates, slots, choice = rest[9:]
+    total, given, pick, put, gates, slots, choice, window = rest[9:]
     step = pl.program_id(0)
     pair = jnp.maximum(step - ROW_STEPS, 0)
 
@@ -993,13 +1042,28 @@
     def _():
         build_pick(0, ALL_CHUNKS, post_ref, None, pick, gates)
         slots[...] = jnp.zeros_like(slots)
-
-    def experts(combine):
-        for start in range(0, SEQ_LEN, ROWS):
-            rows = pl.ds(start, ROWS)
-            if combine:
-                total[rows, :] += dot(put[rows, :], slots[...])
-            build_put(pair * PAIR, rows, pos_ref, put)
+        put[:, : PAIR * WINDOW_SLOTS] = jnp.zeros((SEQ_LEN, PAIR * WINDOW_SLOTS), BF16)
+
+    before = jnp.maximum(pair - 1, 0)
+
+    @pl.when((step > ROW_STEPS) & jnp.logical_not(is_narrow(starts, meta[2])))
+    def _():
+        put_back_wide(before, pos_ref, put, slots, total)
+
+    @pl.when(step == ROW_STEPS + PAIR_STEPS)
+    def _():
+        for chunk in range(ROW_STEPS):
+            rows = chunk_rows(chunk)
+            values = put_back(starts, meta[2], before, chunk, put, slots, window)
+            part_ref[rows, :] = (total[rows, :] + values).astype(BF16)
+
+    @pl.when((step >= ROW_STEPS) & (step < ROW_STEPS + PAIR_STEPS))
+    def _():
+        for chunk in range(ROW_STEPS):
+            total[chunk_rows(chunk), :] += put_back(
+                starts, meta[2], before, chunk, put, slots, window
+            )
+            build_put(starts, meta[2], pair, chunk, pos_ref, put)
         picked = dot(pick[...], given[...]).astype(BF16)
         build_gates(pair * PAIR, post_ref, probs_ref.at[0], gates)
         build_pick(
@@ -1030,19 +1094,8 @@
                 dot_nt(grad_gate, wg_ref[which]) + dot_nt(grad_lift, wu_ref[which])
             ).astype(BF16)
 
-    @pl.when(step == ROW_STEPS)
-    def _():
-        experts(False)
-
-    @pl.when((step > ROW_STEPS) & (step < ROW_STEPS + PAIR_STEPS))
-    def _():
-        experts(True)
-
     @pl.when(step == ROW_STEPS + PAIR_STEPS)
     def _():
-        for start in range(0, SEQ_LEN, ROWS):
-            rows = pl.ds(start, ROWS)
-            part_ref[rows, :] = (total[rows, :] + dot(put[rows, :], slots[...])).astype(BF16)
         half = SEQ_LEN // 2
         blank = jnp.zeros((8, half), F32)
         part_ref[SEQ_LEN:, :] = jnp.concatenate(
@@ -1050,7 +1103,7 @@
         ).astype(BF16)
 
 
-def feed_backward(meta, cotangent, received, post, pos, forward_kept, weights, kept):
+def feed_backward(meta, starts, cotangent, received, post, pos, forward_kept, weights, kept):
     width = cotangent.shape[1]
     wg, wu, wd, wgs, wus, wds = weights
     hidden = wg.shape[2]
@@ -1069,32 +1122,32 @@
     row_at, pair_at = step_specs()
 
     def slot_rows(columns, which):
-        return pl.BlockSpec((1, ROWS, columns), lambda s, m: (m[which], row_at(s), 0))
+        return pl.BlockSpec((1, ROWS, columns), lambda s, m, f: (m[which], row_at(s), 0))
 
     def slot_pair(columns, which):
         return pl.BlockSpec(
-            (1, PAIR, CAPACITY, columns), lambda s, m: (m[which], pair_at(s), 0, 0)
+            (1, PAIR, CAPACITY, columns), lambda s, m, f: (m[which], pair_at(s), 0, 0)
         )
 
     def fixed(shape):
-        return once(shape, lambda s, m: (0,) * len(shape))
+        return once(shape, lambda s, m, f: (0,) * len(shape))
 
     def of_pairs(array):
-        return pl.BlockSpec((PAIR,) + array.shape[1:], lambda s, m: (pair_at(s), 0, 0))
+        return pl.BlockSpec((PAIR,) + array.shape[1:], lambda s, m, f: (pair_at(s), 0, 0))
 
     grid_spec = pltpu.PrefetchScalarGridSpec(
-        num_scalar_prefetch=1,
+        num_scalar_prefetch=2,
         grid=(ROW_STEPS + PAIR_STEPS + 1,),
         in_specs=[
-            pl.BlockSpec((ROWS, width), lambda s, m: (m[2] * ROW_STEPS + row_at(s), 0)),
-            pl.BlockSpec((ROWS, width), lambda s, m: (row_at(s), 0)),
-            once((1, EXPERTS, SEQ_LEN), lambda s, m: (m[2], 0, 0)),
-            once((1, SEQ_LEN, EXPERTS), lambda s, m: (m[2], 0, 0)),
+            pl.BlockSpec((ROWS, width), lambda s, m, f: (m[2] * ROW_STEPS + row_at(s), 0)),
+            pl.BlockSpec((ROWS, width), lambda s, m, f: (row_at(s), 0)),
+            once((1, EXPERTS, SEQ_LEN), lambda s, m, f: (m[2], 0, 0)),
+            once((1, SEQ_LEN, EXPERTS), lambda s, m, f: (m[2], 0, 0)),
             slot_pair(hidden, 3),
             slot_pair(hidden, 3),
             slot_rows(hidden, 3),
             slot_rows(hidden, 3),
-            once((1, EXPERTS, SEQ_LEN), lambda s, m: (m[3], 0, 0)),
+            once((1, EXPERTS, SEQ_LEN), lambda s, m, f: (m[3], 0, 0)),
             of_pairs(wg),
             of_pairs(wu),
             of_pairs(wd),
@@ -1122,18 +1175,20 @@
             pltpu.VMEM((PAIR * CAPACITY, LANES), F32),
             pltpu.VMEM((PAIR * SPAN, width), BF16),
             pltpu.VMEM((EXPERTS, SEQ_LEN), F32),
+            pltpu.VMEM((PAIR * WINDOW_SLOTS, width), BF16),
         ],
     )
     outs = pl.pallas_call(
         functools.partial(feed_backward_kernel, stored),
         grid_spec=grid_spec,
         out_shape=[shape_of((SEQ_LEN + 32, width), BF16)] + saved,
-        input_output_aliases={16 + k: 1 + k for k in range(stored)},
+        input_output_aliases={17 + k: 1 + k for k in range(stored)},
         compiler_params=pltpu.CompilerParams(vmem_limit_bytes=VMEM_BYTES),
         cost_estimate=cost(60),
         name="feed_backward",
     )(
         meta,
+        starts,
         cotangent,
         received,
         post,
@@ -1648,7 +1703,13 @@
     ).astype(BF16)
     rank = jnp.einsum("ts,nse->nte", before, named.astype(BF16), preferred_element_type=F32)
     by_token = jnp.where(named, rank.astype(jnp.int32), -1)
-    return by_token, jnp.swapaxes(by_token, 1, 2)
+    counts = jnp.sum(named.reshape(-1, ROW_STEPS, ROWS, EXPERTS).astype(jnp.int32), axis=2)
+    before = jnp.cumsum(jnp.pad(counts, ((0, 0), (1, 0), (0, 0))), axis=1)
+    starts = jnp.swapaxes(before, 1, 2)
+    held = starts[:, :, 1:] <= starts[:, :, :-1] // 16 * 16 + WINDOW_SLOTS
+    narrow = jnp.all(held, axis=(1, 2)).astype(jnp.int32)
+    starts = jnp.concatenate([starts.reshape(-1), narrow])
+    return by_token, jnp.swapaxes(by_token, 1, 2), starts
 
 
 def first_allowed(lengths):
@@ -1695,7 +1756,7 @@
         w_up_sh[0],
         w_down_sh[0],
     )
-    pos, post = places(routes[0].reshape(count, SEQ_LEN, 2))
+    pos, post, starts = places(routes[0].reshape(count, SEQ_LEN, 2))
     low = first_allowed(doc_lengths)
     first_block = (low[:, ::BLOCK] // KEYS).reshape(-1)
     back_first = (low[:, ::BACK_BLOCK] // BACK_KEYS).reshape(-1)
@@ -1735,6 +1796,7 @@
     def feed(meta, gathered, kept):
         return feed_forward(
             meta,
+            starts,
             attention_kept[0],
             gathered,
             out_weight,
@@ -1748,7 +1810,7 @@
 
     def feed_back(meta, received):
         return feed_backward(
-            meta, cotangent, received, post, pos, feed_kept, feed_weights, grads_kept
+            meta, starts, cotangent, received, post, pos, feed_kept, feed_weights, grads_kept
         )
 
     def attend_back(meta, summed):

time: 1130 us -> 1110 us (0.982)
  Pallas kernels: 907 us -> 883 us
    pallas_call x3, Pallas kernels: 189 us -> 163 us  [feed_backward(): pl.pallas_call(functools.partial(feed_backward_kernel, stored), grid_spec...]
  transfers between devices with their start and end apart: 8 -> 8, of which waited for: 4 -> 4; matrix products, arithmetic and copies ran while one was open for 5% -> 6% of each run, Pallas kernels for 36% -> 35%
where the time goes in v5:
time: 1110 us
  Pallas kernels  883 us (80%)
  waiting for transfers between devices  137 us (12%)
  other arithmetic  44.1 us (4%)
  local copies, waits for them, and re-layouts  24.6 us (2%)
  between operations  15.2 us (1%)
    pallas_call x3, Pallas kernels, feed_forward(): pl.pallas_call(functools.partial(feed_forward_kernel, stored), grid_spec=...  169 us
    pallas_call x3, Pallas kernels, feed_backward(): pl.pallas_call(functools.partial(feed_backward_kernel, stored), grid_spec...  163 us
    pallas_call x3, Pallas kernels, input_relay(): pl.pallas_call(functools.partial(input_kernel, pieces, tick), out_shape=[...  120 us
    reduce_scatter x4, waiting for transfers between devices, spread(): return lax.psum_scatter(array, 'dp', scatter_dimension=0, tiled=False)  118 us
    pallas_call x3, Pallas kernels, output_relay(): pl.pallas_call(functools.partial(output_kernel, pieces, tick), out_shape=...  112 us
    pallas_call x3, Pallas kernels, attention_backward(): pl.pallas_call(functools.partial(attention_backward_kernel, stored), grid...  88.2 us
    pallas_call x3, Pallas kernels, attention_forward(): pl.pallas_call(functools.partial(attention_forward_kernel, stored), grid_...  65.5 us
    pallas_call x2, Pallas kernels, tensor_sum(): pl.pallas_call(functools.partial(sum_kernel, pieces), out_shape=shape_of(...  64.1 us
  transfers between devices with their start and end apart: 8, of which 4 were waited for; matrix products, arithmetic and copies ran while one was open for 6% of the time, Pallas kernels for 35%

profile of v5, /device:TPU:0, one launch (start us, length us, event | category | flops | bytes accessed | tf_op | source)
XLA Modules:
  0.0 1106.5 jit_solution(5423722721833052071)
XLA Ops:
  7.2 0.7 all-gather.9.cloned.1.call-update
  8.0 0.9 reduce_window_sum.23
  8.9 1.3 convert_element_type.49.gain_ref
  11.0 1.0 slice_negate_fusion.1
  12.0 1.0 pad_maximum_fusion.3
  13.3 1.0 slice_negate_fusion
  14.3 1.0 pad_maximum_fusion.4
  16.5 1.5 broadcast_maximum_fusion.low_ref
  18.0 1.4 pad_maximum_fusion.1.wall_ref
  20.0 1.6 broadcast_10_rec_ref.2.rec_ref
  21.5 20.8 %attention_forward.3 = (bf16[768,384]{1,0:T(8,128)(2,1)}, bf16[3,1536,768]{2,1,0:T(8,128)(2,1)}, bf16[3,1536,768]{2,1,0:T(8,128)(2,1)}, bf16[3,1536,1152]{2,1,0:...) custom-call(s32[3]{0:T(128)} %get-tuple-element.388.meta, s32[6]{0:T(128)} %reshape.145.first_block, ...), custom_call_target="tpu_custom_call" | custom-call | flops 27599998976 | bytes 86400000 | tf_op jit(solution)/shard_map/attention_forward/pallas_call | solution.py:643
  45.6 0.9 concatenate.45
  46.5 2.2 bitcast_select_fusion.1
  48.7 1.1 copy.232.post_ref
  54.0 1.3 bitcast_select_fusion.pos_ref
  55.4 15.6 %all-gather.7.cloned.1.call-done = bf16[3072,384]{1,0:T(8,128)(2,1)} async-done(((bf16[768,384]{1,0:T(8,128)(2,1)}), bf16[3072,384]{1,0:T(8,128)(2,1)}) %all-gather.7.cloned.1.call-update) | async-done | bytes 2359312 | tf_op jit(solution)/shard_map/all_gather | solution.py:1837
  70.9 64.1 %feed_forward.3 = (bf16[1536,768]{1,0:T(8,128)(2,1)}, f32[3,1536,768]{2,1,0:T(8,128)}, bf16[3,1536,768]{2,1,0:T(8,128)(2,1)}, bf16[3,8,480,768]{3,2,1,0:T(8,128)...) custom-call(s32[3]{0:T(128)} %get-tuple-element.388.meta, ...), custom_call_target="tpu_custom_call", output_to_operand_aliasing={{1}: (15, {}), {2}: (16, {}), {3}: (17, {}), {4}: (18, {}),... | custom-call | flops 64399998976 | bytes 201600000 | tf_op jit(solution)/shard_map/feed_forward/pallas_call | solution.py:957
  135.0 36.9 %output_relay.3 = (bf16[1536,768]{1,0:T(8,128)(2,1)}, bf16[1536,768]{1,0:T(8,128)(2,1)}) custom-call(bf16[1536,768]{1,0:T(8,128)(2,1)} %get-tuple-element.163.part_ref, f32[3,1536,768]{2,1,0:T(8,128)} %get-tuple-element.164.states_ref.rest_0_), custom_call_target="tpu_custom_call" | custom-call | flops 43699998720 | bytes 136800000 | tf_op jit(solution)/shard_map/output_relay/pallas_call | solution.py:334
  171.9 22.3 %attention_forward.4 = (bf16[768,384]{1,0:T(8,128)(2,1)}, bf16[3,1536,768]{2,1,0:T(8,128)(2,1)}, bf16[3,1536,768]{2,1,0:T(8,128)(2,1)}, bf16[3,1536,1152]{2,1,0:...) custom-call(s32[3]{0:T(128)} %get-tuple-element.389.meta, ...), custom_call_target="tpu_custom_call", output_to_operand_aliasing={{1}: (9, {}), {2}: (10, {}), {3}: (11, {}), {4}: (12, {}), ... | custom-call | flops 27599998976 | bytes 86400000 | tf_op jit(solution)/shard_map/attention_forward/pallas_call | solution.py:643
  194.3 20.1 %tensor_gather.1.ag_ref = bf16[4,768,384]{2,1,0:T(8,128)(2,1)} custom-call(bf16[768,384]{1,0:T(8,128)(2,1)} %get-tuple-element.172.own_ref), custom_call_target="tpu_custom_call" | custom-call | flops 20700000256 | bytes 64800000 | tf_op jit(solution)/shard_map/tensor_gather/pallas_call | solution.py:235
  214.4 52.5 %feed_forward.4 = (bf16[1536,768]{1,0:T(8,128)(2,1)}, f32[3,1536,768]{2,1,0:T(8,128)}, bf16[3,1536,768]{2,1,0:T(8,128)(2,1)}, bf16[3,8,480,768]{3,2,1,0:T(8,128)...) custom-call(s32[3]{0:T(128)} %get-tuple-element.389.meta, ...), custom_call_target="tpu_custom_call", output_to_operand_aliasing={{1}: (15, {}), {2}: (16, {}), {3}: (17, {}), {4}: (18, {}),... | custom-call | flops 64399998976 | bytes 201600000 | tf_op jit(solution)/shard_map/feed_forward/pallas_call | solution.py:957
  266.9 36.7 %output_relay.4 = (bf16[1536,768]{1,0:T(8,128)(2,1)}, bf16[1536,768]{1,0:T(8,128)(2,1)}) custom-call(bf16[1536,768]{1,0:T(8,128)(2,1)} %get-tuple-element.180.part_ref, f32[3,1536,768]{2,1,0:T(8,128)} %get-tuple-element.181.states_ref.rest_0_), custom_call_target="tpu_custom_call" | custom-call | flops 43699998720 | bytes 136800000 | tf_op jit(solution)/shard_map/output_relay/pallas_call | solution.py:334
  303.7 22.3 %attention_forward.5 = (bf16[768,384]{1,0:T(8,128)(2,1)}, bf16[3,1536,768]{2,1,0:T(8,128)(2,1)}, bf16[3,1536,768]{2,1,0:T(8,128)(2,1)}, bf16[3,1536,1152]{2,1,0:...) custom-call(s32[3]{0:T(128)} %pad_add_fusion.4.meta, ...), custom_call_target="tpu_custom_call", output_to_operand_aliasing={{1}: (9, {}), {2}: (10, {}), {3}: (11, {}), {4}: (12, {}), ... | custom-call | flops 27599998976 | bytes 86400000 | tf_op jit(solution)/shard_map/attention_forward/pallas_call | solution.py:643
  326.0 54.3 %feed_backward.3 = (bf16[1568,768]{1,0:T(8,128)(2,1)}, bf16[3,1536,768]{2,1,0:T(8,128)(2,1)}, bf16[3,8,480,512]{3,2,1,0:T(8,128)(2,1)}, bf16[3,8,480,512]{3,2,1,...) custom-call(s32[4]{0:T(128)} %pad_add_fusion.3.meta, ...), custom_call_target="tpu_custom_call", output_to_operand_aliasing={{1}: (17, {}), {2}: (18, {}), {3}: (19, {}), {4}: (20, {}),... | custom-call | flops 69000003584 | bytes 216000000 | tf_op jit(solution)/shard_map/feed_backward/pallas_call | solution.py:1181
  380.4 52.6 %feed_forward.5 = (bf16[1536,768]{1,0:T(8,128)(2,1)}, f32[3,1536,768]{2,1,0:T(8,128)}, bf16[3,1536,768]{2,1,0:T(8,128)(2,1)}, bf16[3,8,480,768]{3,2,1,0:T(8,128)...) custom-call(s32[3]{0:T(128)} %pad_add_fusion.4.meta, ...), custom_call_target="tpu_custom_call", output_to_operand_aliasing={{1}: (15, {}), {2}: (16, {}), {3}: (17, {}), {4}: (18, {}),... | custom-call | flops 64399998976 | bytes 201600000 | tf_op jit(solution)/shard_map/feed_forward/pallas_call | solution.py:957
  433.0 2.2 all-reduce.5.cloned.1.call-done.sum_ref.choice_ref
  435.3 28.0 %attention_backward.3 = (bf16[1536,768]{1,0:T(8,128)(2,1)}, f32[1536,768]{1,0:T(8,128)}, f32[1,768]{1,0:T(1,128)}, f32[8,768]{1,0:T(8,128)}, bf16[3,1536,1152]{2...) custom-call(s32[4]{0:T(128)} %pad_add_fusion.3.meta, s32[8]{0:T(128)} %reshape.149.first_block, ...), custom_call_target="tpu_custom_call" | custom-call | flops 42550001664 | bytes 133200000 | tf_op jit(solution)/shard_map/attention_backward/pallas_call | solution.py:1378
  463.3 39.1 %input_relay.3 = (f32[1536,768]{1,0:T(8,128)}, bf16[1536,768]{1,0:T(8,128)(2,1)}, f32[1,768]{1,0:T(1,128)}) custom-call(bf16[1536,768]{1,0:T(8,128)(2,1)} %get-tuple-element.221.part_ref, bf16[3,1536,768]{2,1,0:T(8,128)(2,1)} %get-tuple-element.205.x_ref.layers_ref, f32[1536,768]{1,0:T(8,128)} %get-tuple-element.222.grad_state_ref, ...), custom_call_target="tpu_custom_call" | custom-call | flops 48299999232 | bytes 151200000 | tf_op jit(solution)/shard_map/input_relay/pallas_call | solution.py:468
  502.3 54.5 %feed_backward.4 = (bf16[1568,768]{1,0:T(8,128)(2,1)}, bf16[3,1536,768]{2,1,0:T(8,128)(2,1)}, bf16[3,8,480,512]{3,2,1,0:T(8,128)(2,1)}, bf16[3,8,480,512]{3,2,1,...) custom-call(s32[4]{0:T(128)} %pad_add_fusion.5.meta, ...), custom_call_target="tpu_custom_call", output_to_operand_aliasing={{1}: (17, {}), {2}: (18, {}), {3}: (19, {}), {4}: (20, {}),... | custom-call | flops 69000003584 | bytes 216000000 | tf_op jit(solution)/shard_map/feed_backward/pallas_call | solution.py:1181
  556.8 32.1 %tensor_sum.2.sum_ref.choice_ref = bf16[1568,768]{1,0:T(8,128)(2,1)} custom-call(bf16[1568,768]{1,0:T(8,128)(2,1)} %get-tuple-element.235.part_ref), custom_call_target="tpu_custom_call" | custom-call | flops 36800000000 | bytes 115200000 | tf_op jit(solution)/shard_map/tensor_sum/pallas_call | solution.py:175
  588.9 27.8 %attention_backward.4 = (bf16[1536,768]{1,0:T(8,128)(2,1)}, f32[1536,768]{1,0:T(8,128)}, f32[1,768]{1,0:T(1,128)}, f32[8,768]{1,0:T(8,128)}, bf16[3,1536,1152]{2...) custom-call(s32[4]{0:T(128)} %pad_add_fusion.5.meta, ...), custom_call_target="tpu_custom_call", output_to_operand_aliasing={{4}: (18, {}), {5}: (19, {})} | custom-call | flops 42550001664 | bytes 133200000 | tf_op jit(solution)/shard_map/attention_backward/pallas_call | solution.py:1378
  616.7 43.6 %input_relay.4 = (f32[1536,768]{1,0:T(8,128)}, bf16[1536,768]{1,0:T(8,128)(2,1)}, f32[1,768]{1,0:T(1,128)}) custom-call(bf16[1536,768]{1,0:T(8,128)(2,1)} %get-tuple-element.239.part_ref, bf16[3,1536,768]{2,1,0:T(8,128)(2,1)} %get-tuple-element.205.x_ref.layers_ref, f32[1536,768]{1,0:T(8,128)} %get-tuple-element.240.grad_state_ref, ...), custom_call_target="tpu_custom_call" | custom-call | flops 48299999232 | bytes 151200000 | tf_op jit(solution)/shard_map/input_relay/pallas_call | solution.py:468
  660.3 17.2 %lead_grads.1 = bf16[4,6,192,512]{3,2,1,0:T(8,128)(2,1)} custom-call(s32[4]{0:T(128)} %pad_add_fusion.7.meta, bf16[3072,768]{1,0:T(8,128)(2,1)} %cot_ref.7, bf16[1536,768]{1,0:T(8,128)(2,1)} %get-tuple-element.243.rec_ref, s32[2,8,1536]{2,1,0:T(8,128)} %copy.232.post_ref, f32[3,8,1536]{2,1,0:T(8,128)} %get-tuple-element.215.probs_ref, ...), custom_call_target="tpu_custom_call" | custom-call | flops 23000000512 | bytes 72000000 | tf_op jit(solution)/shard_map/lead_grads/pallas_call | solution.py:1556
  677.6 54.7 %feed_backward.5 = (bf16[1568,768]{1,0:T(8,128)(2,1)}, bf16[3,1536,768]{2,1,0:T(8,128)(2,1)}, bf16[3,8,480,512]{3,2,1,0:T(8,128)(2,1)}, bf16[3,8,480,512]{3,2,1,...) custom-call(s32[4]{0:T(128)} %pad_add_fusion.6.meta, ...), custom_call_target="tpu_custom_call", output_to_operand_aliasing={{1}: (17, {}), {2}: (18, {}), {3}: (19, {}), {4}: (20, {}),... | custom-call | flops 69000003584 | bytes 216000000 | tf_op jit(solution)/shard_map/feed_backward/pallas_call | solution.py:1181
  732.3 17.5 %expert_grads.2 = bf16[4,9,192,512]{3,2,1,0:T(8,128)(2,1)} custom-call(bf16[3,8,480,768]{3,2,1,0:T(8,128)(2,1)} %get-tuple-element.262.xa_ref.xb_ref.refs_0_.refs_1_, bf16[3,8,480,768]{3,2,1,0:T(8,128)(2,1)} %get-tuple-element.262.xa_ref.xb_ref.refs_0_.refs_1_, bf16[3,8,480,512]{3,2,1,0:T(8,128)(2,1)} %get-tuple-element.263.refs_2_.refs_3_, ...), custom_call_target="tpu_custom_call" | custom-call | flops 20700000256 | bytes 64800000 | tf_op jit(solution)/shard_map/expert_grads/pallas_call | solution.py:1443
  749.9 17.4 %expert_grads.3.before_ref = bf16[4,12,192,512]{3,2,1,0:T(8,128)(2,1)} custom-call(bf16[3,8,480,768]{3,2,1,0:T(8,128)(2,1)} %get-tuple-element.262.xa_ref.xb_ref.refs_0_.refs_1_, bf16[3,8,480,768]{3,2,1,0:T(8,128)(2,1)} %get-tuple-element.262.xa_ref.xb_ref.refs_0_.refs_1_, bf16[3,8,480,512]{3,2,1,0:T(8,128)(2,1)} %get-tuple-element.263.refs_2_.refs_3_, ...), custom_call_target="tpu_custom_call" | custom-call | flops 20700000256 | bytes 64800000 | tf_op jit(solution)/shard_map/expert_grads/pallas_call | solution.py:1443
  767.3 14.4 %shared_grads.1 = bf16[4,12,192,512]{3,2,1,0:T(8,128)(2,1)} custom-call(bf16[3,1536,768]{2,1,0:T(8,128)(2,1)} %get-tuple-element.217.b_ref, bf16[3,1536,768]{2,1,0:T(8,128)(2,1)} %get-tuple-element.254.dy_ref, bf16[3,1536,512]{2,1,0:T(8,128)(2,1)} %get-tuple-element.255.gate_ref, ...), custom_call_target="tpu_custom_call", output_to_operand_aliasing={{}: (5, {})} | custom-call | flops 14949999616 | bytes 46800000 | tf_op jit(solution)/shard_map/shared_grads/pallas_call | solution.py:1611
  781.8 32.1 %tensor_sum.3.sum_ref.choice_ref = bf16[1568,768]{1,0:T(8,128)(2,1)} custom-call(bf16[1568,768]{1,0:T(8,128)(2,1)} %get-tuple-element.264.part_ref), custom_call_target="tpu_custom_call" | custom-call | flops 36800000000 | bytes 115200000 | tf_op jit(solution)/shard_map/tensor_sum/pallas_call | solution.py:175
  813.9 32.4 %attention_backward.5 = (bf16[1536,768]{1,0:T(8,128)(2,1)}, f32[1536,768]{1,0:T(8,128)}, f32[1,768]{1,0:T(1,128)}, f32[8,768]{1,0:T(8,128)}, bf16[3,1536,1152]{2...) custom-call(s32[4]{0:T(128)} %pad_add_fusion.6.meta, ...), custom_call_target="tpu_custom_call", output_to_operand_aliasing={{4}: (18, {}), {5}: (19, {})} | custom-call | flops 42550001664 | bytes 133200000 | tf_op jit(solution)/shard_map/attention_backward/pallas_call | solution.py:1378
  846.2 14.2 %token_grads.1 = (bf16[768,1152]{1,0:T(8,128)(2,1)}, bf16[768,384]{1,0:T(8,128)(2,1)}) custom-call(bf16[3,1536,768]{2,1,0:T(8,128)(2,1)} %get-tuple-element.270.refs_0_, bf16[3,1536,768]{2,1,0:T(8,128)(2,1)} %get-tuple-element.271.refs_1_, bf16[3,1536,1152]{2,1,0:T(8,128)(2,1)} %get-tuple-element.272.refs_2_, ...), custom_call_target="tpu_custom_call" | custom-call | flops 16099999744 | bytes 50400000 | tf_op jit(solution)/shard_map/token_grads/pallas_call | solution.py:1654
  860.4 1.1 slice.94
  861.5 1.3 slice.92
  862.9 1.3 copy.241
  864.2 0.9 copy.239
  865.4 37.6 %input_relay.5 = (f32[1536,768]{1,0:T(8,128)}, bf16[1536,768]{1,0:T(8,128)(2,1)}, f32[1,768]{1,0:T(1,128)}) custom-call(bf16[1536,768]{1,0:T(8,128)(2,1)} %get-tuple-element.267.part_ref, bf16[3,1536,768]{2,1,0:T(8,128)(2,1)} %get-tuple-element.205.x_ref.layers_ref, f32[1536,768]{1,0:T(8,128)} %get-tuple-element.268.grad_state_ref, ...), custom_call_target="tpu_custom_call" | custom-call | flops 48299999232 | bytes 151200000 | tf_op jit(solution)/shard_map/input_relay/pallas_call | solution.py:468
  903.2 0.7 fusion.8
  903.9 1.1 pad_maximum_fusion.2
  905.0 38.1 %output_relay.5 = (bf16[1536,768]{1,0:T(8,128)(2,1)}, bf16[1536,768]{1,0:T(8,128)(2,1)}) custom-call(bf16[1536,768]{1,0:T(8,128)(2,1)} %get-tuple-element.210.part_ref, f32[3,1536,768]{2,1,0:T(8,128)} %get-tuple-element.211.states_ref.h_ref), custom_call_target="tpu_custom_call" | custom-call | flops 43699998720 | bytes 136800000 | tf_op jit(solution)/shard_map/output_relay/pallas_call | solution.py:334
  943.1 4.3 broadcast_select_fusion.3
  947.5 6.9 broadcast_select_fusion.1
  954.3 104.9 %reduce-scatter.9.cloned.1.call-done = bf16[1,12,192,512]{3,2,1,0:T(8,128)(2,1)} async-done(((bf16[4,12,192,512]{3,2,1,0:T(8,128)(2,1)}), bf16[1,12,192,512]{3,2,1,0:T(8,128)(2,1)}) %reduce-scatter.9.cloned.1.call-update) | async-done | bytes 2359312 | tf_op jit(solution)/shard_map/reduce_scatter | solution.py:1771
  1059.2 2.5 copy.242
  1061.8 4.3 maximum_bitcast_fusion.1
  1066.1 6.9 maximum_bitcast_fusion
  1073.2 1.3 copy-done.2
  1075.0 1.3 convert.9
  1076.5 1.0 slice_bitcast_fusion.3
  1077.5 4.0 slice_bitcast_fusion
  1081.5 13.4 %reduce-scatter.11.cloned.1.call-done = bf16[1,192,784]{2,1,0:T(8,128)(2,1)} async-done(((bf16[4,192,784]{2,1,0:T(8,128)(2,1)}), bf16[1,192,784]{2,1,0:T(8,128)(2,1)}) %reduce-scatter.11.cloned.1.call-update) | async-done | bytes 301072 | tf_op jit(solution)/shard_map/reduce_scatter | solution.py:1771
  1095.0 1.0 bitcast_convert_fusion
  1096.0 0.8 slice_reduce_fusion
  1096.9 0.9 slice_bitcast_fusion.4
  1097.8 0.7 copy.247
  1098.4 0.8 copy.246
  (106 shorter events, 12.1 us)
Async XLA Ops:
  7.2 8.5 copy-start.5
  7.2 48.2 %all-gather.9.cloned.1.call-start = ((), (), s32[]{:S(2)}) async-start(), calls=%async_computation.10 | async-start | bytes 1474560 | tf_op jit(solution)/shard_map/all_gather | solution.py:1748
  7.9 63.0 %all-gather.7.cloned.1.call-start = ((), (), s32[]{:S(2)}) async-start(), calls=%async_computation.9 | async-start | bytes 2949120 | tf_op jit(solution)/shard_map/all_gather | solution.py:1837
  8.0 8.5 copy-start.7
  21.5 21.0 %copy-start.12 = (s32[1,3072,2]{1,2,0:T(2,128)S(1)}, s32[1,3072,2]{1,2,0:T(2,128)}, u32[]{:S(2)}) copy-start(s32[1,3072,2]{1,2,0:T(2,128)} %param.21) | copy-start | bytes 73732
  21.5 21.8 %copy-start.13 = (bf16[1,768]{1,0:T(2,128)(2,1)S(1)}, bf16[1,768]{1,0:T(2,128)(2,1)}, u32[]{:S(2)}) copy-start(bf16[1,768]{1,0:T(2,128)(2,1)} %param.27) | copy-start | bytes 4612
  21.5 24.1 %copy-start.4 = (bf16[1,192,768]{2,1,0:T(8,128)(2,1)S(1)}, bf16[1,192,768]{2,1,0:T(8,128)(2,1)}, u32[]{:S(2)}) copy-start(bf16[1,192,768]{2,1,0:T(8,128)(2,1)} %param.26) | copy-start | bytes 884740
  42.4 338.0 %all-gather.11.cloned.1.call-start = ((), (), s32[]{:S(2)}) async-start(), calls=%async_computation.11 | async-start | bytes 2949120 | tf_op jit(solution)/shard_map/all_gather | solution.py:1846
  42.6 3.0 copy-start.6
  49.8 0.7 copy-start.19
  49.8 3.7 copy-start.8
  326.0 109.3 %all-reduce.5.cloned.1.call-start = ((), (), s32[]{:S(2)}) async-start(), calls=%async_computation.4 | async-start | bytes 4816896 | tf_op jit(solution)/shard_map/psum | solution.py:1849
  380.4 574.0 %reduce-scatter.5.cloned.1.call-start = ((), (), s32[]{:S(2)}) async-start(), calls=%async_computation.5 | async-start | bytes 5898240 | tf_op jit(solution)/shard_map/reduce_scatter | solution.py:1771
  677.5 276.8 %reduce-scatter.7.cloned.1.call-start = ((), (), s32[]{:S(2)}) async-start(), calls=%async_computation.6 | async-start | bytes 8847360 | tf_op jit(solution)/shard_map/reduce_scatter | solution.py:1771
  749.9 309.3 %reduce-scatter.9.cloned.1.call-start = ((), (), s32[]{:S(2)}) async-start(), calls=%async_computation.7 | async-start | bytes 11796480 | tf_op jit(solution)/shard_map/reduce_scatter | solution.py:1771
  781.7 313.2 %reduce-scatter.11.cloned.1.call-start = ((), (), s32[]{:S(2)}) async-start(), calls=%async_computation.8 | async-start | bytes 1720320 | tf_op jit(solution)/shard_map/reduce_scatter | solution.py:1771
  865.4 37.7 %copy-start.9 = (f32[8,768]{1,0:T(8,128)S(1)}, f32[8,768]{1,0:T(8,128)}, u32[]{:S(2)}) copy-start(f32[8,768]{1,0:T(8,128)} %get-tuple-element.277) | copy-start | bytes 73732
  865.4 37.7 %copy-start.10 = (f32[8,768]{1,0:T(8,128)S(1)}, f32[8,768]{1,0:T(8,128)}, u32[]{:S(2)}) copy-start(f32[8,768]{1,0:T(8,128)} %get-tuple-element.280) | copy-start | bytes 73732
  865.4 37.7 %copy-start.11 = (f32[8,768]{1,0:T(8,128)S(1)}, f32[8,768]{1,0:T(8,128)}, u32[]{:S(2)}) copy-start(f32[8,768]{1,0:T(8,128)} %get-tuple-element.283) | copy-start | bytes 73732
  865.4 37.7 %copy-start.14 = (f32[1,768]{1,0:T(1,128)S(1)}, f32[1,768]{1,0:T(1,128)}, u32[]{:S(2)}) copy-start(f32[1,768]{1,0:T(1,128)} %get-tuple-element.276) | copy-start | bytes 9220
  865.4 37.7 %copy-start.15 = (f32[1,768]{1,0:T(1,128)S(1)}, f32[1,768]{1,0:T(1,128)}, u32[]{:S(2)}) copy-start(f32[1,768]{1,0:T(1,128)} %get-tuple-element.275) | copy-start | bytes 9220
  865.4 37.7 %copy-start.16 = (f32[1,768]{1,0:T(1,128)S(1)}, f32[1,768]{1,0:T(1,128)}, u32[]{:S(2)}) copy-start(f32[1,768]{1,0:T(1,128)} %get-tuple-element.279) | copy-start | bytes 9220
  865.4 37.7 %copy-start.17 = (f32[1,768]{1,0:T(1,128)S(1)}, f32[1,768]{1,0:T(1,128)}, u32[]{:S(2)}) copy-start(f32[1,768]{1,0:T(1,128)} %get-tuple-element.278) | copy-start | bytes 9220
  865.4 37.7 %copy-start.18 = (f32[1,768]{1,0:T(1,128)S(1)}, f32[1,768]{1,0:T(1,128)}, u32[]{:S(2)}) copy-start(f32[1,768]{1,0:T(1,128)} %get-tuple-element.282) | copy-start | bytes 9220
  943.1 4.3 copy-start
  1061.7 4.3 slice-start
  1061.7 4.3 slice-start.1
  1066.1 6.9 copy-start.1
  1066.1 7.1 copy-start.3
  1073.0 1.5 copy-start.2
Sparse Core Ops, SparseCore 0:
  9.6 20.1 all-gather.8
  42.5 28.3 all-gather.6
  326.1 22.5 all-gather.10
  380.5 54.7 all-reduce.4
  677.7 90.3 reduce-scatter.4
  770.3 123.9 reduce-scatter.6
  897.4 161.7 reduce-scatter.8
  1061.9 33.0 reduce-scatter.10

commit v6 on v5

--- a/solution.py
+++ b/solution.py
@@ -663,13 +663,36 @@
     return outs[0], outs[1:]
 
 
+def touch_kernel(*refs):
+    outs, zeros, semaphores = refs[:-2], refs[-2], refs[-1]
+    zeros[...] = jnp.zeros_like(zeros)
+    copies = []
+    for out in outs:
+        if out.dtype != BF16 or out.shape[-1] > zeros.shape[-1]:
+            continue
+        source = zeros.at[:, : out.shape[-1]]
+        for slot in range(out.shape[0]):
+            if len(out.shape) == 3:
+                places = [out.at[slot, row : row + 16] for row in range(0, out.shape[1], 512)]
+            else:
+                places = [out.at[slot, step, 0:16] for step in range(0, out.shape[1], 2)]
+            for place in places:
+                copies.append(pltpu.make_async_copy(source, place, semaphores.at[len(copies)]))
+    for copy in copies:
+        copy.start()
+    for copy in copies:
+        copy.wait()
+
+
 def reserve(shapes):
+    width = max(shape.shape[-1] for shape in shapes if shape.dtype == BF16)
     return pl.pallas_call(
-        lambda *refs: None,
+        touch_kernel,
         out_shape=shapes,
         out_specs=[pl.BlockSpec(memory_space=pl.ANY)] * len(shapes),
+        scratch_shapes=[pltpu.VMEM((16, width), BF16), pltpu.SemaphoreType.DMA((128,))],
         compiler_params=pltpu.CompilerParams(has_side_effects=True),
-        cost_estimate=cost(1),
+        cost_estimate=cost(3),
         name="reserve",
     )()
 
@@ -1854,7 +1877,7 @@
         if tick > 0:
             back_meta = backward_meta(tick)
         if tick == count:
-            lead, middle = 2, 3
+            lead = 3
             lead_meta = jnp.stack(
                 [2 - section, jnp.full_like(section, count - 1), jnp.full_like(section, count)]
                 + [jnp.full_like(section, count - 1)]
@@ -1877,20 +1900,12 @@
             dy, hid, grad_gate, grad_lift, grad_expert, hid_sh, grad_gate_sh, grad_lift_sh = (
                 grads_kept
             )
-            picked = feed_kept[2]
-            middle_part = expert_grads(
-                lead, middle, 0, devices, picked, hid, grad_gate, grad_lift, grad_expert
-            )
-            middle_part, picked, grad_gate = lax.optimization_barrier(
-                (middle_part, picked, grad_gate)
-            )
-            first = lead + middle
             last_grads = expert_grads(
-                first,
-                EXPERTS - first,
+                lead,
+                EXPERTS - lead,
                 3,
                 devices,
-                picked,
+                feed_kept[2],
                 hid,
                 grad_gate,
                 grad_lift,
@@ -1900,7 +1915,7 @@
                 last_grads, feed_kept[1], dy, grad_gate_sh, grad_lift_sh, hid_sh
             )
             part, last_grads = lax.optimization_barrier((part, last_grads))
-            parts = [spread(lead_part), spread(middle_part), spread(last_grads)]
+            parts = [spread(lead_part), spread(last_grads)]
         if tick > 0:
             summed = tensor_sum(part, 2, 7)
         (part, grad_state, gain_grad, router_grad), attention_grads_kept = attend_back(
@@ -1931,8 +1946,8 @@
     )
     packed, *parts = lax.optimization_barrier((packed, *parts))
     packed = spread(packed.reshape(devices, rows, -1)).astype(F32)
-    shared = parts[2][-3:].astype(F32)
-    experts = jnp.concatenate([parts[0], parts[1], parts[2][:-3]], axis=0).astype(F32)
+    shared = parts[1][-3:].astype(F32)
+    experts = jnp.concatenate([parts[0], parts[1][:-3]], axis=0).astype(F32)
     experts = experts.reshape(EXPERTS, 3, rows, -1)
 
     def choose(items):

time: 1110 us -> 1090 us (0.982)
    pallas_call x3, Pallas kernels: 169 us -> 157 us  [feed_forward(): pl.pallas_call(functools.partial(feed_forward_kernel, stored), grid_spec=...]
    pallas_call x2 -> x1, Pallas kernels: 34.9 us -> 26.4 us  [expert_grads(): pl.pallas_call(expert_grads_kernel, grid=(count,), in_specs=pair(width) +...]
    reduce_scatter x4 -> x3, waiting for transfers between devices: 118 us -> 116 us  [spread(): return lax.psum_scatter(array, 'dp', scatter_dimension=0, tiled=False)]
  transfers between devices with their start and end apart: 8 -> 7, of which waited for: 4 -> 4; matrix products, arithmetic and copies ran while one was open for 6% -> 6% of each run, Pallas kernels for 35% -> 35%
where the time goes in v6:
time: 1090 us
  Pallas kernels  874 us (80%)
  waiting for transfers between devices  128 us (12%)
  other arithmetic  42.8 us (4%)
  local copies, waits for them, and re-layouts  24.8 us (2%)
  between operations  15.1 us (1%)
    pallas_call x3, Pallas kernels, feed_backward(): pl.pallas_call(functools.partial(feed_backward_kernel, stored), grid_spec...  163 us
    pallas_call x3, Pallas kernels, feed_forward(): pl.pallas_call(functools.partial(feed_forward_kernel, stored), grid_spec=...  157 us
    pallas_call x3, Pallas kernels, input_relay(): pl.pallas_call(functools.partial(input_kernel, pieces, tick), out_shape=[...  121 us
    reduce_scatter x3, waiting for transfers between devices, spread(): return lax.psum_scatter(array, 'dp', scatter_dimension=0, tiled=False)  116 us
    pallas_call x3, Pallas kernels, output_relay(): pl.pallas_call(functools.partial(output_kernel, pieces, tick), out_shape=...  112 us
    pallas_call x3, Pallas kernels, attention_backward(): pl.pallas_call(functools.partial(attention_backward_kernel, stored), grid...  88.3 us
    pallas_call x3, Pallas kernels, attention_forward(): pl.pallas_call(functools.partial(attention_forward_kernel, stored), grid_...  67.1 us
    pallas_call x2, Pallas kernels, tensor_sum(): pl.pallas_call(functools.partial(sum_kernel, pieces), out_shape=shape_of(...  64.1 us
  transfers between devices with their start and end apart: 7, of which 4 were waited for; matrix products, arithmetic and copies ran while one was open for 6% of the time, Pallas kernels for 35%

profile of v6, /device:TPU:0, one launch (start us, length us, event | category | flops | bytes accessed | tf_op | source)
XLA Modules:
  0.0 1087.3 jit_solution(4220858654232923462)
XLA Ops:
  8.0 0.9 reduce_window_sum.23
  8.9 1.3 convert_element_type.49.gain_ref
  11.0 1.0 slice_negate_fusion.1
  12.0 1.0 pad_maximum_fusion.3
  13.4 1.0 slice_negate_fusion
  14.4 1.0 pad_maximum_fusion.4
  16.6 1.4 broadcast_maximum_fusion.low_ref
  18.0 1.4 pad_maximum_fusion.1.wall_ref
  19.9 1.6 broadcast_10_rec_ref.2.rec_ref
  21.5 22.5 %attention_forward.3 = (bf16[768,384]{1,0:T(8,128)(2,1)}, bf16[3,1536,768]{2,1,0:T(8,128)(2,1)}, bf16[3,1536,768]{2,1,0:T(8,128)(2,1)}, bf16[3,1536,1152]{2,1,0:...) custom-call(s32[3]{0:T(128)} %get-tuple-element.380.meta, s32[6]{0:T(128)} %reshape.145.first_block, ...), custom_call_target="tpu_custom_call" | custom-call | flops 27599998976 | bytes 86400000 | tf_op jit(solution)/shard_map/attention_forward/pallas_call | solution.py:643
  47.2 0.9 concatenate.45
  48.1 2.2 bitcast_select_fusion.1
  50.3 1.1 copy.232.post_ref
  52.0 1.3 pad_add_fusion.1.starts
  55.6 2.1 reserve.2
  57.8 2.3 reserve.3
  60.7 1.3 bitcast_select_fusion.pos_ref
  62.1 8.9 all-gather.7.cloned.1.call-done
  70.9 52.5 %feed_forward.3 = (bf16[1536,768]{1,0:T(8,128)(2,1)}, f32[3,1536,768]{2,1,0:T(8,128)}, bf16[3,1536,768]{2,1,0:T(8,128)(2,1)}, bf16[3,8,480,768]{3,2,1,0:T(8,128)...) custom-call(s32[3]{0:T(128)} %get-tuple-element.380.meta, ...), custom_call_target="tpu_custom_call", output_to_operand_aliasing={{1}: (15, {}), {2}: (16, {}), {3}: (17, {}), {4}: (18, {}),... | custom-call | flops 64399998976 | bytes 201600000 | tf_op jit(solution)/shard_map/feed_forward/pallas_call | solution.py:980
  123.5 37.1 %output_relay.3 = (bf16[1536,768]{1,0:T(8,128)(2,1)}, bf16[1536,768]{1,0:T(8,128)(2,1)}) custom-call(bf16[1536,768]{1,0:T(8,128)(2,1)} %get-tuple-element.159.part_ref, f32[3,1536,768]{2,1,0:T(8,128)} %get-tuple-element.160.states_ref.rest_0_), custom_call_target="tpu_custom_call" | custom-call | flops 43699998720 | bytes 136800000 | tf_op jit(solution)/shard_map/output_relay/pallas_call | solution.py:334
  160.5 22.3 %attention_forward.4 = (bf16[768,384]{1,0:T(8,128)(2,1)}, bf16[3,1536,768]{2,1,0:T(8,128)(2,1)}, bf16[3,1536,768]{2,1,0:T(8,128)(2,1)}, bf16[3,1536,1152]{2,1,0:...) custom-call(s32[3]{0:T(128)} %get-tuple-element.381.meta, ...), custom_call_target="tpu_custom_call", output_to_operand_aliasing={{1}: (9, {}), {2}: (10, {}), {3}: (11, {}), {4}: (12, {}), ... | custom-call | flops 27599998976 | bytes 86400000 | tf_op jit(solution)/shard_map/attention_forward/pallas_call | solution.py:643
  182.9 20.1 %tensor_gather.1.ag_ref = bf16[4,768,384]{2,1,0:T(8,128)(2,1)} custom-call(bf16[768,384]{1,0:T(8,128)(2,1)} %get-tuple-element.168.own_ref), custom_call_target="tpu_custom_call" | custom-call | flops 20700000256 | bytes 64800000 | tf_op jit(solution)/shard_map/tensor_gather/pallas_call | solution.py:235
  203.0 52.2 %feed_forward.4 = (bf16[1536,768]{1,0:T(8,128)(2,1)}, f32[3,1536,768]{2,1,0:T(8,128)}, bf16[3,1536,768]{2,1,0:T(8,128)(2,1)}, bf16[3,8,480,768]{3,2,1,0:T(8,128)...) custom-call(s32[3]{0:T(128)} %get-tuple-element.381.meta, ...), custom_call_target="tpu_custom_call", output_to_operand_aliasing={{1}: (15, {}), {2}: (16, {}), {3}: (17, {}), {4}: (18, {}),... | custom-call | flops 64399998976 | bytes 201600000 | tf_op jit(solution)/shard_map/feed_forward/pallas_call | solution.py:980
  255.2 36.8 %output_relay.4 = (bf16[1536,768]{1,0:T(8,128)(2,1)}, bf16[1536,768]{1,0:T(8,128)(2,1)}) custom-call(bf16[1536,768]{1,0:T(8,128)(2,1)} %get-tuple-element.176.part_ref, f32[3,1536,768]{2,1,0:T(8,128)} %get-tuple-element.177.states_ref.rest_0_), custom_call_target="tpu_custom_call" | custom-call | flops 43699998720 | bytes 136800000 | tf_op jit(solution)/shard_map/output_relay/pallas_call | solution.py:334
  292.0 22.3 %attention_forward.5 = (bf16[768,384]{1,0:T(8,128)(2,1)}, bf16[3,1536,768]{2,1,0:T(8,128)(2,1)}, bf16[3,1536,768]{2,1,0:T(8,128)(2,1)}, bf16[3,1536,1152]{2,1,0:...) custom-call(s32[3]{0:T(128)} %pad_add_fusion.4.meta, ...), custom_call_target="tpu_custom_call", output_to_operand_aliasing={{1}: (9, {}), {2}: (10, {}), {3}: (11, {}), {4}: (12, {}), ... | custom-call | flops 27599998976 | bytes 86400000 | tf_op jit(solution)/shard_map/attention_forward/pallas_call | solution.py:643
  314.4 54.5 %feed_backward.3 = (bf16[1568,768]{1,0:T(8,128)(2,1)}, bf16[3,1536,768]{2,1,0:T(8,128)(2,1)}, bf16[3,8,480,512]{3,2,1,0:T(8,128)(2,1)}, bf16[3,8,480,512]{3,2,1,...) custom-call(s32[4]{0:T(128)} %pad_add_fusion.3.meta, ...), custom_call_target="tpu_custom_call", output_to_operand_aliasing={{1}: (17, {}), {2}: (18, {}), {3}: (19, {}), {4}: (20, {}),... | custom-call | flops 69000003584 | bytes 216000000 | tf_op jit(solution)/shard_map/feed_backward/pallas_call | solution.py:1204
  369.0 52.6 %feed_forward.5 = (bf16[1536,768]{1,0:T(8,128)(2,1)}, f32[3,1536,768]{2,1,0:T(8,128)}, bf16[3,1536,768]{2,1,0:T(8,128)(2,1)}, bf16[3,8,480,768]{3,2,1,0:T(8,128)...) custom-call(s32[3]{0:T(128)} %pad_add_fusion.4.meta, ...), custom_call_target="tpu_custom_call", output_to_operand_aliasing={{1}: (15, {}), {2}: (16, {}), {3}: (17, {}), {4}: (18, {}),... | custom-call | flops 64399998976 | bytes 201600000 | tf_op jit(solution)/shard_map/feed_forward/pallas_call | solution.py:980
  421.5 2.2 all-reduce.5.cloned.1.call-done.sum_ref.choice_ref
  423.7 28.0 %attention_backward.3 = (bf16[1536,768]{1,0:T(8,128)(2,1)}, f32[1536,768]{1,0:T(8,128)}, f32[1,768]{1,0:T(1,128)}, f32[8,768]{1,0:T(8,128)}, bf16[3,1536,1152]{2...) custom-call(s32[4]{0:T(128)} %pad_add_fusion.3.meta, s32[8]{0:T(128)} %reshape.149.first_block, ...), custom_call_target="tpu_custom_call" | custom-call | flops 42550001664 | bytes 133200000 | tf_op jit(solution)/shard_map/attention_backward/pallas_call | solution.py:1401
  451.7 39.1 %input_relay.3 = (f32[1536,768]{1,0:T(8,128)}, bf16[1536,768]{1,0:T(8,128)(2,1)}, f32[1,768]{1,0:T(1,128)}) custom-call(bf16[1536,768]{1,0:T(8,128)(2,1)} %get-tuple-element.217.part_ref, bf16[3,1536,768]{2,1,0:T(8,128)(2,1)} %get-tuple-element.201.x_ref.layers_ref, f32[1536,768]{1,0:T(8,128)} %get-tuple-element.218.grad_state_ref, ...), custom_call_target="tpu_custom_call" | custom-call | flops 48299999232 | bytes 151200000 | tf_op jit(solution)/shard_map/input_relay/pallas_call | solution.py:468
  490.8 54.3 %feed_backward.4 = (bf16[1568,768]{1,0:T(8,128)(2,1)}, bf16[3,1536,768]{2,1,0:T(8,128)(2,1)}, bf16[3,8,480,512]{3,2,1,0:T(8,128)(2,1)}, bf16[3,8,480,512]{3,2,1,...) custom-call(s32[4]{0:T(128)} %pad_add_fusion.5.meta, ...), custom_call_target="tpu_custom_call", output_to_operand_aliasing={{1}: (17, {}), {2}: (18, {}), {3}: (19, {}), {4}: (20, {}),... | custom-call | flops 69000003584 | bytes 216000000 | tf_op jit(solution)/shard_map/feed_backward/pallas_call | solution.py:1204
  545.0 32.1 %tensor_sum.2.sum_ref.choice_ref = bf16[1568,768]{1,0:T(8,128)(2,1)} custom-call(bf16[1568,768]{1,0:T(8,128)(2,1)} %get-tuple-element.231.part_ref), custom_call_target="tpu_custom_call" | custom-call | flops 36800000000 | bytes 115200000 | tf_op jit(solution)/shard_map/tensor_sum/pallas_call | solution.py:175
  577.1 27.8 %attention_backward.4 = (bf16[1536,768]{1,0:T(8,128)(2,1)}, f32[1536,768]{1,0:T(8,128)}, f32[1,768]{1,0:T(1,128)}, f32[8,768]{1,0:T(8,128)}, bf16[3,1536,1152]{2...) custom-call(s32[4]{0:T(128)} %pad_add_fusion.5.meta, ...), custom_call_target="tpu_custom_call", output_to_operand_aliasing={{4}: (18, {}), {5}: (19, {})} | custom-call | flops 42550001664 | bytes 133200000 | tf_op jit(solution)/shard_map/attention_backward/pallas_call | solution.py:1401
  604.9 43.8 %input_relay.4 = (f32[1536,768]{1,0:T(8,128)}, bf16[1536,768]{1,0:T(8,128)(2,1)}, f32[1,768]{1,0:T(1,128)}) custom-call(bf16[1536,768]{1,0:T(8,128)(2,1)} %get-tuple-element.235.part_ref, bf16[3,1536,768]{2,1,0:T(8,128)(2,1)} %get-tuple-element.201.x_ref.layers_ref, f32[1536,768]{1,0:T(8,128)} %get-tuple-element.236.grad_state_ref, ...), custom_call_target="tpu_custom_call" | custom-call | flops 48299999232 | bytes 151200000 | tf_op jit(solution)/shard_map/input_relay/pallas_call | solution.py:468
  648.7 22.6 %lead_grads.1 = bf16[4,9,192,512]{3,2,1,0:T(8,128)(2,1)} custom-call(s32[4]{0:T(128)} %pad_add_fusion.7.meta, bf16[3072,768]{1,0:T(8,128)(2,1)} %cot_ref.7, bf16[1536,768]{1,0:T(8,128)(2,1)} %get-tuple-element.239.rec_ref, s32[2,8,1536]{2,1,0:T(8,128)} %copy.232.post_ref, f32[3,8,1536]{2,1,0:T(8,128)} %get-tuple-element.211.probs_ref, ...), custom_call_target="tpu_custom_call" | custom-call | flops 23000000512 | bytes 72000000 | tf_op jit(solution)/shard_map/lead_grads/pallas_call | solution.py:1579
  671.4 54.7 %feed_backward.5 = (bf16[1568,768]{1,0:T(8,128)(2,1)}, bf16[3,1536,768]{2,1,0:T(8,128)(2,1)}, bf16[3,8,480,512]{3,2,1,0:T(8,128)(2,1)}, bf16[3,8,480,512]{3,2,1,...) custom-call(s32[4]{0:T(128)} %pad_add_fusion.6.meta, ...), custom_call_target="tpu_custom_call", output_to_operand_aliasing={{1}: (17, {}), {2}: (18, {}), {3}: (19, {}), {4}: (20, {}),... | custom-call | flops 69000003584 | bytes 216000000 | tf_op jit(solution)/shard_map/feed_backward/pallas_call | solution.py:1204
  726.1 26.4 %expert_grads.1.before_ref = bf16[4,18,192,512]{3,2,1,0:T(8,128)(2,1)} custom-call(bf16[3,8,480,768]{3,2,1,0:T(8,128)(2,1)} %get-tuple-element.240.xa_ref.xb_ref.refs_0_.refs_1_, bf16[3,8,480,768]{3,2,1,0:T(8,128)(2,1)} %get-tuple-element.240.xa_ref.xb_ref.refs_0_.refs_1_, bf16[3,8,480,512]{3,2,1,0:T(8,128)(2,1)} %get-tuple-element.254.refs_2_.refs_3_, ...), custom_call_target="tpu_custom_call" | custom-call | flops 34500001792 | bytes 108000000 | tf_op jit(solution)/shard_map/expert_grads/pallas_call | solution.py:1466
  752.4 13.5 %shared_grads.1 = bf16[4,18,192,512]{3,2,1,0:T(8,128)(2,1)} custom-call(bf16[3,1536,768]{2,1,0:T(8,128)(2,1)} %get-tuple-element.213.b_ref, bf16[3,1536,768]{2,1,0:T(8,128)(2,1)} %get-tuple-element.250.dy_ref, bf16[3,1536,512]{2,1,0:T(8,128)(2,1)} %get-tuple-element.251.gate_ref, ...), custom_call_target="tpu_custom_call", output_to_operand_aliasing={{}: (5, {})} | custom-call | flops 14949999616 | bytes 46800000 | tf_op jit(solution)/shard_map/shared_grads/pallas_call | solution.py:1634
  766.0 32.1 %tensor_sum.3.sum_ref.choice_ref = bf16[1568,768]{1,0:T(8,128)(2,1)} custom-call(bf16[1568,768]{1,0:T(8,128)(2,1)} %get-tuple-element.258.part_ref), custom_call_target="tpu_custom_call" | custom-call | flops 36800000000 | bytes 115200000 | tf_op jit(solution)/shard_map/tensor_sum/pallas_call | solution.py:175
  798.0 32.5 %attention_backward.5 = (bf16[1536,768]{1,0:T(8,128)(2,1)}, f32[1536,768]{1,0:T(8,128)}, f32[1,768]{1,0:T(1,128)}, f32[8,768]{1,0:T(8,128)}, bf16[3,1536,1152]{2...) custom-call(s32[4]{0:T(128)} %pad_add_fusion.6.meta, ...), custom_call_target="tpu_custom_call", output_to_operand_aliasing={{4}: (18, {}), {5}: (19, {})} | custom-call | flops 42550001664 | bytes 133200000 | tf_op jit(solution)/shard_map/attention_backward/pallas_call | solution.py:1401
  830.5 14.3 %token_grads.1 = (bf16[768,1152]{1,0:T(8,128)(2,1)}, bf16[768,384]{1,0:T(8,128)(2,1)}) custom-call(bf16[3,1536,768]{2,1,0:T(8,128)(2,1)} %get-tuple-element.264.refs_0_, bf16[3,1536,768]{2,1,0:T(8,128)(2,1)} %get-tuple-element.265.refs_1_, bf16[3,1536,1152]{2,1,0:T(8,128)(2,1)} %get-tuple-element.266.refs_2_, ...), custom_call_target="tpu_custom_call" | custom-call | flops 16099999744 | bytes 50400000 | tf_op jit(solution)/shard_map/token_grads/pallas_call | solution.py:1677
  844.8 1.1 slice.94
  846.0 1.3 slice.92
  847.3 1.3 copy.241
  848.7 0.9 copy.239
  849.9 37.8 %input_relay.5 = (f32[1536,768]{1,0:T(8,128)}, bf16[1536,768]{1,0:T(8,128)(2,1)}, f32[1,768]{1,0:T(1,128)}) custom-call(bf16[1536,768]{1,0:T(8,128)(2,1)} %get-tuple-element.261.part_ref, bf16[3,1536,768]{2,1,0:T(8,128)(2,1)} %get-tuple-element.201.x_ref.layers_ref, f32[1536,768]{1,0:T(8,128)} %get-tuple-element.262.grad_state_ref, ...), custom_call_target="tpu_custom_call" | custom-call | flops 48299999232 | bytes 151200000 | tf_op jit(solution)/shard_map/input_relay/pallas_call | solution.py:468
  887.8 0.7 fusion.8
  888.7 8.4 broadcast_select_fusion.1
  897.1 37.9 %output_relay.5 = (bf16[1536,768]{1,0:T(8,128)(2,1)}, bf16[1536,768]{1,0:T(8,128)(2,1)}) custom-call(bf16[1536,768]{1,0:T(8,128)(2,1)} %get-tuple-element.206.part_ref, f32[3,1536,768]{2,1,0:T(8,128)} %get-tuple-element.207.states_ref.h_ref), custom_call_target="tpu_custom_call" | custom-call | flops 43699998720 | bytes 136800000 | tf_op jit(solution)/shard_map/output_relay/pallas_call | solution.py:334
  935.0 105.1 %reduce-scatter.6.cloned.1.call-done = bf16[1,18,192,512]{3,2,1,0:T(8,128)(2,1)} async-done(((bf16[4,18,192,512]{3,2,1,0:T(8,128)(2,1)}), bf16[1,18,192,512]{3,2,1,0:T(8,128)(2,1)}) %reduce-scatter.6.cloned.1.call-update) | async-done | bytes 3538960 | tf_op jit(solution)/shard_map/reduce_scatter | solution.py:1794
  1040.2 1.8 copy.242
  1042.0 2.9 broadcast_select_fusion.3
  1044.9 2.5 maximum_bitcast_fusion.1
  1047.4 6.8 maximum_bitcast_fusion
  1054.2 2.2 slice.104
  1057.0 1.3 convert.9
  1058.3 1.2 slice_convert_fusion
  1059.6 1.0 slice_bitcast_fusion.3
  1060.6 4.0 slice_bitcast_fusion
  1064.6 11.3 %reduce-scatter.8.cloned.1.call-done = bf16[1,192,784]{2,1,0:T(8,128)(2,1)} async-done(((bf16[4,192,784]{2,1,0:T(8,128)(2,1)}), bf16[1,192,784]{2,1,0:T(8,128)(2,1)}) %reduce-scatter.8.cloned.1.call-update) | async-done | bytes 301072 | tf_op jit(solution)/shard_map/reduce_scatter | solution.py:1794
  1075.9 1.0 bitcast_convert_fusion
  1076.9 0.8 slice_reduce_fusion
  1077.8 0.9 slice_bitcast_fusion.4
  1079.4 0.8 copy.246
  (94 shorter events, 12.6 us)
Async XLA Ops:
  7.2 8.5 copy-start.2
  7.2 54.9 %all-gather.9.cloned.1.call-start = ((), (), s32[]{:S(2)}) async-start(), calls=%async_computation.8 | async-start | bytes 1474560 | tf_op jit(solution)/shard_map/all_gather | solution.py:1771
  7.9 63.0 %all-gather.7.cloned.1.call-start = ((), (), s32[]{:S(2)}) async-start(), calls=%async_computation.7 | async-start | bytes 2949120 | tf_op jit(solution)/shard_map/all_gather | solution.py:1860
  8.0 8.6 copy-start.4
  21.5 22.7 %copy-start.9 = (s32[1,3072,2]{1,2,0:T(2,128)S(1)}, s32[1,3072,2]{1,2,0:T(2,128)}, u32[]{:S(2)}) copy-start(s32[1,3072,2]{1,2,0:T(2,128)} %param.21) | copy-start | bytes 73732
  21.5 23.4 %copy-start.10 = (bf16[1,768]{1,0:T(2,128)(2,1)S(1)}, bf16[1,768]{1,0:T(2,128)(2,1)}, u32[]{:S(2)}) copy-start(bf16[1,768]{1,0:T(2,128)(2,1)} %param.27) | copy-start | bytes 4612
  21.5 25.7 %copy-start.1 = (bf16[1,192,768]{2,1,0:T(8,128)(2,1)S(1)}, bf16[1,192,768]{2,1,0:T(8,128)(2,1)}, u32[]{:S(2)}) copy-start(bf16[1,192,768]{2,1,0:T(8,128)(2,1)} %param.26) | copy-start | bytes 884740
  44.0 325.0 %all-gather.11.cloned.1.call-start = ((), (), s32[]{:S(2)}) async-start(), calls=%async_computation.9 | async-start | bytes 2949120 | tf_op jit(solution)/shard_map/all_gather | solution.py:1869
  44.2 3.0 copy-start.3
  57.8 2.3 copy-start.5
  314.4 109.4 %all-reduce.5.cloned.1.call-start = ((), (), s32[]{:S(2)}) async-start(), calls=%async_computation.3 | async-start | bytes 4816896 | tf_op jit(solution)/shard_map/psum | solution.py:1872
  368.9 566.1 %reduce-scatter.4.cloned.1.call-start = ((), (), s32[]{:S(2)}) async-start(), calls=%async_computation.4 | async-start | bytes 8847360 | tf_op jit(solution)/shard_map/reduce_scatter | solution.py:1794
  671.3 368.9 %reduce-scatter.6.cloned.1.call-start = ((), (), s32[]{:S(2)}) async-start(), calls=%async_computation.5 | async-start | bytes 17694720 | tf_op jit(solution)/shard_map/reduce_scatter | solution.py:1794
  765.9 310.0 %reduce-scatter.8.cloned.1.call-start = ((), (), s32[]{:S(2)}) async-start(), calls=%async_computation.6 | async-start | bytes 1720320 | tf_op jit(solution)/shard_map/reduce_scatter | solution.py:1794
  849.8 37.9 %copy-start.6 = (f32[8,768]{1,0:T(8,128)S(1)}, f32[8,768]{1,0:T(8,128)}, u32[]{:S(2)}) copy-start(f32[8,768]{1,0:T(8,128)} %get-tuple-element.271) | copy-start | bytes 73732
  849.8 37.9 %copy-start.7 = (f32[8,768]{1,0:T(8,128)S(1)}, f32[8,768]{1,0:T(8,128)}, u32[]{:S(2)}) copy-start(f32[8,768]{1,0:T(8,128)} %get-tuple-element.274) | copy-start | bytes 73732
  849.8 37.9 %copy-start.8 = (f32[8,768]{1,0:T(8,128)S(1)}, f32[8,768]{1,0:T(8,128)}, u32[]{:S(2)}) copy-start(f32[8,768]{1,0:T(8,128)} %get-tuple-element.277) | copy-start | bytes 73732
  849.8 37.9 %copy-start.11 = (f32[1,768]{1,0:T(1,128)S(1)}, f32[1,768]{1,0:T(1,128)}, u32[]{:S(2)}) copy-start(f32[1,768]{1,0:T(1,128)} %get-tuple-element.270) | copy-start | bytes 9220
  849.9 37.9 %copy-start.12 = (f32[1,768]{1,0:T(1,128)S(1)}, f32[1,768]{1,0:T(1,128)}, u32[]{:S(2)}) copy-start(f32[1,768]{1,0:T(1,128)} %get-tuple-element.269) | copy-start | bytes 9220
  849.9 37.9 %copy-start.13 = (f32[1,768]{1,0:T(1,128)S(1)}, f32[1,768]{1,0:T(1,128)}, u32[]{:S(2)}) copy-start(f32[1,768]{1,0:T(1,128)} %get-tuple-element.273) | copy-start | bytes 9220
  849.9 37.9 %copy-start.14 = (f32[1,768]{1,0:T(1,128)S(1)}, f32[1,768]{1,0:T(1,128)}, u32[]{:S(2)}) copy-start(f32[1,768]{1,0:T(1,128)} %get-tuple-element.272) | copy-start | bytes 9220
  849.9 37.9 %copy-start.15 = (f32[1,768]{1,0:T(1,128)S(1)}, f32[1,768]{1,0:T(1,128)}, u32[]{:S(2)}) copy-start(f32[1,768]{1,0:T(1,128)} %get-tuple-element.276) | copy-start | bytes 9220
  1040.2 7.2 slice-start
  1042.0 5.4 slice-start.1
  1054.2 2.4 copy-start
Sparse Core Ops, SparseCore 0:
  9.6 20.1 all-gather.8
  44.1 26.7 all-gather.6
  314.5 22.4 all-gather.10
  369.0 54.6 all-reduce.4
  671.4 128.5 reduce-scatter.3
  802.4 237.7 reduce-scatter.5
  1042.6 33.2 reduce-scatter.7

commit v7 on v6

--- a/solution.py
+++ b/solution.py
@@ -1442,12 +1442,9 @@
     devices, unused, rows, unused = out_ref.shape
     pairs = [((xa, xb), (ga, gb)), ((xa, xb), (ua, ub)), ((ea, eb), (ha, hb))]
     for number, (left, right) in enumerate(pairs):
+        grads = dot_tn(left[0][0, 0], right[0][0, 0]) + dot_tn(left[1][0, 0], right[1][0, 0])
         for device in range(devices):
-            columns = slice(device * rows, (device + 1) * rows)
-            out_ref[device, number] = (
-                dot_tn(left[0][0, 0, :, columns], right[0][0, 0])
-                + dot_tn(left[1][0, 0, :, columns], right[1][0, 0])
-            ).astype(BF16)
+            out_ref[device, number] = grads[device * rows : (device + 1) * rows].astype(BF16)
 
 
 def expert_grads(first, count, extra, devices, picked, hid, grad_gate, grad_lift, grad_expert):
@@ -1526,12 +1523,9 @@
             (ea_ref.at[0, 0], ha_ref.at[0, 0], grad_rows, hidden),
         ]
         for number, (left, right, left_last, right_last) in enumerate(pairs):
+            grads = dot_tn(left[...], right[...]) + dot_tn(left_last[...], right_last[...])
             for device in range(devices):
-                columns = slice(device * rows, (device + 1) * rows)
-                out_ref[device, number] = (
-                    dot_tn(left[:, columns], right[...])
-                    + dot_tn(left_last[:, columns], right_last[...])
-                ).astype(BF16)
+                out_ref[device, number] = grads[device * rows : (device + 1) * rows].astype(BF16)
 
 
 def lead_grads(count, devices, meta, cotangent, received, post, forward_kept, kept, down):
@@ -1785,7 +1779,7 @@
     back_first = (low[:, ::BACK_BLOCK] // BACK_KEYS).reshape(-1)
     low_column, low_row = low[:, :, None], low[:, None, :]
 
-    received = jnp.zeros((SEQ_LEN, width), BF16)
+    received = tokens
     attention_kept, feed_kept, results = None, None, []
     grads_kept, attention_grads_kept, inputs = None, None, []
     small = jnp.zeros((10, width), F32)
@@ -1862,7 +1856,7 @@
         result, received = output_relay(part, feed_kept[0], tick, 4 + tick)
         results.append(result)
 
-    blank = jnp.zeros((SEQ_LEN, width), BF16)
+    blank = cotangent
     meta, back_meta = forward_meta(count), backward_meta(0)
     own, attention_kept = attend(meta, received, attention_kept)
     back_meta, own = after(back_meta, own)

time: 1090 us -> 1090 us (level)
  transfers between devices with their start and end apart: 7 -> 7, of which waited for: 4 -> 4; matrix products, arithmetic and copies ran while one was open for 6% -> 6% of each run, Pallas kernels for 35% -> 34%
where the time goes in v7:
time: 1090 us
  Pallas kernels  866 us (79%)
  waiting for transfers between devices  138 us (13%)
  other arithmetic  43 us (4%)
  local copies, waits for them, and re-layouts  23.2 us (2%)
  between operations  15 us (1%)
    pallas_call x3, Pallas kernels, feed_backward(): pl.pallas_call(functools.partial(feed_backward_kernel, stored), grid_spec...  163 us
    pallas_call x3, Pallas kernels, feed_forward(): pl.pallas_call(functools.partial(feed_forward_kernel, stored), grid_spec=...  157 us
    reduce_scatter x3, waiting for transfers between devices, spread(): return lax.psum_scatter(array, 'dp', scatter_dimension=0, tiled=False)  123 us
    pallas_call x3, Pallas kernels, input_relay(): pl.pallas_call(functools.partial(input_kernel, pieces, tick), out_shape=[...  118 us
    pallas_call x3, Pallas kernels, output_relay(): pl.pallas_call(functools.partial(output_kernel, pieces, tick), out_shape=...  110 us
    pallas_call x3, Pallas kernels, attention_backward(): pl.pallas_call(functools.partial(attention_backward_kernel, stored), grid...  92.7 us
    pallas_call x3, Pallas kernels, attention_forward(): pl.pallas_call(functools.partial(attention_forward_kernel, stored), grid_...  67 us
    pallas_call x2, Pallas kernels, tensor_sum(): pl.pallas_call(functools.partial(sum_kernel, pieces), out_shape=shape_of(...  64.1 us
  transfers between devices with their start and end apart: 7, of which 4 were waited for; matrix products, arithmetic and copies ran while one was open for 6% of the time, Pallas kernels for 34%

profile of v7, /device:TPU:0, one launch (start us, length us, event | category | flops | bytes accessed | tf_op | source)
XLA Modules:
  0.0 1087.0 jit_solution(11139357905887794102)
XLA Ops:
  7.2 0.7 all-gather.9.cloned.1.call-update
  8.0 0.9 reduce_window_sum.23
  8.9 1.3 convert_element_type.49.gain_ref
  11.0 1.0 slice_negate_fusion.1
  12.0 1.0 pad_maximum_fusion.3
  13.4 1.0 slice_negate_fusion
  14.4 1.0 pad_maximum_fusion.4
  16.6 1.4 broadcast_maximum_fusion.low_ref
  18.0 1.4 pad_maximum_fusion.1.wall_ref
  19.9 22.4 %attention_forward.3 = (bf16[768,384]{1,0:T(8,128)(2,1)}, bf16[3,1536,768]{2,1,0:T(8,128)(2,1)}, bf16[3,1536,768]{2,1,0:T(8,128)(2,1)}, bf16[3,1536,1152]{2,1,0:...) custom-call(s32[3]{0:T(128)} %get-tuple-element.380.meta, s32[6]{0:T(128)} %reshape.145.first_block, ...), custom_call_target="tpu_custom_call" | custom-call | flops 27599998976 | bytes 86400000 | tf_op jit(solution)/shard_map/attention_forward/pallas_call | solution.py:643
  45.6 0.9 concatenate.45
  46.5 2.2 bitcast_select_fusion.1
  48.7 1.1 copy.232.post_ref
  50.3 1.3 pad_add_fusion.1.starts
  54.0 2.1 reserve.2
  56.2 2.3 reserve.3
  59.1 1.3 bitcast_select_fusion.pos_ref
  60.5 8.9 all-gather.7.cloned.1.call-done
  69.4 52.6 %feed_forward.3 = (bf16[1536,768]{1,0:T(8,128)(2,1)}, f32[3,1536,768]{2,1,0:T(8,128)}, bf16[3,1536,768]{2,1,0:T(8,128)(2,1)}, bf16[3,8,480,768]{3,2,1,0:T(8,128)...) custom-call(s32[3]{0:T(128)} %get-tuple-element.380.meta, ...), custom_call_target="tpu_custom_call", output_to_operand_aliasing={{1}: (15, {}), {2}: (16, {}), {3}: (17, {}), {4}: (18, {}),... | custom-call | flops 64399998976 | bytes 201600000 | tf_op jit(solution)/shard_map/feed_forward/pallas_call | solution.py:980
  122.0 37.0 %output_relay.3 = (bf16[1536,768]{1,0:T(8,128)(2,1)}, bf16[1536,768]{1,0:T(8,128)(2,1)}) custom-call(bf16[1536,768]{1,0:T(8,128)(2,1)} %get-tuple-element.159.part_ref, f32[3,1536,768]{2,1,0:T(8,128)} %get-tuple-element.160.states_ref.rest_0_), custom_call_target="tpu_custom_call" | custom-call | flops 43699998720 | bytes 136800000 | tf_op jit(solution)/shard_map/output_relay/pallas_call | solution.py:334
  159.0 22.3 %attention_forward.4 = (bf16[768,384]{1,0:T(8,128)(2,1)}, bf16[3,1536,768]{2,1,0:T(8,128)(2,1)}, bf16[3,1536,768]{2,1,0:T(8,128)(2,1)}, bf16[3,1536,1152]{2,1,0:...) custom-call(s32[3]{0:T(128)} %get-tuple-element.381.meta, ...), custom_call_target="tpu_custom_call", output_to_operand_aliasing={{1}: (9, {}), {2}: (10, {}), {3}: (11, {}), {4}: (12, {}), ... | custom-call | flops 27599998976 | bytes 86400000 | tf_op jit(solution)/shard_map/attention_forward/pallas_call | solution.py:643
  181.3 20.1 %tensor_gather.1.ag_ref = bf16[4,768,384]{2,1,0:T(8,128)(2,1)} custom-call(bf16[768,384]{1,0:T(8,128)(2,1)} %get-tuple-element.168.own_ref), custom_call_target="tpu_custom_call" | custom-call | flops 20700000256 | bytes 64800000 | tf_op jit(solution)/shard_map/tensor_gather/pallas_call | solution.py:235
  201.4 52.3 %feed_forward.4 = (bf16[1536,768]{1,0:T(8,128)(2,1)}, f32[3,1536,768]{2,1,0:T(8,128)}, bf16[3,1536,768]{2,1,0:T(8,128)(2,1)}, bf16[3,8,480,768]{3,2,1,0:T(8,128)...) custom-call(s32[3]{0:T(128)} %get-tuple-element.381.meta, ...), custom_call_target="tpu_custom_call", output_to_operand_aliasing={{1}: (15, {}), {2}: (16, {}), {3}: (17, {}), {4}: (18, {}),... | custom-call | flops 64399998976 | bytes 201600000 | tf_op jit(solution)/shard_map/feed_forward/pallas_call | solution.py:980
  253.7 36.8 %output_relay.4 = (bf16[1536,768]{1,0:T(8,128)(2,1)}, bf16[1536,768]{1,0:T(8,128)(2,1)}) custom-call(bf16[1536,768]{1,0:T(8,128)(2,1)} %get-tuple-element.176.part_ref, f32[3,1536,768]{2,1,0:T(8,128)} %get-tuple-element.177.states_ref.rest_0_), custom_call_target="tpu_custom_call" | custom-call | flops 43699998720 | bytes 136800000 | tf_op jit(solution)/shard_map/output_relay/pallas_call | solution.py:334
  290.5 22.3 %attention_forward.5 = (bf16[768,384]{1,0:T(8,128)(2,1)}, bf16[3,1536,768]{2,1,0:T(8,128)(2,1)}, bf16[3,1536,768]{2,1,0:T(8,128)(2,1)}, bf16[3,1536,1152]{2,1,0:...) custom-call(s32[3]{0:T(128)} %pad_add_fusion.4.meta, ...), custom_call_target="tpu_custom_call", output_to_operand_aliasing={{1}: (9, {}), {2}: (10, {}), {3}: (11, {}), {4}: (12, {}), ... | custom-call | flops 27599998976 | bytes 86400000 | tf_op jit(solution)/shard_map/attention_forward/pallas_call | solution.py:643
  312.8 54.1 %feed_backward.3 = (bf16[1568,768]{1,0:T(8,128)(2,1)}, bf16[3,1536,768]{2,1,0:T(8,128)(2,1)}, bf16[3,8,480,512]{3,2,1,0:T(8,128)(2,1)}, bf16[3,8,480,512]{3,2,1,...) custom-call(s32[4]{0:T(128)} %pad_add_fusion.3.meta, ...), custom_call_target="tpu_custom_call", output_to_operand_aliasing={{1}: (17, {}), {2}: (18, {}), {3}: (19, {}), {4}: (20, {}),... | custom-call | flops 69000003584 | bytes 216000000 | tf_op jit(solution)/shard_map/feed_backward/pallas_call | solution.py:1204
  367.0 52.1 %feed_forward.5 = (bf16[1536,768]{1,0:T(8,128)(2,1)}, f32[3,1536,768]{2,1,0:T(8,128)}, bf16[3,1536,768]{2,1,0:T(8,128)(2,1)}, bf16[3,8,480,768]{3,2,1,0:T(8,128)...) custom-call(s32[3]{0:T(128)} %pad_add_fusion.4.meta, ...), custom_call_target="tpu_custom_call", output_to_operand_aliasing={{1}: (15, {}), {2}: (16, {}), {3}: (17, {}), {4}: (18, {}),... | custom-call | flops 64399998976 | bytes 201600000 | tf_op jit(solution)/shard_map/feed_forward/pallas_call | solution.py:980
  419.2 4.9 all-reduce.5.cloned.1.call-done.sum_ref.choice_ref
  424.0 32.5 %attention_backward.3 = (bf16[1536,768]{1,0:T(8,128)(2,1)}, f32[1536,768]{1,0:T(8,128)}, f32[1,768]{1,0:T(1,128)}, f32[8,768]{1,0:T(8,128)}, bf16[3,1536,1152]{2...) custom-call(s32[4]{0:T(128)} %pad_add_fusion.3.meta, s32[8]{0:T(128)} %reshape.149.first_block, ...), custom_call_target="tpu_custom_call" | custom-call | flops 42550001664 | bytes 133200000 | tf_op jit(solution)/shard_map/attention_backward/pallas_call | solution.py:1401
  456.6 39.1 %input_relay.3 = (f32[1536,768]{1,0:T(8,128)}, bf16[1536,768]{1,0:T(8,128)(2,1)}, f32[1,768]{1,0:T(1,128)}) custom-call(bf16[1536,768]{1,0:T(8,128)(2,1)} %get-tuple-element.217.part_ref, bf16[3,1536,768]{2,1,0:T(8,128)(2,1)} %get-tuple-element.201.x_ref.layers_ref, f32[1536,768]{1,0:T(8,128)} %get-tuple-element.218.grad_state_ref, ...), custom_call_target="tpu_custom_call" | custom-call | flops 48299999232 | bytes 151200000 | tf_op jit(solution)/shard_map/input_relay/pallas_call | solution.py:468
  495.7 54.3 %feed_backward.4 = (bf16[1568,768]{1,0:T(8,128)(2,1)}, bf16[3,1536,768]{2,1,0:T(8,128)(2,1)}, bf16[3,8,480,512]{3,2,1,0:T(8,128)(2,1)}, bf16[3,8,480,512]{3,2,1,...) custom-call(s32[4]{0:T(128)} %pad_add_fusion.5.meta, ...), custom_call_target="tpu_custom_call", output_to_operand_aliasing={{1}: (17, {}), {2}: (18, {}), {3}: (19, {}), {4}: (20, {}),... | custom-call | flops 69000003584 | bytes 216000000 | tf_op jit(solution)/shard_map/feed_backward/pallas_call | solution.py:1204
  549.9 32.1 %tensor_sum.2.sum_ref.choice_ref = bf16[1568,768]{1,0:T(8,128)(2,1)} custom-call(bf16[1568,768]{1,0:T(8,128)(2,1)} %get-tuple-element.231.part_ref), custom_call_target="tpu_custom_call" | custom-call | flops 36800000000 | bytes 115200000 | tf_op jit(solution)/shard_map/tensor_sum/pallas_call | solution.py:175
  582.0 32.4 %attention_backward.4 = (bf16[1536,768]{1,0:T(8,128)(2,1)}, f32[1536,768]{1,0:T(8,128)}, f32[1,768]{1,0:T(1,128)}, f32[8,768]{1,0:T(8,128)}, bf16[3,1536,1152]{2...) custom-call(s32[4]{0:T(128)} %pad_add_fusion.5.meta, ...), custom_call_target="tpu_custom_call", output_to_operand_aliasing={{4}: (18, {}), {5}: (19, {})} | custom-call | flops 42550001664 | bytes 133200000 | tf_op jit(solution)/shard_map/attention_backward/pallas_call | solution.py:1401
  614.4 38.4 %input_relay.4 = (f32[1536,768]{1,0:T(8,128)}, bf16[1536,768]{1,0:T(8,128)(2,1)}, f32[1,768]{1,0:T(1,128)}) custom-call(bf16[1536,768]{1,0:T(8,128)(2,1)} %get-tuple-element.235.part_ref, bf16[3,1536,768]{2,1,0:T(8,128)(2,1)} %get-tuple-element.201.x_ref.layers_ref, f32[1536,768]{1,0:T(8,128)} %get-tuple-element.236.grad_state_ref, ...), custom_call_target="tpu_custom_call" | custom-call | flops 48299999232 | bytes 151200000 | tf_op jit(solution)/shard_map/input_relay/pallas_call | solution.py:468
  652.7 22.1 %lead_grads.1 = bf16[4,9,192,512]{3,2,1,0:T(8,128)(2,1)} custom-call(s32[4]{0:T(128)} %pad_add_fusion.7.meta, bf16[3072,768]{1,0:T(8,128)(2,1)} %cot_ref.7, bf16[1536,768]{1,0:T(8,128)(2,1)} %get-tuple-element.239.rec_ref, s32[2,8,1536]{2,1,0:T(8,128)} %copy.232.post_ref, f32[3,8,1536]{2,1,0:T(8,128)} %get-tuple-element.211.probs_ref, ...), custom_call_target="tpu_custom_call" | custom-call | flops 23000000512 | bytes 72000000 | tf_op jit(solution)/shard_map/lead_grads/pallas_call | solution.py:1573
  674.9 54.3 %feed_backward.5 = (bf16[1568,768]{1,0:T(8,128)(2,1)}, bf16[3,1536,768]{2,1,0:T(8,128)(2,1)}, bf16[3,8,480,512]{3,2,1,0:T(8,128)(2,1)}, bf16[3,8,480,512]{3,2,1,...) custom-call(s32[4]{0:T(128)} %pad_add_fusion.6.meta, ...), custom_call_target="tpu_custom_call", output_to_operand_aliasing={{1}: (17, {}), {2}: (18, {}), {3}: (19, {}), {4}: (20, {}),... | custom-call | flops 69000003584 | bytes 216000000 | tf_op jit(solution)/shard_map/feed_backward/pallas_call | solution.py:1204
  729.2 19.4 %expert_grads.1.before_ref = bf16[4,18,192,512]{3,2,1,0:T(8,128)(2,1)} custom-call(bf16[3,8,480,768]{3,2,1,0:T(8,128)(2,1)} %get-tuple-element.240.xa_ref.xb_ref.refs_0_.refs_1_, bf16[3,8,480,768]{3,2,1,0:T(8,128)(2,1)} %get-tuple-element.240.xa_ref.xb_ref.refs_0_.refs_1_, bf16[3,8,480,512]{3,2,1,0:T(8,128)(2,1)} %get-tuple-element.254.refs_2_.refs_3_, ...), custom_call_target="tpu_custom_call" | custom-call | flops 34500001792 | bytes 108000000 | tf_op jit(solution)/shard_map/expert_grads/pallas_call | solution.py:1463
  748.5 13.6 %shared_grads.1 = bf16[4,18,192,512]{3,2,1,0:T(8,128)(2,1)} custom-call(bf16[3,1536,768]{2,1,0:T(8,128)(2,1)} %get-tuple-element.213.b_ref, bf16[3,1536,768]{2,1,0:T(8,128)(2,1)} %get-tuple-element.250.dy_ref, bf16[3,1536,512]{2,1,0:T(8,128)(2,1)} %get-tuple-element.251.gate_ref, ...), custom_call_target="tpu_custom_call", output_to_operand_aliasing={{}: (5, {})} | custom-call | flops 14949999616 | bytes 46800000 | tf_op jit(solution)/shard_map/shared_grads/pallas_call | solution.py:1628
  762.2 32.1 %tensor_sum.3.sum_ref.choice_ref = bf16[1568,768]{1,0:T(8,128)(2,1)} custom-call(bf16[1568,768]{1,0:T(8,128)(2,1)} %get-tuple-element.258.part_ref), custom_call_target="tpu_custom_call" | custom-call | flops 36800000000 | bytes 115200000 | tf_op jit(solution)/shard_map/tensor_sum/pallas_call | solution.py:175
  794.3 27.8 %attention_backward.5 = (bf16[1536,768]{1,0:T(8,128)(2,1)}, f32[1536,768]{1,0:T(8,128)}, f32[1,768]{1,0:T(1,128)}, f32[8,768]{1,0:T(8,128)}, bf16[3,1536,1152]{2...) custom-call(s32[4]{0:T(128)} %pad_add_fusion.6.meta, ...), custom_call_target="tpu_custom_call", output_to_operand_aliasing={{4}: (18, {}), {5}: (19, {})} | custom-call | flops 42550001664 | bytes 133200000 | tf_op jit(solution)/shard_map/attention_backward/pallas_call | solution.py:1401
  822.1 14.2 %token_grads.1 = (bf16[768,1152]{1,0:T(8,128)(2,1)}, bf16[768,384]{1,0:T(8,128)(2,1)}) custom-call(bf16[3,1536,768]{2,1,0:T(8,128)(2,1)} %get-tuple-element.264.refs_0_, bf16[3,1536,768]{2,1,0:T(8,128)(2,1)} %get-tuple-element.265.refs_1_, bf16[3,1536,1152]{2,1,0:T(8,128)(2,1)} %get-tuple-element.266.refs_2_, ...), custom_call_target="tpu_custom_call" | custom-call | flops 16099999744 | bytes 50400000 | tf_op jit(solution)/shard_map/token_grads/pallas_call | solution.py:1671
  836.3 1.1 slice.94
  837.4 1.3 slice.92
  838.8 1.3 copy.241
  840.1 0.9 copy.239
  841.4 40.6 %input_relay.5 = (f32[1536,768]{1,0:T(8,128)}, bf16[1536,768]{1,0:T(8,128)(2,1)}, f32[1,768]{1,0:T(1,128)}) custom-call(bf16[1536,768]{1,0:T(8,128)(2,1)} %get-tuple-element.261.part_ref, bf16[3,1536,768]{2,1,0:T(8,128)(2,1)} %get-tuple-element.201.x_ref.layers_ref, f32[1536,768]{1,0:T(8,128)} %get-tuple-element.262.grad_state_ref, ...), custom_call_target="tpu_custom_call" | custom-call | flops 48299999232 | bytes 151200000 | tf_op jit(solution)/shard_map/input_relay/pallas_call | solution.py:468
  882.0 0.7 fusion.8
  882.9 8.6 broadcast_select_fusion.1
  891.5 36.5 %output_relay.5 = (bf16[1536,768]{1,0:T(8,128)(2,1)}, bf16[1536,768]{1,0:T(8,128)(2,1)}) custom-call(bf16[1536,768]{1,0:T(8,128)(2,1)} %get-tuple-element.206.part_ref, f32[3,1536,768]{2,1,0:T(8,128)} %get-tuple-element.207.states_ref.h_ref), custom_call_target="tpu_custom_call" | custom-call | flops 43699998720 | bytes 136800000 | tf_op jit(solution)/shard_map/output_relay/pallas_call | solution.py:334
  928.0 111.9 %reduce-scatter.6.cloned.1.call-done = bf16[1,18,192,512]{3,2,1,0:T(8,128)(2,1)} async-done(((bf16[4,18,192,512]{3,2,1,0:T(8,128)(2,1)}), bf16[1,18,192,512]{3,2,1,0:T(8,128)(2,1)}) %reduce-scatter.6.cloned.1.call-update) | async-done | bytes 3538960 | tf_op jit(solution)/shard_map/reduce_scatter | solution.py:1788
  1039.9 1.8 copy.242
  1041.7 2.9 broadcast_select_fusion.3
  1044.6 2.5 maximum_bitcast_fusion.1
  1047.1 6.8 maximum_bitcast_fusion
  1053.9 2.2 slice.104
  1056.7 1.3 convert.9
  1058.1 1.2 slice_convert_fusion
  1059.3 1.0 slice_bitcast_fusion.3
  1060.3 4.0 slice_bitcast_fusion
  1064.4 11.2 %reduce-scatter.8.cloned.1.call-done = bf16[1,192,784]{2,1,0:T(8,128)(2,1)} async-done(((bf16[4,192,784]{2,1,0:T(8,128)(2,1)}), bf16[1,192,784]{2,1,0:T(8,128)(2,1)}) %reduce-scatter.8.cloned.1.call-update) | async-done | bytes 301072 | tf_op jit(solution)/shard_map/reduce_scatter | solution.py:1788
  1075.6 1.0 bitcast_convert_fusion
  1076.6 0.8 slice_reduce_fusion
  1077.5 0.9 slice_bitcast_fusion.4
  1079.1 0.8 copy.246
  (93 shorter events, 12.0 us)
Async XLA Ops:
  7.2 8.5 copy-start.2
  7.2 53.3 %all-gather.9.cloned.1.call-start = ((), (), s32[]{:S(2)}) async-start(), calls=%async_computation.8 | async-start | bytes 1474560 | tf_op jit(solution)/shard_map/all_gather | solution.py:1765
  7.9 61.5 %all-gather.7.cloned.1.call-start = ((), (), s32[]{:S(2)}) async-start(), calls=%async_computation.7 | async-start | bytes 2949120 | tf_op jit(solution)/shard_map/all_gather | solution.py:1854
  8.0 8.6 copy-start.4
  19.9 22.6 %copy-start.9 = (s32[1,3072,2]{1,2,0:T(2,128)S(1)}, s32[1,3072,2]{1,2,0:T(2,128)}, u32[]{:S(2)}) copy-start(s32[1,3072,2]{1,2,0:T(2,128)} %param.21) | copy-start | bytes 73732
  19.9 23.3 %copy-start.10 = (bf16[1,768]{1,0:T(2,128)(2,1)S(1)}, bf16[1,768]{1,0:T(2,128)(2,1)}, u32[]{:S(2)}) copy-start(bf16[1,768]{1,0:T(2,128)(2,1)} %param.27) | copy-start | bytes 4612
  19.9 25.7 %copy-start.1 = (bf16[1,192,768]{2,1,0:T(8,128)(2,1)S(1)}, bf16[1,192,768]{2,1,0:T(8,128)(2,1)}, u32[]{:S(2)}) copy-start(bf16[1,192,768]{2,1,0:T(8,128)(2,1)} %param.26) | copy-start | bytes 884740
  42.4 324.6 %all-gather.11.cloned.1.call-start = ((), (), s32[]{:S(2)}) async-start(), calls=%async_computation.9 | async-start | bytes 2949120 | tf_op jit(solution)/shard_map/all_gather | solution.py:1863
  42.6 3.0 copy-start.3
  56.2 2.3 copy-start.5
  312.8 111.3 %all-reduce.5.cloned.1.call-start = ((), (), s32[]{:S(2)}) async-start(), calls=%async_computation.3 | async-start | bytes 4816896 | tf_op jit(solution)/shard_map/psum | solution.py:1866
  367.0 561.1 %reduce-scatter.4.cloned.1.call-start = ((), (), s32[]{:S(2)}) async-start(), calls=%async_computation.4 | async-start | bytes 8847360 | tf_op jit(solution)/shard_map/reduce_scatter | solution.py:1788
  674.8 365.1 %reduce-scatter.6.cloned.1.call-start = ((), (), s32[]{:S(2)}) async-start(), calls=%async_computation.5 | async-start | bytes 17694720 | tf_op jit(solution)/shard_map/reduce_scatter | solution.py:1788
  762.1 313.5 %reduce-scatter.8.cloned.1.call-start = ((), (), s32[]{:S(2)}) async-start(), calls=%async_computation.6 | async-start | bytes 1720320 | tf_op jit(solution)/shard_map/reduce_scatter | solution.py:1788
  841.3 40.7 %copy-start.6 = (f32[8,768]{1,0:T(8,128)S(1)}, f32[8,768]{1,0:T(8,128)}, u32[]{:S(2)}) copy-start(f32[8,768]{1,0:T(8,128)} %get-tuple-element.271) | copy-start | bytes 73732
  841.3 40.7 %copy-start.7 = (f32[8,768]{1,0:T(8,128)S(1)}, f32[8,768]{1,0:T(8,128)}, u32[]{:S(2)}) copy-start(f32[8,768]{1,0:T(8,128)} %get-tuple-element.274) | copy-start | bytes 73732
  841.3 40.7 %copy-start.8 = (f32[8,768]{1,0:T(8,128)S(1)}, f32[8,768]{1,0:T(8,128)}, u32[]{:S(2)}) copy-start(f32[8,768]{1,0:T(8,128)} %get-tuple-element.277) | copy-start | bytes 73732
  841.3 40.7 %copy-start.11 = (f32[1,768]{1,0:T(1,128)S(1)}, f32[1,768]{1,0:T(1,128)}, u32[]{:S(2)}) copy-start(f32[1,768]{1,0:T(1,128)} %get-tuple-element.270) | copy-start | bytes 9220
  841.3 40.7 %copy-start.12 = (f32[1,768]{1,0:T(1,128)S(1)}, f32[1,768]{1,0:T(1,128)}, u32[]{:S(2)}) copy-start(f32[1,768]{1,0:T(1,128)} %get-tuple-element.269) | copy-start | bytes 9220
  841.3 40.7 %copy-start.13 = (f32[1,768]{1,0:T(1,128)S(1)}, f32[1,768]{1,0:T(1,128)}, u32[]{:S(2)}) copy-start(f32[1,768]{1,0:T(1,128)} %get-tuple-element.273) | copy-start | bytes 9220
  841.3 40.7 %copy-start.14 = (f32[1,768]{1,0:T(1,128)S(1)}, f32[1,768]{1,0:T(1,128)}, u32[]{:S(2)}) copy-start(f32[1,768]{1,0:T(1,128)} %get-tuple-element.272) | copy-start | bytes 9220
  841.4 40.7 %copy-start.15 = (f32[1,768]{1,0:T(1,128)S(1)}, f32[1,768]{1,0:T(1,128)}, u32[]{:S(2)}) copy-start(f32[1,768]{1,0:T(1,128)} %get-tuple-element.276) | copy-start | bytes 9220
  1039.9 7.2 slice-start
  1041.7 5.4 slice-start.1
  1053.9 2.4 copy-start
Sparse Core Ops, SparseCore 0:
  9.6 20.1 all-gather.8
  42.5 26.8 all-gather.6
  312.9 24.2 all-gather.10
  367.1 56.9 all-reduce.4
  675.0 124.7 reduce-scatter.3
  802.1 237.7 reduce-scatter.5
  1042.3 33.2 reduce-scatter.7
